TPU v7x, 32 devices: a whole 2x2x4 slice. The times are simulated.
32 devices in a mesh: ctx: 8 (over z, x), wsh: 4 (over y, core).
Axes of the slice: x: 2, y: 2, z: 4, core: 2. Of those that a mesh axis runs over, the one named last changes fastest.
Arguments:
- inputs: bfloat16 [2, 4, 2048, 1024], P(None, 'wsh', 'ctx'), may hold values from -6 to 6
- cotangent: bfloat16 [2, 4, 2048, 1024], P(None, 'wsh', 'ctx'), may hold values from -6 to 6
- lengths: int32 [2, 4, 4], P(None, 'wsh'), may hold values from 0 to 2048, as said below
- norm1_gain: float32 [1024], replicated, may hold values from 0.5 to 1.5
- in_weight: bfloat16 [1024, 3328], P('wsh'), may hold values from -0.1875 to 0.1875
- dt_weight: bfloat16 [1024, 24], P('wsh'), may hold values from -0.1875 to 0.1875
- conv_weight: float32 [4, 1792], replicated, may hold values from -3 to 3
- conv_bias: float32 [1792], replicated, may hold values from -3 to 3
- dt_bias: float32 [24], replicated, may hold values from -2 to 0
- decay_rate: float32 [24], replicated, may hold values from 0.00012207031 to 0.1
- skip_gain: float32 [24], replicated, may hold values from 0.5 to 1.5
- mamba_gain: float32 [1536], replicated, may hold values from 0.5 to 1.5
- out_weight: bfloat16 [1536, 1024], P('wsh'), may hold values from -0.15625 to 0.15625
- q_weight: bfloat16 [1024, 512], P('wsh'), may hold values from -0.1875 to 0.1875
- kv_weight: bfloat16 [1024, 256], P('wsh'), may hold values from -0.1875 to 0.1875
- o_weight: bfloat16 [512, 1024], P('wsh'), may hold values from -1 to 1
- norm2_gain: float32 [1024], replicated, may hold values from 0.5 to 1.5
- gu_weight: bfloat16 [1024, 4096], P('wsh'), may hold values from -0.1875 to 0.1875
- down_weight: bfloat16 [2048, 1024], P('wsh'), may hold values from -0.125 to 0.125
Outputs:
- layer_out: bfloat16 [2, 4, 2048, 1024], P(None, 'wsh', 'ctx')
- input_grad: bfloat16 [2, 4, 2048, 1024], P(None, 'wsh', 'ctx')
- grad_norm1_gain: float32 [1024], replicated
- grad_in_weight: float32 [1024, 3328], P('wsh')
- grad_dt_weight: float32 [1024, 24], P('wsh')
- grad_conv_weight: float32 [4, 1792], replicated
- grad_conv_bias: float32 [1792], replicated
- grad_dt_bias: float32 [24], replicated
- grad_decay_rate: float32 [24], replicated
- grad_skip_gain: float32 [24], replicated
- grad_mamba_gain: float32 [1536], replicated
- grad_out_weight: float32 [1536, 1024], P('wsh')
- grad_q_weight: float32 [1024, 512], P('wsh')
- grad_kv_weight: float32 [1024, 256], P('wsh')
- grad_o_weight: float32 [512, 1024], P('wsh')
- grad_norm2_gain: float32 [1024], replicated
- grad_gu_weight: float32 [1024, 4096], P('wsh')
- grad_down_weight: float32 [2048, 1024], P('wsh')
Inputs may be any that keep to these rules, and one draw needn't show every extreme that they name: Each row (micro-batch, group) lists the stream's sequence lengths in order; they sum to 2048, zeros stand only at the end, every nonzero length is at least min(1024, 2048), and in each group one micro-batch holds a single sequence of 2048 tokens.
All inputs are finite; a program needn't handle non-finite values.
Results may differ from a plain program's by a relative error of at most 0.02.
Values may be sent and summed in bfloat16 or wider, within the bound.
A program may use at most 320 MiB of HBM per device.

v0:
```python
import jax
import jax.numpy as jnp
from jax import lax
from jax.sharding import PartitionSpec as P

FF = 2048
MHEADS = 24
MDIM = 64
STATE = 128
KVHEADS = 2
HDIM = 64
DSSM = 1536


NORM_EPS = 1e-05
PRECISE = lax.Precision.HIGHEST
MASKED_SCORE = -1e30


def passed_along(block, axis, distance):
    devices = range(lax.axis_size(axis))
    route = [(i - distance, i) for i in devices if i - distance in devices]
    return lax.ppermute(block, axis, route)


def carried_in(array, axis, join, neutral):
    place = lax.axis_index(axis)
    gathered = jax.tree.map(
        lambda a, kind: lax.all_gather(a.astype(kind), axis), array, (jnp.bfloat16, jnp.bfloat16)
    )
    state = jax.tree.map(lambda a, e: jnp.zeros_like(a) + jnp.asarray(e, a.dtype), array, neutral)

    def one(lap, state):
        return join(
            state,
            jax.tree.map(
                lambda a, own: lax.dynamic_index_in_dim(a, lap, 0, False).astype(own.dtype),
                gathered,
                array,
            ),
        )

    return lax.fori_loop(0, place, one, state)


def carried_in_2(array, axis, combine, identity):
    length, mine = (lax.axis_size(axis), lax.axis_index(axis))
    everything = jax.tree.map(
        lambda part, kind: lax.all_gather(part.astype(kind), axis),
        array,
        jax.tree.map(lambda a: jnp.bfloat16 if a.dtype == jnp.float32 else a.dtype, array),
    )
    start = jax.tree.map(
        lambda part, zero: jnp.broadcast_to(jnp.asarray(zero, part.dtype), part.shape),
        array,
        identity,
    )

    def lap(k, before):
        at = length - 1 - k
        reached = at > mine
        new = combine(
            before, jax.tree.map(lambda part, own: part[at].astype(own.dtype), everything, array)
        )
        return jax.tree.map(lambda a, b: jnp.where(reached, a, b), new, before)

    return lax.fori_loop(0, length, lap, start)


def shortened(array):

    def short(part):
        return part.astype(jnp.bfloat16) if part.dtype == jnp.float32 else part

    return jax.tree.map(short, array)


def mat_low(left, right):
    return jnp.dot(left, right, preferred_element_type=jnp.float32)


def mat_left_t(left, right):
    return lax.dot_general(
        left, right, (((0,), (0,)), ((), ())), preferred_element_type=jnp.float32
    )


def mat_right_t(left, right):
    return lax.dot_general(
        left, right, (((1,), (1,)), ((), ())), preferred_element_type=jnp.float32
    )


def add_tuples(first_set, second_set):
    return tuple((left + right for left, right in zip(first_set, second_set)))


def keep_carry(carry_in):
    return carry_in


def rms_scale(features, gain_row):
    return (
        features
        * lax.rsqrt(jnp.mean(features * features, axis=-1, keepdims=True) + NORM_EPS)
        * gain_row
    )


def seq_starts(lengths_row, positions):
    end_points = jnp.cumsum(lengths_row, dtype=jnp.int32)
    begins = end_points - lengths_row
    picked = jnp.where(begins[None, :] <= positions[:, None], begins[None, :], 0)
    return jnp.max(picked, axis=1)


def conv_apply(extended, weight, bias_row, positions, starts):
    row_count = positions.shape[0]
    tap_count = weight.shape[0]
    conv_sum = jnp.zeros((row_count, weight.shape[1]), jnp.float32) + bias_row
    for tap_index in range(tap_count):
        valid_rows = (positions - (tap_count - 1) + tap_index >= starts).astype(jnp.float32)
        conv_sum = (
            conv_sum
            + weight[tap_index] * extended[tap_index : tap_index + row_count] * valid_rows[:, None]
        )
    return conv_sum


def decay_sums(step_sizes, decay_rates):
    return jnp.cumsum(-step_sizes * decay_rates[None, :], axis=0)


def ssd_output(
    inner_x,
    b_rows,
    c_rows,
    step_sizes,
    decay_rates,
    skip_gains,
    state_in,
    positions,
    starts,
    first_pos,
):
    log_decay = decay_sums(step_sizes, decay_rates)
    allowed = (positions[None, :] <= positions[:, None]) & (positions[None, :] >= starts[:, None])
    log_gaps = log_decay.T[:, :, None] - log_decay.T[:, None, :]
    decays = jnp.where(allowed[None], jnp.exp(jnp.where(allowed[None], log_gaps, 0.0)), 0.0)
    inner_prod = jnp.dot(c_rows, b_rows.T, precision=PRECISE)
    scaled = inner_x * step_sizes[:, :, None]
    local_part = jnp.einsum("hij,jhp->ihp", decays * inner_prod[None], scaled, precision=PRECISE)
    carried = (starts < first_pos).astype(jnp.float32)
    incoming = jnp.einsum("in,hpn->ihp", c_rows, state_in, precision=PRECISE)
    return (
        local_part
        + jnp.exp(log_decay)[:, :, None] * carried[:, None, None] * incoming
        + skip_gains[None, :, None] * inner_x
    )


def ssd_state(inner_x, b_rows, step_sizes, decay_rates, positions, starts, first_pos):
    log_decay = decay_sums(step_sizes, decay_rates)
    keep_rows = (positions >= starts[-1]).astype(jnp.float32)
    factors = jnp.exp(log_decay[-1][None, :] - log_decay) * step_sizes * keep_rows[:, None]
    fresh_state = jnp.einsum("jh,jhp,jn->hpn", factors, inner_x, b_rows, precision=PRECISE)
    decay_total = jnp.exp(log_decay[-1]) * (starts[-1] < first_pos).astype(jnp.float32)
    return (decay_total, fresh_state)


def chain_join(earlier, later):
    return (earlier[0] * later[0], earlier[1] * later[0][:, None, None] + later[1])


def chain_back(earlier, later):
    return (earlier[0] * later[0], later[1] + later[0][:, None, None] * earlier[1])


def head_split(rows_in, kv_heads, head_dim):
    return rows_in.reshape(rows_in.shape[0], kv_heads, -1, head_dim)


def span_tools(q_heads, key_table, pos_span, start_span, key_pos, k_span, head_dim):
    kv_heads = q_heads.shape[1]
    kv_width = kv_heads * head_dim
    score_scale = head_dim ** (-0.5)
    top_pos = jnp.max(pos_span)
    least_start = jnp.min(start_span)

    def block_parts(block_index):
        begin_row = block_index * k_span
        key_block = lax.dynamic_slice_in_dim(key_table, begin_row, k_span, 0)
        key_heads = key_block[:, :kv_width].reshape(k_span, kv_heads, head_dim)
        value_heads = key_block[:, kv_width:].reshape(k_span, kv_heads, head_dim)
        scores = (
            jnp.einsum("rghd,kgd->ghrk", q_heads, key_heads, preferred_element_type=jnp.float32)
            * score_scale
        )
        block_pos = lax.dynamic_slice_in_dim(key_pos, begin_row, k_span, 0)
        allowed = (block_pos[None, :] <= pos_span[:, None]) & (
            block_pos[None, :] >= start_span[:, None]
        )
        return (scores, allowed[None, None], key_heads, value_heads)

    def needed(block_index):
        begin_row = block_index * k_span
        return (top_pos >= begin_row) & (least_start < begin_row + k_span)

    return (block_parts, needed)


def attend_forward(queries, key_table, q_pos, q_start, key_pos, kv_heads, head_dim):
    row_count = queries.shape[0]
    key_count = key_table.shape[0]
    q_span = min(128, row_count)
    k_span = min(512, key_count)
    blocks = key_count // k_span
    outputs = []
    log_parts = []
    for span_index in range(row_count // q_span):
        lower_row = span_index * q_span
        q_heads = head_split(queries[lower_row : lower_row + q_span], kv_heads, head_dim)
        groups = q_heads.shape[2]
        block_parts, needed = span_tools(
            q_heads,
            key_table,
            q_pos[lower_row : lower_row + q_span],
            q_start[lower_row : lower_row + q_span],
            key_pos,
            k_span,
            head_dim,
        )

        def first_pass(block_index, carry_now):

            def first_compute(carry_in):
                run_max, run_sum = carry_in
                scores, allowed, key_heads, value_heads = block_parts(block_index)
                masked = jnp.where(allowed, scores, MASKED_SCORE)
                new_max = jnp.maximum(run_max, jnp.max(masked, axis=-1))
                expo_terms = jnp.where(allowed, jnp.exp(masked - new_max[..., None]), 0.0)
                return (
                    new_max,
                    run_sum * jnp.exp(run_max - new_max) + jnp.sum(expo_terms, axis=-1),
                )

            return lax.cond(needed(block_index), first_compute, keep_carry, carry_now)

        start_carry = (
            jnp.full((kv_heads, groups, q_span), MASKED_SCORE, jnp.float32),
            jnp.zeros((kv_heads, groups, q_span), jnp.float32),
        )
        run_max, run_sum = lax.fori_loop(0, blocks, first_pass, start_carry)
        log_total = run_max + jnp.log(run_sum)

        def second_pass(block_index, carry_now):

            def second_compute(carry_in):
                scores, allowed, key_heads, value_heads = block_parts(block_index)
                shifted = jnp.where(allowed, scores - log_total[..., None], MASKED_SCORE)
                prob_rows = jnp.where(allowed, jnp.exp(shifted), 0.0).astype(jnp.bfloat16)
                return carry_in + jnp.einsum(
                    "ghrk,kgd->rghd", prob_rows, value_heads, preferred_element_type=jnp.float32
                )

            return lax.cond(needed(block_index), second_compute, keep_carry, carry_now)

        summed = lax.fori_loop(
            0, blocks, second_pass, jnp.zeros((q_span, kv_heads, groups, head_dim), jnp.float32)
        )
        outputs.append(summed.reshape(q_span, -1).astype(jnp.bfloat16))
        log_parts.append(log_total)
    return (jnp.concatenate(outputs, axis=0), jnp.concatenate(log_parts, axis=-1))


def attend_backward(
    queries, key_table, attended, log_totals, grad_out, q_pos, q_start, key_pos, kv_heads, head_dim
):
    row_count = queries.shape[0]
    key_count = key_table.shape[0]
    q_span = min(128, row_count)
    k_span = min(512, key_count)
    blocks = key_count // k_span
    kv_width = kv_heads * head_dim
    score_scale = head_dim ** (-0.5)
    grad_table = jnp.zeros((key_count, 2 * kv_width), jnp.float32)
    grad_parts = []
    for span_index in range(row_count // q_span):
        lower_row = span_index * q_span
        q_heads = head_split(queries[lower_row : lower_row + q_span], kv_heads, head_dim)
        grad_heads = head_split(grad_out[lower_row : lower_row + q_span], kv_heads, head_dim)
        out_heads = head_split(attended[lower_row : lower_row + q_span], kv_heads, head_dim)
        log_span = log_totals[..., lower_row : lower_row + q_span]
        delta_rows = jnp.einsum(
            "rghd,rghd->ghr", grad_heads, out_heads, preferred_element_type=jnp.float32
        )
        block_parts, needed = span_tools(
            q_heads,
            key_table,
            q_pos[lower_row : lower_row + q_span],
            q_start[lower_row : lower_row + q_span],
            key_pos,
            k_span,
            head_dim,
        )

        def back_pass(block_index, carry_now):

            def back_compute(carry_in):
                grad_query, table_now = carry_in
                scores, allowed, key_heads, value_heads = block_parts(block_index)
                shifted = jnp.where(allowed, scores - log_span[..., None], MASKED_SCORE)
                prob_rows = jnp.where(allowed, jnp.exp(shifted), 0.0)
                grad_probs = jnp.einsum(
                    "rghd,kgd->ghrk", grad_heads, value_heads, preferred_element_type=jnp.float32
                )
                grad_scores = (prob_rows * (grad_probs - delta_rows[..., None])).astype(
                    jnp.bfloat16
                )
                grad_query = (
                    grad_query
                    + jnp.einsum(
                        "ghrk,kgd->rghd", grad_scores, key_heads, preferred_element_type=jnp.float32
                    )
                    * score_scale
                )
                grad_keys = (
                    jnp.einsum(
                        "ghrk,rghd->kgd", grad_scores, q_heads, preferred_element_type=jnp.float32
                    )
                    * score_scale
                )
                grad_values = jnp.einsum(
                    "ghrk,rghd->kgd",
                    prob_rows.astype(jnp.bfloat16),
                    grad_heads,
                    preferred_element_type=jnp.float32,
                )
                update = jnp.concatenate(
                    [grad_keys.reshape(k_span, kv_width), grad_values.reshape(k_span, kv_width)],
                    axis=1,
                )
                begin_row = block_index * k_span
                current = lax.dynamic_slice_in_dim(table_now, begin_row, k_span, 0)
                table_now = lax.dynamic_update_slice_in_dim(
                    table_now, current + update, begin_row, 0
                )
                return (grad_query, table_now)

            return lax.cond(needed(block_index), back_compute, keep_carry, carry_now)

        grad_query, grad_table = lax.fori_loop(
            0, blocks, back_pass, (jnp.zeros(q_heads.shape, jnp.float32), grad_table)
        )
        grad_parts.append(grad_query.reshape(q_span, -1))
    return (jnp.concatenate(grad_parts, axis=0), grad_table)


def reduce_weights(weight_grads):
    return (
        lax.psum_scatter(
            weight_grads[0].astype(jnp.bfloat16), "wsh", scatter_dimension=0, tiled=True
        ).astype(jnp.float32),
        lax.psum_scatter(
            weight_grads[1].astype(jnp.bfloat16), "wsh", scatter_dimension=0, tiled=True
        ).astype(jnp.float32),
        lax.psum_scatter(
            weight_grads[2].astype(jnp.bfloat16), "wsh", scatter_dimension=0, tiled=True
        ).astype(jnp.float32),
        lax.psum_scatter(
            weight_grads[3].astype(jnp.bfloat16), "wsh", scatter_dimension=0, tiled=True
        ).astype(jnp.float32),
        lax.psum_scatter(
            weight_grads[4].astype(jnp.bfloat16), "wsh", scatter_dimension=0, tiled=True
        ).astype(jnp.float32),
        lax.psum_scatter(
            weight_grads[5].astype(jnp.bfloat16), "wsh", scatter_dimension=0, tiled=True
        ).astype(jnp.float32),
        lax.psum_scatter(
            weight_grads[6].astype(jnp.bfloat16), "wsh", scatter_dimension=0, tiled=True
        ).astype(jnp.float32),
        lax.psum_scatter(
            weight_grads[7].astype(jnp.bfloat16), "wsh", scatter_dimension=0, tiled=True
        ).astype(jnp.float32),
    )


def local(
    inputs,
    cotangent,
    lengths,
    norm1_gain,
    in_weight,
    dt_weight,
    conv_weight,
    conv_bias,
    dt_bias,
    decay_rate,
    skip_gain,
    mamba_gain,
    out_weight,
    q_weight,
    kv_weight,
    o_weight,
    norm2_gain,
    gu_weight,
    down_weight,
):
    micro_count = inputs.shape[0]
    row_count = inputs.shape[2]
    ctx_count = lax.axis_size("ctx")
    my_index = lax.axis_index("ctx")
    stream_len = row_count * ctx_count
    first_pos = my_index * row_count
    own_pos = first_pos + jnp.arange(row_count, dtype=jnp.int32)
    all_pos = jnp.arange(stream_len, dtype=jnp.int32)
    tap_count = conv_weight.shape[0]
    sharded = (
        in_weight,
        dt_weight,
        out_weight,
        q_weight,
        kv_weight,
        o_weight,
        gu_weight,
        down_weight,
    )
    small_params = (
        norm1_gain,
        conv_weight,
        conv_bias,
        dt_bias,
        decay_rate,
        skip_gain,
        mamba_gain,
        norm2_gain,
    )
    small_sums = tuple((jnp.zeros(tensor.shape, jnp.float32) for tensor in small_params))
    shard_sums = tuple((jnp.zeros(tensor.shape, jnp.float32) for tensor in sharded))
    identity = (jnp.ones((MHEADS,), jnp.float32), jnp.zeros((MHEADS, MDIM, STATE), jnp.float32))
    layer_rows = []
    grad_rows = []
    for micro_index in range(micro_count):
        full_in, full_dt, full_out, full_query, full_kv, full_o, full_gu, full_down = (
            lax.all_gather(sharded[0], "wsh", axis=0, tiled=True),
            lax.all_gather(sharded[1], "wsh", axis=0, tiled=True),
            lax.all_gather(sharded[2], "wsh", axis=0, tiled=True),
            lax.all_gather(sharded[3], "wsh", axis=0, tiled=True),
            lax.all_gather(sharded[4], "wsh", axis=0, tiled=True),
            lax.all_gather(sharded[5], "wsh", axis=0, tiled=True),
            lax.all_gather(sharded[6], "wsh", axis=0, tiled=True),
            lax.all_gather(sharded[7], "wsh", axis=0, tiled=True),
        )
        features = inputs[micro_index, 0].astype(jnp.float32)
        lengths_row = lengths[micro_index, 0]
        own_start = seq_starts(lengths_row, own_pos)
        normed_f, norm_one_pull = jax.vjp(rms_scale, features, norm1_gain)
        normed = normed_f.astype(jnp.bfloat16)
        projected = mat_low(normed, full_in)
        gate_z = projected[:, :DSSM]
        conv_rows = projected[:, DSSM:]
        dt_raw = mat_low(normed, full_dt)
        step_sizes = jax.nn.softplus(dt_raw + dt_bias)
        edge_rows = passed_along(conv_rows[row_count - tap_count + 1 :], "ctx", 1)
        extended = jnp.concatenate([edge_rows, conv_rows], axis=0)

        def conv_layer(ext_arg, weight_arg, bias_arg):
            return jax.nn.silu(conv_apply(ext_arg, weight_arg, bias_arg, own_pos, own_start))

        activated, conv_pull = jax.vjp(conv_layer, extended, conv_weight, conv_bias)
        inner_x = activated[:, :DSSM].reshape(row_count, MHEADS, MDIM)
        b_rows = activated[:, DSSM : DSSM + STATE]
        c_rows = activated[:, DSSM + STATE :]

        def state_core(inner_arg, b_arg, dt_arg, rate_arg):
            return ssd_state(inner_arg, b_arg, dt_arg, rate_arg, own_pos, own_start, first_pos)

        (decay_total, fresh_state), state_pull = jax.vjp(
            state_core, inner_x, b_rows, step_sizes, decay_rate
        )
        chain_total, state_in = carried_in((decay_total, fresh_state), "ctx", chain_join, identity)

        def mamba_core(inner_arg, b_arg, c_arg, dt_arg, rate_arg, skip_arg, state_arg):
            return ssd_output(
                inner_arg,
                b_arg,
                c_arg,
                dt_arg,
                rate_arg,
                skip_arg,
                state_arg,
                own_pos,
                own_start,
                first_pos,
            )

        scanned, core_pull = jax.vjp(
            mamba_core, inner_x, b_rows, c_rows, step_sizes, decay_rate, skip_gain, state_in
        )

        def gated_norm(scan_arg, gate_arg, gain_arg):
            return rms_scale(scan_arg.reshape(row_count, DSSM) * jax.nn.silu(gate_arg), gain_arg)

        gated_rows, gated_pull = jax.vjp(gated_norm, scanned, gate_z, mamba_gain)
        mixed_rows = gated_rows.astype(jnp.bfloat16)
        mamba_out = mat_low(mixed_rows, full_out)
        queries = mat_low(normed, full_query).astype(jnp.bfloat16)
        kv_rows = mat_low(normed, full_kv).astype(jnp.bfloat16)
        key_table = lax.all_gather(kv_rows, "ctx", axis=0, tiled=True)
        q_start = seq_starts(lengths_row, own_pos)
        attended_here, log_totals = attend_forward(
            queries, key_table, own_pos, q_start, all_pos, KVHEADS, HDIM
        )
        attn_out = mat_low(attended_here, full_o)
        middle = features + mamba_out + attn_out
        norm_two, norm_two_pull = jax.vjp(rms_scale, middle, norm2_gain)
        normed_two = norm_two.astype(jnp.bfloat16)
        gate_up = mat_low(normed_two, full_gu)
        gate_part = gate_up[:, :FF]
        up_part = gate_up[:, FF:]
        sig_gate = jax.nn.sigmoid(gate_part)
        hidden = (gate_part * sig_gate * up_part).astype(jnp.bfloat16)
        layer_rows.append((middle + mat_low(hidden, full_down)).astype(jnp.bfloat16))
        grad_top = cotangent[micro_index, 0]
        grad_down = mat_left_t(hidden, grad_top)
        grad_hidden = mat_right_t(grad_top, full_down)
        grad_gate = grad_hidden * up_part * sig_gate * (1.0 + gate_part * (1.0 - sig_gate))
        grad_up = grad_hidden * gate_part * sig_gate
        grad_gu_rows = jnp.concatenate([grad_gate, grad_up], axis=1).astype(jnp.bfloat16)
        grad_gu = mat_left_t(normed_two, grad_gu_rows)
        grad_normed_two = mat_right_t(grad_gu_rows, full_gu)
        grad_middle_norm, grad_norm2 = norm_two_pull(grad_normed_two)
        grad_middle = grad_top.astype(jnp.float32) + grad_middle_norm
        branch_grad = grad_middle.astype(jnp.bfloat16)
        grad_o = mat_left_t(attended_here, branch_grad)
        grad_attended = mat_right_t(branch_grad, full_o).astype(jnp.bfloat16)
        grad_out_w = mat_left_t(mixed_rows, branch_grad)
        grad_mixed = mat_right_t(branch_grad, full_out)
        grad_q_here, kv_partial = attend_backward(
            queries,
            key_table,
            attended_here,
            log_totals,
            grad_attended,
            own_pos,
            q_start,
            all_pos,
            KVHEADS,
            HDIM,
        )
        grad_queries = grad_q_here.astype(jnp.bfloat16)
        grad_kv_rows = lax.psum_scatter(
            kv_partial.astype(jnp.bfloat16), "ctx", scatter_dimension=0, tiled=True
        )
        grad_query_w = mat_left_t(normed, grad_queries)
        grad_kv_w = mat_left_t(normed, grad_kv_rows)
        grad_normed = mat_right_t(grad_queries, full_query) + mat_right_t(grad_kv_rows, full_kv)
        grad_scanned, grad_gate_z, grad_mamba_gain = gated_pull(grad_mixed)
        grad_inner, grad_b, grad_c, grad_dt, grad_rate, grad_skip, grad_state = core_pull(
            grad_scanned
        )
        later_total, state_later = carried_in_2(
            (decay_total, grad_state), "ctx", chain_back, identity
        )
        grad_total = jnp.sum(state_later * state_in, axis=(1, 2))
        grad_inner_end, grad_b_end, grad_dt_end, grad_rate_end = state_pull(
            (grad_total, state_later)
        )
        grad_act = jnp.concatenate(
            [(grad_inner + grad_inner_end).reshape(row_count, DSSM), grad_b + grad_b_end, grad_c],
            axis=1,
        )
        grad_extended, grad_conv_w, grad_conv_b = conv_pull(grad_act)
        edge_back = passed_along(grad_extended[: tap_count - 1], "ctx", -1)
        grad_conv_rows = (
            grad_extended[tap_count - 1 :].at[row_count - tap_count + 1 :].add(edge_back)
        )
        grad_dt_raw = (grad_dt + grad_dt_end) * jax.nn.sigmoid(dt_raw + dt_bias)
        grad_dt_bias = jnp.sum(grad_dt_raw, axis=0)
        dt_rounded = grad_dt_raw.astype(jnp.bfloat16)
        grad_proj = jnp.concatenate([grad_gate_z, grad_conv_rows], axis=1).astype(jnp.bfloat16)
        grad_in_w = mat_left_t(normed, grad_proj)
        grad_dt_w = mat_left_t(normed, dt_rounded)
        grad_normed = (
            grad_normed + mat_right_t(grad_proj, full_in) + mat_right_t(dt_rounded, full_dt)
        )
        grad_feat_norm, grad_norm1 = norm_one_pull(grad_normed)
        grad_rows.append((grad_middle + grad_feat_norm).astype(jnp.bfloat16))
        small_sums = add_tuples(
            small_sums,
            (
                grad_norm1,
                grad_conv_w,
                grad_conv_b,
                grad_dt_bias,
                grad_rate + grad_rate_end,
                grad_skip,
                grad_mamba_gain,
                grad_norm2,
            ),
        )
        weight_grads = (
            grad_in_w,
            grad_dt_w,
            grad_out_w,
            grad_query_w,
            grad_kv_w,
            grad_o,
            grad_gu,
            grad_down,
        )
        shard_sums = add_tuples(shard_sums, reduce_weights(weight_grads))
    totals = jax.tree.map(
        lambda part: part.astype(jnp.float32), lax.psum(shortened(shard_sums), "ctx")
    )
    small_totals = lax.psum(small_sums, ("ctx", "wsh"))
    layer_out = jnp.stack(layer_rows)[:, None]
    input_grad = jnp.stack(grad_rows)[:, None]
    return (
        layer_out,
        input_grad,
        small_totals[0],
        totals[0],
        totals[1],
        small_totals[1],
        small_totals[2],
        small_totals[3],
        small_totals[4],
        small_totals[5],
        small_totals[6],
        totals[2],
        totals[3],
        totals[4],
        totals[5],
        small_totals[7],
        totals[6],
        totals[7],
    )


def solution(mesh):
    in_specs = (
        P(None, "wsh", "ctx", None),
        P(None, "wsh", "ctx", None),
        P(None, "wsh", None),
        P(),
        P("wsh", None),
        P("wsh", None),
        P(),
        P(),
        P(),
        P(),
        P(),
        P(),
        P("wsh", None),
        P("wsh", None),
        P("wsh", None),
        P("wsh", None),
        P(),
        P("wsh", None),
        P("wsh", None),
    )
    out_specs = (
        P(None, "wsh", "ctx", None),
        P(None, "wsh", "ctx", None),
        P(),
        P("wsh", None),
        P("wsh", None),
        P(),
        P(),
        P(),
        P(),
        P(),
        P(),
        P("wsh", None),
        P("wsh", None),
        P("wsh", None),
        P("wsh", None),
        P(),
        P("wsh", None),
        P("wsh", None),
    )
    return jax.shard_map(local, mesh=mesh, in_specs=in_specs, out_specs=out_specs, check_vma=False)
```

profile of v0, /device:TPU:0, one launch (start us, length us, event | category | flops | bytes accessed | tf_op | source)
XLA Modules:
  0.0 1670.3 jit_solution(18140026336404398380)
XLA Ops:
  33.2 28.8 %all-gather.19.cloned.1.call-done = bf16[1024,3328]{1,0:T(8,128)(2,1)} async-done(((bf16[256,3328]{1,0:T(8,128)(2,1)}), bf16[1024,3328]{1,0:T(8,128)(2,1)}) %all-gather.19.cloned.1.call-update) | async-done | bytes 6815760 | tf_op jit(solution)/shard_map/all_gather | solution.py:445
  109.3 21.5 %all-gather.5 = bf16[8,1,24]{2,1,0:T(2,128)(2,1)S(1)} all-gather(bf16[1,1,24]{2,1,0:T(2,128)(2,1)S(1)} %bitcast.1154), channel_id=1, replica_groups=mesh['ctx'=8,'wsh'=4] {'ctx'}, dimensions={0}, use_global_device_ids=true | all-gather | bytes 432 | tf_op jit(solution)/shard_map/all_gather | solution.py:29
  131.6 16.2 all-gather.4
  214.1 12.6 all-gather.37.cloned.1.call-done
  241.5 47.0 %all-gather.35.cloned.1.call-done = bf16[192,64,128]{2,1,0:T(8,128)(2,1)} async-done(((bf16[24,64,128]{2,1,0:T(8,128)(2,1)}), bf16[192,64,128]{2,1,0:T(8,128)(2,1)}) %all-gather.35.cloned.1.call-update) | async-done | bytes 3145744 | tf_op jit(solution)/shard_map/all_gather | solution.py:29
  321.6 13.9 all-gather.27.cloned.1.call-done
  345.2 50.3 %all-gather.29.cloned.1.call-done = bf16[1024,4096]{1,0:T(8,128)(2,1)} async-done(((bf16[256,4096]{1,0:T(8,128)(2,1)}), bf16[1024,4096]{1,0:T(8,128)(2,1)}) %all-gather.29.cloned.1.call-update) | async-done | bytes 8388624 | tf_op jit(solution)/shard_map/all_gather | solution.py:451
  407.9 23.5 %all-gather.31.cloned.1.call-done = bf16[2048,1024]{1,0:T(8,128)(2,1)} async-done(((bf16[512,1024]{1,0:T(8,128)(2,1)}), bf16[2048,1024]{1,0:T(8,128)(2,1)}) %all-gather.31.cloned.1.call-update) | async-done | bytes 4194320 | tf_op jit(solution)/shard_map/all_gather | solution.py:452
  452.8 14.4 while.266
  468.5 11.4 while.267
  485.3 10.4 while.264
  496.6 11.5 while.265
  556.8 27.4 %reduce-scatter.21.cloned.1.call-done = bf16[256,256]{0,1:T(8,128)(2,1)} async-done(((bf16[2048,256]{0,1:T(8,128)(2,1)}), bf16[256,256]{0,1:T(8,128)(2,1)}) %reduce-scatter.21.cloned.1.call-update) | async-done | bytes 131088 | tf_op jit(solution)/shard_map/reduce_scatter | solution.py:552
  586.6 64.1 %reduce-scatter.19.cloned.1.call-done = bf16[256,256]{0,1:T(8,128)(2,1)} async-done(((bf16[2048,256]{0,1:T(8,128)(2,1)}), bf16[256,256]{0,1:T(8,128)(2,1)}) %reduce-scatter.19.cloned.1.call-update) | async-done | bytes 131088 | tf_op jit(solution)/shard_map/reduce_scatter | solution.py:552
  693.7 11.4 fusion.149
  731.9 15.3 while.269
  756.8 16.8 %all-gather.39.cloned.1.call-done = bf16[192,64,128]{2,1,0:T(8,128)(2,1)} async-done(((bf16[24,64,128]{2,1,0:T(8,128)(2,1)}), bf16[192,64,128]{2,1,0:T(8,128)(2,1)}) %all-gather.39.cloned.1.call-update) | async-done | bytes 3145744 | tf_op jit(solution)/shard_map/all_gather | solution.py:49
  773.5 15.1 while.268
  854.2 27.5 %reduce-scatter.43.cloned.1.call-done = bf16[128,1024]{1,0:T(8,128)(2,1)} async-done(((bf16[512,1024]{1,0:T(8,128)(2,1)}), bf16[128,1024]{1,0:T(8,128)(2,1)}) %reduce-scatter.43.cloned.1.call-update) | async-done | bytes 262160 | tf_op jit(solution)/shard_map/reduce_scatter | solution.py:376
  883.5 22.4 %reduce-scatter.41.cloned.1.call-done = bf16[256,256]{1,0:T(8,128)(2,1)} async-done(((bf16[1024,256]{1,0:T(8,128)(2,1)}), bf16[256,256]{1,0:T(8,128)(2,1)}) %reduce-scatter.41.cloned.1.call-update) | async-done | bytes 131088 | tf_op jit(solution)/shard_map/reduce_scatter | solution.py:373
  905.8 24.2 %reduce-scatter.39.cloned.1.call-done = bf16[256,256]{1,0:T(8,128)(2,1)} async-done(((bf16[1024,256]{1,0:T(8,128)(2,1)}), bf16[256,256]{1,0:T(8,128)(2,1)}) %reduce-scatter.39.cloned.1.call-update) | async-done | bytes 131088 | tf_op jit(solution)/shard_map/reduce_scatter | solution.py:373
  949.9 20.7 %reduce-scatter.33.cloned.1.call-done = bf16[384,1024]{1,0:T(8,128)(2,1)} async-done(((bf16[1536,1024]{1,0:T(8,128)(2,1)}), bf16[384,1024]{1,0:T(8,128)(2,1)}) %reduce-scatter.33.cloned.1.call-update) | async-done | bytes 786448 | tf_op jit(solution)/shard_map/reduce_scatter | solution.py:367
  970.6 40.7 %reduce-scatter.31.cloned.1.call-done = bf16[384,1024]{1,0:T(8,128)(2,1)} async-done(((bf16[1536,1024]{1,0:T(8,128)(2,1)}), bf16[384,1024]{1,0:T(8,128)(2,1)}) %reduce-scatter.31.cloned.1.call-update) | async-done | bytes 786448 | tf_op jit(solution)/shard_map/reduce_scatter | solution.py:367
  1013.8 45.1 %reduce-scatter.53.cloned.1.call-done = bf16[512,1024]{1,0:T(8,128)(2,1)} async-done(((bf16[2048,1024]{1,0:T(8,128)(2,1)}), bf16[512,1024]{1,0:T(8,128)(2,1)}) %reduce-scatter.53.cloned.1.call-update) | async-done | bytes 1048592 | tf_op jit(solution)/shard_map/reduce_scatter | solution.py:382
  1058.9 47.1 %reduce-scatter.51.cloned.1.call-done = bf16[512,1024]{1,0:T(8,128)(2,1)} async-done(((bf16[2048,1024]{1,0:T(8,128)(2,1)}), bf16[512,1024]{1,0:T(8,128)(2,1)}) %reduce-scatter.51.cloned.1.call-update) | async-done | bytes 1048592 | tf_op jit(solution)/shard_map/reduce_scatter | solution.py:382
  1108.9 71.4 %reduce-scatter.49.cloned.1.call-done = bf16[256,4096]{1,0:T(8,128)(2,1)} async-done(((bf16[1024,4096]{1,0:T(8,128)(2,1)}), bf16[256,4096]{1,0:T(8,128)(2,1)}) %reduce-scatter.49.cloned.1.call-update) | async-done | bytes 2097168 | tf_op jit(solution)/shard_map/reduce_scatter | solution.py:379
  1180.3 74.4 %reduce-scatter.47.cloned.1.call-done = bf16[256,4096]{1,0:T(8,128)(2,1)} async-done(((bf16[1024,4096]{1,0:T(8,128)(2,1)}), bf16[256,4096]{1,0:T(8,128)(2,1)}) %reduce-scatter.47.cloned.1.call-update) | async-done | bytes 2097168 | tf_op jit(solution)/shard_map/reduce_scatter | solution.py:379
  1259.0 59.9 %reduce-scatter.25.cloned.1.call-done = bf16[256,3328]{1,0:T(8,128)(2,1)} async-done(((bf16[1024,3328]{1,0:T(8,128)(2,1)}), bf16[256,3328]{1,0:T(8,128)(2,1)}) %reduce-scatter.25.cloned.1.call-update) | async-done | bytes 1703952 | tf_op jit(solution)/shard_map/reduce_scatter | solution.py:361
  1319.0 64.7 %reduce-scatter.23.cloned.1.call-done = bf16[256,3328]{1,0:T(8,128)(2,1)} async-done(((bf16[1024,3328]{1,0:T(8,128)(2,1)}), bf16[256,3328]{1,0:T(8,128)(2,1)}) %reduce-scatter.23.cloned.1.call-update) | async-done | bytes 1703952 | tf_op jit(solution)/shard_map/reduce_scatter | solution.py:361
  1410.1 41.2 %all-reduce.20 = (f32[1024]{0:T(1024)}, f32[4,1792]{1,0:T(4,128)}, f32[1792]{0:T(1024)}, f32[24]{0:T(128)}, f32[24]{0:T(128)}, /*index=5*/f32[24]{0:T(128)}, f32[1536]{0:T(1024)}, f32[1024]{0:T(1024)}) all-reduce(f32[1024]{0:T(1024)S(1)} %add.1094, ...), channel_id=1, replica_groups=mesh['ctx'=8,'wsh'=4] {'ctx','wsh'}, use_global_device_ids=true, to_apply=%region_116.117 | all-reduce | flops 12616 | bytes 100928 | tf_op jit(solution)/shard_map/psum | solution.py:616
  1456.4 38.9 %psum.114 = bf16[256,24]{0,1:T(8,128)(2,1)S(1)} all-reduce(bf16[256,24]{0,1:T(8,128)(2,1)S(1)} %add_convert_fusion.7), channel_id=1, replica_groups=mesh['ctx'=8,'wsh'=4] {'ctx'}, use_global_device_ids=true, to_apply=%region_122.123 | all-reduce | flops 6144 | bytes 24576 | tf_op jit(solution)/shard_map/psum | solution.py:614
  1495.9 156.1 %all-reduce.24.cloned.1.call-done = (bf16[256,3328]{1,0:T(8,128)(2,1)}, bf16[384,1024]{1,0:T(8,128)(2,1)}, bf16[256,512]{1,0:T(8,128)(2,1)}, bf16[256,256]{1,0:T...) async-done(((bf16[256,3328]{1,0:T(8,128)(2,1)}, bf16[384,1024]{1,0:T(8,128)(2,1)}, bf16[256,512]{1,0:T(8,128)(2,1)}, ...) | async-done | bytes 6291472 | tf_op jit(solution)/shard_map/psum | solution.py:614
  (1246 shorter events, 603.6 us)
Async XLA Ops:
  7.2 54.8 %all-gather.19.cloned.1.call-start = ((), (), s32[]{:S(2)}) async-start(), calls=%async_computation.18 | async-start | bytes 8519680 | tf_op jit(solution)/shard_map/all_gather | solution.py:445
  8.0 140.3 %all-gather.25.cloned.1.call-start = ((), (), s32[]{:S(2)}) async-start(), calls=%async_computation.21 | async-start | bytes 1310720 | tf_op jit(solution)/shard_map/all_gather | solution.py:448
  8.7 142.5 %all-gather.33.cloned.1.call-start = ((), (), s32[]{:S(2)}) async-start(), calls=%async_computation.25 | async-start | bytes 1179648 | tf_op jit(solution)/shard_map/all_gather | solution.py:509
  18.8 162.4 %all-gather.23.cloned.1.call-start = ((), (), s32[]{:S(2)}) async-start(), calls=%async_computation.20 | async-start | bytes 1179648 | tf_op jit(solution)/shard_map/all_gather | solution.py:509
  20.0 206.7 %all-gather.37.cloned.1.call-start = ((), (), s32[]{:S(2)}) async-start(), calls=%async_computation.45 | async-start | bytes 3538944 | tf_op jit(solution)/shard_map/all_gather | solution.py:29
  80.6 207.9 %all-gather.35.cloned.1.call-start = ((), (), s32[]{:S(2)}) async-start(), calls=%async_computation.44 | async-start | bytes 3538944 | tf_op jit(solution)/shard_map/all_gather | solution.py:29
  101.9 215.3 %all-gather.21.cloned.1.call-start = ((), (), s32[]{:S(2)}) async-start(), calls=%async_computation.19 | async-start | bytes 3932160 | tf_op jit(solution)/shard_map/all_gather | solution.py:447
  102.7 232.8 %all-gather.27.cloned.1.call-start = ((), (), s32[]{:S(2)}) async-start(), calls=%async_computation.22 | async-start | bytes 1310720 | tf_op jit(solution)/shard_map/all_gather | solution.py:450
  103.5 292.0 %all-gather.29.cloned.1.call-start = ((), (), s32[]{:S(2)}) async-start(), calls=%async_computation.23 | async-start | bytes 10485760 | tf_op jit(solution)/shard_map/all_gather | solution.py:451
  104.2 327.1 %all-gather.31.cloned.1.call-start = ((), (), s32[]{:S(2)}) async-start(), calls=%async_computation.24 | async-start | bytes 5242880 | tf_op jit(solution)/shard_map/all_gather | solution.py:452
  104.8 479.4 %reduce-scatter.21.cloned.1.call-start = ((), (), s32[]{:S(2)}) async-start(), calls=%async_computation.27 | async-start | bytes 1179648 | tf_op jit(solution)/shard_map/reduce_scatter | solution.py:552
  482.7 168.0 %reduce-scatter.19.cloned.1.call-start = ((), (), s32[]{:S(2)}) async-start(), calls=%async_computation.26 | async-start | bytes 1179648 | tf_op jit(solution)/shard_map/reduce_scatter | solution.py:552
  516.1 215.8 %all-gather.41.cloned.1.call-start = ((), (), s32[]{:S(2)}) async-start(), calls=%async_computation.47 | async-start | bytes 3538944 | tf_op jit(solution)/shard_map/all_gather | solution.py:49
  535.7 237.8 %all-gather.39.cloned.1.call-start = ((), (), s32[]{:S(2)}) async-start(), calls=%async_computation.46 | async-start | bytes 3538944 | tf_op jit(solution)/shard_map/all_gather | solution.py:49
  542.7 306.5 %reduce-scatter.37.cloned.1.call-start = ((), (), s32[]{:S(2)}) async-start(), calls=%async_computation.35 | async-start | bytes 1310720 | tf_op jit(solution)/shard_map/reduce_scatter | solution.py:370
  547.1 302.1 %reduce-scatter.35.cloned.1.call-start = ((), (), s32[]{:S(2)}) async-start(), calls=%async_computation.34 | async-start | bytes 1310720 | tf_op jit(solution)/shard_map/reduce_scatter | solution.py:370
  551.5 302.8 %reduce-scatter.45.cloned.1.call-start = ((), (), s32[]{:S(2)}) async-start(), calls=%async_computation.39 | async-start | bytes 1310720 | tf_op jit(solution)/shard_map/reduce_scatter | solution.py:376
  554.0 327.6 %reduce-scatter.43.cloned.1.call-start = ((), (), s32[]{:S(2)}) async-start(), calls=%async_computation.38 | async-start | bytes 1310720 | tf_op jit(solution)/shard_map/reduce_scatter | solution.py:376
  556.7 349.1 %reduce-scatter.41.cloned.1.call-start = ((), (), s32[]{:S(2)}) async-start(), calls=%async_computation.37 | async-start | bytes 655360 | tf_op jit(solution)/shard_map/reduce_scatter | solution.py:373
  586.6 343.5 %reduce-scatter.39.cloned.1.call-start = ((), (), s32[]{:S(2)}) async-start(), calls=%async_computation.36 | async-start | bytes 655360 | tf_op jit(solution)/shard_map/reduce_scatter | solution.py:373
  653.0 317.5 %reduce-scatter.33.cloned.1.call-start = ((), (), s32[]{:S(2)}) async-start(), calls=%async_computation.33 | async-start | bytes 3932160 | tf_op jit(solution)/shard_map/reduce_scatter | solution.py:367
  656.9 354.3 %reduce-scatter.31.cloned.1.call-start = ((), (), s32[]{:S(2)}) async-start(), calls=%async_computation.32 | async-start | bytes 3932160 | tf_op jit(solution)/shard_map/reduce_scatter | solution.py:367
  660.8 398.1 %reduce-scatter.53.cloned.1.call-start = ((), (), s32[]{:S(2)}) async-start(), calls=%async_computation.43 | async-start | bytes 5242880 | tf_op jit(solution)/shard_map/reduce_scatter | solution.py:382
  665.6 440.3 %reduce-scatter.51.cloned.1.call-start = ((), (), s32[]{:S(2)}) async-start(), calls=%async_computation.42 | async-start | bytes 5242880 | tf_op jit(solution)/shard_map/reduce_scatter | solution.py:382
  670.3 510.0 %reduce-scatter.49.cloned.1.call-start = ((), (), s32[]{:S(2)}) async-start(), calls=%async_computation.41 | async-start | bytes 10485760 | tf_op jit(solution)/shard_map/reduce_scatter | solution.py:379
  678.0 576.7 %reduce-scatter.47.cloned.1.call-start = ((), (), s32[]{:S(2)}) async-start(), calls=%async_computation.40 | async-start | bytes 10485760 | tf_op jit(solution)/shard_map/reduce_scatter | solution.py:379
  685.7 633.3 %reduce-scatter.25.cloned.1.call-start = ((), (), s32[]{:S(2)}) async-start(), calls=%async_computation.29 | async-start | bytes 8519680 | tf_op jit(solution)/shard_map/reduce_scatter | solution.py:361
  833.9 549.7 %reduce-scatter.23.cloned.1.call-start = ((), (), s32[]{:S(2)}) async-start(), calls=%async_computation.28 | async-start | bytes 8519680 | tf_op jit(solution)/shard_map/reduce_scatter | solution.py:361
  835.1 6.0 collective-permute-start.2
  849.1 606.6 %reduce-scatter.29.cloned.1.call-start = ((), (), s32[]{:S(2)}) async-start(), calls=%async_computation.31 | async-start | bytes 61440 | tf_op jit(solution)/shard_map/reduce_scatter | solution.py:364
  947.9 507.8 %reduce-scatter.27.cloned.1.call-start = ((), (), s32[]{:S(2)}) async-start(), calls=%async_computation.30 | async-start | bytes 61440 | tf_op jit(solution)/shard_map/reduce_scatter | solution.py:364
  949.7 702.3 %all-reduce.24.cloned.1.call-start = ((), (), s32[]{:S(2)}) async-start(), calls=%async_computation.48 | async-start | bytes 12582912 | tf_op jit(solution)/shard_map/psum | solution.py:614
  (333 other events, 4560.7 us)
Sparse Core Ops, SparseCore 0:
  9.6 52.3 all-gather.18
  63.5 16.7 all-gather.24
  83.0 40.2 all-gather.32
  125.9 39.0 all-gather.22
  167.5 59.1 all-gather.36
  229.3 59.1 all-gather.34
  290.0 27.1 all-gather.20
  318.8 16.7 all-gather.26
  337.1 58.2 all-gather.28
  396.9 34.4 all-gather.30
  482.9 101.2 reduce-scatter.20
  587.8 62.8 reduce-scatter.18
  652.9 59.4 all-gather.40
  714.4 59.0 all-gather.38
  775.9 23.5 reduce-scatter.36
  802.0 24.8 reduce-scatter.34
  829.3 24.8 reduce-scatter.44
  856.8 24.8 reduce-scatter.42
  884.2 21.6 reduce-scatter.40
  908.3 21.6 reduce-scatter.38
  932.6 37.9 reduce-scatter.32
  973.3 37.9 reduce-scatter.30
  1014.4 44.4 reduce-scatter.52
  1061.4 44.4 reduce-scatter.50
  1108.5 71.7 reduce-scatter.48
  1182.9 71.7 reduce-scatter.46
  1257.1 61.8 reduce-scatter.24
  1321.7 61.9 reduce-scatter.22
  1386.0 19.3 reduce-scatter.28
  1407.9 19.4 reduce-scatter.26
  1434.4 217.5 all-reduce.23
where the time goes:
time: 1680 us; the launch traced here: 1670 us
  waiting for transfers between devices  962 us (57%)
  matrix products  259 us (15%)
  other arithmetic  150 us (9%)
  blocking collectives  132 us (8%)
  local copies, waits for them, and re-layouts  68.2 us (4%)
  loops' own time  66.4 us (4%)
  between operations  20.1 us (1%)
    psum x1, waiting for transfers between devices, local(): lax.psum(shortened(shard_sums), 'ctx')  156 us
    reduce_scatter x2, waiting for transfers between devices, reduce_weights(): lax.psum_scatter(weight_grads[6].astype(jnp.bfloat16), 'wsh', scatter_dim...  146 us
    reduce_scatter x2, waiting for transfers between devices, reduce_weights(): lax.psum_scatter(weight_grads[0].astype(jnp.bfloat16), 'wsh', scatter_dim...  125 us
    reduce_scatter x2, waiting for transfers between devices, reduce_weights(): lax.psum_scatter(weight_grads[7].astype(jnp.bfloat16), 'wsh', scatter_dim...  92.1 us
    reduce_scatter x2, waiting for transfers between devices, local(): lax.psum_scatter(kv_partial.astype(jnp.bfloat16), 'ctx', scatter_dimensio...  91.5 us
    reduce_scatter x2, waiting for transfers between devices, reduce_weights(): lax.psum_scatter(weight_grads[2].astype(jnp.bfloat16), 'wsh', scatter_dim...  61.3 us
    all_gather x2, waiting for transfers between devices, carried_in(): lax.all_gather(a.astype(kind), axis)  59.6 us
    dot_general x16, matrix products, mat_left_t(): lax.dot_general(left, right, (((0,), (0,)), ((), ())), preferred_element_...  54.6 us
  transfers between devices with their start and end apart: 35, of which 27 were waited for; matrix products, arithmetic and copies ran while one was open for 24% of the time, Pallas kernels for 0%

commit v1 on v0

v1 whole, which is shorter than its diff:
```python
import functools

import jax
import jax.numpy as jnp
from jax import lax
from jax.experimental import pallas as pl
from jax.experimental.pallas import tpu as pltpu
from jax.sharding import PartitionSpec as P

FF = 2048
MHEADS = 24
MDIM = 64
STATE = 128
QHEADS = 8
KVHEADS = 2
HDIM = 64
DSSM = 1536
HGROUP = 8
NGROUP = MHEADS // HGROUP
GWIDTH = HGROUP * MDIM
PAIR = 2 * MDIM

NORM_EPS = 1e-05
PRECISE = lax.Precision.HIGHEST
MASKED_SCORE = -1e30
MIB = 2**20
F32 = jnp.float32
BF16 = jnp.bfloat16


def dot_as(left, right, left_dim, right_dim):
    return lax.dot_general(
        left, right, (((left_dim,), (right_dim,)), ((), ())), preferred_element_type=F32
    )


def mat(left, right):
    return dot_as(left, right, 1, 0)


def mat_left_t(left, right):
    return dot_as(left, right, 0, 0)


def mat_right_t(left, right):
    return dot_as(left, right, 1, 1)


def inv_rms(rows):
    return lax.rsqrt(jnp.mean(rows * rows, axis=-1, keepdims=True) + NORM_EPS)


def rms_pull(rows, scale, gain, grad):
    scaled = rows * scale
    grad_gain = jnp.sum(grad * scaled, axis=0)
    through = grad * gain
    inner = jnp.mean(through * scaled, axis=-1, keepdims=True)
    return scale * (through - scaled * inner), grad_gain


def seq_starts(lengths_row, positions):
    begins = jnp.cumsum(lengths_row, dtype=jnp.int32) - lengths_row
    picked = jnp.where(begins[None, :] <= positions[:, None], begins[None, :], 0)
    return jnp.max(picked, axis=1)


def head_lanes(rows):
    return lax.broadcasted_iota(jnp.int32, (rows, PAIR), 1) < MDIM


def masked_products(b_low, c_low, rel_start):
    rows = b_low.shape[0]
    at_row = lax.broadcasted_iota(jnp.int32, (rows, rows), 0)
    at_col = lax.broadcasted_iota(jnp.int32, (rows, rows), 1)
    allowed = (at_col <= at_row) & (at_col >= rel_start)
    return allowed, jnp.where(allowed, mat_right_t(c_low, b_low), 0.0)


def pair_columns(first_half, columns, head):
    return jnp.where(first_half, columns[:, head : head + 1], columns[:, head + 1 : head + 2])


def ssd_forward_kernel(
    x_ref, b_ref, c_ref, step_ref, decay_ref, decay_t_ref, start_ref, state_ref, skip_ref, y_ref
):
    rows = x_ref.shape[1]
    b_low = b_ref[0].astype(BF16)
    c_low = c_ref[0].astype(BF16)
    rel_start = start_ref[0]
    _, products = masked_products(b_low, c_low, rel_start)
    incoming = mat_right_t(c_low, state_ref[0].astype(BF16))
    first_half = head_lanes(rows)
    steps = step_ref[0, 0]
    decay = decay_ref[0, 0]
    reach = jnp.where(rel_start < 0, jnp.exp(decay), 0.0)
    for head in range(0, HGROUP, 2):
        lanes = slice(head * MDIM, head * MDIM + PAIR)
        x_pair = x_ref[0, :, lanes]
        scaled = (x_pair * pair_columns(first_half, steps, head)).astype(BF16)
        parts = []
        for one in (head, head + 1):
            gaps = decay[:, one : one + 1] - decay_t_ref[0, 0, one : one + 1, :]
            weights = (jnp.exp(jnp.minimum(gaps, 0.0)) * products).astype(BF16)
            parts.append(mat(weights, scaled))
        y_ref[0, :, lanes] = (
            jnp.where(first_half, parts[0], parts[1])
            + pair_columns(first_half, reach, head) * incoming[:, lanes]
            + skip_ref[:, lanes] * x_pair
        )


def ssd_backward_kernel(
    x_ref,
    b_ref,
    c_ref,
    step_ref,
    decay_ref,
    decay_t_ref,
    start_ref,
    state_ref,
    skip_ref,
    y_ref,
    dy_ref,
    later_ref,
    keep_ref,
    dx_ref,
    db_ref,
    dc_ref,
    row_ref,
    u_ref,
    v_ref,
    dskip_ref,
    one_sum,
    two_sum,
    three_sum,
    mixed_y,
    mixed_x,
):
    rows = x_ref.shape[1]
    b_low = b_ref[0].astype(BF16)
    c_low = c_ref[0].astype(BF16)
    rel_start = start_ref[0]
    allowed, products = masked_products(b_low, c_low, rel_start)
    state_low = state_ref[0].astype(BF16)
    later_low = later_ref[0].astype(BF16)
    spread = mat_right_t(b_low, later_low)
    first_half = head_lanes(rows)
    steps = step_ref[0, 0]
    decay = decay_ref[0, 0]
    reach = jnp.where(rel_start < 0, jnp.exp(decay), 0.0)
    to_end = jnp.exp(decay[rows - 1 : rows, :] - decay) * steps * keep_ref[0]
    product_grad = jnp.zeros((rows, rows), F32)
    for head in range(0, HGROUP, 2):
        lanes = slice(head * MDIM, head * MDIM + PAIR)
        x_pair = x_ref[0, :, lanes]
        dy_pair = dy_ref[0, :, lanes]
        step_pair = pair_columns(first_half, steps, head)
        scaled = (x_pair * step_pair).astype(BF16)
        dy_low = dy_pair.astype(BF16)
        parts = []
        for one in (head, head + 1):
            gaps = decay[:, one : one + 1] - decay_t_ref[0, 0, one : one + 1, :]
            decays = jnp.exp(jnp.minimum(gaps, 0.0))
            mine = first_half if one == head else ~first_half
            dy_mine = jnp.where(mine, dy_pair, 0.0).astype(BF16)
            weight_grad = mat_right_t(dy_mine, scaled)
            product_grad = product_grad + weight_grad * decays
            parts.append(mat_left_t((decays * products).astype(BF16), dy_low))
        dz_pair = jnp.where(first_half, parts[0], parts[1])
        skip_pair = skip_ref[:, lanes]
        end_pair = pair_columns(first_half, to_end, head)
        spread_pair = spread[:, lanes]
        dx_ref[0, :, lanes] = skip_pair * dy_pair + step_pair * dz_pair + end_pair * spread_pair
        one_sum[:, lanes] = dy_pair * (y_ref[0, :, lanes] - skip_pair * x_pair)
        two_sum[:, lanes] = x_pair * dz_pair
        three_sum[:, lanes] = x_pair * spread_pair
        mixed_y[:, lanes] = (dy_pair * pair_columns(first_half, reach, head)).astype(BF16)
        mixed_x[:, lanes] = (x_pair * end_pair).astype(BF16)
        dskip_ref[0, 0, :, lanes] = jnp.sum(dy_pair * x_pair, axis=0, keepdims=True)
    grad_low = jnp.where(allowed, product_grad, 0.0).astype(BF16)
    dc = mat(grad_low, b_low) + mat(mixed_y[...], state_low)
    db = mat_left_t(grad_low, c_low) + mat(mixed_x[...], later_low)
    group = pl.program_id(1)

    @pl.when(group == 0)
    def _():
        dc_ref[0] = dc
        db_ref[0] = db

    @pl.when(group > 0)
    def _():
        dc_ref[0] += dc
        db_ref[0] += db

    owner = lax.broadcasted_iota(jnp.int32, (GWIDTH, 128), 0) // MDIM
    picks = (owner == lax.broadcasted_iota(jnp.int32, (GWIDTH, 128), 1)).astype(F32)
    for source, target in ((one_sum, row_ref), (two_sum, u_ref), (three_sum, v_ref)):
        sums = lax.dot_general(
            source[...],
            picks,
            (((1,), (0,)), ((), ())),
            precision=PRECISE,
            preferred_element_type=F32,
        )
        target[0, 0] = sums[:, :HGROUP]


def ssd_specs(rows):
    wide = pl.BlockSpec((1, rows, GWIDTH), lambda b, g: (b, 0, g))
    narrow = pl.BlockSpec((1, rows, STATE), lambda b, g: (b, 0, 0))
    heads = pl.BlockSpec((1, 1, rows, HGROUP), lambda b, g: (b, g, 0, 0))
    heads_t = pl.BlockSpec((1, 1, HGROUP, rows), lambda b, g: (b, g, 0, 0))
    column = pl.BlockSpec((1, rows, 1), lambda b, g: (b, 0, 0))
    state = pl.BlockSpec((1, GWIDTH, STATE), lambda b, g: (b, g, 0))
    skip = pl.BlockSpec((1, GWIDTH), lambda b, g: (0, g))
    return wide, narrow, heads, heads_t, column, state, skip


def ssd_forward(inner, b_rows, c_rows, steps, decay, decay_t, rel_start, state_in, skip_row):
    count, rows, _ = inner.shape
    wide, narrow, heads, heads_t, column, state, skip = ssd_specs(rows)
    return pl.pallas_call(
        ssd_forward_kernel,
        grid=(count, NGROUP),
        in_specs=[wide, narrow, narrow, heads, heads, heads_t, column, state, skip],
        out_specs=wide,
        out_shape=jax.ShapeDtypeStruct(inner.shape, F32),
        compiler_params=pltpu.CompilerParams(vmem_limit_bytes=40 * MIB),
        cost_estimate=pl.CostEstimate(
            flops=count * MHEADS * rows * rows * 400, bytes_accessed=8 * MIB, transcendentals=0
        ),
        name="ssd_forward",
    )(inner, b_rows, c_rows, steps, decay, decay_t, rel_start, state_in, skip_row)


def ssd_backward(
    inner,
    b_rows,
    c_rows,
    steps,
    decay,
    decay_t,
    rel_start,
    state_in,
    skip_row,
    scanned,
    grad_scanned,
    later,
    keep,
):
    count, rows, _ = inner.shape
    wide, narrow, heads, heads_t, column, state, skip = ssd_specs(rows)
    head_shape = jax.ShapeDtypeStruct((count, NGROUP, rows, HGROUP), F32)
    return pl.pallas_call(
        ssd_backward_kernel,
        grid=(count, NGROUP),
        in_specs=[
            wide,
            narrow,
            narrow,
            heads,
            heads,
            heads_t,
            column,
            state,
            skip,
            wide,
            wide,
            state,
            column,
        ],
        out_specs=[
            wide,
            narrow,
            narrow,
            heads,
            heads,
            heads,
            pl.BlockSpec((1, 1, 1, GWIDTH), lambda b, g: (b, g, 0, 0)),
        ],
        out_shape=[
            jax.ShapeDtypeStruct(inner.shape, F32),
            jax.ShapeDtypeStruct(b_rows.shape, F32),
            jax.ShapeDtypeStruct(b_rows.shape, F32),
            head_shape,
            head_shape,
            head_shape,
            jax.ShapeDtypeStruct((count, NGROUP, 1, GWIDTH), F32),
        ],
        scratch_shapes=[pltpu.VMEM((rows, GWIDTH), F32)] * 3
        + [pltpu.VMEM((rows, GWIDTH), BF16)] * 2,
        compiler_params=pltpu.CompilerParams(vmem_limit_bytes=40 * MIB),
        cost_estimate=pl.CostEstimate(
            flops=count * MHEADS * rows * rows * 1000, bytes_accessed=16 * MIB, transcendentals=0
        ),
        name="ssd_backward",
    )(
        inner,
        b_rows,
        c_rows,
        steps,
        decay,
        decay_t,
        rel_start,
        state_in,
        skip_row,
        scanned,
        grad_scanned,
        later,
        keep,
    )


def spread_heads(source_ref, target, factor):
    width = source_ref.shape[1]
    target[...] = jnp.zeros(target.shape, target.dtype)
    for head in range(QHEADS):
        group = head // (QHEADS // KVHEADS)
        value = source_ref[head * HDIM : (head + 1) * HDIM, :]
        target[group * HDIM : (group + 1) * HDIM, head * width : (head + 1) * width] = (
            value * factor if factor != 1.0 else value
        )


def attend_allowed(block, first_pos, starts, width):
    key_pos = block * width + lax.broadcasted_iota(jnp.int32, (width, width), 0)
    query_pos = first_pos + lax.broadcasted_iota(jnp.int32, (width, width), 1)
    return (key_pos <= query_pos) & (key_pos >= starts)


def attend_forward_kernel(bounds, start_ref, q_ref, kv_ref, out_ref, log_ref, q_wide, top, total, acc):
    width = q_ref.shape[1]
    batch = pl.program_id(0)
    spread_heads(q_ref, q_wide, HDIM**-0.5)
    top[...] = jnp.full(top.shape, MASKED_SCORE, F32)
    total[...] = jnp.zeros(total.shape, F32)
    acc[...] = jnp.zeros(acc.shape, F32)
    last = bounds[pl.num_programs(0)]
    first_pos = (last - 1) * width

    def one_block(block, carry):
        kv_rows = kv_ref[bounds[pl.num_programs(0) + 1 + block], 0]
        keys = kv_rows[:, : KVHEADS * HDIM]
        values_t = kv_rows[:, KVHEADS * HDIM :].T
        allowed = attend_allowed(block, first_pos, start_ref[0], width)
        for head in range(QHEADS):
            group = head // (QHEADS // KVHEADS)
            scores = mat(keys, q_wide[:, head * width : (head + 1) * width])
            scores = jnp.where(allowed, scores, MASKED_SCORE)
            old = top[head : head + 1, :]
            new = jnp.maximum(old, jnp.max(scores, axis=0, keepdims=True))
            terms = jnp.exp(scores - new)
            shrink = jnp.exp(old - new)
            top[head : head + 1, :] = new
            total[head : head + 1, :] = total[head : head + 1, :] * shrink + jnp.sum(
                terms, axis=0, keepdims=True
            )
            acc[head] = acc[head] * shrink + mat(
                values_t[group * HDIM : (group + 1) * HDIM, :], terms.astype(BF16)
            )
        return carry

    lax.fori_loop(bounds[batch], last, one_block, 0)
    for head in range(QHEADS):
        out_ref[head * HDIM : (head + 1) * HDIM, :] = (
            acc[head] / total[head : head + 1, :]
        ).astype(BF16)
    log_ref[0] = top[...] + jnp.log(total[...])


def attend_forward(bounds, starts, queries_t, key_table):
    blocks, count, width, kv_width = key_table.shape
    column = pl.BlockSpec((QHEADS * HDIM, width), lambda b, s: (0, b))
    logs = pl.BlockSpec((1, QHEADS, width), lambda b, s: (b, 0, 0))
    return pl.pallas_call(
        attend_forward_kernel,
        grid_spec=pltpu.PrefetchScalarGridSpec(
            num_scalar_prefetch=1,
            grid=(count,),
            in_specs=[
                pl.BlockSpec((1, 1, width), lambda b, s: (b, 0, 0)),
                column,
                pl.BlockSpec((blocks, 1, width, kv_width), lambda b, s: (0, b, 0, 0)),
            ],
            out_specs=[column, logs],
            scratch_shapes=[
                pltpu.VMEM((KVHEADS * HDIM, QHEADS * width), BF16),
                pltpu.VMEM((QHEADS, width), F32),
                pltpu.VMEM((QHEADS, width), F32),
                pltpu.VMEM((QHEADS, HDIM, width), F32),
            ],
        ),
        out_shape=[
            jax.ShapeDtypeStruct(queries_t.shape, BF16),
            jax.ShapeDtypeStruct((count, QHEADS, width), F32),
        ],
        compiler_params=pltpu.CompilerParams(vmem_limit_bytes=40 * MIB),
        cost_estimate=pl.CostEstimate(
            flops=count * blocks * width * width * 8 * 1000,
            bytes_accessed=4 * MIB,
            transcendentals=0,
        ),
        name="attend_forward",
    )(bounds, starts, queries_t, key_table)


def attend_backward_kernel(
    bounds,
    start_ref,
    q_ref,
    kv_ref,
    out_ref,
    grad_ref,
    log_ref,
    dq_ref,
    dkv_ref,
    q_wide,
    g_wide,
    q_tall,
    g_tall,
    delta,
    acc,
):
    width = q_ref.shape[1]
    kv_width = KVHEADS * HDIM
    batch = pl.program_id(0)
    spread_heads(q_ref, q_wide, HDIM**-0.5)
    spread_heads(grad_ref, g_wide, 1.0)
    acc[...] = jnp.zeros(acc.shape, F32)
    dkv_ref[...] = jnp.zeros(dkv_ref.shape, BF16)
    for head in range(QHEADS):
        columns = slice(head * width, (head + 1) * width)
        q_tall[columns, :] = q_wide[:, columns].T
        g_tall[columns, :] = g_wide[:, columns].T
        span = slice(head * HDIM, (head + 1) * HDIM)
        delta[head : head + 1, :] = jnp.sum(
            out_ref[span, :].astype(F32) * grad_ref[span, :].astype(F32), axis=0, keepdims=True
        )
    last = bounds[pl.num_programs(0)]
    first_pos = (last - 1) * width

    def one_block(block, carry):
        place = bounds[pl.num_programs(0) + 1 + block]
        kv_rows = kv_ref[place, 0]
        keys = kv_rows[:, :kv_width]
        values = kv_rows[:, kv_width:]
        keys_t = keys.T
        allowed = attend_allowed(block, first_pos, start_ref[0], width)
        dk = jnp.zeros((width, kv_width), F32)
        dv = jnp.zeros((width, kv_width), F32)
        for head in range(QHEADS):
            group = head // (QHEADS // KVHEADS)
            columns = slice(head * width, (head + 1) * width)
            scores = mat(keys, q_wide[:, columns])
            shifted = jnp.where(allowed, scores - log_ref[0, head : head + 1, :], MASKED_SCORE)
            probs = jnp.exp(shifted)
            grad_probs = mat(values, g_wide[:, columns])
            grad_scores = (probs * (grad_probs - delta[head : head + 1, :])).astype(BF16)
            dk = dk + mat(grad_scores, q_tall[columns, :])
            dv = dv + mat(probs.astype(BF16), g_tall[columns, :])
            acc[head] += mat(keys_t[group * HDIM : (group + 1) * HDIM, :], grad_scores)
        dkv_ref[place, 0] = jnp.concatenate([dk, dv], axis=1).astype(BF16)
        return carry

    lax.fori_loop(bounds[batch], last, one_block, 0)
    for head in range(QHEADS):
        dq_ref[head * HDIM : (head + 1) * HDIM, :] = (acc[head] * HDIM**-0.5).astype(BF16)


def attend_backward(bounds, starts, queries_t, key_table, out_t, grad_t, logs):
    blocks, count, width, kv_width = key_table.shape
    column = pl.BlockSpec((QHEADS * HDIM, width), lambda b, s: (0, b))
    table = pl.BlockSpec((blocks, 1, width, kv_width), lambda b, s: (0, b, 0, 0))
    wide = pltpu.VMEM((KVHEADS * HDIM, QHEADS * width), BF16)
    tall = pltpu.VMEM((QHEADS * width, KVHEADS * HDIM), BF16)
    return pl.pallas_call(
        attend_backward_kernel,
        grid_spec=pltpu.PrefetchScalarGridSpec(
            num_scalar_prefetch=1,
            grid=(count,),
            in_specs=[
                pl.BlockSpec((1, 1, width), lambda b, s: (b, 0, 0)),
                column,
                table,
                column,
                column,
                pl.BlockSpec((1, QHEADS, width), lambda b, s: (b, 0, 0)),
            ],
            out_specs=[column, table],
            scratch_shapes=[
                wide,
                wide,
                tall,
                tall,
                pltpu.VMEM((QHEADS, width), F32),
                pltpu.VMEM((QHEADS, HDIM, width), F32),
            ],
        ),
        out_shape=[
            jax.ShapeDtypeStruct(queries_t.shape, BF16),
            jax.ShapeDtypeStruct(key_table.shape, BF16),
        ],
        compiler_params=pltpu.CompilerParams(vmem_limit_bytes=48 * MIB),
        cost_estimate=pl.CostEstimate(
            flops=count * blocks * width * width * 8 * 2000,
            bytes_accessed=8 * MIB,
            transcendentals=0,
        ),
        name="attend_backward",
    )(bounds, starts, queries_t, key_table, out_t, grad_t, logs)


def passed_along(block, axis, distance):
    devices = range(lax.axis_size(axis))
    route = [(i - distance, i) for i in devices if i - distance in devices]
    return lax.ppermute(block, axis, route)


def swapped(block, axis, bit):
    return lax.ppermute(block, axis, [(i, i ^ bit) for i in range(lax.axis_size(axis))])


def bits_of(axis):
    return [1 << k for k in range(lax.axis_size(axis).bit_length() - 1)]


def gathered_near(shard):
    half = jnp.concatenate([shard, swapped(shard, "wsh", 2)], axis=0)
    return jnp.concatenate([half, swapped(half, "wsh", 1)], axis=0)


def near_order(array, axis):
    here = lax.axis_index("wsh")
    block = array.shape[axis] // 4
    return jnp.concatenate(
        [
            lax.dynamic_slice_in_dim(array, (here ^ step) * block, block, axis)
            for step in (0, 2, 1, 3)
        ],
        axis=axis,
    )


def natural_order(array, axis):
    here = lax.axis_index("wsh")
    block = array.shape[axis] // 4
    places = []
    for index in range(4):
        step = here ^ index
        place = jnp.where(step == 1, 2, jnp.where(step == 2, 1, step))
        places.append(lax.dynamic_slice_in_dim(array, place * block, block, axis))
    return jnp.concatenate(places, axis=axis)


def reduced_over_wsh(send, keep):
    came = swapped(send.astype(BF16), "wsh", 1)
    both = keep + came.astype(F32)
    block = both.shape[0] // 2
    crossed = swapped(both[block:].astype(BF16), "wsh", 2)
    return both[:block] + crossed.astype(F32)


def pick_half(array, upper):
    half = array.shape[0] // 2
    return lax.dynamic_slice_in_dim(array, upper * half, half, 0)


def joined(mine, other, upper):
    return jnp.where(
        upper == 1,
        jnp.concatenate([other, mine], axis=0),
        jnp.concatenate([mine, other], axis=0),
    )


def summed_over_ctx(part):
    here = lax.axis_index("ctx")
    bits = bits_of("ctx")
    for bit in bits:
        upper = (here // bit) % 2
        came = swapped(pick_half(part, 1 - upper).astype(BF16), "ctx", bit)
        part = pick_half(part, upper) + came.astype(F32)
    part = part.astype(BF16)
    for bit in bits[::-1]:
        part = joined(part, swapped(part, "ctx", bit), (here // bit) % 2)
    return part.astype(F32)


def summed_everywhere(vector):
    for axis in ("wsh", "ctx"):
        for bit in bits_of(axis):
            vector = vector + swapped(vector, axis, bit)
    return vector


def table_gather(rows):
    table = rows[None]
    for bit in bits_of("ctx")[::-1]:
        table = jnp.concatenate([table, swapped(table, "ctx", bit)], axis=0)
    return table


def table_places(here, count):
    bits = count.bit_length() - 1
    apart = jnp.arange(count, dtype=jnp.int32) ^ here
    return sum(((apart >> bit) & 1) << (bits - 1 - bit) for bit in range(bits))


def table_scatter(table):
    for bit in bits_of("ctx"):
        half = table.shape[0] // 2
        table = (
            table[:half].astype(F32) + swapped(table[half:], "ctx", bit).astype(F32)
        ).astype(BF16)
    return table[0]


def widened_rows(factor):
    return jnp.repeat(factor, MDIM, axis=1)[..., None]


def chain_scan(total, state, forward):
    here = lax.axis_index("ctx")
    bits = bits_of("ctx")
    reached = jnp.zeros_like(state)
    reach = jnp.ones_like(total)
    for bit in bits:
        late = ((here // bit) % 2 == 1) == forward
        other_total = swapped(total, "ctx", bit)
        other = swapped(state.astype(BF16), "ctx", bit).astype(F32)
        reached = jnp.where(late, reached + widened_rows(reach) * other, reached)
        reach = jnp.where(late, reach * other_total, reach)
        state = jnp.where(
            late,
            widened_rows(total) * other + state,
            widened_rows(other_total) * state + other,
        )
        total = total * other_total
    return reached


def local(
    inputs,
    cotangent,
    lengths,
    norm1_gain,
    in_weight,
    dt_weight,
    conv_weight,
    conv_bias,
    dt_bias,
    decay_rate,
    skip_gain,
    mamba_gain,
    out_weight,
    q_weight,
    kv_weight,
    o_weight,
    norm2_gain,
    gu_weight,
    down_weight,
):
    count, _, rows, features = inputs.shape
    here = lax.axis_index("ctx")
    ctx_count = lax.axis_size("ctx")
    tokens = count * rows
    first_pos = here * rows
    own_pos = first_pos + jnp.arange(rows, dtype=jnp.int32)
    starts = jax.vmap(lambda row: seq_starts(row, own_pos))(lengths[:, 0])
    rel_start = starts - first_pos
    taps = conv_weight.shape[0]

    full_kv, full_in, full_dt, full_q, full_out, full_o, full_gu, full_down = [
        gathered_near(shard)
        for shard in (
            kv_weight,
            in_weight,
            dt_weight,
            q_weight,
            out_weight,
            o_weight,
            gu_weight,
            down_weight,
        )
    ]

    x = inputs.reshape(tokens, features).astype(F32)
    scale_one = inv_rms(x)
    normed = near_order((x * scale_one * norm1_gain).astype(BF16), 1)
    kv_rows = mat(normed, full_kv).astype(BF16)
    key_table = table_gather(kv_rows.reshape(count, rows, -1))
    projected = mat(normed, full_in)
    gate_z = projected[:, :DSSM]
    conv_rows = projected[:, DSSM:].reshape(count, rows, -1)
    dt_raw = mat(normed, full_dt) + dt_bias
    steps = jax.nn.softplus(dt_raw).reshape(count, rows, MHEADS)
    edge = passed_along(conv_rows[:, rows - taps + 1 :], "ctx", 1)
    extended = jnp.concatenate([edge, conv_rows], axis=1)
    valid = [
        (own_pos[None] - (taps - 1) + tap >= starts).astype(F32)[..., None] for tap in range(taps)
    ]
    conv_sum = jnp.zeros_like(conv_rows) + conv_bias
    for tap in range(taps):
        conv_sum = conv_sum + conv_weight[tap] * extended[:, tap : tap + rows] * valid[tap]
    conv_gate = jax.nn.sigmoid(conv_sum)
    activated = conv_sum * conv_gate
    inner = activated[..., :DSSM]
    b_rows = activated[..., DSSM : DSSM + STATE]
    c_rows = activated[..., DSSM + STATE :]

    lower = (own_pos[:, None] >= own_pos[None, :]).astype(F32)
    drop = -steps * decay_rate
    decay = jnp.einsum("ik,bkh->bih", lower, drop, precision=PRECISE)
    end = decay[:, -1:]
    keep = (own_pos[None] >= starts[:, -1:]).astype(F32)[..., None]
    to_end = jnp.exp(end - decay) * keep
    reach = jnp.where(rel_start[..., None] < 0, jnp.exp(decay), 0.0)
    carried = (starts[:, -1:] < first_pos).astype(F32)
    total = jnp.exp(end[:, 0]) * carried

    def grouped(columns):
        return columns.reshape(count, rows, NGROUP, HGROUP).transpose(0, 2, 1, 3)

    def ungrouped(columns):
        return columns.transpose(0, 2, 1, 3).reshape(count, rows, MHEADS)

    def widened(columns):
        return jnp.repeat(columns, MDIM, axis=-1)

    def outer(left, right):
        return jnp.einsum(
            "bti,btn->bin", left.astype(BF16), right.astype(BF16), preferred_element_type=F32
        )

    fresh = outer(inner * widened(to_end * steps), b_rows)
    state_in = chain_scan(total, fresh, True)

    queries_t = dot_as(full_q, normed, 0, 1).astype(BF16)
    bounds = jnp.concatenate(
        [starts[:, 0] // rows, jnp.full((1,), here + 1, jnp.int32), table_places(here, ctx_count)]
    )
    starts_row = starts[:, None, :]
    attended_t, logs = attend_forward(bounds, starts_row, queries_t, key_table)

    steps_g = grouped(steps)
    decay_g = grouped(decay)
    decay_t = decay_g.transpose(0, 1, 3, 2)
    skip_row = widened(skip_gain)[None]
    rel_column = rel_start[..., None]
    scanned = ssd_forward(
        inner, b_rows, c_rows, steps_g, decay_g, decay_t, rel_column, state_in, skip_row
    )
    flat = scanned.reshape(tokens, DSSM)
    gate_sig = jax.nn.sigmoid(gate_z)
    gated = flat * gate_z * gate_sig
    scale_m = inv_rms(gated)
    mixed = near_order((gated * scale_m * mamba_gain).astype(BF16), 1)
    attended_near = near_order(attended_t, 0)
    middle = x + mat(mixed, full_out) + mat_left_t(attended_near, full_o)
    scale_two = inv_rms(middle)
    normed_two = near_order((middle * scale_two * norm2_gain).astype(BF16), 1)
    gate_up = mat(normed_two, full_gu)
    gate_part = gate_up[:, :FF]
    up_part = gate_up[:, FF:]
    sig = jax.nn.sigmoid(gate_part)
    hidden = near_order((gate_part * sig * up_part).astype(BF16), 1)
    layer_out = (middle + mat(hidden, full_down)).astype(BF16)

    grad_top = cotangent.reshape(tokens, features)
    half = hidden.shape[1] // 2
    down_shard = reduced_over_wsh(
        mat_left_t(hidden[:, half:], grad_top), mat_left_t(hidden[:, :half], grad_top)
    )
    grad_hidden = natural_order(mat_right_t(grad_top, full_down), 1)
    grad_gate = grad_hidden * up_part * sig * (1.0 + gate_part * (1.0 - sig))
    grad_up = grad_hidden * gate_part * sig
    grad_gu_rows = jnp.concatenate([grad_gate, grad_up], axis=1).astype(BF16)
    half = normed_two.shape[1] // 2
    gu_shard = reduced_over_wsh(
        mat_left_t(normed_two[:, half:], grad_gu_rows),
        mat_left_t(normed_two[:, :half], grad_gu_rows),
    )
    grad_two, grad_norm2 = rms_pull(
        middle, scale_two, norm2_gain, natural_order(mat_right_t(grad_gu_rows, full_gu), 1)
    )
    grad_middle = grad_top.astype(F32) + grad_two
    branch = grad_middle.astype(BF16)
    half = attended_near.shape[0] // 2
    o_shard = reduced_over_wsh(mat(attended_near[half:], branch), mat(attended_near[:half], branch))
    grad_attended_t = natural_order(dot_as(full_o, branch, 1, 1).astype(BF16), 0)
    half = mixed.shape[1] // 2
    out_shard = reduced_over_wsh(
        mat_left_t(mixed[:, half:], branch), mat_left_t(mixed[:, :half], branch)
    )
    grad_mixed = natural_order(mat_right_t(branch, full_out), 1)
    grad_gated, grad_mamba = rms_pull(gated, scale_m, mamba_gain, grad_mixed)
    grad_gate_z = grad_gated * flat * gate_sig * (1.0 + gate_z * (1.0 - gate_sig))
    grad_scanned = (grad_gated * gate_z * gate_sig).reshape(count, rows, DSSM)
    grad_state = outer(grad_scanned * widened(reach), c_rows)
    later = chain_scan(total, grad_state, False)

    dq_t, dkv_table = attend_backward(
        bounds, starts_row, queries_t, key_table, attended_t, grad_attended_t, logs
    )
    grad_kv_rows = table_scatter(dkv_table).reshape(tokens, -1)
    dx, db, dc, row_dot, u_dot, v_dot, dskip = ssd_backward(
        inner,
        b_rows,
        c_rows,
        steps_g,
        decay_g,
        decay_t,
        rel_column,
        state_in,
        skip_row,
        scanned,
        grad_scanned,
        later,
        keep,
    )
    row_dot, u_dot, v_dot = ungrouped(row_dot), ungrouped(u_dot), ungrouped(v_dot)
    to_last = v_dot * to_end * steps
    grad_total = jnp.sum((later * state_in).reshape(count, MHEADS, MDIM * STATE), axis=-1) * total
    grad_decay = row_dot - u_dot * steps - to_last
    grad_drop = (
        jnp.einsum("ki,bkh->bih", lower, grad_decay, precision=PRECISE)
        + (jnp.sum(to_last, axis=1) + grad_total)[:, None]
    )
    grad_rate = jnp.sum(-steps * grad_drop, axis=(0, 1))
    grad_steps = u_dot + v_dot * to_end - decay_rate * grad_drop
    grad_dt_raw = grad_steps.reshape(tokens, MHEADS) * jax.nn.sigmoid(dt_raw)
    grad_dt_bias = jnp.sum(grad_dt_raw, axis=0)
    dt_low = grad_dt_raw.astype(BF16)
    grad_skip = jnp.sum(dskip.reshape(count, MHEADS, MDIM), axis=(0, 2))

    grad_act = jnp.concatenate([dx, db, dc], axis=-1)
    grad_conv = grad_act * conv_gate * (1.0 + conv_sum * (1.0 - conv_gate))
    grad_conv_b = jnp.sum(grad_conv, axis=(0, 1))
    grad_conv_w = jnp.stack(
        [
            jnp.sum(grad_conv * extended[:, tap : tap + rows] * valid[tap], axis=(0, 1))
            for tap in range(taps)
        ]
    )
    grad_extended = jnp.zeros_like(extended)
    for tap in range(taps):
        grad_extended = grad_extended + jnp.pad(
            conv_weight[tap] * grad_conv * valid[tap], ((0, 0), (tap, taps - 1 - tap), (0, 0))
        )
    edge_back = passed_along(grad_extended[:, : taps - 1], "ctx", -1)
    grad_conv_rows = grad_extended[:, taps - 1 :] + jnp.pad(
        edge_back, ((0, 0), (rows - taps + 1, 0), (0, 0))
    )
    grad_proj = jnp.concatenate(
        [grad_gate_z, grad_conv_rows.reshape(tokens, -1)], axis=1
    ).astype(BF16)
    half = features // 2

    def shard_sum(grad, dim):
        return reduced_over_wsh(
            dot_as(normed[:, half:], grad, 0, dim), dot_as(normed[:, :half], grad, 0, dim)
        )

    q_shard = shard_sum(dq_t, 1)
    kv_shard = shard_sum(grad_kv_rows, 0)
    dt_shard = shard_sum(dt_low, 0)
    in_shard = shard_sum(grad_proj, 0)
    grad_normed = (
        dot_as(dq_t, full_q, 0, 1)
        + mat_right_t(grad_kv_rows, full_kv)
        + mat_right_t(grad_proj, full_in)
        + mat_right_t(dt_low, full_dt)
    )
    grad_normed = natural_order(grad_normed, 1)
    grad_one, grad_norm1 = rms_pull(x, scale_one, norm1_gain, grad_normed)
    input_grad = (grad_middle + grad_one).astype(BF16)

    totals_w = [
        summed_over_ctx(shard)
        for shard in (in_shard, dt_shard, out_shard, q_shard, kv_shard, o_shard, gu_shard, down_shard)
    ]
    pieces = (
        grad_norm1,
        grad_conv_w,
        grad_conv_b,
        grad_dt_bias,
        grad_rate,
        grad_skip,
        grad_mamba,
        grad_norm2,
    )
    packed = jnp.concatenate([piece.reshape(-1) for piece in pieces])
    packed = jnp.pad(packed, (0, -packed.size % 1024)).reshape(-1, 128)
    packed = summed_everywhere(packed).reshape(-1)
    small = []
    place = 0
    for piece in pieces:
        small.append(packed[place : place + piece.size].reshape(piece.shape))
        place += piece.size
    shape = (count, 1, rows, features)
    return (
        layer_out.reshape(shape),
        input_grad.reshape(shape),
        small[0],
        totals_w[0],
        totals_w[1],
        small[1],
        small[2],
        small[3],
        small[4],
        small[5],
        small[6],
        totals_w[2],
        totals_w[3],
        totals_w[4],
        totals_w[5],
        small[7],
        totals_w[6],
        totals_w[7],
    )


def solution(mesh):
    stream = P(None, "wsh", "ctx", None)
    shard = P("wsh", None)
    in_specs = (
        stream,
        stream,
        P(None, "wsh", None),
        P(),
        shard,
        shard,
        P(),
        P(),
        P(),
        P(),
        P(),
        P(),
        shard,
        shard,
        shard,
        shard,
        P(),
        shard,
        shard,
    )
    out_specs = (
        stream,
        stream,
        P(),
        shard,
        shard,
        P(),
        P(),
        P(),
        P(),
        P(),
        P(),
        shard,
        shard,
        shard,
        shard,
        P(),
        shard,
        shard,
    )
    return jax.shard_map(local, mesh=mesh, in_specs=in_specs, out_specs=out_specs, check_vma=False)
```

time: 1680 us -> 830 us (0.49)
  waiting for transfers between devices: 962 us -> 365 us
  matrix products: 259 us -> 81.3 us
  blocking collectives: 132 us -> 0 us
  starting transfers between devices: 12.5 us -> 137 us
  loops' own time: 66.4 us -> 0 us
  other arithmetic: 150 us -> 98.4 us
  Pallas kernels: 0 us -> 47.9 us
  local copies, waits for them, and re-layouts: 68.2 us -> 86.1 us
    reduce_scatter x18 -> x0, waiting for transfers between devices: 593 us -> none  [the longest x2 146 us: reduce_weights(): lax.psum_scatter(weight_grads[6].astype(jnp.bfloat16), 'wsh', scatter_dim...]
    ppermute x0 -> x99, waiting for transfers between devices: none -> 365 us  [swapped(): lax.ppermute(block, axis, [(i, i ^ bit) for i in range(lax.axis_size(axis...]
    all_gather x12 -> x0, waiting for transfers between devices: 203 us -> none  [the longest x2 59.6 us: carried_in(): lax.all_gather(a.astype(kind), axis)]
    dot_general x100 -> x36, matrix products: 259 us -> 81.3 us  [the longest x32 76.8 us: dot_as(): lax.dot_general(left, right, (((left_dim,), (right_dim,)), ((), ())), pre...]
    psum x1 -> x0, waiting for transfers between devices: 156 us -> none  [local(): lax.psum(shortened(shard_sums), 'ctx')]
    ppermute x0 -> x99, starting transfers between devices: none -> 132 us  [swapped(): lax.ppermute(block, axis, [(i, i ^ bit) for i in range(lax.axis_size(axis...]
    psum x2 -> x0, blocking collectives: 80.1 us -> none  [the longest x1 41.2 us: local(): small_totals = lax.psum(small_sums, ('ctx', 'wsh'))]
    another operation x64 -> x0, loops' own time: 66.4 us -> none  [the longest x4 21.6 us: attend_backward(): lax.fori_loop(0, blocks, back_pass, (jnp.zeros(q_heads.shape, jnp.float32...]
  transfers between devices with their start and end apart: 35 -> 101, of which waited for: 27 -> 51; matrix products, arithmetic and copies ran while one was open for 24% -> 24% of each run, Pallas kernels for 0% -> 5%
where the time goes in v1:
time: 830 us; the launch traced here: 820 us
  waiting for transfers between devices  365 us (44%)
  starting transfers between devices  137 us (17%)
  other arithmetic  98.4 us (12%)
  local copies, waits for them, and re-layouts  86.1 us (10%)
  matrix products  81.3 us (10%)
  Pallas kernels  47.9 us (6%)
    ppermute x99, waiting for transfers between devices, swapped(): lax.ppermute(block, axis, [(i, i ^ bit) for i in range(lax.axis_size(axis...  365 us
    ppermute x99, starting transfers between devices, swapped(): lax.ppermute(block, axis, [(i, i ^ bit) for i in range(lax.axis_size(axis...  132 us
    dot_general x32, matrix products, dot_as(): lax.dot_general(left, right, (((left_dim,), (right_dim,)), ((), ())), pre...  76.8 us
    unnamed x351, local copies, waits for them, and re-layouts  38 us
    pallas_call x1, Pallas kernels, ssd_backward(): pl.pallas_call(ssd_backward_kernel, grid=(count, NGROUP), in_specs=[wide,...  27.5 us
  transfers between devices with their start and end apart: 101, of which 51 were waited for; matrix products, arithmetic and copies ran while one was open for 24% of the time, Pallas kernels for 5%

profile of v1, /device:TPU:0, one launch (start us, length us, event | category | flops | bytes accessed | tf_op | source)
XLA Modules:
  0.0 820.3 jit_solution(5805162885696430787)
XLA Ops:
  28.6 26.8 %collective-permute-done.3 = bf16[256,24]{0,1:T(8,128)(2,1)S(1)} collective-permute-done((bf16[256,24]{0,1:T(8,128)(2,1)}, bf16[256,24]{0,1:T(8,128)(2,1)S(1)}, u32[]{:S(2)}, u32[]{:S(2)}) %collective-permute-start.3) | collective-permute-done | bytes 12320 | tf_op jit(solution)/shard_map/ppermute | solution.py:520
  115.0 25.8 %collective-permute-done.10 = bf16[384,1024]{1,0:T(8,128)(2,1)S(1)} collective-permute-done((bf16[384,1024]{1,0:T(8,128)(2,1)}, bf16[384,1024]{1,0:T(8,128)(2,1)S(1)}, u32[]{:S(2)}, u32[]{:S(2)}) %collective-permute-start.10) | collective-permute-done | bytes 786464 | tf_op jit(solution)/shard_map/ppermute | solution.py:520
  143.0 19.1 %collective-permute-done.23 = bf16[512,1024]{1,0:T(8,128)(2,1)S(1)} collective-permute-done((bf16[512,1024]{1,0:T(8,128)(2,1)S(1)}, bf16[512,1024]{1,0:T(8,128)(2,1)S(1)}, u32[]{:S(2)}, u32[]{:S(2)}) %collective-permute-start.23) | collective-permute-done | bytes 1048608 | tf_op jit(solution)/shard_map/ppermute | solution.py:520
  209.9 8.3 %collective-permute-done.5 = bf16[2,1536,128]{2,1,0:T(8,128)(2,1)S(1)} collective-permute-done((bf16[2,1536,128]{2,1,0:T(8,128)(2,1)S(1)}, bf16[2,1536,128]{2,1,0:T(8,128)(2,1)S(1)}, u32[]{:S(2)}, u32[]{:S(2)}) %collective-permute-start.5) | collective-permute-done | bytes 786464 | tf_op jit(solution)/shard_map/ppermute | solution.py:520
  226.6 11.5 %collective-permute-done.7 = bf16[2,1536,128]{2,1,0:T(8,128)(2,1)S(1)} collective-permute-done((bf16[2,1536,128]{2,1,0:T(8,128)(2,1)S(1)}, bf16[2,1536,128]{2,1,0:T(8,128)(2,1)S(1)}, u32[]{:S(2)}, u32[]{:S(2)}) %collective-permute-start.7) | collective-permute-done | bytes 786464 | tf_op jit(solution)/shard_map/ppermute | solution.py:520
  240.1 11.7 %collective-permute-start.9 = (bf16[2,1536,128]{2,1,0:T(8,128)(2,1)S(1)}, bf16[2,1536,128]{2,1,0:T(8,128)(2,1)S(1)}, u32[]{:S(2)}, u32[]{:S(2)}) collective-permute-start(bf16[2,1536,128]{2,1,0:T(8,128)(2,1)S(1)} %fusion.36), channel_id=1, source_target_pairs={{0,16},{4,20},{8,24},{12,28},{16,0},{20,4},{24,8},{28,12},{1,17},{... | collective-permute-start | bytes 2359304 | tf_op jit(solution)/shard_map/ppermute | solution.py:520
  256.5 28.0 %collective-permute-done.9 = bf16[2,1536,128]{2,1,0:T(8,128)(2,1)S(1)} collective-permute-done((bf16[2,1536,128]{2,1,0:T(8,128)(2,1)S(1)}, bf16[2,1536,128]{2,1,0:T(8,128)(2,1)S(1)}, u32[]{:S(2)}, u32[]{:S(2)}) %collective-permute-start.9) | collective-permute-done | bytes 786464 | tf_op jit(solution)/shard_map/ppermute | solution.py:520
  285.6 8.2 ssd_forward.1.y_ref
  303.6 7.6 fusion.56
  316.8 10.6 %fusion.55 = f32[512,1024]{1,0:T(8,128)} fusion(bf16[1024,4096]{1,0:T(8,128)(2,1)} %constant_dynamic-update-slice_fusion.18, bf16[512,2048]{1,0:T(8,128)(2,1)} %get-tuple-element.170, bf16[512,2048]{1,0:T(8,128)(2,1)S(1)} %get-tuple-element.169), kind=kOutput, calls=%fused_computation.153 | convolution fusion | flops 4303355904 | bytes 14680064 | tf_op jit(solution)/shard_map/dot_general | solution.py:32
  353.9 5.9 collective-permute-start.28
  359.9 6.8 attend_backward.1
  372.2 5.7 add_convert_fusion.1
  385.9 5.7 collective-permute-done.62
  393.3 6.2 collective-permute-done.78
  409.5 8.3 %collective-permute-start.64 = (bf16[64,512]{1,0:T(8,128)(2,1)S(1)}, bf16[64,512]{1,0:T(8,128)(2,1)S(1)}, u32[]{:S(2)}, u32[]{:S(2)}) collective-permute-start(bf16[64,512]{1,0:T(8,128)(2,1)S(1)} %dynamic-slice_convert_fusion.16), channel_id=1, source_target_pairs={{0,8},{4,12},{8,0},{12,4},{16,24},{20,28},{24,16},{28,20},{1,9},{5... | collective-permute-start | bytes 196616 | tf_op jit(solution)/shard_map/ppermute | solution.py:520
  422.1 11.3 %collective-permute-start.65 = (bf16[32,512]{1,0:T(8,128)(2,1)S(1)}, bf16[32,512]{1,0:T(8,128)(2,1)S(1)}, u32[]{:S(2)}, u32[]{:S(2)}) collective-permute-start(bf16[32,512]{1,0:T(8,128)(2,1)S(1)} %dynamic-slice_convert_fusion.19), channel_id=1, source_target_pairs={{0,16},{4,20},{8,24},{12,28},{16,0},{20,4},{24,8},{28,12},{1,17},{... | collective-permute-start | bytes 98312 | tf_op jit(solution)/shard_map/ppermute | solution.py:520
  438.8 7.8 collective-permute-done.26
  452.5 5.8 collective-permute-done.27
  483.0 8.4 %collective-permute-done.29 = bf16[2,1536,128]{2,1,0:T(8,128)(2,1)S(1)} collective-permute-done((bf16[2,1536,128]{2,1,0:T(8,128)(2,1)S(1)}, bf16[2,1536,128]{2,1,0:T(8,128)(2,1)S(1)}, u32[]{:S(2)}, u32[]{:S(2)}) %collective-permute-start.29) | collective-permute-done | bytes 786464 | tf_op jit(solution)/shard_map/ppermute | solution.py:520
  498.2 24.4 %collective-permute-done.73 = bf16[32,256]{1,0:T(8,128)(2,1)S(1)} collective-permute-done((bf16[32,256]{1,0:T(8,128)(2,1)S(1)}, bf16[32,256]{1,0:T(8,128)(2,1)S(1)}, u32[]{:S(2)}, u32[]{:S(2)}) %collective-permute-start.73) | collective-permute-done | bytes 16416 | tf_op jit(solution)/shard_map/ppermute | solution.py:520
  532.8 27.5 %ssd_backward.1 = (f32[2,256,1536]{2,1,0:T(8,128)S(1)}, f32[2,256,128]{2,1,0:T(8,128)S(1)}, f32[2,256,128]{2,1,0:T(8,128)S(1)}, f32[2,3,256,8]{3,2,1,0:T(8,128)S...) custom-call(f32[2,256,1536]{2,1,0:T(8,128)} %copy-done.1, ...), custom_call_target="tpu_custom_call" | custom-call | flops 3145728000 | bytes 16777216 | tf_op jit(solution)/shard_map/ssd_backward/pallas_call | solution.py:254
  560.4 6.6 fusion.179
  588.9 6.8 fusion.75
  662.5 18.0 %collective-permute-done.86 = bf16[256,4096]{1,0:T(8,128)(2,1)S(1)} collective-permute-done((bf16[256,4096]{1,0:T(8,128)(2,1)S(1)}, bf16[256,4096]{1,0:T(8,128)(2,1)S(1)}, u32[]{:S(2)}, u32[]{:S(2)}) %collective-permute-start.86) | collective-permute-done | bytes 2097184 | tf_op jit(solution)/shard_map/ppermute | solution.py:520
  691.4 9.4 %collective-permute-done.87 = bf16[128,4096]{1,0:T(8,128)(2,1)S(1)} collective-permute-done((bf16[128,4096]{1,0:T(8,128)(2,1)S(1)}, bf16[128,4096]{1,0:T(8,128)(2,1)S(1)}, u32[]{:S(2)}, u32[]{:S(2)}) %collective-permute-start.87) | collective-permute-done | bytes 1048608 | tf_op jit(solution)/shard_map/ppermute | solution.py:520
  701.4 17.4 %collective-permute-done.38 = bf16[256,3328]{1,0:T(8,128)(2,1)S(1)} collective-permute-done((bf16[256,3328]{1,0:T(8,128)(2,1)S(1)}, bf16[256,3328]{1,0:T(8,128)(2,1)S(1)}, u32[]{:S(2)}, u32[]{:S(2)}) %collective-permute-start.38) | collective-permute-done | bytes 1703968 | tf_op jit(solution)/shard_map/ppermute | solution.py:520
  722.4 10.1 %collective-permute-done.39 = bf16[128,3328]{1,0:T(8,128)(2,1)S(1)} collective-permute-done((bf16[128,3328]{1,0:T(8,128)(2,1)S(1)}, bf16[128,3328]{1,0:T(8,128)(2,1)S(1)}, u32[]{:S(2)}, u32[]{:S(2)}) %collective-permute-start.39) | collective-permute-done | bytes 852000 | tf_op jit(solution)/shard_map/ppermute | solution.py:520
  736.1 12.9 %collective-permute-done.40 = bf16[64,3328]{1,0:T(8,128)(2,1)S(1)} collective-permute-done((bf16[64,3328]{1,0:T(8,128)(2,1)S(1)}, bf16[64,3328]{1,0:T(8,128)(2,1)S(1)}, u32[]{:S(2)}, u32[]{:S(2)}) %collective-permute-start.40) | collective-permute-done | bytes 426016 | tf_op jit(solution)/shard_map/ppermute | solution.py:520
  752.1 7.9 collective-permute-done.41
  778.8 18.6 %collective-permute-done.60 = bf16[192,1024]{1,0:T(8,128)(2,1)S(1)} collective-permute-done((bf16[192,1024]{1,0:T(8,128)(2,1)S(1)}, bf16[192,1024]{1,0:T(8,128)(2,1)S(1)}, u32[]{:S(2)}, u32[]{:S(2)}) %collective-permute-start.60) | collective-permute-done | bytes 393248 | tf_op jit(solution)/shard_map/ppermute | solution.py:520
  798.8 9.9 %collective-permute-done.100 = bf16[256,1024]{1,0:T(8,128)(2,1)S(1)} collective-permute-done((bf16[256,1024]{1,0:T(8,128)(2,1)S(1)}, bf16[256,1024]{1,0:T(8,128)(2,1)S(1)}, u32[]{:S(2)}, u32[]{:S(2)}) %collective-permute-start.100) | collective-permute-done | bytes 524320 | tf_op jit(solution)/shard_map/ppermute | solution.py:520
  (815 shorter events, 416.7 us)
Async XLA Ops:
  0.7 79.8 %collective-permute-start.19 = (bf16[128,1024]{1,0:T(8,128)(2,1)}, bf16[128,1024]{1,0:T(8,128)(2,1)}, u32[]{:S(2)}, u32[]{:S(2)}) collective-permute-start(bf16[128,1024]{1,0:T(8,128)(2,1)} %param.34), channel_id=1, source_target_pairs={{0,2},{1,3},{2,0},{3,1},{4,6},{5,7},{6,4},{7,5},{8,10},{9,11},{10,... | collective-permute-start | bytes 786440 | tf_op jit(solution)/shard_map/ppermute | solution.py:520
  3.7 80.1 %collective-permute-start.12 = (bf16[256,512]{1,0:T(8,128)(2,1)}, bf16[256,512]{1,0:T(8,128)(2,1)}, u32[]{:S(2)}, u32[]{:S(2)}) collective-permute-start(bf16[256,512]{1,0:T(8,128)(2,1)} %param.32), channel_id=1, source_target_pairs={{0,2},{1,3},{2,0},{3,1},{4,6},{5,7},{6,4},{7,5},{8,10},{9,11},{10,... | collective-permute-start | bytes 786440 | tf_op jit(solution)/shard_map/ppermute | solution.py:520
  3.8 74.0 %collective-permute-start.14 = (bf16[256,256]{1,0:T(8,128)(2,1)}, bf16[256,256]{1,0:T(8,128)(2,1)}, u32[]{:S(2)}, u32[]{:S(2)}) collective-permute-start(bf16[256,256]{1,0:T(8,128)(2,1)} %param.33), channel_id=1, source_target_pairs={{0,2},{1,3},{2,0},{3,1},{4,6},{5,7},{6,4},{7,5},{8,10},{9,11},{10,... | collective-permute-start | bytes 393224 | tf_op jit(solution)/shard_map/ppermute | solution.py:520
  5.7 83.5 %collective-permute-start = (bf16[256,3328]{1,0:T(8,128)(2,1)}, bf16[256,3328]{1,0:T(8,128)(2,1)}, u32[]{:S(2)}, u32[]{:S(2)}) collective-permute-start(bf16[256,3328]{1,0:T(8,128)(2,1)} %param.23), channel_id=1, source_target_pairs={{0,2},{1,3},{2,0},{3,1},{4,6},{5,7},{6,4},{7,5},{8,10},{9,11},{10,... | collective-permute-start | bytes 5111816 | tf_op jit(solution)/shard_map/ppermute | solution.py:520
  5.8 49.6 %collective-permute-start.3 = (bf16[256,24]{0,1:T(8,128)(2,1)}, bf16[256,24]{0,1:T(8,128)(2,1)S(1)}, u32[]{:S(2)}, u32[]{:S(2)}) collective-permute-start(bf16[256,24]{0,1:T(8,128)(2,1)} %param.24), channel_id=1, source_target_pairs={{0,2},{1,3},{2,0},{3,1},{4,6},{5,7},{6,4},{7,5},{8,10},{9,11},{10,... | collective-permute-start | bytes 36872 | tf_op jit(solution)/shard_map/ppermute | solution.py:520
  75.2 92.9 %collective-permute-start.21 = (bf16[256,4096]{1,0:T(8,128)(2,1)}, bf16[256,4096]{1,0:T(8,128)(2,1)}, u32[]{:S(2)}, u32[]{:S(2)}) collective-permute-start(bf16[256,4096]{1,0:T(8,128)(2,1)} %param.36), channel_id=1, source_target_pairs={{0,2},{1,3},{2,0},{3,1},{4,6},{5,7},{6,4},{7,5},{8,10},{9,11},{10,... | collective-permute-start | bytes 6291464 | tf_op jit(solution)/shard_map/ppermute | solution.py:520
  95.2 80.8 %collective-permute-start.1 = (bf16[512,3328]{1,0:T(8,128)(2,1)}, bf16[512,3328]{1,0:T(8,128)(2,1)}, u32[]{:S(2)}, u32[]{:S(2)}) collective-permute-start(bf16[512,3328]{1,0:T(8,128)(2,1)} %pad_maximum_fusion.4), channel_id=1, source_target_pairs={{0,1},{1,0},{2,3},{3,2},{4,5},{5,4},{6,7},{7,6},{8,9},{9,8},{10,11... | collective-permute-start | bytes 10223624 | tf_op jit(solution)/shard_map/ppermute | solution.py:520
  104.3 36.5 %collective-permute-start.10 = (bf16[384,1024]{1,0:T(8,128)(2,1)}, bf16[384,1024]{1,0:T(8,128)(2,1)S(1)}, u32[]{:S(2)}, u32[]{:S(2)}) collective-permute-start(bf16[384,1024]{1,0:T(8,128)(2,1)} %param.31), channel_id=1, source_target_pairs={{0,2},{1,3},{2,0},{3,1},{4,6},{5,7},{6,4},{7,5},{8,10},{9,11},{10,... | collective-permute-start | bytes 2359304 | tf_op jit(solution)/shard_map/ppermute | solution.py:520
  104.8 57.3 %collective-permute-start.23 = (bf16[512,1024]{1,0:T(8,128)(2,1)S(1)}, bf16[512,1024]{1,0:T(8,128)(2,1)S(1)}, u32[]{:S(2)}, u32[]{:S(2)}) collective-permute-start(bf16[512,1024]{1,0:T(8,128)(2,1)S(1)} %copy-done.42), channel_id=1, source_target_pairs={{0,2},{1,3},{2,0},{3,1},{4,6},{5,7},{6,4},{7,5},{8,10},{9,11},{10,... | collective-permute-start | bytes 3145736 | tf_op jit(solution)/shard_map/ppermute | solution.py:520
  111.0 53.8 %collective-permute-start.17 = (bf16[2,2,256,256]{3,2,1,0:T(8,128)(2,1)S(1)}, bf16[2,2,256,256]{3,2,1,0:T(8,128)(2,1)S(1)}, u32[]{:S(2)}, u32[]{:S(2)}) collective-permute-start(bf16[2,2,256,256]{3,2,1,0:T(8,128)(2,1)S(1)} %pad_maximum_fusion.25), channel_id=1, source_target_pairs={{0,8},{4,12},{8,0},{12,4},{16,24},{20,28},{24,16},{28,20},{1,9},{5... | collective-permute-start | bytes 1572872 | tf_op jit(solution)/shard_map/ppermute | solution.py:520
  142.1 64.9 %collective-permute-start.11 = (bf16[768,1024]{1,0:T(8,128)(2,1)}, bf16[768,1024]{1,0:T(8,128)(2,1)}, u32[]{:S(2)}, u32[]{:S(2)}) collective-permute-start(bf16[768,1024]{1,0:T(8,128)(2,1)} %pad_maximum_fusion.11), channel_id=1, source_target_pairs={{0,1},{1,0},{2,3},{3,2},{4,5},{5,4},{6,7},{7,6},{8,9},{9,8},{10,11... | collective-permute-start | bytes 4718600 | tf_op jit(solution)/shard_map/ppermute | solution.py:520
  163.8 45.1 %collective-permute-start.24 = (bf16[1024,1024]{1,0:T(8,128)(2,1)}, bf16[1024,1024]{1,0:T(8,128)(2,1)S(1)}, u32[]{:S(2)}, u32[]{:S(2)}) collective-permute-start(bf16[1024,1024]{1,0:T(8,128)(2,1)} %pad_maximum_fusion.8), channel_id=1, source_target_pairs={{0,1},{1,0},{2,3},{3,2},{4,5},{5,4},{6,7},{7,6},{8,9},{9,8},{10,11... | collective-permute-start | bytes 6291464 | tf_op jit(solution)/shard_map/ppermute | solution.py:520
  172.6 79.2 %collective-permute-start.22 = (bf16[512,4096]{1,0:T(8,128)(2,1)}, bf16[512,4096]{1,0:T(8,128)(2,1)}, u32[]{:S(2)}, u32[]{:S(2)}) collective-permute-start(bf16[512,4096]{1,0:T(8,128)(2,1)} %pad_maximum_fusion), channel_id=1, source_target_pairs={{0,1},{1,0},{2,3},{3,2},{4,5},{5,4},{6,7},{7,6},{8,9},{9,8},{10,11... | collective-permute-start | bytes 12582920 | tf_op jit(solution)/shard_map/ppermute | solution.py:520
  240.1 44.4 %collective-permute-start.9 = (bf16[2,1536,128]{2,1,0:T(8,128)(2,1)S(1)}, bf16[2,1536,128]{2,1,0:T(8,128)(2,1)S(1)}, u32[]{:S(2)}, u32[]{:S(2)}) collective-permute-start(bf16[2,1536,128]{2,1,0:T(8,128)(2,1)S(1)} %fusion.36), channel_id=1, source_target_pairs={{0,16},{4,20},{8,24},{12,28},{16,0},{20,4},{24,8},{28,12},{1,17},{... | collective-permute-start | bytes 2359304 | tf_op jit(solution)/shard_map/ppermute | solution.py:520
  366.9 55.3 %collective-permute-start.25 = (bf16[4,2,256,256]{3,2,1,0:T(8,128)(2,1)S(1)}, bf16[4,2,256,256]{3,2,1,0:T(8,128)(2,1)S(1)}, u32[]{:S(2)}, u32[]{:S(2)}) collective-permute-start(bf16[4,2,256,256]{3,2,1,0:T(8,128)(2,1)S(1)} %slice.221), channel_id=1, source_target_pairs={{0,4},{4,0},{8,12},{12,8},{16,20},{20,16},{24,28},{28,24},{1,5},{5... | collective-permute-start | bytes 3145736 | tf_op jit(solution)/shard_map/ppermute | solution.py:520
  370.7 107.9 %collective-permute-start.53 = (bf16[768,1024]{1,0:T(8,128)(2,1)}, bf16[768,1024]{1,0:T(8,128)(2,1)S(1)}, u32[]{:S(2)}, u32[]{:S(2)}) collective-permute-start(bf16[768,1024]{1,0:T(8,128)(2,1)} %convolution_convert_fusion.3), channel_id=1, source_target_pairs={{0,1},{1,0},{2,3},{3,2},{4,5},{5,4},{6,7},{7,6},{8,9},{9,8},{10,11... | collective-permute-start | bytes 4718600 | tf_op jit(solution)/shard_map/ppermute | solution.py:520
  381.2 249.5 %collective-permute-start.85 = (bf16[512,4096]{1,0:T(8,128)(2,1)}, bf16[512,4096]{1,0:T(8,128)(2,1)}, u32[]{:S(2)}, u32[]{:S(2)}) collective-permute-start(bf16[512,4096]{1,0:T(8,128)(2,1)} %convolution_convert_fusion.1), channel_id=1, source_target_pairs={{0,1},{1,0},{2,3},{3,2},{4,5},{5,4},{6,7},{7,6},{8,9},{9,8},{10,11... | collective-permute-start | bytes 12582920 | tf_op jit(solution)/shard_map/ppermute | solution.py:520
  382.3 140.4 %collective-permute-start.93 = (bf16[1024,1024]{1,0:T(8,128)(2,1)S(1)}, bf16[1024,1024]{1,0:T(8,128)(2,1)S(1)}, u32[]{:S(2)}, u32[]{:S(2)}) collective-permute-start(bf16[1024,1024]{1,0:T(8,128)(2,1)S(1)} %convolution_convert_fusion.2), channel_id=1, source_target_pairs={{0,1},{1,0},{2,3},{3,2},{4,5},{5,4},{6,7},{7,6},{8,9},{9,8},{10,11... | collective-permute-start | bytes 6291464 | tf_op jit(solution)/shard_map/ppermute | solution.py:520
  479.8 49.4 %collective-permute-start.54 = (bf16[384,1024]{1,0:T(8,128)(2,1)S(1)}, bf16[384,1024]{1,0:T(8,128)(2,1)S(1)}, u32[]{:S(2)}, u32[]{:S(2)}) collective-permute-start(bf16[384,1024]{1,0:T(8,128)(2,1)S(1)} %slice.381), channel_id=1, source_target_pairs={{0,2},{1,3},{2,0},{3,1},{4,6},{5,7},{6,4},{7,5},{8,10},{9,11},{10,... | collective-permute-start | bytes 2359304 | tf_op jit(solution)/shard_map/ppermute | solution.py:520
  493.3 37.3 %collective-permute-start.30 = (bf16[2,1536,128]{2,1,0:T(8,128)(2,1)S(1)}, bf16[2,1536,128]{2,1,0:T(8,128)(2,1)S(1)}, u32[]{:S(2)}, u32[]{:S(2)}) collective-permute-start(bf16[2,1536,128]{2,1,0:T(8,128)(2,1)S(1)} %fusion.41), channel_id=1, source_target_pairs={{0,16},{4,20},{8,24},{12,28},{16,0},{20,4},{24,8},{28,12},{1,17},{... | collective-permute-start | bytes 2359304 | tf_op jit(solution)/shard_map/ppermute | solution.py:520
  525.3 112.5 %collective-permute-start.94 = (bf16[512,1024]{1,0:T(8,128)(2,1)}, bf16[512,1024]{1,0:T(8,128)(2,1)}, u32[]{:S(2)}, u32[]{:S(2)}) collective-permute-start(bf16[512,1024]{1,0:T(8,128)(2,1)} %slice.380), channel_id=1, source_target_pairs={{0,2},{1,3},{2,0},{3,1},{4,6},{5,7},{6,4},{7,5},{8,10},{9,11},{10,... | collective-permute-start | bytes 3145736 | tf_op jit(solution)/shard_map/ppermute | solution.py:520
  527.3 51.8 %collective-permute-start.75 = (bf16[64,256]{1,0:T(8,128)(2,1)S(1)}, bf16[64,256]{1,0:T(8,128)(2,1)}, u32[]{:S(2)}, u32[]{:S(2)}) collective-permute-start(bf16[64,256]{1,0:T(8,128)(2,1)S(1)} %maximum_select_fusion.20), channel_id=1, source_target_pairs={{0,8},{4,12},{8,0},{12,4},{16,24},{20,28},{24,16},{28,20},{1,9},{5... | collective-permute-start | bytes 98312 | tf_op jit(solution)/shard_map/ppermute | solution.py:520
  530.5 98.1 %collective-permute-start.55 = (bf16[192,1024]{1,0:T(8,128)(2,1)}, bf16[192,1024]{1,0:T(8,128)(2,1)}, u32[]{:S(2)}, u32[]{:S(2)}) collective-permute-start(bf16[192,1024]{1,0:T(8,128)(2,1)} %dynamic-slice_convert_fusion.5), channel_id=1, source_target_pairs={{0,4},{4,0},{8,12},{12,8},{16,20},{20,16},{24,28},{28,24},{1,5},{5... | collective-permute-start | bytes 1179656 | tf_op jit(solution)/shard_map/ppermute | solution.py:520
  582.9 61.2 %collective-permute-start.76 = (bf16[128,256]{1,0:T(8,128)(2,1)S(1)}, bf16[128,256]{1,0:T(8,128)(2,1)S(1)}, u32[]{:S(2)}, u32[]{:S(2)}) collective-permute-start(bf16[128,256]{1,0:T(8,128)(2,1)S(1)} %maximum_select_fusion.18), channel_id=1, source_target_pairs={{0,4},{4,0},{8,12},{12,8},{16,20},{20,16},{24,28},{28,24},{1,5},{5... | collective-permute-start | bytes 196616 | tf_op jit(solution)/shard_map/ppermute | solution.py:520
  637.8 42.7 %collective-permute-start.86 = (bf16[256,4096]{1,0:T(8,128)(2,1)S(1)}, bf16[256,4096]{1,0:T(8,128)(2,1)S(1)}, u32[]{:S(2)}, u32[]{:S(2)}) collective-permute-start(bf16[256,4096]{1,0:T(8,128)(2,1)S(1)} %slice.378), channel_id=1, source_target_pairs={{0,2},{1,3},{2,0},{3,1},{4,6},{5,7},{6,4},{7,5},{8,10},{9,11},{10,... | collective-permute-start | bytes 6291464 | tf_op jit(solution)/shard_map/ppermute | solution.py:520
  644.1 40.1 %collective-permute-start.37 = (bf16[512,3328]{1,0:T(8,128)(2,1)S(1)}, bf16[512,3328]{1,0:T(8,128)(2,1)S(1)}, u32[]{:S(2)}, u32[]{:S(2)}) collective-permute-start(bf16[512,3328]{1,0:T(8,128)(2,1)S(1)} %copy-done.160), channel_id=1, source_target_pairs={{0,1},{1,0},{2,3},{3,2},{4,5},{5,4},{6,7},{7,6},{8,9},{9,8},{10,11... | collective-permute-start | bytes 10223624 | tf_op jit(solution)/shard_map/ppermute | solution.py:520
  686.4 32.4 %collective-permute-start.38 = (bf16[256,3328]{1,0:T(8,128)(2,1)S(1)}, bf16[256,3328]{1,0:T(8,128)(2,1)S(1)}, u32[]{:S(2)}, u32[]{:S(2)}) collective-permute-start(bf16[256,3328]{1,0:T(8,128)(2,1)S(1)} %slice.379), channel_id=1, source_target_pairs={{0,2},{1,3},{2,0},{3,1},{4,6},{5,7},{6,4},{7,5},{8,10},{9,11},{10,... | collective-permute-start | bytes 5111816 | tf_op jit(solution)/shard_map/ppermute | solution.py:520
  688.3 84.5 %collective-permute-start.59 = (bf16[96,1024]{1,0:T(8,128)(2,1)S(1)}, bf16[96,1024]{1,0:T(8,128)(2,1)}, u32[]{:S(2)}, u32[]{:S(2)}) collective-permute-start(bf16[96,1024]{1,0:T(8,128)(2,1)S(1)} %maximum_select_fusion.13), channel_id=1, source_target_pairs={{0,8},{4,12},{8,0},{12,4},{16,24},{20,28},{24,16},{28,20},{1,9},{5... | collective-permute-start | bytes 589832 | tf_op jit(solution)/shard_map/ppermute | solution.py:520
  690.5 83.8 %collective-permute-start.99 = (bf16[128,1024]{1,0:T(8,128)(2,1)S(1)}, bf16[128,1024]{1,0:T(8,128)(2,1)}, u32[]{:S(2)}, u32[]{:S(2)}) collective-permute-start(bf16[128,1024]{1,0:T(8,128)(2,1)S(1)} %maximum_select_fusion.12), channel_id=1, source_target_pairs={{0,8},{4,12},{8,0},{12,4},{16,24},{20,28},{24,16},{28,20},{1,9},{5... | collective-permute-start | bytes 786440 | tf_op jit(solution)/shard_map/ppermute | solution.py:520
  762.7 47.7 %collective-permute-start.92 = (bf16[128,4096]{1,0:T(8,128)(2,1)S(1)}, bf16[128,4096]{1,0:T(8,128)(2,1)S(1)}, u32[]{:S(2)}, u32[]{:S(2)}) collective-permute-start(bf16[128,4096]{1,0:T(8,128)(2,1)S(1)} %maximum_select_fusion.2), channel_id=1, source_target_pairs={{0,4},{4,0},{8,12},{12,8},{16,20},{20,16},{24,28},{28,24},{1,5},{5... | collective-permute-start | bytes 3145736 | tf_op jit(solution)/shard_map/ppermute | solution.py:520
  775.5 33.2 %collective-permute-start.100 = (bf16[256,1024]{1,0:T(8,128)(2,1)S(1)}, bf16[256,1024]{1,0:T(8,128)(2,1)S(1)}, u32[]{:S(2)}, u32[]{:S(2)}) collective-permute-start(bf16[256,1024]{1,0:T(8,128)(2,1)S(1)} %maximum_select_fusion.7), channel_id=1, source_target_pairs={{0,4},{4,0},{8,12},{12,8},{16,20},{20,16},{24,28},{28,24},{1,5},{5... | collective-permute-start | bytes 1572872 | tf_op jit(solution)/shard_map/ppermute | solution.py:520
  777.4 40.6 %collective-permute-start.44 = (bf16[128,3328]{1,0:T(8,128)(2,1)S(1)}, bf16[128,3328]{1,0:T(8,128)(2,1)S(1)}, u32[]{:S(2)}, u32[]{:S(2)}) collective-permute-start(bf16[128,3328]{1,0:T(8,128)(2,1)S(1)} %maximum_select_fusion.4), channel_id=1, source_target_pairs={{0,4},{4,0},{8,12},{12,8},{16,20},{20,16},{24,28},{28,24},{1,5},{5... | collective-permute-start | bytes 2555912 | tf_op jit(solution)/shard_map/ppermute | solution.py:520
  (235 other events, 2898.6 us)

commit v2 on v1

--- a/solution.py
+++ b/solution.py
@@ -510,6 +510,259 @@
     )(bounds, starts, queries_t, key_table, out_t, grad_t, logs)
 
 
+NEAR = (0, 2, 1, 3)
+
+
+def near_at(step, size):
+    return pl.ds(pl.multiple_of((lax.axis_index("wsh") ^ step) * size, 128), size)
+
+
+def project_kernel(x_ref, *refs):
+    *weights, out_ref = refs
+    size = weights[0].shape[0]
+    total = None
+    for step, weight in zip(NEAR, weights):
+        part = mat(x_ref[:, near_at(step, size)], weight[...])
+        total = part if total is None else total + part
+    out_ref[...] = total
+
+
+def project(x, weights, tile):
+    tokens, depth = x.shape
+    size, columns = weights[0].shape
+    return pl.pallas_call(
+        project_kernel,
+        grid=(columns // tile,),
+        in_specs=[pl.BlockSpec((tokens, depth), lambda i: (0, 0))]
+        + [pl.BlockSpec((size, tile), lambda i: (0, i))] * 4,
+        out_specs=pl.BlockSpec((tokens, tile), lambda i: (0, i)),
+        out_shape=jax.ShapeDtypeStruct((tokens, columns), F32),
+        compiler_params=pltpu.CompilerParams(vmem_limit_bytes=40 * MIB),
+        cost_estimate=pl.CostEstimate(
+            flops=2 * tokens * depth * columns,
+            bytes_accessed=2 * depth * columns + 4 * tokens * columns,
+            transcendentals=0,
+        ),
+        name="project",
+    )(x, *weights)
+
+
+def unproject_kernel(base_ref, grad_ref, *refs):
+    *weights, out_ref = refs
+    size = weights[0].shape[0]
+
+    @pl.when(pl.program_id(0) == 0)
+    def _():
+        out_ref[...] = base_ref[...]
+
+    for step, weight in zip(NEAR, weights):
+        out_ref[:, near_at(step, size)] += mat_right_t(grad_ref[...], weight[...])
+
+
+def unproject(base, grad, weights, tile):
+    tokens, columns = grad.shape
+    size = weights[0].shape[0]
+    whole = pl.BlockSpec((tokens, 4 * size), lambda i: (0, 0))
+    return pl.pallas_call(
+        unproject_kernel,
+        grid=(columns // tile,),
+        in_specs=[whole, pl.BlockSpec((tokens, tile), lambda i: (0, i))]
+        + [pl.BlockSpec((size, tile), lambda i: (0, i))] * 4,
+        out_specs=whole,
+        out_shape=jax.ShapeDtypeStruct((tokens, 4 * size), F32),
+        compiler_params=pltpu.CompilerParams(vmem_limit_bytes=40 * MIB),
+        cost_estimate=pl.CostEstimate(
+            flops=8 * tokens * size * columns,
+            bytes_accessed=8 * size * columns + 2 * tokens * columns,
+            transcendentals=0,
+        ),
+        name="unproject",
+    )(base, grad, *weights)
+
+
+def out_proj_kernel(x_ref, mixed_ref, heads_ref, gain_ref, *refs):
+    *weights, middle_ref, normed_ref = refs
+    wide = mixed_ref.shape[1] // 4
+    narrow = heads_ref.shape[0] // 4
+    middle_ref[...] = x_ref[...].astype(F32)
+    for step, weight in zip(NEAR, weights):
+        middle_ref[...] += mat(mixed_ref[:, near_at(step, wide)], weight[:wide]) + mat_left_t(
+            heads_ref[near_at(step, narrow), :], weight[wide:]
+        )
+    middle = middle_ref[...]
+    normed_ref[...] = (middle * inv_rms(middle) * gain_ref[...]).astype(BF16)
+
+
+def out_project(x, mixed, heads_t, gain, weights):
+    vmem = pl.BlockSpec(memory_space=pltpu.VMEM)
+    return pl.pallas_call(
+        out_proj_kernel,
+        in_specs=[vmem] * 8,
+        out_specs=[vmem, vmem],
+        out_shape=[jax.ShapeDtypeStruct(x.shape, F32), jax.ShapeDtypeStruct(x.shape, BF16)],
+        compiler_params=pltpu.CompilerParams(vmem_limit_bytes=40 * MIB),
+        cost_estimate=pl.CostEstimate(
+            flops=2 * x.size * 2048, bytes_accessed=12 * MIB, transcendentals=0
+        ),
+        name="out_project",
+    )(x, mixed, heads_t, gain[None], *weights)
+
+
+def out_back_kernel(branch_ref, *refs):
+    *weights, mixed_ref, heads_ref = refs
+    wide = mixed_ref.shape[1] // 4
+    narrow = heads_ref.shape[0] // 4
+    for step, weight in zip(NEAR, weights):
+        mixed_ref[:, near_at(step, wide)] = mat_right_t(branch_ref[...], weight[:wide])
+        heads_ref[near_at(step, narrow), :] = mat_right_t(weight[wide:], branch_ref[...]).astype(
+            BF16
+        )
+
+
+def out_unproject(branch, weights, mixed_width, heads_width):
+    vmem = pl.BlockSpec(memory_space=pltpu.VMEM)
+    tokens = branch.shape[0]
+    return pl.pallas_call(
+        out_back_kernel,
+        in_specs=[vmem] * 5,
+        out_specs=[vmem, vmem],
+        out_shape=[
+            jax.ShapeDtypeStruct((tokens, mixed_width), F32),
+            jax.ShapeDtypeStruct((heads_width, tokens), BF16),
+        ],
+        compiler_params=pltpu.CompilerParams(vmem_limit_bytes=40 * MIB),
+        cost_estimate=pl.CostEstimate(
+            flops=2 * branch.size * 2048, bytes_accessed=12 * MIB, transcendentals=0
+        ),
+        name="out_unproject",
+    )(branch, *weights)
+
+
+FF_TILE = 256
+
+
+def mlp_kernel(
+    place_ref, normed_ref, top_ref, middle_ref, gain_ref, *refs
+):
+    gates, ups, downs = refs[0:4], refs[4:8], refs[8:12]
+    layer_ref, grad_ref, branch_ref, gain_grad_ref, hidden_ref, pair_ref = refs[12:18]
+    down_tile, out_sum, back_sum = refs[18:]
+    step_at = pl.program_id(0)
+    per_piece = pl.num_programs(0) // 4
+    size = gates[0].shape[0]
+    for piece in range(4):
+
+        @pl.when(step_at // per_piece == piece)
+        def _():
+            down_tile[...] = downs[piece][...]
+
+    gate = up = None
+    for step, gate_ref, up_ref in zip(NEAR, gates, ups):
+        rows = normed_ref[:, near_at(step, size)]
+        gate_part, up_part = mat(rows, gate_ref[...]), mat(rows, up_ref[...])
+        gate = gate_part if gate is None else gate + gate_part
+        up = up_part if up is None else up + up_part
+    sig = 1.0 / (1.0 + jnp.exp(-gate))
+    silu = gate * sig
+    hidden = (silu * up).astype(BF16)
+    hidden_ref[...] = hidden
+    grad_hidden = mat_right_t(top_ref[...], down_tile[...])
+    grad_gate = (grad_hidden * up * (sig + silu * (1.0 - sig))).astype(BF16)
+    grad_up = (grad_hidden * silu).astype(BF16)
+    pair_ref[0] = grad_gate
+    pair_ref[1] = grad_up
+
+    @pl.when(step_at == 0)
+    def _():
+        out_sum[...] = jnp.zeros(out_sum.shape, F32)
+        back_sum[...] = jnp.zeros(back_sum.shape, F32)
+
+    out_sum[...] += mat(hidden, down_tile[...])
+    for step, gate_ref, up_ref in zip(NEAR, gates, ups):
+        back_sum[:, near_at(step, size)] += mat_right_t(grad_gate, gate_ref[...]) + mat_right_t(
+            grad_up, up_ref[...]
+        )
+
+    @pl.when(step_at == pl.num_programs(0) - 1)
+    def _():
+        middle = middle_ref[...]
+        layer_ref[...] = (middle + out_sum[...]).astype(BF16)
+        grad_rows, grad_gain = rms_pull(middle, inv_rms(middle), gain_ref[...], back_sum[...])
+        grad = top_ref[...].astype(F32) + grad_rows
+        grad_ref[...] = grad
+        branch_ref[...] = grad.astype(BF16)
+        gain_grad_ref[...] = grad_gain[None]
+
+
+def mlp_both(place, normed, top, middle, gain, gu_weights, down_weights):
+    tokens, features = middle.shape
+    size, columns = gu_weights[0].shape
+    width = columns // 2
+    steps = width // FF_TILE
+    per_piece = steps // 4
+
+    def natural(i, p):
+        piece = i // per_piece
+        near = (piece % 2) * 2 + piece // 2
+        return (near ^ p[0]) * per_piece + i % per_piece
+
+    whole = pl.BlockSpec((tokens, features), lambda i, p: (0, 0))
+    gain_spec = pl.BlockSpec((1, features), lambda i, p: (0, 0))
+
+    def down_spec(piece):
+        return pl.BlockSpec(
+            (FF_TILE, features),
+            lambda i, p: (jnp.clip(i - piece * per_piece, 0, per_piece - 1), 0),
+        )
+
+    return pl.pallas_call(
+        mlp_kernel,
+        grid_spec=pltpu.PrefetchScalarGridSpec(
+            num_scalar_prefetch=1,
+            grid=(steps,),
+            in_specs=[whole, whole, whole, gain_spec]
+            + [pl.BlockSpec((size, FF_TILE), lambda i, p: (0, natural(i, p)))] * 4
+            + [pl.BlockSpec((size, FF_TILE), lambda i, p: (0, natural(i, p) + steps))] * 4
+            + [down_spec(piece) for piece in range(4)],
+            out_specs=[
+                whole,
+                whole,
+                whole,
+                gain_spec,
+                pl.BlockSpec((tokens, FF_TILE), lambda i, p: (0, natural(i, p))),
+                pl.BlockSpec((2, tokens, FF_TILE), lambda i, p: (0, 0, natural(i, p))),
+            ],
+            scratch_shapes=[
+                pltpu.VMEM((FF_TILE, features), BF16),
+                pltpu.VMEM((tokens, features), F32),
+                pltpu.VMEM((tokens, features), F32),
+            ],
+        ),
+        out_shape=[
+            jax.ShapeDtypeStruct((tokens, features), BF16),
+            jax.ShapeDtypeStruct((tokens, features), F32),
+            jax.ShapeDtypeStruct((tokens, features), BF16),
+            jax.ShapeDtypeStruct((1, features), F32),
+            jax.ShapeDtypeStruct((tokens, width), BF16),
+            jax.ShapeDtypeStruct((2, tokens, width), BF16),
+        ],
+        compiler_params=pltpu.CompilerParams(vmem_limit_bytes=48 * MIB),
+        cost_estimate=pl.CostEstimate(
+            flops=12 * tokens * features * width, bytes_accessed=30 * MIB, transcendentals=0
+        ),
+        name="mlp_both",
+    )(
+        place,
+        normed,
+        top,
+        middle,
+        gain[None],
+        *gu_weights,
+        *gu_weights,
+        *down_weights,
+    )
+
+
 def passed_along(block, axis, distance):
     devices = range(lax.axis_size(axis))
     route = [(i - distance, i) for i in devices if i - distance in devices]
@@ -524,73 +777,15 @@
     return [1 << k for k in range(lax.axis_size(axis).bit_length() - 1)]
 
 
-def gathered_near(shard):
-    half = jnp.concatenate([shard, swapped(shard, "wsh", 2)], axis=0)
-    return jnp.concatenate([half, swapped(half, "wsh", 1)], axis=0)
-
-
-def near_order(array, axis):
-    here = lax.axis_index("wsh")
-    block = array.shape[axis] // 4
-    return jnp.concatenate(
-        [
-            lax.dynamic_slice_in_dim(array, (here ^ step) * block, block, axis)
-            for step in (0, 2, 1, 3)
-        ],
-        axis=axis,
-    )
-
-
-def natural_order(array, axis):
-    here = lax.axis_index("wsh")
-    block = array.shape[axis] // 4
-    places = []
-    for index in range(4):
-        step = here ^ index
-        place = jnp.where(step == 1, 2, jnp.where(step == 2, 1, step))
-        places.append(lax.dynamic_slice_in_dim(array, place * block, block, axis))
-    return jnp.concatenate(places, axis=axis)
-
-
-def reduced_over_wsh(send, keep):
-    came = swapped(send.astype(BF16), "wsh", 1)
-    both = keep + came.astype(F32)
-    block = both.shape[0] // 2
-    crossed = swapped(both[block:].astype(BF16), "wsh", 2)
-    return both[:block] + crossed.astype(F32)
-
-
-def pick_half(array, upper):
-    half = array.shape[0] // 2
-    return lax.dynamic_slice_in_dim(array, upper * half, half, 0)
-
-
-def joined(mine, other, upper):
-    return jnp.where(
-        upper == 1,
-        jnp.concatenate([other, mine], axis=0),
-        jnp.concatenate([mine, other], axis=0),
-    )
-
-
-def summed_over_ctx(part):
-    here = lax.axis_index("ctx")
-    bits = bits_of("ctx")
-    for bit in bits:
-        upper = (here // bit) % 2
-        came = swapped(pick_half(part, 1 - upper).astype(BF16), "ctx", bit)
-        part = pick_half(part, upper) + came.astype(F32)
-    part = part.astype(BF16)
-    for bit in bits[::-1]:
-        part = joined(part, swapped(part, "ctx", bit), (here // bit) % 2)
-    return part.astype(F32)
-
-
-def summed_everywhere(vector):
-    for axis in ("wsh", "ctx"):
-        for bit in bits_of(axis):
-            vector = vector + swapped(vector, axis, bit)
-    return vector
+def after(value, earlier):
+    return lax.optimization_barrier((value, earlier))[0]
+
+
+def gathered_near(shard, earlier=None):
+    if earlier is not None:
+        shard = after(shard, earlier)
+    across = swapped(shard, "wsh", 2)
+    return [shard, across, swapped(shard, "wsh", 1), swapped(across, "wsh", 1)]
 
 
 def table_gather(rows):
@@ -637,6 +832,343 @@
         )
         total = total * other_total
     return reached
+
+
+TILE_ROWS = 256
+TILE_COLS = 512
+
+
+def ctx_bits(count):
+    return [1 << k for k in range(count.bit_length() - 1)]
+
+
+def partner_wsh(step):
+    return (lax.axis_index("ctx"), lax.axis_index("wsh") ^ step)
+
+
+def partner_ctx(step):
+    return (lax.axis_index("ctx") ^ step, lax.axis_index("wsh"))
+
+
+def remote(source, target, send, recv, device):
+    return pltpu.make_async_remote_copy(
+        src_ref=source,
+        dst_ref=target,
+        send_sem=send,
+        recv_sem=recv,
+        device_id=device,
+        device_id_type=pl.DeviceIdType.MESH,
+    )
+
+
+def grads_kernel(
+    count,
+    split,
+    early_units,
+    late_units,
+    gu_units,
+    one_ref,
+    two_ref,
+    mix_ref,
+    hid_ref,
+    early_ref,
+    late_ref,
+    pair_ref,
+    branch_ref,
+    top_ref,
+    small_ref,
+    early_out,
+    late_out,
+    gu_out,
+    mix_out,
+    down_out,
+    small_out,
+    core_out,
+    work,
+    y_in,
+    ctx_in,
+    final,
+    small_in,
+    core_sems,
+    y_sems,
+    rs_sems,
+    ag_sems,
+    small_sems,
+    out_sems,
+):
+    bits = ctx_bits(count)
+    here = lax.axis_index("ctx")
+    units = work.shape[0]
+    rows = work.shape[2]
+    width = work.shape[3]
+    wsh_steps = (1, 2)
+    barrier = pltpu.get_barrier_semaphore()
+    partners = [partner_wsh(step) for step in wsh_steps] + [partner_ctx(bit) for bit in bits]
+    for device in partners:
+        pl.semaphore_signal(
+            barrier, inc=1, device_id=device, device_id_type=pl.DeviceIdType.MESH
+        )
+    pl.semaphore_wait(barrier, len(partners))
+
+    sizes = [rows >> (k + 1) for k in range(len(bits))]
+    starts = []
+    others = []
+    base = 0
+    for bit, size in zip(bits, sizes):
+        upper = (here // bit) % 2
+        others.append(base + (1 - upper) * size)
+        base = base + upper * size
+        starts.append(base)
+
+    def span(start, size):
+        return pl.ds(pl.multiple_of(start, 16), size)
+
+    def core_copy(u):
+        return remote(
+            core_out.at[u % 2],
+            work.at[u],
+            core_sems.at[0, u],
+            core_sems.at[1, u],
+            partner_wsh(1),
+        )
+
+    def y_copy(u):
+        return remote(work.at[u, 1], y_in.at[u], y_sems.at[0, u], y_sems.at[1, u], partner_wsh(2))
+
+    recv_base = [rows - (rows >> k) for k in range(len(bits))]
+
+    def rs_copy(u, k):
+        return remote(
+            work.at[u, 0, span(others[k], sizes[k])],
+            ctx_in.at[u, pl.ds(recv_base[k], sizes[k])],
+            rs_sems.at[0, k, u],
+            rs_sems.at[1, k, u],
+            partner_ctx(bits[k]),
+        )
+
+    def ag_copy(u, k):
+        return remote(
+            final.at[u, span(starts[k], sizes[k])],
+            final.at[u, span(starts[k], sizes[k])],
+            ag_sems.at[0, k, u],
+            ag_sems.at[1, k, u],
+            partner_ctx(bits[k]),
+        )
+
+    limits = []
+    first_unit = 0
+    for size in (early_units, late_units, gu_units, 4, 4):
+        limits.append((first_unit, first_unit + size))
+        first_unit += size
+    outs = (early_out, late_out, gu_out, mix_out, down_out)
+
+    def by_part(u, action):
+        for part, (low, high) in enumerate(limits):
+            pl.when((u >= low) & (u < high))(functools.partial(action, part, u - low))
+
+    def each_out(u, act):
+        def one(part, v):
+            tall = part >= 3
+            for i in range(split):
+                row = (v // 2) * TILE_ROWS if tall else 0
+                column = ((v % 2) if tall else v) * TILE_COLS + i * width
+                copy = pltpu.make_async_copy(
+                    final.at[u, pl.ds(i * TILE_ROWS, TILE_ROWS)],
+                    outs[part].at[
+                        pl.ds(pl.multiple_of(row, TILE_ROWS), TILE_ROWS),
+                        pl.ds(pl.multiple_of(column, 128), width),
+                    ],
+                    out_sems.at[u, i],
+                )
+                act(copy)
+
+        by_part(u, one)
+
+    def columns_at(v):
+        return pl.ds(pl.multiple_of(v * TILE_COLS, 128), TILE_COLS)
+
+    wide = mix_ref.shape[0] * 3 // 16
+    narrow = mix_ref.shape[0] // 16
+
+    def pieces(u, first, put):
+        steps = NEAR[2 * first : 2 * first + 2]
+
+        def one(part, v):
+            for place, step in enumerate(steps):
+                if part < 2:
+                    left = one_ref[:, near_at(step, TILE_ROWS)]
+                    value = mat_left_t(left, (early_ref, late_ref)[part][:, columns_at(v)])
+                elif part == 2:
+                    left = two_ref[:, near_at(step, TILE_ROWS)]
+                    half = gu_units // 2
+                    value = mat_left_t(left, pair_ref[v // half, :, columns_at(v % half)])
+                elif part == 3:
+                    right = branch_ref[:, columns_at(v % 2)]
+                    other = lax.axis_index("wsh") ^ step
+                    begin = pl.multiple_of(other * wide, 128)
+
+                    @pl.when(v < 2)
+                    def _():
+                        put(place, mat(mix_ref[pl.ds(begin, TILE_ROWS), :], right))
+
+                    @pl.when(v >= 2)
+                    def _():
+                        tail = mat(
+                            mix_ref[pl.ds(begin + TILE_ROWS, wide - TILE_ROWS), :], right
+                        )
+                        heads_at = pl.multiple_of(4 * wide + other * narrow, 128)
+                        heads = mat(mix_ref[pl.ds(heads_at, narrow), :], right)
+                        put(place, jnp.concatenate([tail, heads], axis=0))
+
+                    continue
+                else:
+                    block = hid_ref.shape[1] // 4
+                    start = (lax.axis_index("wsh") ^ step) * block + (v // 2) * TILE_ROWS
+                    left = hid_ref[:, pl.ds(pl.multiple_of(start, 128), TILE_ROWS)]
+                    value = mat_left_t(left, top_ref[:, columns_at(v % 2)])
+                put(place, value)
+
+        by_part(u, one)
+
+    def chunked(value):
+        return [
+            (slice(i * TILE_ROWS, (i + 1) * TILE_ROWS), value[:, i * width : (i + 1) * width])
+            for i in range(split)
+        ]
+
+    def begin(u):
+        def put(place, value):
+            for where, part in chunked(value):
+                core_out[u % 2, place, where] = part.astype(BF16)
+
+        pieces(u, 1, put)
+        core_copy(u).start()
+
+    def after_core(u):
+        core_copy(u).wait()
+
+        def put(place, value):
+            for where, part in chunked(value):
+                work[u, place, where] = (work[u, place, where].astype(F32) + part).astype(BF16)
+
+        pieces(u, 0, put)
+        y_copy(u).start()
+
+    def after_y(u):
+        y_copy(u).wait()
+        work[u, 0] = (work[u, 0].astype(F32) + y_in[u].astype(F32)).astype(BF16)
+        rs_copy(u, 0).start()
+
+    def after_rs(u, k):
+        rs_copy(u, k).wait()
+        mine = span(starts[k], sizes[k])
+        total = work[u, 0, mine].astype(F32) + ctx_in[
+            u, pl.ds(recv_base[k], sizes[k])
+        ].astype(F32)
+        if k + 1 < len(bits):
+            work[u, 0, mine] = total.astype(BF16)
+            rs_copy(u, k + 1).start()
+        else:
+            final[u, mine] = total.astype(BF16)
+            ag_copy(u, k).start()
+
+    def after_ag(u, k):
+        ag_copy(u, k).wait()
+        if k > 0:
+            ag_copy(u, k - 1).start()
+        else:
+            each_out(u, lambda copy: copy.start())
+
+    stages = [(0, begin), (1, after_core), (3, after_y)]
+    delay = 3
+    for k in range(len(bits)):
+        delay += 1
+        stages.append((delay, functools.partial(after_rs, k=k)))
+    for k in range(len(bits) - 1, -1, -1):
+        delay += 1
+        stages.append((delay, functools.partial(after_ag, k=k)))
+
+    small_out[...] = small_ref[...]
+    hops = partners
+
+    def small_copy(k):
+        return remote(
+            small_in.at[k, 0], small_in.at[k, 1], small_sems.at[0, k], small_sems.at[1, k], hops[k]
+        )
+
+    def small_step(k):
+        if k > 0:
+            small_copy(k - 1).wait()
+            small_out[...] += small_in[k - 1, 1]
+        if k < len(hops):
+            small_in[k, 0] = small_out[...]
+            small_copy(k).start()
+
+    def one_step(t, carry):
+        for k in range(len(hops) + 1):
+            pl.when(t == 2 * k + 1)(functools.partial(small_step, k))
+        for offset, stage in stages[::-1]:
+            u = t - offset
+            pl.when((u >= 0) & (u < units))(functools.partial(stage, u))
+        return carry
+
+    lax.fori_loop(0, units + delay, one_step, 0)
+
+    def finish(u, carry):
+        each_out(u, lambda copy: copy.wait())
+        return carry
+
+    lax.fori_loop(0, units, finish, 0)
+
+
+def reduce_grads(
+    count, early_width, one, two, mix_t, hidden, early, late, pair, branch, top, small
+):
+    bits = ctx_bits(count)
+    hops = len(bits) + 2
+    split = max(1, 16 * count // TILE_ROWS)
+    early_units = early_width // TILE_COLS
+    late_units = late.shape[1] // TILE_COLS
+    gu_units = 2 * pair.shape[2] // TILE_COLS
+    units = early_units + late_units + gu_units + 8
+    rows, width = TILE_ROWS * split, TILE_COLS // split
+    dma = pltpu.SemaphoreType.DMA
+    vmem = pl.BlockSpec(memory_space=pltpu.VMEM)
+    hbm = pl.BlockSpec(memory_space=pl.ANY)
+    return pl.pallas_call(
+        functools.partial(grads_kernel, count, split, early_units, late_units, gu_units),
+        in_specs=[vmem] * 10,
+        out_specs=[hbm] * 5 + [vmem],
+        out_shape=[
+            jax.ShapeDtypeStruct((TILE_ROWS, early_units * TILE_COLS), BF16),
+            jax.ShapeDtypeStruct((TILE_ROWS, late_units * TILE_COLS), BF16),
+            jax.ShapeDtypeStruct((TILE_ROWS, gu_units * TILE_COLS), BF16),
+            jax.ShapeDtypeStruct((2 * TILE_ROWS, 2 * TILE_COLS), BF16),
+            jax.ShapeDtypeStruct((2 * TILE_ROWS, 2 * TILE_COLS), BF16),
+            jax.ShapeDtypeStruct(small.shape, F32),
+        ],
+        scratch_shapes=[
+            pltpu.VMEM((2, 2, rows, width), BF16),
+            pltpu.VMEM((units, 2, rows, width), BF16),
+            pltpu.VMEM((units, rows, width), BF16),
+            pltpu.VMEM((units, rows, width), BF16),
+            pltpu.VMEM((units, rows, width), BF16),
+            pltpu.VMEM((hops, 2) + small.shape, F32),
+            dma((2, units)),
+            dma((2, units)),
+            dma((2, len(bits), units)),
+            dma((2, len(bits), units)),
+            dma((2, hops)),
+            dma((units, split)),
+        ],
+        compiler_params=pltpu.CompilerParams(
+            collective_id=1, has_side_effects=True, vmem_limit_bytes=62 * MIB
+        ),
+        cost_estimate=pl.CostEstimate(
+            flops=13_000_000_000, bytes_accessed=30 * MIB, transcendentals=0
+        ),
+        name="reduce_grads",
+    )(one, two, mix_t, hidden, early, late, pair, branch, top, small)
 
 
 def local(
@@ -670,29 +1202,32 @@
     rel_start = starts - first_pos
     taps = conv_weight.shape[0]
 
-    full_kv, full_in, full_dt, full_q, full_out, full_o, full_gu, full_down = [
-        gathered_near(shard)
-        for shard in (
+    features_in = in_weight.shape[1]
+    early_shard = jnp.concatenate(
+        [
             kv_weight,
-            in_weight,
-            dt_weight,
-            q_weight,
-            out_weight,
-            o_weight,
-            gu_weight,
-            down_weight,
-        )
-    ]
+            in_weight[:, DSSM:],
+            jnp.pad(dt_weight, ((0, 0), (0, 256 - dt_weight.shape[1]))),
+        ],
+        axis=1,
+    )
+    early = gathered_near(early_shard)
+    late_shard = jnp.concatenate([in_weight[:, :DSSM], q_weight], axis=1)
+    late = gathered_near(late_shard, early[1])
+    outs = gathered_near(jnp.concatenate([out_weight, o_weight], axis=0), late[1])
+    gu_full = gathered_near(gu_weight, outs[1])
+    down_full = gathered_near(down_weight, gu_full[1])
+    kv_width = kv_weight.shape[1]
+    conv_width = features_in - DSSM
 
     x = inputs.reshape(tokens, features).astype(F32)
     scale_one = inv_rms(x)
-    normed = near_order((x * scale_one * norm1_gain).astype(BF16), 1)
-    kv_rows = mat(normed, full_kv).astype(BF16)
+    normed = (x * scale_one * norm1_gain).astype(BF16)
+    early_rows = project(normed, early, 768)
+    kv_rows = early_rows[:, :kv_width].astype(BF16)
     key_table = table_gather(kv_rows.reshape(count, rows, -1))
-    projected = mat(normed, full_in)
-    gate_z = projected[:, :DSSM]
-    conv_rows = projected[:, DSSM:].reshape(count, rows, -1)
-    dt_raw = mat(normed, full_dt) + dt_bias
+    conv_rows = early_rows[:, kv_width : kv_width + conv_width].reshape(count, rows, -1)
+    dt_raw = early_rows[:, kv_width + conv_width :][:, :MHEADS] + dt_bias
     steps = jax.nn.softplus(dt_raw).reshape(count, rows, MHEADS)
     edge = passed_along(conv_rows[:, rows - taps + 1 :], "ctx", 1)
     extended = jnp.concatenate([edge, conv_rows], axis=1)
@@ -735,7 +1270,9 @@
     fresh = outer(inner * widened(to_end * steps), b_rows)
     state_in = chain_scan(total, fresh, True)
 
-    queries_t = dot_as(full_q, normed, 0, 1).astype(BF16)
+    late_rows = project(normed, late, 1024)
+    gate_z = late_rows[:, :DSSM]
+    queries_t = late_rows[:, DSSM:].astype(BF16).T
     bounds = jnp.concatenate(
         [starts[:, 0] // rows, jnp.full((1,), here + 1, jnp.int32), table_places(here, ctx_count)]
     )
@@ -754,45 +1291,21 @@
     gate_sig = jax.nn.sigmoid(gate_z)
     gated = flat * gate_z * gate_sig
     scale_m = inv_rms(gated)
-    mixed = near_order((gated * scale_m * mamba_gain).astype(BF16), 1)
-    attended_near = near_order(attended_t, 0)
-    middle = x + mat(mixed, full_out) + mat_left_t(attended_near, full_o)
-    scale_two = inv_rms(middle)
-    normed_two = near_order((middle * scale_two * norm2_gain).astype(BF16), 1)
-    gate_up = mat(normed_two, full_gu)
-    gate_part = gate_up[:, :FF]
-    up_part = gate_up[:, FF:]
-    sig = jax.nn.sigmoid(gate_part)
-    hidden = near_order((gate_part * sig * up_part).astype(BF16), 1)
-    layer_out = (middle + mat(hidden, full_down)).astype(BF16)
-
+    mixed = (gated * scale_m * mamba_gain).astype(BF16)
+    middle, normed_two = out_project(
+        inputs.reshape(tokens, features), mixed, attended_t, norm2_gain, outs
+    )
     grad_top = cotangent.reshape(tokens, features)
-    half = hidden.shape[1] // 2
-    down_shard = reduced_over_wsh(
-        mat_left_t(hidden[:, half:], grad_top), mat_left_t(hidden[:, :half], grad_top)
-    )
-    grad_hidden = natural_order(mat_right_t(grad_top, full_down), 1)
-    grad_gate = grad_hidden * up_part * sig * (1.0 + gate_part * (1.0 - sig))
-    grad_up = grad_hidden * gate_part * sig
-    grad_gu_rows = jnp.concatenate([grad_gate, grad_up], axis=1).astype(BF16)
-    half = normed_two.shape[1] // 2
-    gu_shard = reduced_over_wsh(
-        mat_left_t(normed_two[:, half:], grad_gu_rows),
-        mat_left_t(normed_two[:, :half], grad_gu_rows),
-    )
-    grad_two, grad_norm2 = rms_pull(
-        middle, scale_two, norm2_gain, natural_order(mat_right_t(grad_gu_rows, full_gu), 1)
-    )
-    grad_middle = grad_top.astype(F32) + grad_two
-    branch = grad_middle.astype(BF16)
-    half = attended_near.shape[0] // 2
-    o_shard = reduced_over_wsh(mat(attended_near[half:], branch), mat(attended_near[:half], branch))
-    grad_attended_t = natural_order(dot_as(full_o, branch, 1, 1).astype(BF16), 0)
-    half = mixed.shape[1] // 2
-    out_shard = reduced_over_wsh(
-        mat_left_t(mixed[:, half:], branch), mat_left_t(mixed[:, :half], branch)
-    )
-    grad_mixed = natural_order(mat_right_t(branch, full_out), 1)
+    layer_out, grad_middle, branch, grad_norm2, hidden, grad_pair = mlp_both(
+        lax.axis_index("wsh").astype(jnp.int32)[None],
+        normed_two,
+        grad_top,
+        middle,
+        norm2_gain,
+        gu_full,
+        down_full,
+    )
+    grad_mixed, grad_attended_t = out_unproject(branch, outs, DSSM, QHEADS * HDIM)
     grad_gated, grad_mamba = rms_pull(gated, scale_m, mamba_gain, grad_mixed)
     grad_gate_z = grad_gated * flat * gate_sig * (1.0 + gate_z * (1.0 - gate_sig))
     grad_scanned = (grad_gated * gate_z * gate_sig).reshape(count, rows, DSSM)
@@ -802,6 +1315,7 @@
     dq_t, dkv_table = attend_backward(
         bounds, starts_row, queries_t, key_table, attended_t, grad_attended_t, logs
     )
+    dq_rows = dq_t.T
     grad_kv_rows = table_scatter(dkv_table).reshape(tokens, -1)
     dx, db, dc, row_dot, u_dot, v_dot, dskip = ssd_backward(
         inner,
@@ -851,34 +1365,21 @@
     grad_conv_rows = grad_extended[:, taps - 1 :] + jnp.pad(
         edge_back, ((0, 0), (rows - taps + 1, 0), (0, 0))
     )
-    grad_proj = jnp.concatenate(
-        [grad_gate_z, grad_conv_rows.reshape(tokens, -1)], axis=1
-    ).astype(BF16)
-    half = features // 2
-
-    def shard_sum(grad, dim):
-        return reduced_over_wsh(
-            dot_as(normed[:, half:], grad, 0, dim), dot_as(normed[:, :half], grad, 0, dim)
-        )
-
-    q_shard = shard_sum(dq_t, 1)
-    kv_shard = shard_sum(grad_kv_rows, 0)
-    dt_shard = shard_sum(dt_low, 0)
-    in_shard = shard_sum(grad_proj, 0)
-    grad_normed = (
-        dot_as(dq_t, full_q, 0, 1)
-        + mat_right_t(grad_kv_rows, full_kv)
-        + mat_right_t(grad_proj, full_in)
-        + mat_right_t(dt_low, full_dt)
-    )
-    grad_normed = natural_order(grad_normed, 1)
+    grad_late = jnp.concatenate([grad_gate_z.astype(BF16), dq_rows], axis=1)
+    grad_early = jnp.concatenate(
+        [
+            grad_kv_rows,
+            grad_conv_rows.reshape(tokens, -1).astype(BF16),
+            jnp.pad(dt_low, ((0, 0), (0, 256 - MHEADS))),
+        ],
+        axis=1,
+    )
+    grad_dt_w = mat_left_t(normed, dt_low)
+    grad_normed = unproject(jnp.zeros((tokens, features), F32), grad_late, late, 1024)
+    grad_normed = unproject(grad_normed, grad_early, early, 768)
     grad_one, grad_norm1 = rms_pull(x, scale_one, norm1_gain, grad_normed)
     input_grad = (grad_middle + grad_one).astype(BF16)
 
-    totals_w = [
-        summed_over_ctx(shard)
-        for shard in (in_shard, dt_shard, out_shard, q_shard, kv_shard, o_shard, gu_shard, down_shard)
-    ]
     pieces = (
         grad_norm1,
         grad_conv_w,
@@ -887,36 +1388,67 @@
         grad_rate,
         grad_skip,
         grad_mamba,
-        grad_norm2,
+        grad_norm2[0],
+        grad_dt_w,
     )
     packed = jnp.concatenate([piece.reshape(-1) for piece in pieces])
     packed = jnp.pad(packed, (0, -packed.size % 1024)).reshape(-1, 128)
-    packed = summed_everywhere(packed).reshape(-1)
+    mix_t = jnp.concatenate([mixed.T, attended_t], axis=0)
+    early_sum, late_sum, gu_sum, mix_sum, down_sum, packed = reduce_grads(
+        ctx_count,
+        kv_width + conv_width,
+        normed,
+        normed_two,
+        mix_t,
+        hidden,
+        grad_early,
+        grad_late,
+        grad_pair,
+        branch,
+        grad_top,
+        packed,
+    )
+    packed = packed.reshape(-1)
+    split_row = out_weight.shape[0]
+    totals_w = [
+        part.astype(F32)
+        for part in (
+            jnp.concatenate([late_sum[:, :DSSM], early_sum[:, kv_width:]], axis=1),
+            mix_sum[:split_row],
+            late_sum[:, DSSM:],
+            early_sum[:, :kv_width],
+            mix_sum[split_row:],
+            gu_sum,
+            down_sum,
+        )
+    ]
     small = []
     place = 0
     for piece in pieces:
         small.append(packed[place : place + piece.size].reshape(piece.shape))
         place += piece.size
+    dt_rows = dt_weight.shape[0]
+    dt_sum = lax.dynamic_slice_in_dim(small[8], lax.axis_index("wsh") * dt_rows, dt_rows, 0)
     shape = (count, 1, rows, features)
     return (
         layer_out.reshape(shape),
         input_grad.reshape(shape),
         small[0],
         totals_w[0],
-        totals_w[1],
+        dt_sum,
         small[1],
         small[2],
         small[3],
         small[4],
         small[5],
         small[6],
+        totals_w[1],
         totals_w[2],
         totals_w[3],
         totals_w[4],
+        small[7],
         totals_w[5],
-        small[7],
         totals_w[6],
-        totals_w[7],
     )
 
 

time: 830 us -> 666 us (0.80)
  Pallas kernels: 47.9 us -> 293 us
  waiting for transfers between devices: 365 us -> 124 us
  starting transfers between devices: 137 us -> 57.1 us
  matrix products: 81.3 us -> 5.3 us
    pallas_call x0 -> x8, Pallas kernels: none -> 246 us  [the longest x1 185 us: reduce_grads(): pl.pallas_call(functools.partial(grads_kernel, count, split, early_units,...]
    ppermute x99 -> x29, waiting for transfers between devices: 365 us -> 124 us  [swapped(): lax.ppermute(block, axis, [(i, i ^ bit) for i in range(lax.axis_size(axis...]
    ppermute x99 -> x29, starting transfers between devices: 132 us -> 52.2 us  [swapped(): lax.ppermute(block, axis, [(i, i ^ bit) for i in range(lax.axis_size(axis...]
    dot_general x32 -> x1, matrix products: 76.8 us -> 0.47 us  [dot_as(): lax.dot_general(left, right, (((left_dim,), (right_dim,)), ((), ())), pre...]
    unnamed x351 -> x258, local copies, waits for them, and re-layouts: 38 us -> 21.3 us
    another operation x3 -> x0, other arithmetic: 13.1 us -> none
    concatenate x8 -> x1, local copies, waits for them, and re-layouts: 13.3 us -> 3.95 us  [local(): mix_t = jnp.concatenate([mixed.T, attended_t], axis=0)]
    convert_element_type x20 -> x10, other arithmetic: 13.8 us -> 16.7 us  [the longest x7 13.7 us: local(): part.astype(F32)]
  transfers between devices with their start and end apart: 101 -> 31, of which waited for: 51 -> 10; matrix products, arithmetic and copies ran while one was open for 24% -> 16% of each run, Pallas kernels for 5% -> 6%
where the time goes in v2:
time: 666 us; the launch traced here: 660 us
  Pallas kernels  293 us (44%)
  waiting for transfers between devices  124 us (19%)
  other arithmetic  96.8 us (15%)
  local copies, waits for them, and re-layouts  80.9 us (12%)
  starting transfers between devices  57.1 us (9%)
    pallas_call x1, Pallas kernels, reduce_grads(): pl.pallas_call(functools.partial(grads_kernel, count, split, early_units,...  185 us
    ppermute x29, waiting for transfers between devices, swapped(): lax.ppermute(block, axis, [(i, i ^ bit) for i in range(lax.axis_size(axis...  124 us
    ppermute x29, starting transfers between devices, swapped(): lax.ppermute(block, axis, [(i, i ^ bit) for i in range(lax.axis_size(axis...  52.2 us
    pallas_call x1, Pallas kernels, mlp_both(): pl.pallas_call(mlp_kernel, grid_spec=pltpu.PrefetchScalarGridSpec(num_sca...  29.5 us
    pallas_call x1, Pallas kernels, ssd_backward(): pl.pallas_call(ssd_backward_kernel, grid=(count, NGROUP), in_specs=[wide,...  27.2 us
    unnamed x258, local copies, waits for them, and re-layouts  21.3 us
    convert_element_type x7, other arithmetic, local(): part.astype(F32)  13.7 us
  transfers between devices with their start and end apart: 31, of which 10 were waited for; matrix products, arithmetic and copies ran while one was open for 16% of the time, Pallas kernels for 6%

profile of v2, /device:TPU:0, one launch (start us, length us, event | category | flops | bytes accessed | tf_op | source)
XLA Modules:
  0.0 660.4 jit_solution(6916144182023144175)
XLA Ops:
  12.3 20.5 %collective-permute-done.refs_1_ = bf16[256,2304]{1,0:T(8,128)(2,1)S(1)} collective-permute-done((bf16[256,2304]{1,0:T(8,128)(2,1)S(1)}, bf16[256,2304]{1,0:T(8,128)(2,1)S(1)}, u32[]{:S(2)}, u32[]{:S(2)}) %collective-permute-start) | collective-permute-done | bytes 1179680 | tf_op jit(solution)/shard_map/ppermute | solution.py:773
  40.7 20.0 %collective-permute-done.9.refs_1_ = bf16[256,2048]{1,0:T(8,128)(2,1)} collective-permute-done((bf16[256,2048]{1,0:T(8,128)(2,1)}, bf16[256,2048]{1,0:T(8,128)(2,1)}, u32[]{:S(2)}, u32[]{:S(2)}) %collective-permute-start.9) | collective-permute-done | bytes 1048608 | tf_op jit(solution)/shard_map/ppermute | solution.py:773
  62.5 4.6 project.2
  72.4 3.6 collective-permute-start.3
  79.8 3.6 copy.128
  83.5 11.1 %fusion.5 = (f32[2,256,1792]{2,1,0:T(8,128)S(1)}, f32[2,256,1792]{2,1,0:T(8,128)}) fusion(f32[2,256]{1,0:T(2,128)S(1)} %get-tuple-element.203, f32[2,256,1792]{2,1,0:T(8,128)} %bitcast.127, f32[1792]{0:T(1024)S(1)} %get-tuple-element.166, f32[2,256]{1,0:T(2,128)S(1)} %get-tuple-element.204, f32[2,3,1792]{2,1,0:T(4,128)S(1)} %collective-permute-done.3, ...), kind=kLoop, calls=%fused_computation.21 | loop fusion | flops 17432576 | bytes 11097088 | tf_op jit(solution)/shard_map/mul | solution.py:1241
  110.5 3.6 copy.136
  122.2 10.4 %collective-permute-done.13 = bf16[2,2,256,256]{3,2,1,0:T(8,128)(2,1)S(1)} collective-permute-done((bf16[2,2,256,256]{3,2,1,0:T(8,128)(2,1)S(1)}, bf16[2,2,256,256]{3,2,1,0:T(8,128)(2,1)S(1)}, u32[]{:S(2)}, u32[]{:S(2)}) %collective-permute-start.13) | collective-permute-done | bytes 524320 | tf_op jit(solution)/shard_map/ppermute | solution.py:773
  144.8 4.3 project.3
  154.2 4.7 fusion.16
  167.3 5.5 attend_forward.1
  175.7 21.1 %collective-permute-done.8 = bf16[2,1536,128]{2,1,0:T(8,128)(2,1)} collective-permute-done((bf16[2,1536,128]{2,1,0:T(8,128)(2,1)}, bf16[2,1536,128]{2,1,0:T(8,128)(2,1)}, u32[]{:S(2)}, u32[]{:S(2)}) %collective-permute-start.8) | collective-permute-done | bytes 786464 | tf_op jit(solution)/shard_map/ppermute | solution.py:773
  199.5 7.8 %ssd_forward.1.y_ref = f32[2,256,1536]{2,1,0:T(8,128)S(1)} custom-call(f32[2,256,1536]{2,1,0:T(8,128)S(1)} %slice.206.x_ref, f32[2,256,128]{2,1,0:T(8,128)S(1)} %copy-done.30, f32[2,256,128]{2,1,0:T(8,128)S(1)} %copy-done.28, f32[2,3,256,8]{3,2,1,0:T(8,128)S(1)} %bitcast.111, f32[2,3,256,8]{3,2,1,0:T(8,128)S(1)} %copy-done.21, ...), custom_call_target="tpu_custom_call" | custom-call | flops 1258291200 | bytes 8388608 | tf_op jit(solution)/shard_map/ssd_forward/pallas_call | solution.py:222
  211.8 5.5 out_project.1
  224.1 29.5 %mlp_both.1 = (bf16[512,1024]{1,0:T(8,128)(2,1)}, f32[512,1024]{1,0:T(8,128)}, bf16[512,1024]{1,0:T(8,128)(2,1)S(1)}, f32[1,1024]{1,0:T(1,128)S(1)}, bf16[512,20...) custom-call(s32[1]{0:T(128)} %bitcast.place_ref, bf16[512,1024]{1,0:T(8,128)(2,1)S(1)} %copy-done.49, ...), custom_call_target="tpu_custom_call" | custom-call | flops 12884901888 | bytes 31457280 | tf_op jit(solution)/shard_map/mlp_both/pallas_call | solution.py:718
  253.6 5.7 out_unproject.1
  260.7 3.5 multiply_multiply_fusion.4
  266.7 6.8 %attend_backward.1 = (bf16[512,512]{1,0:T(8,128)(2,1)S(1)}, bf16[8,2,256,256]{3,2,1,0:T(8,128)(2,1)S(1)}) custom-call(s32[11]{0:T(128)S(1)} %pad_add_fusion.2.bounds, s32[2,1,256]{2,1,0:T(1,128)S(1)} %broadcast_in_dim.65.start_ref, bf16[512,512]{1,0:T(8,128)(2,1)S(1)} %bitcast.120, bf16[8,2,256,256]{3,2,1,0:T(8,128)(2,1)} %copy-done.32, ...), custom_call_target="tpu_custom_call" | custom-call | flops 16777216000 | bytes 8388608 | tf_op jit(solution)/shard_map/attend_backward/pallas_call | solution.py:476
  275.3 5.4 collective-permute-start.24
  280.7 5.8 collective-permute-done.27
  291.6 3.9 copy.155.mix_ref
  297.6 11.2 %collective-permute-done.24 = bf16[4,2,256,256]{3,2,1,0:T(8,128)(2,1)} collective-permute-done((bf16[4,2,256,256]{3,2,1,0:T(8,128)(2,1)}, bf16[4,2,256,256]{3,2,1,0:T(8,128)(2,1)}, u32[]{:S(2)}, u32[]{:S(2)}) %collective-permute-start.24) | collective-permute-done | bytes 1048608 | tf_op jit(solution)/shard_map/ppermute | solution.py:773
  316.8 12.4 %collective-permute-start.29 = (bf16[2,1536,128]{2,1,0:T(8,128)(2,1)S(1)}, bf16[2,1536,128]{2,1,0:T(8,128)(2,1)S(1)}, u32[]{:S(2)}, u32[]{:S(2)}) collective-permute-start(bf16[2,1536,128]{2,1,0:T(8,128)(2,1)S(1)} %fusion.21), channel_id=1, source_target_pairs={{0,16},{4,20},{8,24},{12,28},{16,0},{20,4},{24,8},{28,12},{1,17},{... | collective-permute-start | bytes 2359304 | tf_op jit(solution)/shard_map/ppermute | solution.py:773
  329.4 9.3 %collective-permute-start.26 = (bf16[1,2,256,256]{3,2,1,0:T(8,128)(2,1)S(1)}, bf16[1,2,256,256]{3,2,1,0:T(8,128)(2,1)S(1)}, u32[]{:S(2)}, u32[]{:S(2)}) collective-permute-start(bf16[1,2,256,256]{3,2,1,0:T(8,128)(2,1)S(1)} %slice.219), channel_id=1, source_target_pairs={{0,16},{4,20},{8,24},{12,28},{16,0},{20,4},{24,8},{28,12},{1,17},{... | collective-permute-start | bytes 786440 | tf_op jit(solution)/shard_map/ppermute | solution.py:773
  339.3 5.5 unproject.2.base_ref
  344.9 29.8 %collective-permute-done.26 = bf16[1,2,256,256]{3,2,1,0:T(8,128)(2,1)S(1)} collective-permute-done((bf16[1,2,256,256]{3,2,1,0:T(8,128)(2,1)S(1)}, bf16[1,2,256,256]{3,2,1,0:T(8,128)(2,1)S(1)}, u32[]{:S(2)}, u32[]{:S(2)}) %collective-permute-start.26) | collective-permute-done | bytes 262176 | tf_op jit(solution)/shard_map/ppermute | solution.py:773
  375.5 3.7 multiply_reduce_fusion.10
  379.3 27.2 %ssd_backward.1 = (f32[2,256,1536]{2,1,0:T(8,128)S(1)}, f32[2,256,128]{2,1,0:T(8,128)S(1)}, f32[2,256,128]{2,1,0:T(8,128)S(1)}, f32[2,3,256,8]{3,2,1,0:T(8,128)S...) custom-call(f32[2,256,1536]{2,1,0:T(8,128)} %copy-done.4, ...), custom_call_target="tpu_custom_call" | custom-call | flops 3145728000 | bytes 16777216 | tf_op jit(solution)/shard_map/ssd_backward/pallas_call | solution.py:254
  406.6 10.1 %fusion.53 = (f32[1792]{0:T(1024)}, f32[1792]{0:T(1024)S(1)}, f32[1792]{0:T(1024)S(1)}, f32[1792]{0:T(1024)S(1)}, f32[1792]{0:T(1024)S(1)}, /*index=5*/f32[2,256,1792]{2,1,0:T(8,128)S(1)}) fusion(f32[2,256]{1,0:T(2,128)S(1)} %copy-done.97, f32[512,2304]{1,0:T(8,128)S(1)} %bitcast.109, f32[2,256]{1,0:T(2,128)S(1)} %copy-done.101, ...), kind=kLoop, calls=%fused_computation.173 | loop fusion | flops 23846144 | bytes 18437120 | tf_op jit(solution)/shard_map/reduce_sum | solution.py:1352
  442.3 5.6 unproject.3
  450.8 185.3 %reduce_grads.1 = (bf16[256,2048]{1,0:T(8,128)(2,1)}, bf16[256,2048]{1,0:T(8,128)(2,1)}, bf16[256,4096]{1,0:T(8,128)(2,1)}, bf16[512,1024]{1,0:T(8,128)(2,1)}, b...) custom-call(bf16[512,1024]{1,0:T(8,128)(2,1)} %copy-done.9, bf16[512,1024]{1,0:T(8,128)(2,1)} %copy-done.48, ...), custom_call_target="tpu_custom_call" | custom-call | flops 12999999488 | bytes 31457280 | tf_op jit(solution)/shard_map/reduce_grads/pallas_call | solution.py:1138
  654.8 3.5 maximum_convert_fusion
  (460 shorter events, 167.0 us)
Async XLA Ops:
  3.9 29.0 %collective-permute-start = (bf16[256,2304]{1,0:T(8,128)(2,1)S(1)}, bf16[256,2304]{1,0:T(8,128)(2,1)S(1)}, u32[]{:S(2)}, u32[]{:S(2)}) collective-permute-start(bf16[256,2304]{1,0:T(8,128)(2,1)S(1)} %fusion.24.refs_0_), channel_id=1, source_target_pairs={{0,2},{1,3},{2,0},{3,1},{4,6},{5,7},{6,4},{7,5},{8,10},{9,11},{10,... | collective-permute-start | bytes 3538952 | tf_op jit(solution)/shard_map/ppermute | solution.py:773
  6.9 55.6 %collective-permute-start.1 = (bf16[256,2304]{1,0:T(8,128)(2,1)S(1)}, bf16[256,2304]{1,0:T(8,128)(2,1)}, u32[]{:S(2)}, u32[]{:S(2)}) collective-permute-start(bf16[256,2304]{1,0:T(8,128)(2,1)S(1)} %fusion.24.refs_0_), channel_id=1, source_target_pairs={{0,1},{1,0},{2,3},{3,2},{4,5},{5,4},{6,7},{7,6},{8,9},{9,8},{10,11... | collective-permute-start | bytes 3538952 | tf_op jit(solution)/shard_map/ppermute | solution.py:773
  6.9 91.3 %copy-start.89 = (s32[256]{0:T(256)}, s32[256]{0:T(256)S(1)}, u32[]{:S(2)}) copy-start(s32[256]{0:T(256)S(1)} %iota_add_fusion) | copy-start | bytes 3076
  32.9 29.7 %collective-permute-start.2 = (bf16[256,2304]{1,0:T(8,128)(2,1)S(1)}, bf16[256,2304]{1,0:T(8,128)(2,1)}, u32[]{:S(2)}, u32[]{:S(2)}) collective-permute-start(bf16[256,2304]{1,0:T(8,128)(2,1)S(1)} %collective-permute-done.refs_1_), channel_id=1, source_target_pairs={{0,1},{1,0},{2,3},{3,2},{4,5},{5,4},{6,7},{7,6},{8,9},{9,8},{10,11... | collective-permute-start | bytes 3538952 | tf_op jit(solution)/shard_map/ppermute | solution.py:773
  35.1 25.7 %collective-permute-start.9 = (bf16[256,2048]{1,0:T(8,128)(2,1)}, bf16[256,2048]{1,0:T(8,128)(2,1)}, u32[]{:S(2)}, u32[]{:S(2)}) collective-permute-start(bf16[256,2048]{1,0:T(8,128)(2,1)} %pad_maximum_fusion.4.refs_0_), channel_id=1, source_target_pairs={{0,2},{1,3},{2,0},{3,1},{4,6},{5,7},{6,4},{7,5},{8,10},{9,11},{10,... | collective-permute-start | bytes 3145736 | tf_op jit(solution)/shard_map/ppermute | solution.py:773
  60.8 57.6 %collective-permute-start.15 = (bf16[512,1024]{1,0:T(8,128)(2,1)}, bf16[512,1024]{1,0:T(8,128)(2,1)S(1)}, u32[]{:S(2)}, u32[]{:S(2)}) collective-permute-start(bf16[512,1024]{1,0:T(8,128)(2,1)} %pad_maximum_fusion.6.refs_0_), channel_id=1, source_target_pairs={{0,2},{1,3},{2,0},{3,1},{4,6},{5,7},{6,4},{7,5},{8,10},{9,11},{10,... | collective-permute-start | bytes 3145736 | tf_op jit(solution)/shard_map/ppermute | solution.py:773
  72.4 11.0 %collective-permute-start.3 = (f32[2,3,1792]{2,1,0:T(4,128)S(1)}, f32[2,3,1792]{2,1,0:T(4,128)S(1)}, u32[]{:S(2)}, u32[]{:S(2)}) collective-permute-start(f32[2,3,1792]{2,1,0:T(4,128)S(1)} %slice.201), channel_id=1, source_target_pairs={{0,4},{4,8},{8,12},{12,16},{16,20},{20,24},{24,28},{1,5},{5,9},{9,... | collective-permute-start | bytes 129032 | tf_op jit(solution)/shard_map/ppermute | solution.py:769
  96.7 22.3 %collective-permute-start.4 = (bf16[2,1536,128]{2,1,0:T(8,128)(2,1)}, bf16[2,1536,128]{2,1,0:T(8,128)(2,1)}, u32[]{:S(2)}, u32[]{:S(2)}) collective-permute-start(bf16[2,1536,128]{2,1,0:T(8,128)(2,1)} %get-tuple-element.208), channel_id=1, source_target_pairs={{0,4},{4,0},{8,12},{12,8},{16,20},{20,16},{24,28},{28,24},{1,5},{5... | collective-permute-start | bytes 2359304 | tf_op jit(solution)/shard_map/ppermute | solution.py:773
  99.0 45.2 %collective-permute-start.10 = (bf16[256,2048]{1,0:T(8,128)(2,1)}, bf16[256,2048]{1,0:T(8,128)(2,1)}, u32[]{:S(2)}, u32[]{:S(2)}) collective-permute-start(bf16[256,2048]{1,0:T(8,128)(2,1)} %pad_maximum_fusion.4.refs_0_), channel_id=1, source_target_pairs={{0,1},{1,0},{2,3},{3,2},{4,5},{5,4},{6,7},{7,6},{8,9},{9,8},{10,11... | collective-permute-start | bytes 3145736 | tf_op jit(solution)/shard_map/ppermute | solution.py:773
  100.1 15.6 %collective-permute-start.12 = (bf16[1,2,256,256]{3,2,1,0:T(8,128)(2,1)S(1)}, bf16[1,2,256,256]{3,2,1,0:T(8,128)(2,1)}, u32[]{:S(2)}, u32[]{:S(2)}) collective-permute-start(bf16[1,2,256,256]{3,2,1,0:T(8,128)(2,1)S(1)} %bitcast.144), channel_id=1, source_target_pairs={{0,16},{4,20},{8,24},{12,28},{16,0},{20,4},{24,8},{28,12},{1,17},{... | collective-permute-start | bytes 786440 | tf_op jit(solution)/shard_map/ppermute | solution.py:773
  103.7 11.7 %collective-permute-start.5 = (f32[2,24]{1,0:T(2,128)S(1)}, f32[2,24]{1,0:T(2,128)S(1)}, u32[]{:S(2)}, u32[]{:S(2)}) collective-permute-start(f32[2,24]{1,0:T(2,128)S(1)} %exponential_multiply_fusion.1), channel_id=1, source_target_pairs={{0,4},{4,0},{8,12},{12,8},{16,20},{20,16},{24,28},{28,24},{1,5},{5... | collective-permute-start | bytes 584 | tf_op jit(solution)/shard_map/ppermute | solution.py:773
  115.4 28.9 %collective-permute-start.11 = (bf16[256,2048]{1,0:T(8,128)(2,1)}, bf16[256,2048]{1,0:T(8,128)(2,1)}, u32[]{:S(2)}, u32[]{:S(2)}) collective-permute-start(bf16[256,2048]{1,0:T(8,128)(2,1)} %collective-permute-done.9.refs_1_), channel_id=1, source_target_pairs={{0,1},{1,0},{2,3},{3,2},{4,5},{5,4},{6,7},{7,6},{8,9},{9,8},{10,11... | collective-permute-start | bytes 3145736 | tf_op jit(solution)/shard_map/ppermute | solution.py:773
  115.8 19.3 %collective-permute-start.7 = (f32[2,24]{1,0:T(2,128)S(1)}, f32[2,24]{1,0:T(2,128)S(1)}, u32[]{:S(2)}, u32[]{:S(2)}) collective-permute-start(f32[2,24]{1,0:T(2,128)S(1)} %fusion.66), channel_id=1, source_target_pairs={{0,8},{4,12},{8,0},{12,4},{16,24},{20,28},{24,16},{28,20},{1,9},{5... | collective-permute-start | bytes 584 | tf_op jit(solution)/shard_map/ppermute | solution.py:773
  118.4 14.1 %collective-permute-start.13 = (bf16[2,2,256,256]{3,2,1,0:T(8,128)(2,1)S(1)}, bf16[2,2,256,256]{3,2,1,0:T(8,128)(2,1)S(1)}, u32[]{:S(2)}, u32[]{:S(2)}) collective-permute-start(bf16[2,2,256,256]{3,2,1,0:T(8,128)(2,1)S(1)} %pad_maximum_fusion.7), channel_id=1, source_target_pairs={{0,8},{4,12},{8,0},{12,4},{16,24},{20,28},{24,16},{28,20},{1,9},{5... | collective-permute-start | bytes 1572872 | tf_op jit(solution)/shard_map/ppermute | solution.py:773
  118.9 47.8 %collective-permute-start.18 = (bf16[256,4096]{1,0:T(8,128)(2,1)}, bf16[256,4096]{1,0:T(8,128)(2,1)}, u32[]{:S(2)}, u32[]{:S(2)}) collective-permute-start(bf16[256,4096]{1,0:T(8,128)(2,1)} %refs_4_), channel_id=1, source_target_pairs={{0,2},{1,3},{2,0},{3,1},{4,6},{5,7},{6,4},{7,5},{8,10},{9,11},{10,... | collective-permute-start | bytes 6291464 | tf_op jit(solution)/shard_map/ppermute | solution.py:773
  132.6 21.5 %collective-permute-start.6 = (bf16[2,1536,128]{2,1,0:T(8,128)(2,1)}, bf16[2,1536,128]{2,1,0:T(8,128)(2,1)}, u32[]{:S(2)}, u32[]{:S(2)}) collective-permute-start(bf16[2,1536,128]{2,1,0:T(8,128)(2,1)} %fusion.26), channel_id=1, source_target_pairs={{0,8},{4,12},{8,0},{12,4},{16,24},{20,28},{24,16},{28,20},{1,9},{5... | collective-permute-start | bytes 2359304 | tf_op jit(solution)/shard_map/ppermute | solution.py:773
  135.0 24.6 %collective-permute-start.14 = (bf16[4,2,256,256]{3,2,1,0:T(8,128)(2,1)}, bf16[4,2,256,256]{3,2,1,0:T(8,128)(2,1)}, u32[]{:S(2)}, u32[]{:S(2)}) collective-permute-start(bf16[4,2,256,256]{3,2,1,0:T(8,128)(2,1)} %pad_maximum_fusion.5), channel_id=1, source_target_pairs={{0,4},{4,0},{8,12},{12,8},{16,20},{20,16},{24,28},{28,24},{1,5},{5... | collective-permute-start | bytes 3145736 | tf_op jit(solution)/shard_map/ppermute | solution.py:773
  144.2 63.1 %collective-permute-start.16 = (bf16[512,1024]{1,0:T(8,128)(2,1)}, bf16[512,1024]{1,0:T(8,128)(2,1)}, u32[]{:S(2)}, u32[]{:S(2)}) collective-permute-start(bf16[512,1024]{1,0:T(8,128)(2,1)} %pad_maximum_fusion.6.refs_0_), channel_id=1, source_target_pairs={{0,1},{1,0},{2,3},{3,2},{4,5},{5,4},{6,7},{7,6},{8,9},{9,8},{10,11... | collective-permute-start | bytes 3145736 | tf_op jit(solution)/shard_map/ppermute | solution.py:773
  144.3 75.4 %collective-permute-start.19 = (bf16[256,4096]{1,0:T(8,128)(2,1)}, bf16[256,4096]{1,0:T(8,128)(2,1)}, u32[]{:S(2)}, u32[]{:S(2)}) collective-permute-start(bf16[256,4096]{1,0:T(8,128)(2,1)} %refs_4_), channel_id=1, source_target_pairs={{0,1},{1,0},{2,3},{3,2},{4,5},{5,4},{6,7},{7,6},{8,9},{9,8},{10,11... | collective-permute-start | bytes 6291464 | tf_op jit(solution)/shard_map/ppermute | solution.py:773
  154.0 55.3 %collective-permute-start.17 = (bf16[512,1024]{1,0:T(8,128)(2,1)}, bf16[512,1024]{1,0:T(8,128)(2,1)}, u32[]{:S(2)}, u32[]{:S(2)}) collective-permute-start(bf16[512,1024]{1,0:T(8,128)(2,1)} %copy-done.43), channel_id=1, source_target_pairs={{0,1},{1,0},{2,3},{3,2},{4,5},{5,4},{6,7},{7,6},{8,9},{9,8},{10,11... | collective-permute-start | bytes 3145736 | tf_op jit(solution)/shard_map/ppermute | solution.py:773
  159.7 37.1 %collective-permute-start.8 = (bf16[2,1536,128]{2,1,0:T(8,128)(2,1)}, bf16[2,1536,128]{2,1,0:T(8,128)(2,1)}, u32[]{:S(2)}, u32[]{:S(2)}) collective-permute-start(bf16[2,1536,128]{2,1,0:T(8,128)(2,1)} %fusion.16), channel_id=1, source_target_pairs={{0,16},{4,20},{8,24},{12,28},{16,0},{20,4},{24,8},{28,12},{1,17},{... | collective-permute-start | bytes 2359304 | tf_op jit(solution)/shard_map/ppermute | solution.py:773
  166.7 41.2 %collective-permute-start.21 = (bf16[512,1024]{1,0:T(8,128)(2,1)}, bf16[512,1024]{1,0:T(8,128)(2,1)}, u32[]{:S(2)}, u32[]{:S(2)}) collective-permute-start(bf16[512,1024]{1,0:T(8,128)(2,1)} %refs_8_), channel_id=1, source_target_pairs={{0,2},{1,3},{2,0},{3,1},{4,6},{5,7},{6,4},{7,5},{8,10},{9,11},{10,... | collective-permute-start | bytes 3145736 | tf_op jit(solution)/shard_map/ppermute | solution.py:773
  196.8 22.9 %collective-permute-start.20 = (bf16[256,4096]{1,0:T(8,128)(2,1)}, bf16[256,4096]{1,0:T(8,128)(2,1)S(1)}, u32[]{:S(2)}, u32[]{:S(2)}) collective-permute-start(bf16[256,4096]{1,0:T(8,128)(2,1)} %collective-permute-done.18.refs_1_.refs_5_), channel_id=1, source_target_pairs={{0,1},{1,0},{2,3},{3,2},{4,5},{5,4},{6,7},{7,6},{8,9},{9,8},{10,11... | collective-permute-start | bytes 6291464 | tf_op jit(solution)/shard_map/ppermute | solution.py:773
  207.4 12.3 %collective-permute-start.22 = (bf16[512,1024]{1,0:T(8,128)(2,1)}, bf16[512,1024]{1,0:T(8,128)(2,1)S(1)}, u32[]{:S(2)}, u32[]{:S(2)}) collective-permute-start(bf16[512,1024]{1,0:T(8,128)(2,1)} %refs_8_), channel_id=1, source_target_pairs={{0,1},{1,0},{2,3},{3,2},{4,5},{5,4},{6,7},{7,6},{8,9},{9,8},{10,11... | collective-permute-start | bytes 3145736 | tf_op jit(solution)/shard_map/ppermute | solution.py:773
  207.9 11.7 %collective-permute-start.23 = (bf16[512,1024]{1,0:T(8,128)(2,1)}, bf16[512,1024]{1,0:T(8,128)(2,1)S(1)}, u32[]{:S(2)}, u32[]{:S(2)}) collective-permute-start(bf16[512,1024]{1,0:T(8,128)(2,1)} %collective-permute-done.21.refs_9_), channel_id=1, source_target_pairs={{0,1},{1,0},{2,3},{3,2},{4,5},{5,4},{6,7},{7,6},{8,9},{9,8},{10,11... | collective-permute-start | bytes 3145736 | tf_op jit(solution)/shard_map/ppermute | solution.py:773
  266.1 20.4 %collective-permute-start.27 = (bf16[2,1536,128]{2,1,0:T(8,128)(2,1)S(1)}, bf16[2,1536,128]{2,1,0:T(8,128)(2,1)S(1)}, u32[]{:S(2)}, u32[]{:S(2)}) collective-permute-start(bf16[2,1536,128]{2,1,0:T(8,128)(2,1)S(1)} %get-tuple-element.210), channel_id=1, source_target_pairs={{0,4},{4,0},{8,12},{12,8},{16,20},{20,16},{24,28},{28,24},{1,5},{5... | collective-permute-start | bytes 2359304 | tf_op jit(solution)/shard_map/ppermute | solution.py:773
  275.3 33.5 %collective-permute-start.24 = (bf16[4,2,256,256]{3,2,1,0:T(8,128)(2,1)}, bf16[4,2,256,256]{3,2,1,0:T(8,128)(2,1)}, u32[]{:S(2)}, u32[]{:S(2)}) collective-permute-start(bf16[4,2,256,256]{3,2,1,0:T(8,128)(2,1)} %slice.176), channel_id=1, source_target_pairs={{0,4},{4,0},{8,12},{12,8},{16,20},{20,16},{24,28},{28,24},{1,5},{5... | collective-permute-start | bytes 3145736 | tf_op jit(solution)/shard_map/ppermute | solution.py:773
  288.3 25.1 %collective-permute-start.28 = (bf16[2,1536,128]{2,1,0:T(8,128)(2,1)}, bf16[2,1536,128]{2,1,0:T(8,128)(2,1)}, u32[]{:S(2)}, u32[]{:S(2)}) collective-permute-start(bf16[2,1536,128]{2,1,0:T(8,128)(2,1)} %fusion.25), channel_id=1, source_target_pairs={{0,8},{4,12},{8,0},{12,4},{16,24},{20,28},{24,16},{28,20},{1,9},{5... | collective-permute-start | bytes 2359304 | tf_op jit(solution)/shard_map/ppermute | solution.py:773
  310.4 18.8 %collective-permute-start.25 = (bf16[2,2,256,256]{3,2,1,0:T(8,128)(2,1)S(1)}, bf16[2,2,256,256]{3,2,1,0:T(8,128)(2,1)S(1)}, u32[]{:S(2)}, u32[]{:S(2)}) collective-permute-start(bf16[2,2,256,256]{3,2,1,0:T(8,128)(2,1)S(1)} %slice.217), channel_id=1, source_target_pairs={{0,8},{4,12},{8,0},{12,4},{16,24},{20,28},{24,16},{28,20},{1,9},{5... | collective-permute-start | bytes 1572872 | tf_op jit(solution)/shard_map/ppermute | solution.py:773
  316.8 58.7 %collective-permute-start.29 = (bf16[2,1536,128]{2,1,0:T(8,128)(2,1)S(1)}, bf16[2,1536,128]{2,1,0:T(8,128)(2,1)S(1)}, u32[]{:S(2)}, u32[]{:S(2)}) collective-permute-start(bf16[2,1536,128]{2,1,0:T(8,128)(2,1)S(1)} %fusion.21), channel_id=1, source_target_pairs={{0,16},{4,20},{8,24},{12,28},{16,0},{20,4},{24,8},{28,12},{1,17},{... | collective-permute-start | bytes 2359304 | tf_op jit(solution)/shard_map/ppermute | solution.py:773
  329.4 45.3 %collective-permute-start.26 = (bf16[1,2,256,256]{3,2,1,0:T(8,128)(2,1)S(1)}, bf16[1,2,256,256]{3,2,1,0:T(8,128)(2,1)S(1)}, u32[]{:S(2)}, u32[]{:S(2)}) collective-permute-start(bf16[1,2,256,256]{3,2,1,0:T(8,128)(2,1)S(1)} %slice.219), channel_id=1, source_target_pairs={{0,16},{4,20},{8,24},{12,28},{16,0},{20,4},{24,8},{28,12},{1,17},{... | collective-permute-start | bytes 786440 | tf_op jit(solution)/shard_map/ppermute | solution.py:773
  423.4 14.3 %collective-permute-start.30 = (f32[2,3,1792]{2,1,0:T(4,128)S(1)}, f32[2,3,1792]{2,1,0:T(4,128)S(1)}, u32[]{:S(2)}, u32[]{:S(2)}) collective-permute-start(f32[2,3,1792]{2,1,0:T(4,128)S(1)} %pad_add_fusion.1), channel_id=1, source_target_pairs={{4,0},{8,4},{12,8},{16,12},{20,16},{24,20},{28,24},{5,1},{9,5},{13... | collective-permute-start | bytes 129032 | tf_op jit(solution)/shard_map/ppermute | solution.py:769
  (126 other events, 2140.3 us)

commit v3 on v2

v3 whole, which is shorter than its diff:
```python
import functools

import jax
import jax.numpy as jnp
from jax import lax
from jax.experimental import pallas as pl
from jax.experimental.pallas import tpu as pltpu
from jax.sharding import PartitionSpec as P

FF = 2048
MHEADS = 24
MDIM = 64
STATE = 128
QHEADS = 8
KVHEADS = 2
HDIM = 64
DSSM = 1536
HGROUP = 8
NGROUP = MHEADS // HGROUP
GWIDTH = HGROUP * MDIM
PAIR = 2 * MDIM

NORM_EPS = 1e-05
PRECISE = lax.Precision.HIGHEST
MASKED_SCORE = -1e30
MIB = 2**20
F32 = jnp.float32
BF16 = jnp.bfloat16


def dot_as(left, right, left_dim, right_dim):
    return lax.dot_general(
        left, right, (((left_dim,), (right_dim,)), ((), ())), preferred_element_type=F32
    )


def mat(left, right):
    return dot_as(left, right, 1, 0)


def mat_left_t(left, right):
    return dot_as(left, right, 0, 0)


def mat_right_t(left, right):
    return dot_as(left, right, 1, 1)


def inv_rms(rows):
    return lax.rsqrt(jnp.mean(rows * rows, axis=-1, keepdims=True) + NORM_EPS)


def rms_pull(rows, scale, gain, grad):
    scaled = rows * scale
    grad_gain = jnp.sum(grad * scaled, axis=0)
    through = grad * gain
    inner = jnp.mean(through * scaled, axis=-1, keepdims=True)
    return scale * (through - scaled * inner), grad_gain


def seq_starts(lengths_row, positions):
    begins = jnp.cumsum(lengths_row, dtype=jnp.int32) - lengths_row
    picked = jnp.where(begins[None, :] <= positions[:, None], begins[None, :], 0)
    return jnp.max(picked, axis=1)


def head_lanes(rows):
    return lax.broadcasted_iota(jnp.int32, (rows, PAIR), 1) < MDIM


def masked_products(b_low, c_low, rel_start):
    rows = b_low.shape[0]
    at_row = lax.broadcasted_iota(jnp.int32, (rows, rows), 0)
    at_col = lax.broadcasted_iota(jnp.int32, (rows, rows), 1)
    allowed = (at_col <= at_row) & (at_col >= rel_start)
    return allowed, jnp.where(allowed, mat_right_t(c_low, b_low), 0.0)


def pair_columns(first_half, columns, head):
    return jnp.where(first_half, columns[:, head : head + 1], columns[:, head + 1 : head + 2])


def exact(left, right, left_dim, right_dim):
    return lax.dot_general(
        left,
        right,
        (((left_dim,), (right_dim,)), ((), ())),
        precision=PRECISE,
        preferred_element_type=F32,
    )


def lower_ones(rows):
    at_row = lax.broadcasted_iota(jnp.int32, (rows, rows), 0)
    at_col = lax.broadcasted_iota(jnp.int32, (rows, rows), 1)
    return (at_row >= at_col).astype(F32)


def sigmoid(value):
    return 1.0 / (1.0 + jnp.exp(-value))


def softplus(value):
    return jnp.maximum(value, 0.0) + jnp.log1p(jnp.exp(-jnp.abs(value)))


def scaled_rows(target, source_ref, factors):
    first_half = head_lanes(source_ref.shape[0])
    for head in range(0, MHEADS, 2):
        lanes = slice(head * MDIM, head * MDIM + PAIR)
        target[:, lanes] = (
            source_ref[:, lanes] * pair_columns(first_half, factors, head)
        ).astype(BF16)


def ssd_state_kernel(
    act_ref,
    dt_ref,
    bias_ref,
    rate_ref,
    start_ref,
    step_ref,
    decay_ref,
    decay_t_ref,
    end_ref,
    total_ref,
    state_ref,
    scaled,
):
    rows = act_ref.shape[0]
    steps = softplus(dt_ref[:, :128] + bias_ref[...])
    decay = exact(lower_ones(rows), -steps * rate_ref[...], 1, 0)
    rel_start = start_ref[...]
    last_start = rel_start[rows - 1 : rows, :]
    kept = lax.broadcasted_iota(jnp.int32, (rows, 1), 0) >= last_start
    end = decay[rows - 1 : rows, :]
    to_end = jnp.where(kept, jnp.exp(end - decay), 0.0)
    step_ref[...] = steps
    decay_ref[...] = decay
    decay_t_ref[0] = decay.T
    end_ref[...] = to_end
    total_ref[0] = jnp.broadcast_to(jnp.where(last_start < 0, jnp.exp(end), 0.0), (8, 128))
    scaled_rows(scaled, act_ref, to_end * steps)
    state_ref[0] = mat_left_t(scaled[...], act_ref[:, DSSM : DSSM + STATE].astype(BF16))


def row_spec(rows, width, place=0):
    return pl.BlockSpec((rows, width), lambda b: (b, place))


def ssd_state(count, act, dt_rows, bias, rate, rel_start):
    rows = act.shape[0] // count
    lanes = pl.BlockSpec((1, 128), lambda b: (0, 0))
    heads = jax.ShapeDtypeStruct((count * rows, 128), F32)
    return pl.pallas_call(
        ssd_state_kernel,
        grid=(count,),
        in_specs=[
            row_spec(rows, act.shape[1]),
            row_spec(rows, dt_rows.shape[1]),
            lanes,
            lanes,
            row_spec(rows, 1),
        ],
        out_specs=[
            row_spec(rows, 128),
            row_spec(rows, 128),
            pl.BlockSpec((1, 128, rows), lambda b: (b, 0, 0)),
            row_spec(rows, 128),
            pl.BlockSpec((1, 8, 128), lambda b: (b, 0, 0)),
            pl.BlockSpec((1, DSSM, STATE), lambda b: (b, 0, 0)),
        ],
        out_shape=[
            heads,
            heads,
            jax.ShapeDtypeStruct((count, 128, rows), F32),
            heads,
            jax.ShapeDtypeStruct((count, 8, 128), F32),
            jax.ShapeDtypeStruct((count, DSSM, STATE), F32),
        ],
        scratch_shapes=[pltpu.VMEM((rows, DSSM), BF16)],
        compiler_params=pltpu.CompilerParams(vmem_limit_bytes=40 * MIB),
        cost_estimate=pl.CostEstimate(
            flops=1_000_000_000, bytes_accessed=8 * MIB, transcendentals=0
        ),
        name="ssd_state",
    )(act, dt_rows, bias, rate, rel_start)


def state_grad_kernel(dy_ref, c_ref, decay_ref, start_ref, out_ref, scaled):
    reach = jnp.where(start_ref[...] < 0, jnp.exp(decay_ref[...]), 0.0)
    scaled_rows(scaled, dy_ref, reach)
    out_ref[0] = mat_left_t(scaled[...], c_ref[...].astype(BF16))


def state_grad(count, dy, act, decay, rel_start):
    rows = act.shape[0] // count
    return pl.pallas_call(
        state_grad_kernel,
        grid=(count,),
        in_specs=[
            row_spec(rows, DSSM),
            row_spec(rows, STATE, DSSM // STATE + 1),
            row_spec(rows, 128),
            row_spec(rows, 1),
        ],
        out_specs=pl.BlockSpec((1, DSSM, STATE), lambda b: (b, 0, 0)),
        out_shape=jax.ShapeDtypeStruct((count, DSSM, STATE), F32),
        scratch_shapes=[pltpu.VMEM((rows, DSSM), BF16)],
        compiler_params=pltpu.CompilerParams(vmem_limit_bytes=40 * MIB),
        cost_estimate=pl.CostEstimate(
            flops=1_000_000_000, bytes_accessed=8 * MIB, transcendentals=0
        ),
        name="state_grad",
    )(dy, act, decay, rel_start)


def group_heads(ref):
    return pltpu.roll(ref[...], (128 - HGROUP * pl.program_id(1)) % 128, 1)


def group_rows(decay_t_ref):
    return decay_t_ref[0, pl.ds(pl.multiple_of(HGROUP * pl.program_id(1), HGROUP), HGROUP), :]


def ssd_forward_kernel(
    x_ref, b_ref, c_ref, step_ref, decay_ref, decay_t_ref, start_ref, state_ref, skip_ref, y_ref
):
    rows = x_ref.shape[0]
    b_low = b_ref[...].astype(BF16)
    c_low = c_ref[...].astype(BF16)
    rel_start = start_ref[...]
    _, products = masked_products(b_low, c_low, rel_start)
    incoming = mat_right_t(c_low, state_ref[0].astype(BF16))
    first_half = head_lanes(rows)
    steps = group_heads(step_ref)
    decay = group_heads(decay_ref)
    decay_t = group_rows(decay_t_ref)
    reach = jnp.where(rel_start < 0, jnp.exp(decay), 0.0)
    for head in range(0, HGROUP, 2):
        lanes = slice(head * MDIM, head * MDIM + PAIR)
        x_pair = x_ref[:, lanes]
        scaled = (x_pair * pair_columns(first_half, steps, head)).astype(BF16)
        parts = []
        for one in (head, head + 1):
            gaps = decay[:, one : one + 1] - decay_t[one : one + 1, :]
            weights = (jnp.exp(jnp.minimum(gaps, 0.0)) * products).astype(BF16)
            parts.append(mat(weights, scaled))
        y_ref[:, lanes] = (
            jnp.where(first_half, parts[0], parts[1])
            + pair_columns(first_half, reach, head) * incoming[:, lanes]
            + skip_ref[:, lanes] * x_pair
        )


def ssd_backward_kernel(
    x_ref,
    b_ref,
    c_ref,
    step_ref,
    decay_ref,
    decay_t_ref,
    start_ref,
    state_ref,
    skip_ref,
    y_ref,
    dy_ref,
    later_ref,
    end_ref,
    total_ref,
    dt_ref,
    bias_ref,
    rate_ref,
    dx_ref,
    db_ref,
    dc_ref,
    dt_grad_ref,
    small_ref,
    one_sum,
    two_sum,
    three_sum,
    mixed_y,
    mixed_x,
    head_sums,
    row_sums,
):
    rows = x_ref.shape[0]
    b_low = b_ref[...].astype(BF16)
    c_low = c_ref[...].astype(BF16)
    rel_start = start_ref[...]
    allowed, products = masked_products(b_low, c_low, rel_start)
    state_low = state_ref[0].astype(BF16)
    later_low = later_ref[0].astype(BF16)
    spread = mat_right_t(b_low, later_low)
    first_half = head_lanes(rows)
    steps = group_heads(step_ref)
    decay = group_heads(decay_ref)
    decay_t = group_rows(decay_t_ref)
    reach = jnp.where(rel_start < 0, jnp.exp(decay), 0.0)
    to_end = group_heads(end_ref) * steps
    product_grad = jnp.zeros((rows, rows), F32)
    skip_parts = []
    for head in range(0, HGROUP, 2):
        lanes = slice(head * MDIM, head * MDIM + PAIR)
        x_pair = x_ref[:, lanes]
        dy_pair = dy_ref[:, lanes]
        step_pair = pair_columns(first_half, steps, head)
        scaled = (x_pair * step_pair).astype(BF16)
        dy_low = dy_pair.astype(BF16)
        parts = []
        for one in (head, head + 1):
            gaps = decay[:, one : one + 1] - decay_t[one : one + 1, :]
            decays = jnp.exp(jnp.minimum(gaps, 0.0))
            mine = first_half if one == head else ~first_half
            dy_mine = jnp.where(mine, dy_pair, 0.0).astype(BF16)
            weight_grad = mat_right_t(dy_mine, scaled)
            product_grad = product_grad + weight_grad * decays
            parts.append(mat_left_t((decays * products).astype(BF16), dy_low))
        dz_pair = jnp.where(first_half, parts[0], parts[1])
        skip_pair = skip_ref[:, lanes]
        end_pair = pair_columns(first_half, to_end, head)
        spread_pair = spread[:, lanes]
        dx_ref[:, lanes] = skip_pair * dy_pair + step_pair * dz_pair + end_pair * spread_pair
        one_sum[:, lanes] = dy_pair * (y_ref[:, lanes] - skip_pair * x_pair)
        two_sum[:, lanes] = x_pair * dz_pair
        three_sum[:, lanes] = x_pair * spread_pair
        mixed_y[:, lanes] = (dy_pair * pair_columns(first_half, reach, head)).astype(BF16)
        mixed_x[:, lanes] = (x_pair * end_pair).astype(BF16)
        skip_parts.append(jnp.sum(dy_pair * x_pair, axis=0, keepdims=True))
    grad_low = jnp.where(allowed, product_grad, 0.0).astype(BF16)
    dc = mat(grad_low, b_low) + mat(mixed_y[...], state_low)
    db = mat_left_t(grad_low, c_low) + mat(mixed_x[...], later_low)
    group = pl.program_id(1)

    @pl.when(group == 0)
    def _():
        dc_ref[...] = jnp.zeros(dc_ref.shape, F32)
        db_ref[...] = jnp.zeros(db_ref.shape, F32)
        head_sums[...] = jnp.zeros(head_sums.shape, F32)
        row_sums[...] = jnp.zeros(row_sums.shape, F32)

    dc_ref[...] += dc
    db_ref[...] += db
    owner = lax.broadcasted_iota(jnp.int32, (GWIDTH, 128), 0) // MDIM + group * HGROUP
    picks = (owner == lax.broadcasted_iota(jnp.int32, (GWIDTH, 128), 1)).astype(F32)
    for place, source in enumerate((one_sum, two_sum, three_sum)):
        head_sums[place] += exact(source[...], picks, 1, 0)
    skips = jnp.broadcast_to(jnp.concatenate(skip_parts, axis=1), (8, GWIDTH))
    row_sums[0] += exact(skips, picks, 1, 0)
    meets = exact(
        jnp.ones((8, STATE), F32), later_ref[0].astype(F32) * state_ref[0].astype(F32), 1, 1
    )
    row_sums[1] += exact(meets, picks, 1, 0)

    @pl.when(group == pl.num_programs(1) - 1)
    def _():
        all_steps = step_ref[...]
        all_end = end_ref[...]
        rate = rate_ref[...]
        row_dot, u_dot, v_dot = head_sums[0], head_sums[1], head_sums[2]
        to_last = v_dot * all_end * all_steps
        grad_decay = row_dot - u_dot * all_steps - to_last
        at_end = jnp.sum(to_last, axis=0, keepdims=True) + row_sums[1, :1] * total_ref[0, :1]
        grad_drop = exact(lower_ones(rows), grad_decay, 0, 0) + at_end
        grad_steps = u_dot + v_dot * all_end - rate * grad_drop
        grad_dt = grad_steps * sigmoid(dt_ref[:, :128] + bias_ref[...])
        dt_grad_ref[:, :128] = grad_dt.astype(BF16)
        dt_grad_ref[:, 128:] = jnp.zeros((rows, dt_grad_ref.shape[1] - 128), BF16)
        small_ref[0, 0:1] = jnp.sum(grad_dt, axis=0, keepdims=True)
        small_ref[0, 1:2] = jnp.sum(-all_steps * grad_drop, axis=0, keepdims=True)
        small_ref[0, 2:8] = row_sums[0, :6]


def ssd_specs(rows):
    wide = pl.BlockSpec((rows, GWIDTH), lambda b, g: (b, g))
    b_spec = pl.BlockSpec((rows, STATE), lambda b, g: (b, DSSM // STATE))
    c_spec = pl.BlockSpec((rows, STATE), lambda b, g: (b, DSSM // STATE + 1))
    heads = pl.BlockSpec((rows, 128), lambda b, g: (b, 0))
    heads_t = pl.BlockSpec((1, 128, rows), lambda b, g: (b, 0, 0))
    column = pl.BlockSpec((rows, 1), lambda b, g: (b, 0))
    state = pl.BlockSpec((1, GWIDTH, STATE), lambda b, g: (b, g, 0))
    skip = pl.BlockSpec((1, GWIDTH), lambda b, g: (0, g))
    return [wide, b_spec, c_spec, heads, heads, heads_t, column, state, skip]


def ssd_forward(count, act, steps, decay, decay_t, rel_start, state_in, skip_row):
    rows = act.shape[0] // count
    specs = ssd_specs(rows)
    return pl.pallas_call(
        ssd_forward_kernel,
        grid=(count, NGROUP),
        in_specs=specs,
        out_specs=specs[0],
        out_shape=jax.ShapeDtypeStruct((count * rows, DSSM), F32),
        compiler_params=pltpu.CompilerParams(vmem_limit_bytes=40 * MIB),
        cost_estimate=pl.CostEstimate(
            flops=count * MHEADS * rows * rows * 400, bytes_accessed=8 * MIB, transcendentals=0
        ),
        name="ssd_forward",
    )(act, act, act, steps, decay, decay_t, rel_start, state_in, skip_row)


def ssd_backward(
    count,
    act,
    steps,
    decay,
    decay_t,
    rel_start,
    state_in,
    skip_row,
    scanned,
    grad_scanned,
    later,
    to_end,
    total,
    dt_rows,
    bias,
    rate,
):
    rows = act.shape[0] // count
    specs = ssd_specs(rows)
    wide, heads, state = specs[0], specs[3], specs[7]
    row = pl.BlockSpec((1, 128), lambda b, g: (0, 0))
    packed = pl.BlockSpec((1, 8, 128), lambda b, g: (b, 0, 0))
    narrow = pl.BlockSpec((rows, STATE), lambda b, g: (b, 0))
    dt_spec = pl.BlockSpec((rows, dt_rows.shape[1]), lambda b, g: (b, 0))
    tokens = count * rows
    return pl.pallas_call(
        ssd_backward_kernel,
        grid=(count, NGROUP),
        in_specs=specs + [wide, wide, state, heads, packed, dt_spec, row, row],
        out_specs=[wide, narrow, narrow, dt_spec, packed],
        out_shape=[
            jax.ShapeDtypeStruct((tokens, DSSM), F32),
            jax.ShapeDtypeStruct((tokens, STATE), F32),
            jax.ShapeDtypeStruct((tokens, STATE), F32),
            jax.ShapeDtypeStruct(dt_rows.shape, BF16),
            jax.ShapeDtypeStruct((count, 8, 128), F32),
        ],
        scratch_shapes=[pltpu.VMEM((rows, GWIDTH), F32)] * 3
        + [pltpu.VMEM((rows, GWIDTH), BF16)] * 2
        + [pltpu.VMEM((3, rows, 128), F32), pltpu.VMEM((2, 8, 128), F32)],
        compiler_params=pltpu.CompilerParams(vmem_limit_bytes=40 * MIB),
        cost_estimate=pl.CostEstimate(
            flops=count * MHEADS * rows * rows * 1000, bytes_accessed=16 * MIB, transcendentals=0
        ),
        name="ssd_backward",
    )(
        act,
        act,
        act,
        steps,
        decay,
        decay_t,
        rel_start,
        state_in,
        skip_row,
        scanned,
        grad_scanned,
        later,
        to_end,
        total,
        dt_rows,
        bias,
        rate,
    )


def spread_heads(source_ref, target, factor):
    width = source_ref.shape[1]
    target[...] = jnp.zeros(target.shape, target.dtype)
    for head in range(QHEADS):
        group = head // (QHEADS // KVHEADS)
        value = source_ref[head * HDIM : (head + 1) * HDIM, :]
        target[group * HDIM : (group + 1) * HDIM, head * width : (head + 1) * width] = (
            value * factor if factor != 1.0 else value
        )


def attend_allowed(block, first_pos, starts, width):
    key_pos = block * width + lax.broadcasted_iota(jnp.int32, (width, width), 0)
    query_pos = first_pos + lax.broadcasted_iota(jnp.int32, (width, width), 1)
    return (key_pos <= query_pos) & (key_pos >= starts)


NEAR = (0, 2, 1, 3)
TILE_ROWS = 256
TILE_COLS = 512


def near_at(step, size):
    return pl.ds(pl.multiple_of((lax.axis_index("wsh") ^ step) * size, 128), size)


def project_kernel(x_ref, *refs):
    *weights, out_ref = refs
    size = weights[0].shape[0]
    total = None
    for step, weight in zip(NEAR, weights):
        part = mat(x_ref[:, near_at(step, size)], weight[...])
        total = part if total is None else total + part
    out_ref[...] = total.astype(out_ref.dtype)


def project(x, weights, tile, kind=F32):
    tokens, depth = x.shape
    size, columns = weights[0].shape
    return pl.pallas_call(
        project_kernel,
        grid=(columns // tile,),
        in_specs=[pl.BlockSpec((tokens, depth), lambda i: (0, 0))]
        + [pl.BlockSpec((size, tile), lambda i: (0, i))] * 4,
        out_specs=pl.BlockSpec((tokens, tile), lambda i: (0, i)),
        out_shape=jax.ShapeDtypeStruct((tokens, columns), kind),
        compiler_params=pltpu.CompilerParams(vmem_limit_bytes=40 * MIB),
        cost_estimate=pl.CostEstimate(
            flops=2 * tokens * depth * columns,
            bytes_accessed=2 * depth * columns + 4 * tokens * columns,
            transcendentals=0,
        ),
        name="project",
    )(x, *weights)


def unproject_kernel(base_ref, grad_ref, *refs):
    *weights, out_ref = refs
    size = weights[0].shape[0]

    @pl.when(pl.program_id(0) == 0)
    def _():
        out_ref[...] = base_ref[...]

    for step, weight in zip(NEAR, weights):
        out_ref[:, near_at(step, size)] += mat_right_t(grad_ref[...], weight[...])


def unproject(base, grad, weights, tile):
    tokens, columns = grad.shape
    size = weights[0].shape[0]
    whole = pl.BlockSpec((tokens, 4 * size), lambda i: (0, 0))
    return pl.pallas_call(
        unproject_kernel,
        grid=(columns // tile,),
        in_specs=[whole, pl.BlockSpec((tokens, tile), lambda i: (0, i))]
        + [pl.BlockSpec((size, tile), lambda i: (0, i))] * 4,
        out_specs=whole,
        out_shape=jax.ShapeDtypeStruct((tokens, 4 * size), F32),
        compiler_params=pltpu.CompilerParams(vmem_limit_bytes=40 * MIB),
        cost_estimate=pl.CostEstimate(
            flops=8 * tokens * size * columns,
            bytes_accessed=8 * size * columns + 2 * tokens * columns,
            transcendentals=0,
        ),
        name="unproject",
    )(base, grad, *weights)


def out_proj_kernel(x_ref, mixed_ref, heads_ref, gain_ref, *refs):
    *weights, middle_ref, normed_ref = refs
    wide = mixed_ref.shape[1] // 4
    narrow = heads_ref.shape[0] // 4
    middle_ref[...] = x_ref[...].astype(F32)
    for step, weight in zip(NEAR, weights):
        middle_ref[...] += mat(mixed_ref[:, near_at(step, wide)], weight[:wide]) + mat_left_t(
            heads_ref[near_at(step, narrow), :], weight[wide:]
        )
    middle = middle_ref[...]
    normed_ref[...] = (middle * inv_rms(middle) * gain_ref[...]).astype(BF16)


def out_project(x, mixed, heads_t, gain, weights):
    vmem = pl.BlockSpec(memory_space=pltpu.VMEM)
    return pl.pallas_call(
        out_proj_kernel,
        in_specs=[vmem] * 8,
        out_specs=[vmem, vmem],
        out_shape=[jax.ShapeDtypeStruct(x.shape, F32), jax.ShapeDtypeStruct(x.shape, BF16)],
        compiler_params=pltpu.CompilerParams(vmem_limit_bytes=40 * MIB),
        cost_estimate=pl.CostEstimate(
            flops=2 * x.size * 2048, bytes_accessed=12 * MIB, transcendentals=0
        ),
        name="out_project",
    )(x, mixed, heads_t, gain[None], *weights)


def out_back_kernel(branch_ref, *refs):
    *weights, mixed_ref, heads_ref = refs
    wide = mixed_ref.shape[1] // 4
    narrow = heads_ref.shape[0] // 4
    for step, weight in zip(NEAR, weights):
        mixed_ref[:, near_at(step, wide)] = mat_right_t(branch_ref[...], weight[:wide])
        heads_ref[near_at(step, narrow), :] = mat_right_t(weight[wide:], branch_ref[...]).astype(
            BF16
        )


def out_unproject(branch, weights, mixed_width, heads_width):
    vmem = pl.BlockSpec(memory_space=pltpu.VMEM)
    tokens = branch.shape[0]
    return pl.pallas_call(
        out_back_kernel,
        in_specs=[vmem] * 5,
        out_specs=[vmem, vmem],
        out_shape=[
            jax.ShapeDtypeStruct((tokens, mixed_width), F32),
            jax.ShapeDtypeStruct((heads_width, tokens), BF16),
        ],
        compiler_params=pltpu.CompilerParams(vmem_limit_bytes=40 * MIB),
        cost_estimate=pl.CostEstimate(
            flops=2 * branch.size * 2048, bytes_accessed=12 * MIB, transcendentals=0
        ),
        name="out_unproject",
    )(branch, *weights)


FF_TILE = 512


def mlp_kernel(
    place_ref, normed_ref, top_ref, middle_ref, gain_ref, *refs
):
    gates, ups, downs = refs[0:4], refs[4:8], refs[8:12]
    layer_ref, grad_ref, branch_ref, gain_grad_ref, hidden_ref, pair_ref = refs[12:18]
    down_tile, out_sum, back_sum = refs[18:]
    step_at = pl.program_id(0)
    per_piece = pl.num_programs(0) // 4
    size = gates[0].shape[0]
    for piece in range(4):

        @pl.when(step_at // per_piece == piece)
        def _():
            down_tile[...] = downs[piece][...]

    gate = up = None
    for step, gate_ref, up_ref in zip(NEAR, gates, ups):
        rows = normed_ref[:, near_at(step, size)]
        gate_part, up_part = mat(rows, gate_ref[...]), mat(rows, up_ref[...])
        gate = gate_part if gate is None else gate + gate_part
        up = up_part if up is None else up + up_part
    sig = 1.0 / (1.0 + jnp.exp(-gate))
    silu = gate * sig
    hidden = (silu * up).astype(BF16)
    hidden_ref[...] = hidden
    grad_hidden = mat_right_t(top_ref[...], down_tile[...])
    grad_gate = (grad_hidden * up * (sig + silu * (1.0 - sig))).astype(BF16)
    grad_up = (grad_hidden * silu).astype(BF16)
    pair_ref[0] = grad_gate
    pair_ref[1] = grad_up

    @pl.when(step_at == 0)
    def _():
        out_sum[...] = jnp.zeros(out_sum.shape, F32)
        back_sum[...] = jnp.zeros(back_sum.shape, F32)

    out_sum[...] += mat(hidden, down_tile[...])
    for step, gate_ref, up_ref in zip(NEAR, gates, ups):
        back_sum[:, near_at(step, size)] += mat_right_t(grad_gate, gate_ref[...]) + mat_right_t(
            grad_up, up_ref[...]
        )

    @pl.when(step_at == pl.num_programs(0) - 1)
    def _():
        middle = middle_ref[...]
        layer_ref[...] = (middle + out_sum[...]).astype(BF16)
        grad_rows, grad_gain = rms_pull(middle, inv_rms(middle), gain_ref[...], back_sum[...])
        grad = top_ref[...].astype(F32) + grad_rows
        grad_ref[...] = grad
        branch_ref[...] = grad.astype(BF16)
        gain_grad_ref[...] = grad_gain[None]


def mlp_both(place, normed, top, middle, gain, gu_weights, down_weights):
    tokens, features = middle.shape
    size, columns = gu_weights[0].shape
    width = columns // 2
    steps = width // FF_TILE
    per_piece = steps // 4

    def natural(i, p):
        piece = i // per_piece
        near = (piece % 2) * 2 + piece // 2
        return (near ^ p[0]) * per_piece + i % per_piece

    whole = pl.BlockSpec((tokens, features), lambda i, p: (0, 0))
    gain_spec = pl.BlockSpec((1, features), lambda i, p: (0, 0))

    def down_spec(piece):
        return pl.BlockSpec(
            (FF_TILE, features),
            lambda i, p: (jnp.clip(i - piece * per_piece, 0, per_piece - 1), 0),
        )

    return pl.pallas_call(
        mlp_kernel,
        grid_spec=pltpu.PrefetchScalarGridSpec(
            num_scalar_prefetch=1,
            grid=(steps,),
            in_specs=[whole, whole, whole, gain_spec]
            + [pl.BlockSpec((size, FF_TILE), lambda i, p: (0, natural(i, p)))] * 4
            + [pl.BlockSpec((size, FF_TILE), lambda i, p: (0, natural(i, p) + steps))] * 4
            + [down_spec(piece) for piece in range(4)],
            out_specs=[
                whole,
                whole,
                whole,
                gain_spec,
                pl.BlockSpec((tokens, FF_TILE), lambda i, p: (0, natural(i, p))),
                pl.BlockSpec((2, tokens, FF_TILE), lambda i, p: (0, 0, natural(i, p))),
            ],
            scratch_shapes=[
                pltpu.VMEM((FF_TILE, features), BF16),
                pltpu.VMEM((tokens, features), F32),
                pltpu.VMEM((tokens, features), F32),
            ],
        ),
        out_shape=[
            jax.ShapeDtypeStruct((tokens, features), BF16),
            jax.ShapeDtypeStruct((tokens, features), F32),
            jax.ShapeDtypeStruct((tokens, features), BF16),
            jax.ShapeDtypeStruct((1, features), F32),
            jax.ShapeDtypeStruct((tokens, width), BF16),
            jax.ShapeDtypeStruct((2, tokens, width), BF16),
        ],
        compiler_params=pltpu.CompilerParams(vmem_limit_bytes=56 * MIB),
        cost_estimate=pl.CostEstimate(
            flops=12 * tokens * features * width, bytes_accessed=30 * MIB, transcendentals=0
        ),
        name="mlp_both",
    )(
        place,
        normed,
        top,
        middle,
        gain[None],
        *gu_weights,
        *gu_weights,
        *down_weights,
    )


EDGE = 8
EARLY_TILE = 256


def conv_inputs(edge_rows, own_rows):
    return jnp.concatenate([edge_rows, own_rows], axis=0)


def conv_valid(rel_start, tap, taps):
    rows = rel_start.shape[0]
    place = lax.broadcasted_iota(jnp.int32, (rows, 1), 0)
    return place - (taps - 1) + tap >= rel_start


def conv_sums(extended, weights, bias, rel_start):
    taps = weights.shape[0]
    rows = rel_start.shape[0]
    shifted = []
    total = None
    for tap in range(taps):
        begin = EDGE - (taps - 1) + tap
        part = jnp.where(
            conv_valid(rel_start, tap, taps), extended[begin : begin + rows], 0.0
        )
        shifted.append(part)
        term = weights[tap : tap + 1] * part
        total = bias + term if total is None else total + term
    return total, shifted


def early_kernel(
    count, x_ref, edge_ref, start_ref, weight_ref, bias_ref, *refs
):
    *blocks, conv_ref, edge_out, act_ref, dt_ref = refs
    size = blocks[0].shape[0]
    tile = pl.program_id(0)
    last = pl.num_programs(0) - 1

    def product(source):
        total = None
        for step, block in zip(NEAR, blocks):
            part = mat(source[:, near_at(step, size)], block[...])
            total = part if total is None else total + part
        return total

    value = product(x_ref)

    @pl.when(tile == last)
    def _():
        dt_ref[...] = value

    @pl.when(tile < last)
    def _():
        conv_ref[...] = value
        edge = product(edge_ref)
        edge_out[...] = edge
        rows = value.shape[0] // count
        for b in range(count):
            span = slice(b * rows, (b + 1) * rows)
            extended = conv_inputs(edge[b * EDGE : (b + 1) * EDGE], value[span])
            total, _ = conv_sums(extended, weight_ref[...], bias_ref[...], start_ref[span])
            act_ref[span] = total * sigmoid(total)


def conv_tile_spec(rows, count, begin=0):
    return pl.BlockSpec((rows, EARLY_TILE), lambda i: (0, jnp.clip(i - begin, 0, count - 1)))


def project_early(count, x, edge_x, rel_start, conv_weight, conv_bias, blocks):
    tokens, depth = x.shape
    size, columns = blocks[0].shape
    channels = conv_weight.shape[1]
    tiles = columns // EARLY_TILE
    conv_tiles = channels // EARLY_TILE

    def whole(array):
        return pl.BlockSpec(array.shape, lambda i: (0, 0))

    tile_shape = pl.BlockSpec((tokens, EARLY_TILE), lambda i: (0, 0))
    return pl.pallas_call(
        functools.partial(early_kernel, count),
        grid=(tiles,),
        in_specs=[
            whole(x),
            whole(edge_x),
            whole(rel_start),
            conv_tile_spec(conv_weight.shape[0], conv_tiles),
            conv_tile_spec(1, conv_tiles),
        ]
        + [pl.BlockSpec((size, EARLY_TILE), lambda i: (0, i))] * 4,
        out_specs=[
            conv_tile_spec(tokens, conv_tiles),
            conv_tile_spec(edge_x.shape[0], conv_tiles),
            conv_tile_spec(tokens, conv_tiles),
            tile_shape,
        ],
        out_shape=[
            jax.ShapeDtypeStruct((tokens, channels), F32),
            jax.ShapeDtypeStruct((edge_x.shape[0], channels), F32),
            jax.ShapeDtypeStruct((tokens, channels), F32),
            jax.ShapeDtypeStruct((tokens, EARLY_TILE), F32),
        ],
        compiler_params=pltpu.CompilerParams(vmem_limit_bytes=40 * MIB),
        cost_estimate=pl.CostEstimate(
            flops=2 * tokens * depth * columns, bytes_accessed=16 * MIB, transcendentals=0
        ),
        name="project_early",
    )(x, edge_x, rel_start, conv_weight, conv_bias[None], *blocks)


def conv_back(extended, weights, bias, rel_start, grad_act):
    total, shifted = conv_sums(extended, weights, bias, rel_start)
    gate = sigmoid(total)
    return grad_act * gate * (1.0 + total * (1.0 - gate)), shifted


def edge_grad_kernel(
    dx_ref, db_ref, dc_ref, conv_ref, edge_ref, start_ref, weight_ref, bias_ref, out_ref
):
    taps = weight_ref.shape[0]
    grad_act = jnp.concatenate([dx_ref[...], db_ref[...], dc_ref[...]], axis=1)
    extended = conv_inputs(edge_ref[...], conv_ref[...])
    grad, _ = conv_back(extended, weight_ref[...], bias_ref[...], start_ref[...], grad_act)
    total = jnp.zeros(grad.shape, F32)
    for tap in range(taps):
        part = jnp.where(
            conv_valid(start_ref[...], tap, taps), grad * weight_ref[tap : tap + 1], 0.0
        )
        padded = jnp.concatenate([jnp.zeros(part.shape, F32), part], axis=0)
        total = total + padded[taps - 1 - tap : taps - 1 - tap + EDGE]
    out_ref[...] = total


def edge_grads(count, dx, db, dc, conv_rows, edge_rows, rel_start, conv_weight, conv_bias):
    rows = dx.shape[0] // count
    steps = rows // EDGE

    def first(array):
        return pl.BlockSpec((EDGE, array.shape[1]), lambda b: (b * steps, 0))

    channels = conv_weight.shape[1]
    return pl.pallas_call(
        edge_grad_kernel,
        grid=(count,),
        in_specs=[
            first(dx),
            first(db),
            first(dc),
            first(conv_rows),
            pl.BlockSpec((EDGE, channels), lambda b: (b, 0)),
            first(rel_start),
            pl.BlockSpec(conv_weight.shape, lambda b: (0, 0)),
            pl.BlockSpec((1, channels), lambda b: (0, 0)),
        ],
        out_specs=pl.BlockSpec((EDGE, channels), lambda b: (b, 0)),
        out_shape=jax.ShapeDtypeStruct((count * EDGE, channels), F32),
        compiler_params=pltpu.CompilerParams(vmem_limit_bytes=16 * MIB),
        cost_estimate=pl.CostEstimate(flops=MIB, bytes_accessed=MIB, transcendentals=0),
        name="edge_grads",
    )(dx, db, dc, conv_rows, edge_rows, rel_start, conv_weight, conv_bias[None])


def early_back_kernel(
    count,
    base_ref,
    kv_ref,
    dx_ref,
    db_ref,
    dc_ref,
    conv_ref,
    edge_ref,
    came_ref,
    dt_ref,
    start_ref,
    weight_ref,
    bias_ref,
    x_ref,
    gain_ref,
    middle_ref,
    *refs,
):
    *blocks, grad_ref, conv_grad_ref, input_ref, gain_grad_ref, total = refs
    blocks, kv_blocks = blocks[:4], blocks[4:]
    size = blocks[0].shape[0]
    tile = pl.program_id(0)
    last = pl.num_programs(0) - 1
    taps = weight_ref.shape[0]

    @pl.when(tile == 0)
    def _():
        total[...] = base_ref[...]
        grad_ref[...] = kv_ref[...]
        for step, block in zip(NEAR, kv_blocks):
            total[:, near_at(step, size)] += mat_right_t(kv_ref[...], block[...])

    @pl.when(tile == last)
    def _():
        grad_ref[...] = dt_ref[...]

    @pl.when((tile > 0) & (tile < last))
    def _():
        rows = dx_ref.shape[0] // count
        tail = jnp.concatenate([db_ref[...], dc_ref[...]], axis=1)
        grad_act = jnp.where(tile == last - 1, tail, dx_ref[...])
        sums = [None] * (taps + 1)
        for b in range(count):
            span = slice(b * rows, (b + 1) * rows)
            ends = slice(b * EDGE, (b + 1) * EDGE)
            extended = conv_inputs(edge_ref[ends], conv_ref[span])
            rel_start = start_ref[span]
            grad, shifted = conv_back(
                extended, weight_ref[...], bias_ref[...], rel_start, grad_act[span]
            )
            back = jnp.concatenate(
                [jnp.zeros((rows - EDGE, grad.shape[1]), F32), came_ref[ends]], axis=0
            )
            for tap in range(taps):
                part = jnp.where(
                    conv_valid(rel_start, tap, taps), grad * weight_ref[tap : tap + 1], 0.0
                )
                padded = jnp.concatenate([part, jnp.zeros((EDGE, part.shape[1]), F32)], axis=0)
                back = back + padded[taps - 1 - tap : taps - 1 - tap + rows]
                term = jnp.sum(grad * shifted[tap], axis=0, keepdims=True)
                sums[tap] = term if sums[tap] is None else sums[tap] + term
            term = jnp.sum(grad, axis=0, keepdims=True)
            sums[taps] = term if sums[taps] is None else sums[taps] + term
            grad_ref[span] = back.astype(BF16)
        conv_grad_ref[0 : taps + 1] = jnp.concatenate(sums, axis=0)
        conv_grad_ref[taps + 1 :] = jnp.zeros(
            (conv_grad_ref.shape[0] - taps - 1, grad_act.shape[1]), F32
        )

    @pl.when(tile > 0)
    def _():
        for step, block in zip(NEAR, blocks):
            total[:, near_at(step, size)] += mat_right_t(grad_ref[...], block[...])

    @pl.when(tile == last)
    def _():
        x = x_ref[...].astype(F32)
        grad_rows, grad_gain = rms_pull(x, inv_rms(x), gain_ref[...], total[...])
        input_ref[...] = (middle_ref[...] + grad_rows).astype(BF16)
        gain_grad_ref[...] = grad_gain[None]


def early_back(
    count,
    base,
    grad_kv,
    dx,
    db,
    dc,
    conv_rows,
    edge_rows,
    came,
    dt_grad,
    rel_start,
    conv_weight,
    conv_bias,
    x,
    gain,
    grad_middle,
    blocks,
    kv_blocks,
):
    tokens, depth = base.shape
    size, columns = blocks[0].shape
    channels = conv_weight.shape[1]
    tiles = columns // EARLY_TILE + 1
    conv_tiles = channels // EARLY_TILE

    def whole(array):
        return pl.BlockSpec(array.shape, lambda i: (0, 0))

    return pl.pallas_call(
        functools.partial(early_back_kernel, count),
        grid=(tiles,),
        in_specs=[
            whole(base),
            whole(grad_kv),
            conv_tile_spec(tokens, conv_tiles - 1, 1),
            whole(db),
            whole(dc),
            conv_tile_spec(tokens, conv_tiles, 1),
            conv_tile_spec(edge_rows.shape[0], conv_tiles, 1),
            conv_tile_spec(edge_rows.shape[0], conv_tiles, 1),
            whole(dt_grad),
            whole(rel_start),
            conv_tile_spec(conv_weight.shape[0], conv_tiles, 1),
            conv_tile_spec(1, conv_tiles, 1),
            whole(x),
            pl.BlockSpec((1, depth), lambda i: (0, 0)),
            whole(grad_middle),
        ]
        + [pl.BlockSpec((size, EARLY_TILE), lambda i: (0, jnp.maximum(i - 1, 0)))] * 4
        + [pl.BlockSpec((size, EARLY_TILE), lambda i: (0, 0))] * 4,
        out_specs=[
            pl.BlockSpec((tokens, EARLY_TILE), lambda i: (0, i)),
            conv_tile_spec(8, conv_tiles, 1),
            whole(x),
            pl.BlockSpec((1, depth), lambda i: (0, 0)),
        ],
        out_shape=[
            jax.ShapeDtypeStruct((tokens, columns + EARLY_TILE), BF16),
            jax.ShapeDtypeStruct((8, channels), F32),
            jax.ShapeDtypeStruct(x.shape, BF16),
            jax.ShapeDtypeStruct((1, depth), F32),
        ],
        scratch_shapes=[pltpu.VMEM((tokens, depth), F32)],
        compiler_params=pltpu.CompilerParams(vmem_limit_bytes=48 * MIB),
        cost_estimate=pl.CostEstimate(
            flops=2 * tokens * depth * columns, bytes_accessed=20 * MIB, transcendentals=0
        ),
        name="early_back",
    )(
        base,
        grad_kv,
        dx,
        db,
        dc,
        conv_rows,
        edge_rows,
        came,
        dt_grad,
        rel_start,
        conv_weight,
        conv_bias[None],
        x,
        gain[None],
        grad_middle,
        *blocks,
        *kv_blocks,
    )


def block_grads_kernel(steps, left_ref, right_ref, *refs):
    came = refs[0] if len(refs) == 3 else None
    outs = refs[-2:] if came is not None else refs
    size = left_ref.shape[1] // 4
    for place, step in enumerate(steps):
        value = mat_left_t(left_ref[:, near_at(step, size)], right_ref[0])
        if came is None:
            outs[0][place * size : (place + 1) * size] = value.astype(BF16)
        else:
            value = value + came[place * size : (place + 1) * size].astype(F32)
            outs[place][...] = value.astype(BF16)


def block_grads(left, right, steps, came=None):
    tokens, depth = left.shape
    size = depth // 4
    parts, _, width = right.shape
    per_part = width // TILE_COLS
    columns = parts * width
    tall = pl.BlockSpec((2 * size, TILE_COLS), lambda i: (0, i))
    flat = pl.BlockSpec((size, TILE_COLS), lambda i: (0, i))
    operands = [left, right] + ([] if came is None else [came])
    return pl.pallas_call(
        functools.partial(block_grads_kernel, steps),
        grid=(columns // TILE_COLS,),
        in_specs=[
            pl.BlockSpec((tokens, depth), lambda i: (0, 0)),
            pl.BlockSpec((1, tokens, TILE_COLS), lambda i: (i // per_part, 0, i % per_part)),
        ]
        + ([] if came is None else [tall]),
        out_specs=[tall] if came is None else [flat, flat],
        out_shape=[jax.ShapeDtypeStruct((2 * size, columns), BF16)]
        if came is None
        else [jax.ShapeDtypeStruct((size, columns), BF16)] * 2,
        compiler_params=pltpu.CompilerParams(vmem_limit_bytes=32 * MIB),
        cost_estimate=pl.CostEstimate(
            flops=4 * tokens * size * columns, bytes_accessed=6 * MIB, transcendentals=0
        ),
        name="block_grads",
    )(*operands)


def finish_kernel(
    conv_width, early_ref, late_ref, mix_ref, in_ref, q_ref, kv_ref, out_ref, o_ref
):
    kv_width = kv_ref.shape[1]
    gate = in_ref.shape[1] - conv_width
    in_ref[:, :gate] = late_ref[:, :gate].astype(F32)
    in_ref[:, gate:] = early_ref[:, kv_width:].astype(F32)
    q_ref[...] = late_ref[:, gate:].astype(F32)
    kv_ref[...] = early_ref[:, :kv_width].astype(F32)
    split = out_ref.shape[0]
    out_ref[...] = mix_ref[:split].astype(F32)
    o_ref[...] = mix_ref[split:].astype(F32)


def finish(early, late, mix, shapes, conv_width):
    vmem = pl.BlockSpec(memory_space=pltpu.VMEM)
    return pl.pallas_call(
        functools.partial(finish_kernel, conv_width),
        in_specs=[vmem] * 3,
        out_specs=[vmem] * 5,
        out_shape=[jax.ShapeDtypeStruct(shape, F32) for shape in shapes],
        compiler_params=pltpu.CompilerParams(vmem_limit_bytes=32 * MIB),
        cost_estimate=pl.CostEstimate(flops=MIB, bytes_accessed=10 * MIB, transcendentals=0),
        name="finish",
    )(early, late, mix)


def passed_along(block, axis, distance):
    devices = range(lax.axis_size(axis))
    route = [(i - distance, i) for i in devices if i - distance in devices]
    return lax.ppermute(block, axis, route)


def swapped(block, axis, bit):
    return lax.ppermute(block, axis, [(i, i ^ bit) for i in range(lax.axis_size(axis))])


def bits_of(axis):
    return [1 << k for k in range(lax.axis_size(axis).bit_length() - 1)]


def after(value, earlier):
    return lax.optimization_barrier((value, earlier))[0]


def gathered_near(shard, earlier=None, held=None):
    if earlier is not None:
        shard = after(shard, earlier)
    across = swapped(shard, "wsh", 2)
    if held is not None:
        across = after(across, held)
    return [shard, across, swapped(shard, "wsh", 1), swapped(across, "wsh", 1)]


class Gathering:
    def __init__(self, rows, bits):
        self.table = rows[None]
        self.bits = list(bits)
        self.start()

    def start(self):
        if self.bits:
            self.came = swapped(self.table, "ctx", self.bits.pop(0))
        else:
            self.came = None

    def advance(self, held=None):
        if self.came is not None:
            came = self.came if held is None else after(self.came, held)
            self.table = jnp.concatenate([self.table, came], axis=0)
            self.start()
        return self.table

    def finish(self):
        while self.came is not None:
            self.advance()
        return self.table


class Scattering:
    def __init__(self, table, bits):
        self.table = table
        self.bits = list(bits)
        self.start()

    def start(self):
        if self.bits:
            half = self.table.shape[0] // 2
            self.came = swapped(self.table[half:], "ctx", self.bits.pop(0))
        else:
            self.came = None

    def advance(self, held=None):
        if self.came is not None:
            came = self.came if held is None else after(self.came, held)
            half = self.table.shape[0] // 2
            self.table = (self.table[:half].astype(F32) + came.astype(F32)).astype(BF16)
            self.start()
        return self.table

    def finish(self):
        while self.came is not None:
            self.advance()
        return self.table[0]


def ctx_bits(count):
    return [1 << k for k in range(count.bit_length() - 1)]


def partner_wsh(step):
    return (lax.axis_index("ctx"), lax.axis_index("wsh") ^ step)


def partner_ctx(step):
    return (lax.axis_index("ctx") ^ step, lax.axis_index("wsh"))


def remote(source, target, send, recv, device):
    return pltpu.make_async_remote_copy(
        src_ref=source,
        dst_ref=target,
        send_sem=send,
        recv_sem=recv,
        device_id=device,
        device_id_type=pl.DeviceIdType.MESH,
    )


def grads_kernel(
    count,
    split,
    early_units,
    late_units,
    one_ref,
    mix_ref,
    heads_ref,
    early_ref,
    late_ref,
    branch_ref,
    small_ref,
    early_out,
    late_out,
    mix_out,
    small_out,
    core_out,
    work,
    y_in,
    ctx_in,
    final,
    small_in,
    core_sems,
    y_sems,
    rs_sems,
    ag_sems,
    small_sems,
    out_sems,
):
    bits = ctx_bits(count)
    here = lax.axis_index("ctx")
    units = work.shape[0]
    rows = work.shape[2]
    width = work.shape[3]
    wsh_steps = (1, 2)
    barrier = pltpu.get_barrier_semaphore()
    partners = [partner_wsh(step) for step in wsh_steps] + [partner_ctx(bit) for bit in bits]
    for device in partners:
        pl.semaphore_signal(
            barrier, inc=1, device_id=device, device_id_type=pl.DeviceIdType.MESH
        )
    pl.semaphore_wait(barrier, len(partners))

    sizes = [rows >> (k + 1) for k in range(len(bits))]
    starts = []
    others = []
    base = 0
    for bit, size in zip(bits, sizes):
        upper = (here // bit) % 2
        others.append(base + (1 - upper) * size)
        base = base + upper * size
        starts.append(base)

    def span(start, size):
        return pl.ds(pl.multiple_of(start, 16), size)

    def core_copy(u):
        return remote(
            core_out.at[u % 2],
            work.at[u],
            core_sems.at[0, u],
            core_sems.at[1, u],
            partner_wsh(1),
        )

    def y_copy(u):
        return remote(work.at[u, 1], y_in.at[u], y_sems.at[0, u], y_sems.at[1, u], partner_wsh(2))

    recv_base = [rows - (rows >> k) for k in range(len(bits))]

    def rs_copy(u, k):
        return remote(
            work.at[u, 0, span(others[k], sizes[k])],
            ctx_in.at[u, pl.ds(recv_base[k], sizes[k])],
            rs_sems.at[0, k, u],
            rs_sems.at[1, k, u],
            partner_ctx(bits[k]),
        )

    def ag_copy(u, k):
        return remote(
            final.at[u, span(starts[k], sizes[k])],
            final.at[u, span(starts[k], sizes[k])],
            ag_sems.at[0, k, u],
            ag_sems.at[1, k, u],
            partner_ctx(bits[k]),
        )

    limits = []
    first_unit = 0
    for size in (early_units, late_units, 4):
        limits.append((first_unit, first_unit + size))
        first_unit += size
    outs = (early_out, late_out, mix_out)

    def by_part(u, action):
        for part, (low, high) in enumerate(limits):
            pl.when((u >= low) & (u < high))(functools.partial(action, part, u - low))

    def each_out(u, act):
        def one(part, v):
            tall = part == 2
            for i in range(split):
                row = (v // 2) * TILE_ROWS if tall else 0
                column = ((v % 2) if tall else v) * TILE_COLS + i * width
                copy = pltpu.make_async_copy(
                    final.at[u, pl.ds(i * TILE_ROWS, TILE_ROWS)],
                    outs[part].at[
                        pl.ds(pl.multiple_of(row, TILE_ROWS), TILE_ROWS),
                        pl.ds(pl.multiple_of(column, 128), width),
                    ],
                    out_sems.at[u, i],
                )
                act(copy)

        by_part(u, one)

    def columns_at(v):
        return pl.ds(pl.multiple_of(v * TILE_COLS, 128), TILE_COLS)

    wide = mix_ref.shape[1] // 4
    narrow = heads_ref.shape[0] // 4

    def pieces(u, first, put):
        steps = NEAR[2 * first : 2 * first + 2]

        def one(part, v):
            for place, step in enumerate(steps):
                if part < 2:
                    left = one_ref[:, near_at(step, TILE_ROWS)]
                    value = mat_left_t(left, (early_ref, late_ref)[part][:, columns_at(v)])
                else:
                    right = branch_ref[:, columns_at(v % 2)]
                    other = lax.axis_index("wsh") ^ step
                    begin = pl.multiple_of(other * wide, 128)

                    @pl.when(v < 2)
                    def _():
                        put(place, mat_left_t(mix_ref[:, pl.ds(begin, TILE_ROWS)], right))

                    @pl.when(v >= 2)
                    def _():
                        tail_at = pl.multiple_of(begin + TILE_ROWS, 128)
                        tail = mat_left_t(mix_ref[:, pl.ds(tail_at, wide - TILE_ROWS)], right)
                        heads_at = pl.multiple_of(other * narrow, 128)
                        heads = mat(heads_ref[pl.ds(heads_at, narrow), :], right)
                        put(place, jnp.concatenate([tail, heads], axis=0))

                    continue
                put(place, value)

        by_part(u, one)

    def chunked(value):
        return [
            (slice(i * TILE_ROWS, (i + 1) * TILE_ROWS), value[:, i * width : (i + 1) * width])
            for i in range(split)
        ]

    def begin(u):
        def put(place, value):
            for where, part in chunked(value):
                core_out[u % 2, place, where] = part.astype(BF16)

        pieces(u, 1, put)
        core_copy(u).start()

    def after_core(u):
        core_copy(u).wait()

        def put(place, value):
            for where, part in chunked(value):
                work[u, place, where] = (work[u, place, where].astype(F32) + part).astype(BF16)

        pieces(u, 0, put)
        y_copy(u).start()

    def after_y(u):
        y_copy(u).wait()
        work[u, 0] = (work[u, 0].astype(F32) + y_in[u].astype(F32)).astype(BF16)
        rs_copy(u, 0).start()

    def after_rs(u, k):
        rs_copy(u, k).wait()
        mine = span(starts[k], sizes[k])
        total = work[u, 0, mine].astype(F32) + ctx_in[
            u, pl.ds(recv_base[k], sizes[k])
        ].astype(F32)
        if k + 1 < len(bits):
            work[u, 0, mine] = total.astype(BF16)
            rs_copy(u, k + 1).start()
        else:
            final[u, mine] = total.astype(BF16)
            ag_copy(u, k).start()

    def after_ag(u, k):
        ag_copy(u, k).wait()
        if k > 0:
            ag_copy(u, k - 1).start()
        else:
            each_out(u, lambda copy: copy.start())

    stages = [(0, begin), (1, after_core), (3, after_y)]
    delay = 3
    for k in range(len(bits)):
        delay += 1
        stages.append((delay, functools.partial(after_rs, k=k)))
    for k in range(len(bits) - 1, -1, -1):
        delay += 1
        stages.append((delay, functools.partial(after_ag, k=k)))

    small_out[...] = small_ref[...]
    hops = partners

    def small_copy(k):
        return remote(
            small_in.at[k, 0], small_in.at[k, 1], small_sems.at[0, k], small_sems.at[1, k], hops[k]
        )

    def small_step(k):
        if k > 0:
            small_copy(k - 1).wait()
            small_out[...] += small_in[k - 1, 1]
        if k < len(hops):
            small_in[k, 0] = small_out[...]
            small_copy(k).start()

    def one_step(t, carry):
        for k in range(len(hops) + 1):
            pl.when(t == 2 * k + 1)(functools.partial(small_step, k))
        for offset, stage in stages[::-1]:
            u = t - offset
            pl.when((u >= 0) & (u < units))(functools.partial(stage, u))
        return carry

    lax.fori_loop(0, units + delay, one_step, 0)

    def finish(u, carry):
        each_out(u, lambda copy: copy.wait())
        return carry

    lax.fori_loop(0, units, finish, 0)


def reduce_grads(
    count, early_width, one, mixed, heads_t, early, late, branch, small
):
    bits = ctx_bits(count)
    hops = len(bits) + 2
    split = max(1, 16 * count // TILE_ROWS)
    early_units = early_width // TILE_COLS
    late_units = late.shape[1] // TILE_COLS
    units = early_units + late_units + 4
    rows, width = TILE_ROWS * split, TILE_COLS // split
    dma = pltpu.SemaphoreType.DMA
    vmem = pl.BlockSpec(memory_space=pltpu.VMEM)
    hbm = pl.BlockSpec(memory_space=pl.ANY)
    return pl.pallas_call(
        functools.partial(grads_kernel, count, split, early_units, late_units),
        in_specs=[vmem] * 7,
        out_specs=[hbm] * 3 + [vmem],
        out_shape=[
            jax.ShapeDtypeStruct((TILE_ROWS, early_units * TILE_COLS), BF16),
            jax.ShapeDtypeStruct((TILE_ROWS, late_units * TILE_COLS), BF16),
            jax.ShapeDtypeStruct((2 * TILE_ROWS, 2 * TILE_COLS), BF16),
            jax.ShapeDtypeStruct(small.shape, F32),
        ],
        scratch_shapes=[
            pltpu.VMEM((2, 2, rows, width), BF16),
            pltpu.VMEM((units, 2, rows, width), BF16),
            pltpu.VMEM((units, rows, width), BF16),
            pltpu.VMEM((units, rows, width), BF16),
            pltpu.VMEM((units, rows, width), BF16),
            pltpu.VMEM((hops, 2) + small.shape, F32),
            dma((2, units)),
            dma((2, units)),
            dma((2, len(bits), units)),
            dma((2, len(bits), units)),
            dma((2, hops)),
            dma((units, split)),
        ],
        compiler_params=pltpu.CompilerParams(
            collective_id=1, has_side_effects=True, vmem_limit_bytes=62 * MIB
        ),
        cost_estimate=pl.CostEstimate(
            flops=6_500_000_000, bytes_accessed=30 * MIB, transcendentals=0
        ),
        name="reduce_grads",
    )(one, mixed, heads_t, early, late, branch, small)


def exchange_barrier(devices):
    barrier = pltpu.get_barrier_semaphore()
    for device in devices:
        pl.semaphore_signal(
            barrier, inc=1, device_id=device, device_id_type=pl.DeviceIdType.MESH
        )
    pl.semaphore_wait(barrier, len(devices))


def row_factors(totals, owner):
    rows = owner.shape[0]
    picks = (owner == lax.broadcasted_iota(jnp.int32, (rows, 128), 1)).astype(F32)
    return exact(picks, totals, 1, 1)[:, :1]


class StateExchange:
    def __init__(self, count, forward, state_ref, totals, result, sent, came, back, sems):
        self.count, self.forward = count, forward
        self.state_ref, self.totals, self.result = state_ref, totals, result
        self.sent, self.came, self.back, self.sems = sent, came, back, sems
        self.here = lax.axis_index("ctx")
        self.share = state_ref.shape[1] // count

    def rows_of(self, place):
        return pl.ds(pl.multiple_of(place * self.share, 16), self.share)

    def out_copy(self, k):
        return remote(
            self.sent.at[:, self.rows_of(self.here ^ k)],
            self.came.at[self.here],
            self.sems.at[0, k],
            self.sems.at[1, k],
            partner_ctx(k),
        )

    def in_copy(self, k):
        return remote(
            self.sent.at[:, self.rows_of(self.here ^ k)],
            self.came.at[self.here ^ k],
            self.sems.at[0, k],
            self.sems.at[1, k],
            partner_ctx(k),
        )

    def back_copy(self, k):
        return remote(
            self.back.at[self.here ^ k],
            self.result.at[:, self.rows_of(self.here)],
            self.sems.at[2, k],
            self.sems.at[3, k],
            partner_ctx(k),
        )

    def back_in(self, k):
        return remote(
            self.back.at[self.here ^ k],
            self.result.at[:, self.rows_of(self.here ^ k)],
            self.sems.at[2, k],
            self.sems.at[3, k],
            partner_ctx(k),
        )

    def begin(self):
        self.sent[...] = self.state_ref[...].astype(BF16)
        for k in range(1, self.count):
            self.out_copy(k).start()
        self.came[self.here] = self.state_ref[:, self.rows_of(self.here), :].astype(BF16)

    def middle(self):
        for k in range(1, self.count):
            self.out_copy(k).wait_send()
            self.in_copy(k).wait_recv()
        place = lax.broadcasted_iota(jnp.int32, (self.share, 128), 0) + self.here * self.share
        owner = place // MDIM
        order = range(self.count) if self.forward else range(self.count - 1, -1, -1)
        for b in range(self.state_ref.shape[0]):
            total = jnp.zeros((self.share, STATE), F32)
            for block in order:
                self.back[block, b] = total.astype(BF16)
                factor = row_factors(self.totals[block, b], owner)
                total = factor * total + self.came[block, b].astype(F32)
        for k in range(1, self.count):
            self.back_copy(k).start()
        self.result[:, self.rows_of(self.here), :] = self.back[self.here]

    def end(self):
        for k in range(1, self.count):
            self.back_copy(k).wait_send()
            self.back_in(k).wait_recv()


def mix_forward_kernel(
    count,
    start_ref,
    q_ref,
    near_ref,
    state_ref,
    total_ref,
    out_ref,
    log_ref,
    table_out,
    state_out,
    totals_out,
    q_wide,
    top,
    total,
    acc,
    far,
    totals,
    sent,
    came,
    back,
    result,
    total_sems,
    table_sems,
    state_sems,
):
    here = lax.axis_index("ctx")
    batch = near_ref.shape[1]
    width = near_ref.shape[2]
    half = count // 2
    exchange_barrier([partner_ctx(k) for k in range(1, count)])
    totals[here] = total_ref[...]

    def total_copy(k, place):
        return remote(
            totals.at[here],
            totals.at[place],
            total_sems.at[0, k],
            total_sems.at[1, k],
            partner_ctx(k),
        )

    def table_copy(i):
        return remote(
            near_ref.at[i], far.at[i], table_sems.at[0, i], table_sems.at[1, i], partner_ctx(1)
        )

    for k in range(1, count):
        total_copy(k, here).start()
    states = StateExchange(
        count, True, state_ref, totals, result, sent, came, back, state_sems
    )
    states.begin()
    for i in range(half):
        table_copy(i).start()
    for b in range(batch):
        spread_heads(q_ref.at[:, b * width : (b + 1) * width], q_wide.at[b], HDIM**-0.5)
    top[...] = jnp.full(top.shape, MASKED_SCORE, F32)
    total[...] = jnp.zeros(total.shape, F32)
    acc[...] = jnp.zeros(acc.shape, F32)
    first_pos = here * width

    def attend(b, source, i, block):
        kv_rows = source[i, b]
        keys = kv_rows[:, : KVHEADS * HDIM]
        values_t = kv_rows[:, KVHEADS * HDIM :].T
        allowed = attend_allowed(block, first_pos, start_ref[b][:1], width)
        tops, totals_now = top[b], total[b]
        new_tops, new_totals = [], []
        for head in range(QHEADS):
            group = head // (QHEADS // KVHEADS)
            line = slice(head, head + 1)
            scores = mat(keys, q_wide[b, :, head * width : (head + 1) * width])
            scores = jnp.where(allowed, scores, MASKED_SCORE)
            old = tops[line]
            new = jnp.maximum(old, jnp.max(scores, axis=0, keepdims=True))
            terms = jnp.exp(scores - new)
            shrink = jnp.exp(old - new)
            new_tops.append(new)
            new_totals.append(
                totals_now[line] * shrink + jnp.sum(terms, axis=0, keepdims=True)
            )
            acc[b, head] = acc[b, head] * shrink + mat(
                values_t[group * HDIM : (group + 1) * HDIM, :], terms.astype(BF16)
            )
        top[b] = jnp.concatenate(new_tops, axis=0)
        total[b] = jnp.concatenate(new_totals, axis=0)

    bits = ctx_bits(count)
    high = len(bits) - 1

    def step_of(i):
        return sum(((i // (1 << p)) % 2) * (1 << (high - p)) for p in range(high))

    def pair(source, low):
        def one(i, carry):
            block = here ^ (step_of(i) + low)

            @pl.when(block <= here)
            def _():
                for b in range(batch):
                    attend(b, source, i, block)

            return carry

        lax.fori_loop(0, half, one, 0)

    pair(near_ref, 0)
    for k in range(1, count):
        total_copy(k, here).wait_send()
        total_copy(k, here ^ k).wait_recv()
    states.middle()
    for i in range(half):
        table_copy(i).wait()
    pair(far, 1)
    for b in range(batch):
        for head in range(QHEADS):
            out_ref[head * HDIM : (head + 1) * HDIM, b * width : (b + 1) * width] = (
                acc[b, head] / total[b, head : head + 1, :]
            ).astype(BF16)
        log_ref[b] = top[b] + jnp.log(total[b])
    table_out[:half] = near_ref[...]
    table_out[half:] = far[...]
    totals_out[...] = totals[...]
    states.end()
    state_out[...] = result[...]


def mix_forward(count, starts, queries_t, near, state, total):
    half, batch, width, kv_width = near.shape
    vmem = pl.BlockSpec(memory_space=pltpu.VMEM)
    dma = pltpu.SemaphoreType.DMA
    share = state.shape[1] // count
    low = functools.partial(jax.ShapeDtypeStruct, dtype=BF16)
    wide = functools.partial(jax.ShapeDtypeStruct, dtype=F32)
    return pl.pallas_call(
        functools.partial(mix_forward_kernel, count),
        in_specs=[vmem] * 5,
        out_specs=[vmem] * 5,
        out_shape=[
            low(queries_t.shape),
            wide((batch, QHEADS, width)),
            low((count,) + near.shape[1:]),
            low(state.shape),
            wide((count,) + total.shape),
        ],
        scratch_shapes=[
            pltpu.VMEM((batch, KVHEADS * HDIM, QHEADS * width), BF16),
            pltpu.VMEM((batch, QHEADS, width), F32),
            pltpu.VMEM((batch, QHEADS, width), F32),
            pltpu.VMEM((batch, QHEADS, HDIM, width), F32),
            pltpu.VMEM(near.shape, BF16),
            pltpu.VMEM((count,) + total.shape, F32),
            pltpu.VMEM(state.shape, BF16),
            pltpu.VMEM((count, batch, share, STATE), BF16),
            pltpu.VMEM((count, batch, share, STATE), BF16),
            pltpu.VMEM(state.shape, BF16),
            dma((2, count)),
            dma((2, half)),
            dma((4, count)),
        ],
        compiler_params=pltpu.CompilerParams(
            collective_id=2, has_side_effects=True, vmem_limit_bytes=56 * MIB
        ),
        cost_estimate=pl.CostEstimate(
            flops=batch * count * width * width * 8 * 1000,
            bytes_accessed=4 * MIB,
            transcendentals=0,
        ),
        name="mix_forward",
    )(starts, queries_t, near, state, total)


def mix_backward_kernel(
    count,
    start_ref,
    q_ref,
    table_ref,
    attended_ref,
    grad_ref,
    log_ref,
    state_ref,
    totals_ref,
    dq_ref,
    dkv_ref,
    later_ref,
    q_wide,
    g_wide,
    q_tall,
    g_tall,
    delta,
    acc,
    mine,
    theirs,
    far,
    sent,
    came,
    back,
    result,
    table_sems,
    state_sems,
):
    here = lax.axis_index("ctx")
    batch = table_ref.shape[1]
    width = table_ref.shape[2]
    half = count // 2
    kv_width = KVHEADS * HDIM
    exchange_barrier([partner_ctx(k) for k in range(1, count)])
    states = StateExchange(
        count, False, state_ref, totals_ref, result, sent, came, back, state_sems
    )
    states.begin()
    first_pos = here * width
    acc[...] = jnp.zeros(acc.shape, F32)
    mine[...] = jnp.zeros(mine.shape, BF16)
    theirs[...] = jnp.zeros(theirs.shape, BF16)
    for b in range(batch):
        columns = slice(b * width, (b + 1) * width)
        spread_heads(q_ref.at[:, columns], q_wide.at[b], HDIM**-0.5)
        spread_heads(grad_ref.at[:, columns], g_wide.at[b], 1.0)
        for head in range(QHEADS):
            lanes = slice(head * width, (head + 1) * width)
            q_tall[b, lanes, :] = q_wide[b, :, lanes].T
            g_tall[b, lanes, :] = g_wide[b, :, lanes].T
            span = slice(head * HDIM, (head + 1) * HDIM)
            delta[b, head : head + 1, :] = jnp.sum(
                attended_ref[span, columns].astype(F32) * grad_ref[span, columns].astype(F32),
                axis=0,
                keepdims=True,
            )

    def attend(b, place, block, target, i):
        kv_rows = table_ref[place, b]
        keys = kv_rows[:, :kv_width]
        values = kv_rows[:, kv_width:]
        keys_t = keys.T
        allowed = attend_allowed(block, first_pos, start_ref[b][:1], width)
        logs_now, deltas = log_ref[b], delta[b]
        dk = jnp.zeros((width, kv_width), F32)
        dv = jnp.zeros((width, kv_width), F32)
        for head in range(QHEADS):
            group = head // (QHEADS // KVHEADS)
            lanes = slice(head * width, (head + 1) * width)
            line = slice(head, head + 1)
            scores = mat(keys, q_wide[b, :, lanes])
            shifted = jnp.where(allowed, scores - logs_now[line], MASKED_SCORE)
            probs = jnp.exp(shifted)
            grad_probs = mat(values, g_wide[b, :, lanes])
            grad_scores = (probs * (grad_probs - deltas[line])).astype(BF16)
            dk = dk + mat(grad_scores, q_tall[b, lanes, :])
            dv = dv + mat(probs.astype(BF16), g_tall[b, lanes, :])
            acc[b, head] += mat(keys_t[group * HDIM : (group + 1) * HDIM, :], grad_scores)
        target[i, b] = jnp.concatenate([dk, dv], axis=1).astype(BF16)

    bits = ctx_bits(count)
    high = len(bits) - 1

    def step_of(i):
        return sum(((i // (1 << p)) % 2) * (1 << (high - p)) for p in range(high))

    def pair(target, low):
        def one(i, carry):
            block = here ^ (step_of(i) + low)

            @pl.when(block <= here)
            def _():
                for b in range(batch):
                    attend(b, i + low * half, block, target, i)

            return carry

        lax.fori_loop(0, half, one, 0)

    def table_copy(i):
        return remote(
            theirs.at[i], far.at[i], table_sems.at[0, i], table_sems.at[1, i], partner_ctx(1)
        )

    pair(theirs, 1)
    for i in range(half):
        table_copy(i).start()
    states.middle()
    pair(mine, 0)
    for b in range(batch):
        for head in range(QHEADS):
            dq_ref[head * HDIM : (head + 1) * HDIM, b * width : (b + 1) * width] = (
                acc[b, head] * HDIM**-0.5
            ).astype(BF16)
    for i in range(half):
        table_copy(i).wait()
    dkv_ref[...] = (mine[...].astype(F32) + far[...].astype(F32)).astype(BF16)
    states.end()
    later_ref[...] = result[...]


def mix_backward(count, starts, queries_t, table, attended_t, grad_t, logs, state, totals):
    _, batch, width, kv_width = table.shape
    half = count // 2
    vmem = pl.BlockSpec(memory_space=pltpu.VMEM)
    dma = pltpu.SemaphoreType.DMA
    share = state.shape[1] // count
    low = functools.partial(jax.ShapeDtypeStruct, dtype=BF16)
    near = (half, batch, width, kv_width)
    wide = pltpu.VMEM((batch, KVHEADS * HDIM, QHEADS * width), BF16)
    tall = pltpu.VMEM((batch, QHEADS * width, KVHEADS * HDIM), BF16)
    return pl.pallas_call(
        functools.partial(mix_backward_kernel, count),
        in_specs=[vmem] * 8,
        out_specs=[vmem] * 3,
        out_shape=[low(queries_t.shape), low(near), low(state.shape)],
        scratch_shapes=[
            wide,
            wide,
            tall,
            tall,
            pltpu.VMEM((batch, QHEADS, width), F32),
            pltpu.VMEM((batch, QHEADS, HDIM, width), F32),
            pltpu.VMEM(near, BF16),
            pltpu.VMEM(near, BF16),
            pltpu.VMEM(near, BF16),
            pltpu.VMEM(state.shape, BF16),
            pltpu.VMEM((count, batch, share, STATE), BF16),
            pltpu.VMEM((count, batch, share, STATE), BF16),
            pltpu.VMEM(state.shape, BF16),
            dma((2, half)),
            dma((4, count)),
        ],
        compiler_params=pltpu.CompilerParams(
            collective_id=3, has_side_effects=True, vmem_limit_bytes=56 * MIB
        ),
        cost_estimate=pl.CostEstimate(
            flops=batch * count * width * width * 8 * 2000,
            bytes_accessed=8 * MIB,
            transcendentals=0,
        ),
        name="mix_backward",
    )(starts, queries_t, table, attended_t, grad_t, logs, state, totals)


def local(
    inputs,
    cotangent,
    lengths,
    norm1_gain,
    in_weight,
    dt_weight,
    conv_weight,
    conv_bias,
    dt_bias,
    decay_rate,
    skip_gain,
    mamba_gain,
    out_weight,
    q_weight,
    kv_weight,
    o_weight,
    norm2_gain,
    gu_weight,
    down_weight,
):
    count, _, rows, features = inputs.shape
    here = lax.axis_index("ctx")
    ctx_count = lax.axis_size("ctx")
    tokens = count * rows
    first_pos = here * rows
    own_pos = first_pos + jnp.arange(rows, dtype=jnp.int32)
    starts = jax.vmap(lambda row: seq_starts(row, own_pos))(lengths[:, 0])
    rel_start = (starts - first_pos).reshape(tokens, 1)
    taps = conv_weight.shape[0]
    channels = conv_weight.shape[1]
    kv_width = kv_weight.shape[1]
    x_low = inputs.reshape(tokens, features)
    grad_top = cotangent.reshape(tokens, features)

    kv_near = gathered_near(kv_weight)
    early_shard = jnp.concatenate(
        [
            in_weight[:, DSSM:],
            jnp.pad(dt_weight, ((0, 0), (0, EARLY_TILE - dt_weight.shape[1]))),
        ],
        axis=1,
    )
    edge_x = passed_along(inputs[:, 0, rows - EDGE :], "ctx", 1).reshape(count * EDGE, features)

    def normalized(low):
        wide = low.astype(F32)
        return (wide * inv_rms(wide) * norm1_gain).astype(BF16)

    normed = normalized(x_low)
    edge_normed = normalized(edge_x)
    kv_rows = project(normed, kv_near, kv_width, BF16)
    high_bits = bits_of("ctx")[1:]
    keys = Gathering(kv_rows.reshape(count, rows, -1), high_bits[::-1])
    early = gathered_near(early_shard, kv_near[1])
    late_shard = jnp.concatenate([in_weight[:, :DSSM], q_weight], axis=1)
    late = gathered_near(late_shard, early[1])
    conv_rows, edge_rows, act, dt_rows = project_early(
        count,
        after(normed, kv_rows),
        edge_normed,
        rel_start,
        conv_weight,
        conv_bias,
        early,
    )
    outs_shard = jnp.concatenate([out_weight, o_weight], axis=0)
    outs = gathered_near(outs_shard, (late[1], dt_rows))
    gu_full = gathered_near(gu_weight, (late[1], dt_rows))
    down_full = gathered_near(down_weight, (late[1], dt_rows))

    def head_row(values):
        return jnp.pad(values, (0, 128 - MHEADS))[None]

    bias_row, rate_row = head_row(dt_bias), head_row(decay_rate)
    steps, decay, decay_t, to_end, total, fresh = ssd_state(
        count, act, dt_rows, bias_row, rate_row, rel_start
    )
    late_rows = project(normed, late, 1024)
    gate_z = late_rows[:, :DSSM]
    queries_t = late_rows[:, DSSM:].astype(BF16).T
    starts_row = jnp.broadcast_to(starts[:, None, :], (count, 8, rows))
    attended_t, logs, key_table, state_in, totals = mix_forward(
        ctx_count, starts_row, queries_t, keys.finish(), fresh, total
    )

    skip_row = jnp.repeat(skip_gain, MDIM)[None]
    scanned = ssd_forward(count, act, steps, decay, decay_t, rel_start, state_in, skip_row)
    gate_sig = jax.nn.sigmoid(gate_z)
    gated = scanned * gate_z * gate_sig
    scale_m = inv_rms(gated)
    mixed = (gated * scale_m * mamba_gain).astype(BF16)
    middle, normed_two = out_project(x_low, mixed, attended_t, norm2_gain, outs)

    layer_out, grad_middle, branch, grad_norm2, hidden, grad_pair = mlp_both(
        lax.axis_index("wsh").astype(jnp.int32)[None],
        normed_two,
        grad_top,
        middle,
        norm2_gain,
        gu_full,
        down_full,
    )
    gu_send = block_grads(normed_two, grad_pair, NEAR[2:])[0]
    down_send = block_grads(hidden, grad_top[None], NEAR[2:])[0]
    gu_sent = swapped(gu_send, "wsh", 1)
    down_sent = swapped(down_send, "wsh", 1)
    branch = after(branch, (gu_send, down_send))
    grad_mixed, grad_attended_t = out_unproject(branch, outs, DSSM, QHEADS * HDIM)
    grad_gated, grad_mamba = rms_pull(gated, scale_m, mamba_gain, grad_mixed)
    grad_gate_z = grad_gated * scanned * gate_sig * (1.0 + gate_z * (1.0 - gate_sig))
    grad_scanned = grad_gated * gate_z * gate_sig
    grad_state = state_grad(count, grad_scanned, act, decay, rel_start)
    gu_left, down_left = after((normed_two, hidden), grad_state)
    gu_kept, gu_other = block_grads(gu_left, grad_pair, NEAR[:2], gu_sent)
    down_kept, down_other = block_grads(down_left, grad_top[None], NEAR[:2], down_sent)
    gu_crossed = swapped(gu_other, "wsh", 2)
    down_crossed = swapped(down_other, "wsh", 2)

    grad_attended_t = after(grad_attended_t, (gu_other, down_other))
    dq_t, dkv_near, later = mix_backward(
        ctx_count,
        starts_row,
        queries_t,
        key_table,
        attended_t,
        grad_attended_t,
        logs,
        grad_state,
        totals,
    )
    key_grads = Scattering(dkv_near, high_bits)
    grad_late = jnp.concatenate([grad_gate_z.astype(BF16), dq_t.T], axis=1)
    grad_normed = unproject(jnp.zeros((tokens, features), F32), grad_late, late, 1024)

    def total_of(kept, crossed):
        return (kept.astype(F32) + crossed.astype(F32)).astype(BF16)

    parts = total_of(gu_kept, gu_crossed), total_of(down_kept, down_crossed)
    later = after(later, (key_grads.advance(grad_normed), parts))
    dx, db, dc, dt_grad, small_ssd = ssd_backward(
        count,
        act,
        steps,
        decay,
        decay_t,
        rel_start,
        state_in,
        skip_row,
        scanned,
        grad_scanned,
        later,
        to_end,
        total,
        dt_rows,
        bias_row,
        rate_row,
    )
    edge_back = passed_along(
        edge_grads(count, dx, db, dc, conv_rows, edge_rows, rel_start, conv_weight, conv_bias),
        "ctx",
        -1,
    )
    grad_early, conv_grads, input_grad, grad_norm1 = early_back(
        count,
        grad_normed,
        key_grads.finish().reshape(tokens, -1),
        dx,
        db,
        dc,
        conv_rows,
        edge_rows,
        edge_back,
        dt_grad,
        rel_start,
        conv_weight,
        conv_bias,
        x_low,
        norm1_gain,
        grad_middle,
        early,
        kv_near,
    )
    small_ssd = jnp.sum(small_ssd, axis=0)
    grad_dt_w = mat_left_t(normed, dt_grad[:, :MHEADS])

    gu_sum, down_sum = lax.psum(parts, "ctx")
    pieces = (
        grad_norm1[0],
        conv_grads[:taps],
        conv_grads[taps],
        small_ssd[0, :MHEADS],
        small_ssd[1, :MHEADS],
        small_ssd[2, :MHEADS],
        grad_mamba,
        grad_norm2[0],
        grad_dt_w,
    )
    packed = jnp.concatenate(
        [
            jnp.pad(piece.reshape(-1), (0, -piece.size % 1024)).reshape(-1, 128)
            for piece in pieces
        ],
        axis=0,
    )
    early_sum, late_sum, mix_sum, packed = reduce_grads(
        ctx_count,
        kv_width + channels,
        normed,
        mixed,
        attended_t,
        grad_early,
        grad_late,
        branch,
        packed,
    )
    in_sum, q_sum, kv_sum, out_sum, o_sum = finish(
        early_sum,
        late_sum,
        mix_sum,
        [w.shape for w in (in_weight, q_weight, kv_weight, out_weight, o_weight)],
        channels,
    )
    totals_w = [in_sum, out_sum, q_sum, kv_sum, o_sum, gu_sum.astype(F32), down_sum.astype(F32)]
    small = []
    place = 0
    for piece in pieces:
        lines = -(-piece.size // 1024) * 8
        small.append(packed[place : place + lines].reshape(-1)[: piece.size].reshape(piece.shape))
        place += lines
    dt_size = dt_weight.shape[0]
    dt_sum = lax.dynamic_slice_in_dim(small[8], lax.axis_index("wsh") * dt_size, dt_size, 0)
    shape = (count, 1, rows, features)
    return (
        layer_out.reshape(shape),
        input_grad.reshape(shape),
        small[0],
        totals_w[0],
        dt_sum,
        small[1],
        small[2],
        small[3],
        small[4],
        small[5],
        small[6],
        totals_w[1],
        totals_w[2],
        totals_w[3],
        totals_w[4],
        small[7],
        totals_w[5],
        totals_w[6],
    )


def solution(mesh):
    stream = P(None, "wsh", "ctx", None)
    shard = P("wsh", None)
    in_specs = (
        stream,
        stream,
        P(None, "wsh", None),
        P(),
        shard,
        shard,
        P(),
        P(),
        P(),
        P(),
        P(),
        P(),
        shard,
        shard,
        shard,
        shard,
        P(),
        shard,
        shard,
    )
    out_specs = (
        stream,
        stream,
        P(),
        shard,
        shard,
        P(),
        P(),
        P(),
        P(),
        P(),
        P(),
        shard,
        shard,
        shard,
        shard,
        P(),
        shard,
        shard,
    )
    return jax.shard_map(local, mesh=mesh, in_specs=in_specs, out_specs=out_specs, check_vma=False)
```

time: 666 us -> 608 us (0.913)
  Pallas kernels: 293 us -> 394 us
  waiting for transfers between devices: 124 us -> 52 us
  other arithmetic: 96.8 us -> 34.1 us
  starting transfers between devices: 57.1 us -> 30.6 us
  between operations: 2.87 us -> 15.6 us
  local copies, waits for them, and re-layouts: 80.9 us -> 68.6 us
    pallas_call x4 -> x14, Pallas kernels: 47.2 us -> 212 us  [the longest x1 63.9 us: mix_backward(): pl.pallas_call(functools.partial(mix_backward_kernel, count), in_specs=[v...]
    ppermute x29 -> x26, waiting for transfers between devices: 124 us -> 50.9 us  [swapped(): lax.ppermute(block, axis, [(i, i ^ bit) for i in range(lax.axis_size(axis...]
    pallas_call x1, Pallas kernels: 185 us -> 134 us  [reduce_grads(): pl.pallas_call(functools.partial(grads_kernel, count, split, early_units,...]
    ppermute x29 -> x26, starting transfers between devices: 52.2 us -> 25 us  [swapped(): lax.ppermute(block, axis, [(i, i ^ bit) for i in range(lax.axis_size(axis...]
    unnamed x258 -> x230, local copies, waits for them, and re-layouts: 21.3 us -> 48 us
    reduce_sum x8 -> x1, other arithmetic: 19.8 us -> 0.7 us  [local(): small_ssd = jnp.sum(small_ssd, axis=0)]
    mul x7 -> x0, other arithmetic: 16.9 us -> none  [the longest x1 11.1 us: local(): activated = conv_sum * conv_gate]
    convert_element_type x18 -> x9, other arithmetic: 33.7 us -> 19.8 us  [the longest x2 6.32 us: total_of(): return (kept.astype(F32) + crossed.astype(F32)).astype(BF16)]
  transfers between devices with their start and end apart: 31 -> 29, of which waited for: 10 -> 10; matrix products, arithmetic and copies ran while one was open for 16% -> 8% of each run, Pallas kernels for 6% -> 61%
where the time goes in v3:
time: 608 us; the launch traced here: 597 us
  Pallas kernels  394 us (65%)
  local copies, waits for them, and re-layouts  68.6 us (11%)
  waiting for transfers between devices  52 us (9%)
  other arithmetic  34.1 us (6%)
  starting transfers between devices  30.6 us (5%)
  between operations  15.6 us (3%)
    pallas_call x1, Pallas kernels, reduce_grads(): pl.pallas_call(functools.partial(grads_kernel, count, split, early_units,...  134 us
    pallas_call x1, Pallas kernels, mix_backward(): pl.pallas_call(functools.partial(mix_backward_kernel, count), in_specs=[v...  63.9 us
    pallas_call x1, Pallas kernels, mix_forward(): pl.pallas_call(functools.partial(mix_forward_kernel, count), in_specs=[vm...  51.5 us
    ppermute x26, waiting for transfers between devices, swapped(): lax.ppermute(block, axis, [(i, i ^ bit) for i in range(lax.axis_size(axis...  50.9 us
    unnamed x230, local copies, waits for them, and re-layouts  48 us
    pallas_call x1, Pallas kernels, ssd_backward(): pl.pallas_call(ssd_backward_kernel, grid=(count, NGROUP), in_specs=specs...  29.3 us
    pallas_call x1, Pallas kernels, mlp_both(): pl.pallas_call(mlp_kernel, grid_spec=pltpu.PrefetchScalarGridSpec(num_sca...  25.8 us
    ppermute x26, starting transfers between devices, swapped(): lax.ppermute(block, axis, [(i, i ^ bit) for i in range(lax.axis_size(axis...  25 us
  transfers between devices with their start and end apart: 29, of which 10 were waited for; matrix products, arithmetic and copies ran while one was open for 8% of the time, Pallas kernels for 61%

profile of v3, /device:TPU:0, one launch (start us, length us, event | category | flops | bytes accessed | tf_op | source)
XLA Modules:
  0.0 596.9 jit_solution(8879192643528437892)
XLA Ops:
  7.3 3.0 collective-permute-start
  16.4 4.1 collective-permute-start.3
  21.4 17.2 %collective-permute-done.4.refs_1_ = bf16[256,2048]{1,0:T(8,128)(2,1)} collective-permute-done((bf16[256,2048]{1,0:T(8,128)(2,1)}, bf16[256,2048]{1,0:T(8,128)(2,1)}, u32[]{:S(2)}, u32[]{:S(2)}) %collective-permute-start.4) | collective-permute-done | bytes 1048608 | tf_op jit(solution)/shard_map/ppermute | solution.py:1153
  48.4 9.9 %project_early.1 = (f32[512,1792]{1,0:T(8,128)S(1)}, f32[16,1792]{1,0:T(8,128)S(1)}, f32[512,1792]{1,0:T(8,128)S(1)}, f32[512,256]{1,0:T(8,128)S(1)}) custom-call(bf16[512,1024]{1,0:T(8,128)(2,1)S(1)} %multiply_convert_fusion.2.x_ref.one_ref, bf16[16,1024]{1,0:T(8,128)(2,1)S(1)} %fusion.6.edge_ref, s32[512,1]{1,0:T(8,128)S(1)} %bitcast.75, ...), custom_call_target="tpu_custom_call" | custom-call | flops 2147483648 | bytes 16777216 | tf_op jit(solution)/shard_map/project_early/pallas_call | solution.py:821
  61.9 2.9 collective-permute-done.7.refs_1_
  69.4 11.1 %collective-permute-done.10 = bf16[1,2,256,256]{3,2,1,0:T(8,128)(2,1)S(1)} collective-permute-done((bf16[1,2,256,256]{3,2,1,0:T(8,128)(2,1)S(1)}, bf16[1,2,256,256]{3,2,1,0:T(8,128)(2,1)S(1)}, u32[]{:S(2)}, u32[]{:S(2)}) %collective-permute-start.10) | collective-permute-done | bytes 262176 | tf_op jit(solution)/shard_map/ppermute | solution.py:1153
  84.3 2.7 pad_maximum_fusion.3.refs_0_
  87.0 7.4 %collective-permute-done.11 = bf16[2,2,256,256]{3,2,1,0:T(8,128)(2,1)} collective-permute-done((bf16[2,2,256,256]{3,2,1,0:T(8,128)(2,1)}, bf16[2,2,256,256]{3,2,1,0:T(8,128)(2,1)}, u32[]{:S(2)}, u32[]{:S(2)}) %collective-permute-start.11) | collective-permute-done | bytes 524320 | tf_op jit(solution)/shard_map/ppermute | solution.py:1153
  97.4 4.1 ssd_state.1
  107.2 4.1 project.3
  115.7 51.5 %mix_forward.1 = (bf16[512,512]{1,0:T(8,128)(2,1)}, f32[2,8,256]{2,1,0:T(8,128)}, bf16[8,2,256,256]{3,2,1,0:T(8,128)(2,1)}, bf16[2,1536,128]{2,1,0:T(8,128)(2,1)}, f32[8,2,8,128]{3,2,1,0:T(8,128)}) custom-call(s32[2,8,256]{2,1,0:T(8,128)} %broadcast_in_dim.33.start_ref, bf16[512,512]{1,0:T(8,128)(2,1)} %bitcast.96, ...), custom_call_target="tpu_custom_call" | custom-call | flops 8388608000 | bytes 4194304 | tf_op jit(solution)/shard_map/mix_forward/pallas_call | solution.py:1765
  168.4 8.3 %ssd_forward.1.y_ref = f32[512,1536]{1,0:T(8,128)S(1)} custom-call(f32[512,1792]{1,0:T(8,128)S(1)} %copy-done.2, f32[512,1792]{1,0:T(8,128)S(1)} %copy-done.2, f32[512,1792]{1,0:T(8,128)S(1)} %copy-done.2, f32[512,128]{1,0:T(8,128)S(1)} %copy-done.44, f32[512,128]{1,0:T(8,128)S(1)} %copy-done.32, f32[2,128,256]{2,1,0:T(8,128)S(1)} %copy-done.47, ...), custom_call_target="tpu_custom_call" | custom-call | flops 1258291200 | bytes 8388608 | tf_op jit(solution)/shard_map/ssd_forward/pallas_call | solution.py:389
  181.3 5.8 out_project.1
  191.3 25.8 %mlp_both.1 = (bf16[512,1024]{1,0:T(8,128)(2,1)}, f32[512,1024]{1,0:T(8,128)}, bf16[512,1024]{1,0:T(8,128)(2,1)}, f32[1,1024]{1,0:T(1,128)}, bf16[512,2048]{1,0:T(8,128)(2,1)}, /*index=5*/bf16[2,512,2048]{2,1,0:T(8,128)(2,1)}) custom-call(s32[1]{0:T(128)} %bitcast.place_ref, bf16[512,1024]{1,0:T(8,128)(2,1)} %copy-done.26, bf16[512,1024]{1,0:T(8,128)(2,1)} %bitcast.84, ...), custom_call_target="tpu_custom_call" | custom-call | flops 12884901888 | bytes 31457280 | tf_op jit(solution)/shard_map/mlp_both/pallas_call | solution.py:694
  220.5 6.1 %block_grads.4 = bf16[512,4096]{1,0:T(8,128)(2,1)} custom-call(bf16[512,1024]{1,0:T(8,128)(2,1)S(1)} %copy-done.27, bf16[2,512,2048]{2,1,0:T(8,128)(2,1)S(1)} %copy-done.10), custom_call_target="tpu_custom_call" | custom-call | flops 2147483648 | bytes 6291456 | tf_op jit(solution)/shard_map/block_grads/pallas_call | solution.py:1099
  226.7 2.6 block_grads.5
  229.7 5.4 out_unproject.1
  237.6 4.6 multiply_convert_fusion
  242.2 2.8 state_grad.1.state_ref
  245.1 2.9 block_grads.7
  249.5 8.0 %block_grads.6 = (bf16[256,4096]{1,0:T(8,128)(2,1)S(1)}, bf16[256,4096]{1,0:T(8,128)(2,1)}) custom-call(bf16[512,1024]{1,0:T(8,128)(2,1)S(1)} %copy-done.28, bf16[2,512,2048]{2,1,0:T(8,128)(2,1)S(1)} %copy-done.11, bf16[512,4096]{1,0:T(8,128)(2,1)} %collective-permute-done.21.refs_0_), custom_call_target="tpu_custom_call" | custom-call | flops 2147483648 | bytes 6291456 | tf_op jit(solution)/shard_map/block_grads/pallas_call | solution.py:1099
  260.3 63.9 %mix_backward.1 = (bf16[512,512]{1,0:T(8,128)(2,1)}, bf16[4,2,256,256]{3,2,1,0:T(8,128)(2,1)}, bf16[2,1536,128]{2,1,0:T(8,128)(2,1)}) custom-call(s32[2,8,256]{2,1,0:T(8,128)} %broadcast_in_dim.33.start_ref, bf16[512,512]{1,0:T(8,128)(2,1)} %bitcast.97, bf16[8,2,256,256]{3,2,1,0:T(8,128)(2,1)} %get-tuple-element.103.table_ref, ...), custom_call_target="tpu_custom_call" | custom-call | flops 16777216000 | bytes 8388608 | tf_op jit(solution)/shard_map/mix_backward/pallas_call | solution.py:1935
  332.1 5.2 unproject.1.base_ref
  340.6 5.7 collective-permute-start.24
  346.3 2.6 add_convert_fusion.1
  349.0 8.5 %collective-permute-done.24 = bf16[1,2,256,256]{3,2,1,0:T(8,128)(2,1)S(1)} collective-permute-done((bf16[1,2,256,256]{3,2,1,0:T(8,128)(2,1)S(1)}, bf16[1,2,256,256]{3,2,1,0:T(8,128)(2,1)S(1)}, u32[]{:S(2)}, u32[]{:S(2)}) %collective-permute-start.24) | collective-permute-done | bytes 262176 | tf_op jit(solution)/shard_map/ppermute | solution.py:1153
  358.2 3.7 add_convert_fusion
  373.1 29.3 %ssd_backward.1 = (f32[512,1536]{1,0:T(8,128)S(1)}, f32[512,128]{1,0:T(8,128)S(1)}, f32[512,128]{1,0:T(8,128)S(1)}, bf16[512,256]{1,0:T(8,128)(2,1)S(1)}, f32[2,8,128]{2,1,0:T(8,128)S(1)}) custom-call(f32[512,1792]{1,0:T(8,128)} %copy-done, f32[512,1792]{1,0:T(8,128)} %copy-done, f32[512,1792]{1,0:T(8,128)} %copy-done, f32[512,128]{1,0:T(8,128)S(1)} %copy-done.45, ...), custom_call_target="tpu_custom_call" | custom-call | flops 3145728000 | bytes 16777216 | tf_op jit(solution)/shard_map/ssd_backward/pallas_call | solution.py:429
  414.1 19.6 %early_back.1 = (bf16[512,2304]{1,0:T(8,128)(2,1)}, f32[8,1792]{1,0:T(8,128)S(1)}, bf16[512,1024]{1,0:T(8,128)(2,1)}, f32[1,1024]{1,0:T(1,128)S(1)}) custom-call(f32[512,1024]{1,0:T(8,128)} %copy-done.22, bf16[512,256]{1,0:T(8,128)(2,1)S(1)} %bitcast.90, f32[512,1536]{1,0:T(8,128)} %copy-done.14, f32[512,128]{1,0:T(8,128)S(1)} %copy-done.51, ...), custom_call_target="tpu_custom_call" | custom-call | flops 2147483648 | bytes 20971520 | tf_op jit(solution)/shard_map/early_back/pallas_call | solution.py:1016
  434.6 133.9 %reduce_grads.1 = (bf16[256,2048]{1,0:T(8,128)(2,1)}, bf16[256,2048]{1,0:T(8,128)(2,1)}, bf16[512,1024]{1,0:T(8,128)(2,1)}, f32[320,128]{1,0:T(8,128)}) custom-call(bf16[512,1024]{1,0:T(8,128)(2,1)} %copy-done.8, bf16[512,1536]{1,0:T(8,128)(2,1)} %copy-done.41, bf16[512,512]{1,0:T(8,128)(2,1)} %get-tuple-element.91.heads_ref.attended_ref, ...), custom_call_target="tpu_custom_call" | custom-call | flops 6499999744 | bytes 31457280 | tf_op jit(solution)/shard_map/reduce_grads/pallas_call | solution.py:1505
  578.3 3.0 finish.1
  583.9 4.2 convert_element_type.104
  (341 shorter events, 111.4 us)
Async XLA Ops:
  7.2 576.7 %all-reduce.11.cloned.1.call-start = ((), (), s32[]{:S(2)}) async-start(), calls=%async_computation | async-start | bytes 6291456 | tf_op jit(solution)/shard_map/psum | solution.py:2155
  7.3 6.7 %collective-permute-start = (bf16[256,256]{1,0:T(8,128)(2,1)}, bf16[256,256]{1,0:T(8,128)(2,1)S(1)}, u32[]{:S(2)}, u32[]{:S(2)}) collective-permute-start(bf16[256,256]{1,0:T(8,128)(2,1)} %refs_4_.2), channel_id=1, source_target_pairs={{0,2},{1,3},{2,0},{3,1},{4,6},{5,7},{6,4},{7,5},{8,10},{9,11},{10,... | collective-permute-start | bytes 393224 | tf_op jit(solution)/shard_map/ppermute | solution.py:1153
  14.0 24.7 %collective-permute-start.4 = (bf16[256,2048]{1,0:T(8,128)(2,1)}, bf16[256,2048]{1,0:T(8,128)(2,1)}, u32[]{:S(2)}, u32[]{:S(2)}) collective-permute-start(bf16[256,2048]{1,0:T(8,128)(2,1)} %fusion.1.refs_0_), channel_id=1, source_target_pairs={{0,2},{1,3},{2,0},{3,1},{4,6},{5,7},{6,4},{7,5},{8,10},{9,11},{10,... | collective-permute-start | bytes 3145736 | tf_op jit(solution)/shard_map/ppermute | solution.py:1153
  15.8 29.0 %collective-permute-start.1 = (bf16[256,256]{1,0:T(8,128)(2,1)S(1)}, bf16[256,256]{1,0:T(8,128)(2,1)}, u32[]{:S(2)}, u32[]{:S(2)}) collective-permute-start(bf16[256,256]{1,0:T(8,128)(2,1)S(1)} %copy-done.62), channel_id=1, source_target_pairs={{0,1},{1,0},{2,3},{3,2},{4,5},{5,4},{6,7},{7,6},{8,9},{9,8},{10,11... | collective-permute-start | bytes 393224 | tf_op jit(solution)/shard_map/ppermute | solution.py:1153
  16.4 25.8 %collective-permute-start.3 = (bf16[2,8,1024]{2,1,0:T(8,128)(2,1)}, bf16[2,8,1024]{2,1,0:T(8,128)(2,1)}, u32[]{:S(2)}, u32[]{:S(2)}) collective-permute-start(bf16[2,8,1024]{2,1,0:T(8,128)(2,1)} %slice_bitcast_fusion), channel_id=1, source_target_pairs={{0,4},{4,8},{8,12},{12,16},{16,20},{20,24},{24,28},{1,5},{5,9},{9,... | collective-permute-start | bytes 98312 | tf_op jit(solution)/shard_map/ppermute | solution.py:1149
  21.1 86.1 %copy-start.8 = (bf16[512,1024]{1,0:T(8,128)(2,1)}, bf16[512,1024]{1,0:T(8,128)(2,1)S(1)}, u32[]{:S(2)}) copy-start(bf16[512,1024]{1,0:T(8,128)(2,1)S(1)} %multiply_convert_fusion.2.x_ref.one_ref) | copy-start | bytes 3145732
  21.2 26.4 %collective-permute-start.5 = (bf16[256,2048]{1,0:T(8,128)(2,1)}, bf16[256,2048]{1,0:T(8,128)(2,1)}, u32[]{:S(2)}, u32[]{:S(2)}) collective-permute-start(bf16[256,2048]{1,0:T(8,128)(2,1)} %fusion.1.refs_0_), channel_id=1, source_target_pairs={{0,1},{1,0},{2,3},{3,2},{4,5},{5,4},{6,7},{7,6},{8,9},{9,8},{10,11... | collective-permute-start | bytes 3145736 | tf_op jit(solution)/shard_map/ppermute | solution.py:1153
  38.7 8.9 %collective-permute-start.6 = (bf16[256,2048]{1,0:T(8,128)(2,1)}, bf16[256,2048]{1,0:T(8,128)(2,1)}, u32[]{:S(2)}, u32[]{:S(2)}) collective-permute-start(bf16[256,2048]{1,0:T(8,128)(2,1)} %collective-permute-done.4.refs_1_), channel_id=1, source_target_pairs={{0,1},{1,0},{2,3},{3,2},{4,5},{5,4},{6,7},{7,6},{8,9},{9,8},{10,11... | collective-permute-start | bytes 3145736 | tf_op jit(solution)/shard_map/ppermute | solution.py:1153
  38.8 68.4 %copy-start.18 = (bf16[256,2048]{1,0:T(8,128)(2,1)}, bf16[256,2048]{1,0:T(8,128)(2,1)S(1)}, u32[]{:S(2)}) copy-start(bf16[256,2048]{1,0:T(8,128)(2,1)S(1)} %pad_maximum_fusion.1.refs_0_) | copy-start | bytes 3145732
  39.2 25.6 %collective-permute-start.7 = (bf16[256,2048]{1,0:T(8,128)(2,1)S(1)}, bf16[256,2048]{1,0:T(8,128)(2,1)S(1)}, u32[]{:S(2)}, u32[]{:S(2)}) collective-permute-start(bf16[256,2048]{1,0:T(8,128)(2,1)S(1)} %pad_maximum_fusion.1.refs_0_), channel_id=1, source_target_pairs={{0,2},{1,3},{2,0},{3,1},{4,6},{5,7},{6,4},{7,5},{8,10},{9,11},{10,... | collective-permute-start | bytes 3145736 | tf_op jit(solution)/shard_map/ppermute | solution.py:1153
  43.7 1.6 collective-permute-start.2
  64.8 49.6 %collective-permute-start.15 = (bf16[256,4096]{1,0:T(8,128)(2,1)}, bf16[256,4096]{1,0:T(8,128)(2,1)}, u32[]{:S(2)}, u32[]{:S(2)}) collective-permute-start(bf16[256,4096]{1,0:T(8,128)(2,1)} %refs_4_.1), channel_id=1, source_target_pairs={{0,2},{1,3},{2,0},{3,1},{4,6},{5,7},{6,4},{7,5},{8,10},{9,11},{10,... | collective-permute-start | bytes 6291464 | tf_op jit(solution)/shard_map/ppermute | solution.py:1153
  66.3 14.2 %collective-permute-start.10 = (bf16[1,2,256,256]{3,2,1,0:T(8,128)(2,1)S(1)}, bf16[1,2,256,256]{3,2,1,0:T(8,128)(2,1)S(1)}, u32[]{:S(2)}, u32[]{:S(2)}) collective-permute-start(bf16[1,2,256,256]{3,2,1,0:T(8,128)(2,1)S(1)} %bitcast.87), channel_id=1, source_target_pairs={{0,16},{4,20},{8,24},{12,28},{16,0},{20,4},{24,8},{28,12},{1,17},{... | collective-permute-start | bytes 786440 | tf_op jit(solution)/shard_map/ppermute | solution.py:1153
  68.8 36.5 %collective-permute-start.8 = (bf16[256,2048]{1,0:T(8,128)(2,1)S(1)}, bf16[256,2048]{1,0:T(8,128)(2,1)}, u32[]{:S(2)}, u32[]{:S(2)}) collective-permute-start(bf16[256,2048]{1,0:T(8,128)(2,1)S(1)} %pad_maximum_fusion.1.refs_0_), channel_id=1, source_target_pairs={{0,1},{1,0},{2,3},{3,2},{4,5},{5,4},{6,7},{7,6},{8,9},{9,8},{10,11... | collective-permute-start | bytes 3145736 | tf_op jit(solution)/shard_map/ppermute | solution.py:1153
  68.9 37.0 %collective-permute-start.9 = (bf16[256,2048]{1,0:T(8,128)(2,1)S(1)}, bf16[256,2048]{1,0:T(8,128)(2,1)}, u32[]{:S(2)}, u32[]{:S(2)}) collective-permute-start(bf16[256,2048]{1,0:T(8,128)(2,1)S(1)} %collective-permute-done.7.refs_1_), channel_id=1, source_target_pairs={{0,1},{1,0},{2,3},{3,2},{4,5},{5,4},{6,7},{7,6},{8,9},{9,8},{10,11... | collective-permute-start | bytes 3145736 | tf_op jit(solution)/shard_map/ppermute | solution.py:1153
  81.3 13.1 %collective-permute-start.11 = (bf16[2,2,256,256]{3,2,1,0:T(8,128)(2,1)}, bf16[2,2,256,256]{3,2,1,0:T(8,128)(2,1)}, u32[]{:S(2)}, u32[]{:S(2)}) collective-permute-start(bf16[2,2,256,256]{3,2,1,0:T(8,128)(2,1)} %pad_maximum_fusion.4), channel_id=1, source_target_pairs={{0,8},{4,12},{8,0},{12,4},{16,24},{20,28},{24,16},{28,20},{1,9},{5... | collective-permute-start | bytes 1572872 | tf_op jit(solution)/shard_map/ppermute | solution.py:1153
  96.7 80.0 %collective-permute-start.12 = (bf16[512,1024]{1,0:T(8,128)(2,1)}, bf16[512,1024]{1,0:T(8,128)(2,1)}, u32[]{:S(2)}, u32[]{:S(2)}) collective-permute-start(bf16[512,1024]{1,0:T(8,128)(2,1)} %pad_maximum_fusion.3.refs_0_), channel_id=1, source_target_pairs={{0,2},{1,3},{2,0},{3,1},{4,6},{5,7},{6,4},{7,5},{8,10},{9,11},{10,... | collective-permute-start | bytes 3145736 | tf_op jit(solution)/shard_map/ppermute | solution.py:1153
  97.4 79.4 %collective-permute-start.13 = (bf16[512,1024]{1,0:T(8,128)(2,1)}, bf16[512,1024]{1,0:T(8,128)(2,1)}, u32[]{:S(2)}, u32[]{:S(2)}) collective-permute-start(bf16[512,1024]{1,0:T(8,128)(2,1)} %pad_maximum_fusion.3.refs_0_), channel_id=1, source_target_pairs={{0,1},{1,0},{2,3},{3,2},{4,5},{5,4},{6,7},{7,6},{8,9},{9,8},{10,11... | collective-permute-start | bytes 3145736 | tf_op jit(solution)/shard_map/ppermute | solution.py:1153
  105.4 84.0 %collective-permute-start.16 = (bf16[256,4096]{1,0:T(8,128)(2,1)}, bf16[256,4096]{1,0:T(8,128)(2,1)}, u32[]{:S(2)}, u32[]{:S(2)}) collective-permute-start(bf16[256,4096]{1,0:T(8,128)(2,1)} %refs_4_.1), channel_id=1, source_target_pairs={{0,1},{1,0},{2,3},{3,2},{4,5},{5,4},{6,7},{7,6},{8,9},{9,8},{10,11... | collective-permute-start | bytes 6291464 | tf_op jit(solution)/shard_map/ppermute | solution.py:1153
  105.9 71.4 %collective-permute-start.18 = (bf16[512,1024]{1,0:T(8,128)(2,1)}, bf16[512,1024]{1,0:T(8,128)(2,1)}, u32[]{:S(2)}, u32[]{:S(2)}) collective-permute-start(bf16[512,1024]{1,0:T(8,128)(2,1)} %refs_8_), channel_id=1, source_target_pairs={{0,2},{1,3},{2,0},{3,1},{4,6},{5,7},{6,4},{7,5},{8,10},{9,11},{10,... | collective-permute-start | bytes 3145736 | tf_op jit(solution)/shard_map/ppermute | solution.py:1153
  114.4 76.9 %collective-permute-start.17 = (bf16[256,4096]{1,0:T(8,128)(2,1)}, bf16[256,4096]{1,0:T(8,128)(2,1)}, u32[]{:S(2)}, u32[]{:S(2)}) collective-permute-start(bf16[256,4096]{1,0:T(8,128)(2,1)} %collective-permute-done.15.refs_1_.refs_5_), channel_id=1, source_target_pairs={{0,1},{1,0},{2,3},{3,2},{4,5},{5,4},{6,7},{7,6},{8,9},{9,8},{10,11... | collective-permute-start | bytes 6291464 | tf_op jit(solution)/shard_map/ppermute | solution.py:1153
  115.7 51.5 %copy-start.47 = (f32[2,128,256]{2,1,0:T(8,128)S(1)}, f32[2,128,256]{2,1,0:T(8,128)}, u32[]{:S(2)}) copy-start(f32[2,128,256]{2,1,0:T(8,128)} %copy-done.46) | copy-start | bytes 786436
  176.7 12.7 %collective-permute-start.19 = (bf16[512,1024]{1,0:T(8,128)(2,1)}, bf16[512,1024]{1,0:T(8,128)(2,1)S(1)}, u32[]{:S(2)}, u32[]{:S(2)}) collective-permute-start(bf16[512,1024]{1,0:T(8,128)(2,1)} %refs_8_), channel_id=1, source_target_pairs={{0,1},{1,0},{2,3},{3,2},{4,5},{5,4},{6,7},{7,6},{8,9},{9,8},{10,11... | collective-permute-start | bytes 3145736 | tf_op jit(solution)/shard_map/ppermute | solution.py:1153
  176.8 4.3 collective-permute-start.14
  177.3 13.1 %collective-permute-start.20 = (bf16[512,1024]{1,0:T(8,128)(2,1)}, bf16[512,1024]{1,0:T(8,128)(2,1)S(1)}, u32[]{:S(2)}, u32[]{:S(2)}) collective-permute-start(bf16[512,1024]{1,0:T(8,128)(2,1)} %collective-permute-done.18.refs_9_), channel_id=1, source_target_pairs={{0,1},{1,0},{2,3},{3,2},{4,5},{5,4},{6,7},{7,6},{8,9},{9,8},{10,11... | collective-permute-start | bytes 3145736 | tf_op jit(solution)/shard_map/ppermute | solution.py:1153
  226.6 22.9 %collective-permute-start.21 = (bf16[512,4096]{1,0:T(8,128)(2,1)}, bf16[512,4096]{1,0:T(8,128)(2,1)}, u32[]{:S(2)}, u32[]{:S(2)}) collective-permute-start(bf16[512,4096]{1,0:T(8,128)(2,1)} %block_grads.4), channel_id=1, source_target_pairs={{0,1},{1,0},{2,3},{3,2},{4,5},{5,4},{6,7},{7,6},{8,9},{9,8},{10,11... | collective-permute-start | bytes 12582920 | tf_op jit(solution)/shard_map/ppermute | solution.py:1153
  229.3 15.7 %collective-permute-start.22 = (bf16[1024,1024]{1,0:T(8,128)(2,1)}, bf16[1024,1024]{1,0:T(8,128)(2,1)S(1)}, u32[]{:S(2)}, u32[]{:S(2)}) collective-permute-start(bf16[1024,1024]{1,0:T(8,128)(2,1)} %block_grads.5), channel_id=1, source_target_pairs={{0,1},{1,0},{2,3},{3,2},{4,5},{5,4},{6,7},{7,6},{8,9},{9,8},{10,11... | collective-permute-start | bytes 6291464 | tf_op jit(solution)/shard_map/ppermute | solution.py:1153
  249.0 97.4 %collective-permute-start.26 = (bf16[512,1024]{1,0:T(8,128)(2,1)}, bf16[512,1024]{1,0:T(8,128)(2,1)}, u32[]{:S(2)}, u32[]{:S(2)}) collective-permute-start(bf16[512,1024]{1,0:T(8,128)(2,1)} %get-tuple-element.108), channel_id=1, source_target_pairs={{0,2},{1,3},{2,0},{3,1},{4,6},{5,7},{6,4},{7,5},{8,10},{9,11},{10,... | collective-permute-start | bytes 3145736 | tf_op jit(solution)/shard_map/ppermute | solution.py:1153
  258.8 99.4 %collective-permute-start.25 = (bf16[256,4096]{1,0:T(8,128)(2,1)}, bf16[256,4096]{1,0:T(8,128)(2,1)}, u32[]{:S(2)}, u32[]{:S(2)}) collective-permute-start(bf16[256,4096]{1,0:T(8,128)(2,1)} %get-tuple-element.106), channel_id=1, source_target_pairs={{0,2},{1,3},{2,0},{3,1},{4,6},{5,7},{6,4},{7,5},{8,10},{9,11},{10,... | collective-permute-start | bytes 6291464 | tf_op jit(solution)/shard_map/ppermute | solution.py:1153
  326.1 13.4 %collective-permute-start.23 = (bf16[2,2,256,256]{3,2,1,0:T(8,128)(2,1)}, bf16[2,2,256,256]{3,2,1,0:T(8,128)(2,1)}, u32[]{:S(2)}, u32[]{:S(2)}) collective-permute-start(bf16[2,2,256,256]{3,2,1,0:T(8,128)(2,1)} %slice.98), channel_id=1, source_target_pairs={{0,8},{4,12},{8,0},{12,4},{16,24},{20,28},{24,16},{28,20},{1,9},{5... | collective-permute-start | bytes 1572872 | tf_op jit(solution)/shard_map/ppermute | solution.py:1153
  340.6 16.8 %collective-permute-start.24 = (bf16[1,2,256,256]{3,2,1,0:T(8,128)(2,1)S(1)}, bf16[1,2,256,256]{3,2,1,0:T(8,128)(2,1)S(1)}, u32[]{:S(2)}, u32[]{:S(2)}) collective-permute-start(bf16[1,2,256,256]{3,2,1,0:T(8,128)(2,1)S(1)} %slice.124), channel_id=1, source_target_pairs={{0,16},{4,20},{8,24},{12,28},{16,0},{20,4},{24,8},{28,12},{1,17},{... | collective-permute-start | bytes 786440 | tf_op jit(solution)/shard_map/ppermute | solution.py:1153
  404.4 6.8 %collective-permute-start.27 = (f32[16,1792]{1,0:T(8,128)S(1)}, f32[16,1792]{1,0:T(8,128)S(1)}, u32[]{:S(2)}, u32[]{:S(2)}) collective-permute-start(f32[16,1792]{1,0:T(8,128)S(1)} %edge_grads.1), channel_id=1, source_target_pairs={{4,0},{8,4},{12,8},{16,12},{20,16},{24,20},{28,24},{5,1},{9,5},{13... | collective-permute-start | bytes 344072 | tf_op jit(solution)/shard_map/ppermute | solution.py:1149
  (106 other events, 877.6 us)
Sparse Core Ops, SparseCore 0:
  362.0 142.8 all-reduce.10

commit v4 on v3

--- a/solution.py
+++ b/solution.py
@@ -24,6 +24,7 @@
 PRECISE = lax.Precision.HIGHEST
 MASKED_SCORE = -1e30
 MIB = 2**20
+KERNEL_VMEM = 60 * MIB
 F32 = jnp.float32
 BF16 = jnp.bfloat16
 
@@ -88,6 +89,12 @@
         precision=PRECISE,
         preferred_element_type=F32,
     )
+
+
+def sums_by(values, picks):
+    high = values.astype(BF16)
+    low = (values - high.astype(F32)).astype(BF16)
+    return mat(high, picks) + mat(low, picks)
 
 
 def lower_ones(rows):
@@ -179,7 +186,7 @@
             jax.ShapeDtypeStruct((count, DSSM, STATE), F32),
         ],
         scratch_shapes=[pltpu.VMEM((rows, DSSM), BF16)],
-        compiler_params=pltpu.CompilerParams(vmem_limit_bytes=40 * MIB),
+        compiler_params=pltpu.CompilerParams(vmem_limit_bytes=KERNEL_VMEM),
         cost_estimate=pl.CostEstimate(
             flops=1_000_000_000, bytes_accessed=8 * MIB, transcendentals=0
         ),
@@ -207,7 +214,7 @@
         out_specs=pl.BlockSpec((1, DSSM, STATE), lambda b: (b, 0, 0)),
         out_shape=jax.ShapeDtypeStruct((count, DSSM, STATE), F32),
         scratch_shapes=[pltpu.VMEM((rows, DSSM), BF16)],
-        compiler_params=pltpu.CompilerParams(vmem_limit_bytes=40 * MIB),
+        compiler_params=pltpu.CompilerParams(vmem_limit_bytes=KERNEL_VMEM),
         cost_estimate=pl.CostEstimate(
             flops=1_000_000_000, bytes_accessed=8 * MIB, transcendentals=0
         ),
@@ -342,15 +349,15 @@
     dc_ref[...] += dc
     db_ref[...] += db
     owner = lax.broadcasted_iota(jnp.int32, (GWIDTH, 128), 0) // MDIM + group * HGROUP
-    picks = (owner == lax.broadcasted_iota(jnp.int32, (GWIDTH, 128), 1)).astype(F32)
+    picks = (owner == lax.broadcasted_iota(jnp.int32, (GWIDTH, 128), 1)).astype(BF16)
     for place, source in enumerate((one_sum, two_sum, three_sum)):
-        head_sums[place] += exact(source[...], picks, 1, 0)
+        head_sums[place] += sums_by(source[...], picks)
     skips = jnp.broadcast_to(jnp.concatenate(skip_parts, axis=1), (8, GWIDTH))
-    row_sums[0] += exact(skips, picks, 1, 0)
+    row_sums[0] += sums_by(skips, picks)
     meets = exact(
         jnp.ones((8, STATE), F32), later_ref[0].astype(F32) * state_ref[0].astype(F32), 1, 1
     )
-    row_sums[1] += exact(meets, picks, 1, 0)
+    row_sums[1] += sums_by(meets, picks)
 
     @pl.when(group == pl.num_programs(1) - 1)
     def _():
@@ -392,7 +399,7 @@
         in_specs=specs,
         out_specs=specs[0],
         out_shape=jax.ShapeDtypeStruct((count * rows, DSSM), F32),
-        compiler_params=pltpu.CompilerParams(vmem_limit_bytes=40 * MIB),
+        compiler_params=pltpu.CompilerParams(vmem_limit_bytes=KERNEL_VMEM),
         cost_estimate=pl.CostEstimate(
             flops=count * MHEADS * rows * rows * 400, bytes_accessed=8 * MIB, transcendentals=0
         ),
@@ -441,7 +448,7 @@
         scratch_shapes=[pltpu.VMEM((rows, GWIDTH), F32)] * 3
         + [pltpu.VMEM((rows, GWIDTH), BF16)] * 2
         + [pltpu.VMEM((3, rows, 128), F32), pltpu.VMEM((2, 8, 128), F32)],
-        compiler_params=pltpu.CompilerParams(vmem_limit_bytes=40 * MIB),
+        compiler_params=pltpu.CompilerParams(vmem_limit_bytes=KERNEL_VMEM),
         cost_estimate=pl.CostEstimate(
             flops=count * MHEADS * rows * rows * 1000, bytes_accessed=16 * MIB, transcendentals=0
         ),
@@ -513,7 +520,7 @@
         + [pl.BlockSpec((size, tile), lambda i: (0, i))] * 4,
         out_specs=pl.BlockSpec((tokens, tile), lambda i: (0, i)),
         out_shape=jax.ShapeDtypeStruct((tokens, columns), kind),
-        compiler_params=pltpu.CompilerParams(vmem_limit_bytes=40 * MIB),
+        compiler_params=pltpu.CompilerParams(vmem_limit_bytes=KERNEL_VMEM),
         cost_estimate=pl.CostEstimate(
             flops=2 * tokens * depth * columns,
             bytes_accessed=2 * depth * columns + 4 * tokens * columns,
@@ -523,6 +530,14 @@
     )(x, *weights)
 
 
+def near_specs(own, tile, offset):
+    size = own.shape[0]
+    return [pl.BlockSpec((size, tile), lambda i: (0, i + offset))] + [
+        pl.BlockSpec((None, size, tile), lambda i, place=place: (place, 0, i + offset))
+        for place in range(3)
+    ]
+
+
 def unproject_kernel(base_ref, grad_ref, *refs):
     *weights, out_ref = refs
     size = weights[0].shape[0]
@@ -535,7 +550,7 @@
         out_ref[:, near_at(step, size)] += mat_right_t(grad_ref[...], weight[...])
 
 
-def unproject(base, grad, weights, tile):
+def unproject(base, grad, weights, tile, specs=None):
     tokens, columns = grad.shape
     size = weights[0].shape[0]
     whole = pl.BlockSpec((tokens, 4 * size), lambda i: (0, 0))
@@ -543,10 +558,10 @@
         unproject_kernel,
         grid=(columns // tile,),
         in_specs=[whole, pl.BlockSpec((tokens, tile), lambda i: (0, i))]
-        + [pl.BlockSpec((size, tile), lambda i: (0, i))] * 4,
+        + (specs or [pl.BlockSpec((size, tile), lambda i: (0, i))] * 4),
         out_specs=whole,
         out_shape=jax.ShapeDtypeStruct((tokens, 4 * size), F32),
-        compiler_params=pltpu.CompilerParams(vmem_limit_bytes=40 * MIB),
+        compiler_params=pltpu.CompilerParams(vmem_limit_bytes=KERNEL_VMEM),
         cost_estimate=pl.CostEstimate(
             flops=8 * tokens * size * columns,
             bytes_accessed=8 * size * columns + 2 * tokens * columns,
@@ -576,7 +591,7 @@
         in_specs=[vmem] * 8,
         out_specs=[vmem, vmem],
         out_shape=[jax.ShapeDtypeStruct(x.shape, F32), jax.ShapeDtypeStruct(x.shape, BF16)],
-        compiler_params=pltpu.CompilerParams(vmem_limit_bytes=40 * MIB),
+        compiler_params=pltpu.CompilerParams(vmem_limit_bytes=KERNEL_VMEM),
         cost_estimate=pl.CostEstimate(
             flops=2 * x.size * 2048, bytes_accessed=12 * MIB, transcendentals=0
         ),
@@ -606,7 +621,7 @@
             jax.ShapeDtypeStruct((tokens, mixed_width), F32),
             jax.ShapeDtypeStruct((heads_width, tokens), BF16),
         ],
-        compiler_params=pltpu.CompilerParams(vmem_limit_bytes=40 * MIB),
+        compiler_params=pltpu.CompilerParams(vmem_limit_bytes=KERNEL_VMEM),
         cost_estimate=pl.CostEstimate(
             flops=2 * branch.size * 2048, bytes_accessed=12 * MIB, transcendentals=0
         ),
@@ -722,7 +737,7 @@
             jax.ShapeDtypeStruct((tokens, width), BF16),
             jax.ShapeDtypeStruct((2, tokens, width), BF16),
         ],
-        compiler_params=pltpu.CompilerParams(vmem_limit_bytes=56 * MIB),
+        compiler_params=pltpu.CompilerParams(vmem_limit_bytes=KERNEL_VMEM),
         cost_estimate=pl.CostEstimate(
             flops=12 * tokens * features * width, bytes_accessed=30 * MIB, transcendentals=0
         ),
@@ -769,84 +784,10 @@
     return total, shifted
 
 
-def early_kernel(
-    count, x_ref, edge_ref, start_ref, weight_ref, bias_ref, *refs
-):
-    *blocks, conv_ref, edge_out, act_ref, dt_ref = refs
-    size = blocks[0].shape[0]
-    tile = pl.program_id(0)
-    last = pl.num_programs(0) - 1
-
-    def product(source):
-        total = None
-        for step, block in zip(NEAR, blocks):
-            part = mat(source[:, near_at(step, size)], block[...])
-            total = part if total is None else total + part
-        return total
-
-    value = product(x_ref)
-
-    @pl.when(tile == last)
-    def _():
-        dt_ref[...] = value
-
-    @pl.when(tile < last)
-    def _():
-        conv_ref[...] = value
-        edge = product(edge_ref)
-        edge_out[...] = edge
-        rows = value.shape[0] // count
-        for b in range(count):
-            span = slice(b * rows, (b + 1) * rows)
-            extended = conv_inputs(edge[b * EDGE : (b + 1) * EDGE], value[span])
-            total, _ = conv_sums(extended, weight_ref[...], bias_ref[...], start_ref[span])
-            act_ref[span] = total * sigmoid(total)
-
-
-def conv_tile_spec(rows, count, begin=0):
-    return pl.BlockSpec((rows, EARLY_TILE), lambda i: (0, jnp.clip(i - begin, 0, count - 1)))
-
-
-def project_early(count, x, edge_x, rel_start, conv_weight, conv_bias, blocks):
-    tokens, depth = x.shape
-    size, columns = blocks[0].shape
-    channels = conv_weight.shape[1]
-    tiles = columns // EARLY_TILE
-    conv_tiles = channels // EARLY_TILE
-
-    def whole(array):
-        return pl.BlockSpec(array.shape, lambda i: (0, 0))
-
-    tile_shape = pl.BlockSpec((tokens, EARLY_TILE), lambda i: (0, 0))
-    return pl.pallas_call(
-        functools.partial(early_kernel, count),
-        grid=(tiles,),
-        in_specs=[
-            whole(x),
-            whole(edge_x),
-            whole(rel_start),
-            conv_tile_spec(conv_weight.shape[0], conv_tiles),
-            conv_tile_spec(1, conv_tiles),
-        ]
-        + [pl.BlockSpec((size, EARLY_TILE), lambda i: (0, i))] * 4,
-        out_specs=[
-            conv_tile_spec(tokens, conv_tiles),
-            conv_tile_spec(edge_x.shape[0], conv_tiles),
-            conv_tile_spec(tokens, conv_tiles),
-            tile_shape,
-        ],
-        out_shape=[
-            jax.ShapeDtypeStruct((tokens, channels), F32),
-            jax.ShapeDtypeStruct((edge_x.shape[0], channels), F32),
-            jax.ShapeDtypeStruct((tokens, channels), F32),
-            jax.ShapeDtypeStruct((tokens, EARLY_TILE), F32),
-        ],
-        compiler_params=pltpu.CompilerParams(vmem_limit_bytes=40 * MIB),
-        cost_estimate=pl.CostEstimate(
-            flops=2 * tokens * depth * columns, bytes_accessed=16 * MIB, transcendentals=0
-        ),
-        name="project_early",
-    )(x, edge_x, rel_start, conv_weight, conv_bias[None], *blocks)
+def conv_tile_spec(rows, first, last, begin=0):
+    return pl.BlockSpec(
+        (rows, EARLY_TILE), lambda i: (0, jnp.clip(i - begin + first, first, last))
+    )
 
 
 def conv_back(extended, weights, bias, rel_start, grad_act):
@@ -895,7 +836,7 @@
         ],
         out_specs=pl.BlockSpec((EDGE, channels), lambda b: (b, 0)),
         out_shape=jax.ShapeDtypeStruct((count * EDGE, channels), F32),
-        compiler_params=pltpu.CompilerParams(vmem_limit_bytes=16 * MIB),
+        compiler_params=pltpu.CompilerParams(vmem_limit_bytes=KERNEL_VMEM),
         cost_estimate=pl.CostEstimate(flops=MIB, bytes_accessed=MIB, transcendentals=0),
         name="edge_grads",
     )(dx, db, dc, conv_rows, edge_rows, rel_start, conv_weight, conv_bias[None])
@@ -921,7 +862,6 @@
     *refs,
 ):
     *blocks, grad_ref, conv_grad_ref, input_ref, gain_grad_ref, total = refs
-    blocks, kv_blocks = blocks[:4], blocks[4:]
     size = blocks[0].shape[0]
     tile = pl.program_id(0)
     last = pl.num_programs(0) - 1
@@ -931,8 +871,6 @@
     def _():
         total[...] = base_ref[...]
         grad_ref[...] = kv_ref[...]
-        for step, block in zip(NEAR, kv_blocks):
-            total[:, near_at(step, size)] += mat_right_t(kv_ref[...], block[...])
 
     @pl.when(tile == last)
     def _():
@@ -971,10 +909,8 @@
             (conv_grad_ref.shape[0] - taps - 1, grad_act.shape[1]), F32
         )
 
-    @pl.when(tile > 0)
-    def _():
-        for step, block in zip(NEAR, blocks):
-            total[:, near_at(step, size)] += mat_right_t(grad_ref[...], block[...])
+    for step, block in zip(NEAR, blocks):
+        total[:, near_at(step, size)] += mat_right_t(grad_ref[...], block[...])
 
     @pl.when(tile == last)
     def _():
@@ -1001,13 +937,12 @@
     x,
     gain,
     grad_middle,
-    blocks,
-    kv_blocks,
+    own,
+    others,
 ):
     tokens, depth = base.shape
-    size, columns = blocks[0].shape
     channels = conv_weight.shape[1]
-    tiles = columns // EARLY_TILE + 1
+    tiles = conv_weight.shape[1] // EARLY_TILE + 2
     conv_tiles = channels // EARLY_TILE
 
     def whole(array):
@@ -1019,38 +954,37 @@
         in_specs=[
             whole(base),
             whole(grad_kv),
-            conv_tile_spec(tokens, conv_tiles - 1, 1),
+            conv_tile_spec(tokens, 0, conv_tiles - 2, 1),
             whole(db),
             whole(dc),
-            conv_tile_spec(tokens, conv_tiles, 1),
-            conv_tile_spec(edge_rows.shape[0], conv_tiles, 1),
-            conv_tile_spec(edge_rows.shape[0], conv_tiles, 1),
+            conv_tile_spec(tokens, 0, conv_tiles - 1, 1),
+            conv_tile_spec(edge_rows.shape[0], 0, conv_tiles - 1, 1),
+            conv_tile_spec(edge_rows.shape[0], 0, conv_tiles - 1, 1),
             whole(dt_grad),
             whole(rel_start),
-            conv_tile_spec(conv_weight.shape[0], conv_tiles, 1),
-            conv_tile_spec(1, conv_tiles, 1),
+            conv_tile_spec(conv_weight.shape[0], 0, conv_tiles - 1, 1),
+            conv_tile_spec(1, 0, conv_tiles - 1, 1),
             whole(x),
             pl.BlockSpec((1, depth), lambda i: (0, 0)),
             whole(grad_middle),
         ]
-        + [pl.BlockSpec((size, EARLY_TILE), lambda i: (0, jnp.maximum(i - 1, 0)))] * 4
-        + [pl.BlockSpec((size, EARLY_TILE), lambda i: (0, 0))] * 4,
+        + near_specs(own, EARLY_TILE, DSSM // EARLY_TILE),
         out_specs=[
             pl.BlockSpec((tokens, EARLY_TILE), lambda i: (0, i)),
-            conv_tile_spec(8, conv_tiles, 1),
+            conv_tile_spec(8, 0, conv_tiles - 1, 1),
             whole(x),
             pl.BlockSpec((1, depth), lambda i: (0, 0)),
         ],
         out_shape=[
-            jax.ShapeDtypeStruct((tokens, columns + EARLY_TILE), BF16),
+            jax.ShapeDtypeStruct((tokens, tiles * EARLY_TILE), BF16),
             jax.ShapeDtypeStruct((8, channels), F32),
             jax.ShapeDtypeStruct(x.shape, BF16),
             jax.ShapeDtypeStruct((1, depth), F32),
         ],
         scratch_shapes=[pltpu.VMEM((tokens, depth), F32)],
-        compiler_params=pltpu.CompilerParams(vmem_limit_bytes=48 * MIB),
+        compiler_params=pltpu.CompilerParams(vmem_limit_bytes=KERNEL_VMEM),
         cost_estimate=pl.CostEstimate(
-            flops=2 * tokens * depth * columns, bytes_accessed=20 * MIB, transcendentals=0
+            flops=2 * tokens * depth * tiles * EARLY_TILE, bytes_accessed=20 * MIB, transcendentals=0
         ),
         name="early_back",
     )(
@@ -1069,8 +1003,10 @@
         x,
         gain[None],
         grad_middle,
-        *blocks,
-        *kv_blocks,
+        own,
+        others,
+        others,
+        others,
     )
 
 
@@ -1108,7 +1044,7 @@
         out_shape=[jax.ShapeDtypeStruct((2 * size, columns), BF16)]
         if came is None
         else [jax.ShapeDtypeStruct((size, columns), BF16)] * 2,
-        compiler_params=pltpu.CompilerParams(vmem_limit_bytes=32 * MIB),
+        compiler_params=pltpu.CompilerParams(vmem_limit_bytes=KERNEL_VMEM),
         cost_estimate=pl.CostEstimate(
             flops=4 * tokens * size * columns, bytes_accessed=6 * MIB, transcendentals=0
         ),
@@ -1117,30 +1053,30 @@
 
 
 def finish_kernel(
-    conv_width, early_ref, late_ref, mix_ref, in_ref, q_ref, kv_ref, out_ref, o_ref
+    early_ref, gate_ref, mix_ref, q_low_ref, in_ref, q_ref, kv_ref, out_ref, o_ref
 ):
     kv_width = kv_ref.shape[1]
-    gate = in_ref.shape[1] - conv_width
-    in_ref[:, :gate] = late_ref[:, :gate].astype(F32)
+    gate = gate_ref.shape[1]
+    in_ref[:, :gate] = gate_ref[...].astype(F32)
     in_ref[:, gate:] = early_ref[:, kv_width:].astype(F32)
-    q_ref[...] = late_ref[:, gate:].astype(F32)
+    q_ref[...] = q_low_ref[...].astype(F32)
     kv_ref[...] = early_ref[:, :kv_width].astype(F32)
     split = out_ref.shape[0]
     out_ref[...] = mix_ref[:split].astype(F32)
     o_ref[...] = mix_ref[split:].astype(F32)
 
 
-def finish(early, late, mix, shapes, conv_width):
+def finish(early, gate, mix, q, shapes):
     vmem = pl.BlockSpec(memory_space=pltpu.VMEM)
     return pl.pallas_call(
-        functools.partial(finish_kernel, conv_width),
-        in_specs=[vmem] * 3,
+        finish_kernel,
+        in_specs=[vmem] * 4,
         out_specs=[vmem] * 5,
         out_shape=[jax.ShapeDtypeStruct(shape, F32) for shape in shapes],
-        compiler_params=pltpu.CompilerParams(vmem_limit_bytes=32 * MIB),
+        compiler_params=pltpu.CompilerParams(vmem_limit_bytes=KERNEL_VMEM),
         cost_estimate=pl.CostEstimate(flops=MIB, bytes_accessed=10 * MIB, transcendentals=0),
         name="finish",
-    )(early, late, mix)
+    )(early, gate, mix, q)
 
 
 def passed_along(block, axis, distance):
@@ -1168,31 +1104,6 @@
     if held is not None:
         across = after(across, held)
     return [shard, across, swapped(shard, "wsh", 1), swapped(across, "wsh", 1)]
-
-
-class Gathering:
-    def __init__(self, rows, bits):
-        self.table = rows[None]
-        self.bits = list(bits)
-        self.start()
-
-    def start(self):
-        if self.bits:
-            self.came = swapped(self.table, "ctx", self.bits.pop(0))
-        else:
-            self.came = None
-
-    def advance(self, held=None):
-        if self.came is not None:
-            came = self.came if held is None else after(self.came, held)
-            self.table = jnp.concatenate([self.table, came], axis=0)
-            self.start()
-        return self.table
-
-    def finish(self):
-        while self.came is not None:
-            self.advance()
-        return self.table
 
 
 class Scattering:
@@ -1249,16 +1160,19 @@
     count,
     split,
     early_units,
-    late_units,
+    gate_units,
+    q_units,
     one_ref,
     mix_ref,
     heads_ref,
     early_ref,
-    late_ref,
+    gate_ref,
+    q_ref,
     branch_ref,
     small_ref,
     early_out,
-    late_out,
+    gate_out,
+    q_out,
     mix_out,
     small_out,
     core_out,
@@ -1335,10 +1249,10 @@
 
     limits = []
     first_unit = 0
-    for size in (early_units, late_units, 4):
+    for size in (early_units, gate_units, q_units, 4):
         limits.append((first_unit, first_unit + size))
         first_unit += size
-    outs = (early_out, late_out, mix_out)
+    outs = (early_out, gate_out, q_out, mix_out)
 
     def by_part(u, action):
         for part, (low, high) in enumerate(limits):
@@ -1346,7 +1260,7 @@
 
     def each_out(u, act):
         def one(part, v):
-            tall = part == 2
+            tall = part == 3
             for i in range(split):
                 row = (v // 2) * TILE_ROWS if tall else 0
                 column = ((v % 2) if tall else v) * TILE_COLS + i * width
@@ -1373,9 +1287,9 @@
 
         def one(part, v):
             for place, step in enumerate(steps):
-                if part < 2:
+                if part < 3:
                     left = one_ref[:, near_at(step, TILE_ROWS)]
-                    value = mat_left_t(left, (early_ref, late_ref)[part][:, columns_at(v)])
+                    value = mat_left_t(left, (early_ref, gate_ref, q_ref)[part][:, columns_at(v)])
                 else:
                     right = branch_ref[:, columns_at(v % 2)]
                     other = lax.axis_index("wsh") ^ step
@@ -1490,25 +1404,27 @@
 
 
 def reduce_grads(
-    count, early_width, one, mixed, heads_t, early, late, branch, small
+    count, early_width, one, mixed, heads_t, early, gate, q, branch, small
 ):
     bits = ctx_bits(count)
     hops = len(bits) + 2
     split = max(1, 16 * count // TILE_ROWS)
     early_units = early_width // TILE_COLS
-    late_units = late.shape[1] // TILE_COLS
-    units = early_units + late_units + 4
+    gate_units = gate.shape[1] // TILE_COLS
+    q_units = q.shape[1] // TILE_COLS
+    units = early_units + gate_units + q_units + 4
     rows, width = TILE_ROWS * split, TILE_COLS // split
     dma = pltpu.SemaphoreType.DMA
     vmem = pl.BlockSpec(memory_space=pltpu.VMEM)
     hbm = pl.BlockSpec(memory_space=pl.ANY)
     return pl.pallas_call(
-        functools.partial(grads_kernel, count, split, early_units, late_units),
-        in_specs=[vmem] * 7,
-        out_specs=[hbm] * 3 + [vmem],
+        functools.partial(grads_kernel, count, split, early_units, gate_units, q_units),
+        in_specs=[vmem] * 8,
+        out_specs=[hbm] * 4 + [vmem],
         out_shape=[
             jax.ShapeDtypeStruct((TILE_ROWS, early_units * TILE_COLS), BF16),
-            jax.ShapeDtypeStruct((TILE_ROWS, late_units * TILE_COLS), BF16),
+            jax.ShapeDtypeStruct((TILE_ROWS, gate_units * TILE_COLS), BF16),
+            jax.ShapeDtypeStruct((TILE_ROWS, q_units * TILE_COLS), BF16),
             jax.ShapeDtypeStruct((2 * TILE_ROWS, 2 * TILE_COLS), BF16),
             jax.ShapeDtypeStruct(small.shape, F32),
         ],
@@ -1527,13 +1443,13 @@
             dma((units, split)),
         ],
         compiler_params=pltpu.CompilerParams(
-            collective_id=1, has_side_effects=True, vmem_limit_bytes=62 * MIB
+            collective_id=1, has_side_effects=True, vmem_limit_bytes=KERNEL_VMEM
         ),
         cost_estimate=pl.CostEstimate(
             flops=6_500_000_000, bytes_accessed=30 * MIB, transcendentals=0
         ),
         name="reduce_grads",
-    )(one, mixed, heads_t, early, late, branch, small)
+    )(one, mixed, heads_t, early, gate, q, branch, small)
 
 
 def exchange_barrier(devices):
@@ -1547,84 +1463,146 @@
 
 def row_factors(totals, owner):
     rows = owner.shape[0]
-    picks = (owner == lax.broadcasted_iota(jnp.int32, (rows, 128), 1)).astype(F32)
-    return exact(picks, totals, 1, 1)[:, :1]
+    picks = (owner == lax.broadcasted_iota(jnp.int32, (rows, 128), 1)).astype(BF16)
+    high = totals.astype(BF16)
+    low = (totals - high.astype(F32)).astype(BF16)
+    return mat_right_t(picks, high) + mat_right_t(picks, low)
+
+
+STATE_GROUP = 4
 
 
 class StateExchange:
-    def __init__(self, count, forward, state_ref, totals, result, sent, came, back, sems):
-        self.count, self.forward = count, forward
+    def __init__(self, count, forward, state_ref, totals, result, scratch):
+        self.group = min(STATE_GROUP, count)
+        self.groups = count // self.group
+        self.forward = forward
         self.state_ref, self.totals, self.result = state_ref, totals, result
-        self.sent, self.came, self.back, self.sems = sent, came, back, sems
-        self.here = lax.axis_index("ctx")
-        self.share = state_ref.shape[1] // count
+        (
+            self.sent,
+            self.came,
+            self.before,
+            self.back,
+            self.whole,
+            self.cross,
+            self.sems,
+            self.cross_sems,
+        ) = scratch
+        self.place = lax.axis_index("ctx") % self.group
+        self.at = lax.axis_index("ctx") // self.group
+        self.share = state_ref.shape[1] // self.group
+
+    @staticmethod
+    def scratch(count, state):
+        group = min(STATE_GROUP, count)
+        groups = count // group
+        part = (state.shape[0], state.shape[1] // group, STATE)
+        return [
+            pltpu.VMEM(state.shape, BF16),
+            pltpu.VMEM((group,) + part, BF16),
+            pltpu.VMEM((group,) + part, F32),
+            pltpu.VMEM((group,) + part, BF16),
+            pltpu.VMEM(part, BF16),
+            pltpu.VMEM((groups,) + part, BF16),
+            pltpu.SemaphoreType.DMA((4, group)),
+            pltpu.SemaphoreType.DMA((2, groups)),
+        ]
 
     def rows_of(self, place):
         return pl.ds(pl.multiple_of(place * self.share, 16), self.share)
 
-    def out_copy(self, k):
+    def deal(self, k, slot):
         return remote(
-            self.sent.at[:, self.rows_of(self.here ^ k)],
-            self.came.at[self.here],
+            self.sent.at[:, self.rows_of(self.place ^ k)],
+            self.came.at[slot],
             self.sems.at[0, k],
             self.sems.at[1, k],
             partner_ctx(k),
         )
 
-    def in_copy(self, k):
+    def give(self, m, slot):
         return remote(
-            self.sent.at[:, self.rows_of(self.here ^ k)],
-            self.came.at[self.here ^ k],
-            self.sems.at[0, k],
-            self.sems.at[1, k],
-            partner_ctx(k),
-        )
-
-    def back_copy(self, k):
+            self.whole,
+            self.cross.at[slot],
+            self.cross_sems.at[0, m],
+            self.cross_sems.at[1, m],
+            partner_ctx(m * self.group),
+        )
+
+    def give_back(self, k, slot):
         return remote(
-            self.back.at[self.here ^ k],
-            self.result.at[:, self.rows_of(self.here)],
+            self.back.at[self.place ^ k],
+            self.result.at[:, self.rows_of(slot)],
             self.sems.at[2, k],
             self.sems.at[3, k],
             partner_ctx(k),
         )
 
-    def back_in(self, k):
-        return remote(
-            self.back.at[self.here ^ k],
-            self.result.at[:, self.rows_of(self.here ^ k)],
-            self.sems.at[2, k],
-            self.sems.at[3, k],
-            partner_ctx(k),
-        )
+    def order(self, count):
+        return range(count) if self.forward else range(count - 1, -1, -1)
+
+    def factors(self, blocks):
+        part = self.totals[blocks]
+        batch = part.shape[1]
+        place = lax.broadcasted_iota(jnp.int32, (self.share, 128), 0) + self.place * self.share
+        columns = row_factors(part.reshape(-1, 128), place // MDIM)
+
+        def column(block, b):
+            at = (block * batch + b) * 8
+            return columns[:, at : at + 1]
+
+        return column
+
+    def own_blocks(self):
+        return pl.ds(self.at * self.group, self.group)
 
     def begin(self):
         self.sent[...] = self.state_ref[...].astype(BF16)
-        for k in range(1, self.count):
-            self.out_copy(k).start()
-        self.came[self.here] = self.state_ref[:, self.rows_of(self.here), :].astype(BF16)
+        for k in range(1, self.group):
+            self.deal(k, self.place).start()
+        self.came[self.place] = self.state_ref[:, self.rows_of(self.place), :].astype(BF16)
+        self.cross[self.at] = jnp.zeros(self.whole.shape, BF16)
 
     def middle(self):
-        for k in range(1, self.count):
-            self.out_copy(k).wait_send()
-            self.in_copy(k).wait_recv()
-        place = lax.broadcasted_iota(jnp.int32, (self.share, 128), 0) + self.here * self.share
-        owner = place // MDIM
-        order = range(self.count) if self.forward else range(self.count - 1, -1, -1)
-        for b in range(self.state_ref.shape[0]):
+        for k in range(1, self.group):
+            self.deal(k, self.place).wait_send()
+            self.deal(k, self.place ^ k).wait_recv()
+        factor_of = self.factors(self.own_blocks())
+        for b in range(self.whole.shape[0]):
             total = jnp.zeros((self.share, STATE), F32)
-            for block in order:
-                self.back[block, b] = total.astype(BF16)
-                factor = row_factors(self.totals[block, b], owner)
-                total = factor * total + self.came[block, b].astype(F32)
-        for k in range(1, self.count):
-            self.back_copy(k).start()
-        self.result[:, self.rows_of(self.here), :] = self.back[self.here]
+            for j in self.order(self.group):
+                self.before[j, b] = total
+                total = factor_of(j, b) * total + self.came[j, b].astype(F32)
+            self.whole[b] = total.astype(BF16)
+        for m in range(1, self.groups):
+            self.give(m, self.at).start()
+
+    def carry(self):
+        for m in range(1, self.groups):
+            self.give(m, self.at).wait_send()
+            self.give(m, self.at ^ m).wait_recv()
+        factor_of = self.factors(self.own_blocks())
+        any_factor = self.factors(slice(None))
+        for b in range(self.whole.shape[0]):
+            reach = jnp.zeros((self.share, STATE), F32)
+            for g in self.order(self.groups):
+                decay = None
+                for j in range(self.group):
+                    one = any_factor(g * self.group + j, b)
+                    decay = one if decay is None else decay * one
+                earlier = (g < self.at) if self.forward else (g > self.at)
+                reach = jnp.where(earlier, decay * reach + self.cross[g, b].astype(F32), reach)
+            for j in self.order(self.group):
+                self.back[j, b] = (self.before[j, b] + reach).astype(BF16)
+                reach = reach * factor_of(j, b)
+        for k in range(1, self.group):
+            self.give_back(k, self.place).start()
+        self.result[:, self.rows_of(self.place), :] = self.back[self.place]
 
     def end(self):
-        for k in range(1, self.count):
-            self.back_copy(k).wait_send()
-            self.back_in(k).wait_recv()
+        for k in range(1, self.group):
+            self.give_back(k, self.place).wait_send()
+            self.give_back(k, self.place ^ k).wait_recv()
 
 
 def mix_forward_kernel(
@@ -1645,13 +1623,10 @@
     acc,
     far,
     totals,
-    sent,
-    came,
-    back,
     result,
     total_sems,
     table_sems,
-    state_sems,
+    *state_scratch,
 ):
     here = lax.axis_index("ctx")
     batch = near_ref.shape[1]
@@ -1676,9 +1651,7 @@
 
     for k in range(1, count):
         total_copy(k, here).start()
-    states = StateExchange(
-        count, True, state_ref, totals, result, sent, came, back, state_sems
-    )
+    states = StateExchange(count, True, state_ref, totals, result, state_scratch)
     states.begin()
     for i in range(half):
         table_copy(i).start()
@@ -1721,7 +1694,7 @@
     def step_of(i):
         return sum(((i // (1 << p)) % 2) * (1 << (high - p)) for p in range(high))
 
-    def pair(source, low):
+    def pair(source, low, begin=0, end=half):
         def one(i, carry):
             block = here ^ (step_of(i) + low)
 
@@ -1732,13 +1705,15 @@
 
             return carry
 
-        lax.fori_loop(0, half, one, 0)
-
-    pair(near_ref, 0)
+        lax.fori_loop(begin, end, one, 0)
+
+    pair(near_ref, 0, 0, half // 2)
     for k in range(1, count):
         total_copy(k, here).wait_send()
         total_copy(k, here ^ k).wait_recv()
     states.middle()
+    pair(near_ref, 0, half // 2)
+    states.carry()
     for i in range(half):
         table_copy(i).wait()
     pair(far, 1)
@@ -1759,7 +1734,6 @@
     half, batch, width, kv_width = near.shape
     vmem = pl.BlockSpec(memory_space=pltpu.VMEM)
     dma = pltpu.SemaphoreType.DMA
-    share = state.shape[1] // count
     low = functools.partial(jax.ShapeDtypeStruct, dtype=BF16)
     wide = functools.partial(jax.ShapeDtypeStruct, dtype=F32)
     return pl.pallas_call(
@@ -1781,15 +1755,12 @@
             pltpu.VMEM(near.shape, BF16),
             pltpu.VMEM((count,) + total.shape, F32),
             pltpu.VMEM(state.shape, BF16),
-            pltpu.VMEM((count, batch, share, STATE), BF16),
-            pltpu.VMEM((count, batch, share, STATE), BF16),
-            pltpu.VMEM(state.shape, BF16),
             dma((2, count)),
             dma((2, half)),
-            dma((4, count)),
-        ],
+        ]
+        + StateExchange.scratch(count, state),
         compiler_params=pltpu.CompilerParams(
-            collective_id=2, has_side_effects=True, vmem_limit_bytes=56 * MIB
+            collective_id=2, has_side_effects=True, vmem_limit_bytes=KERNEL_VMEM
         ),
         cost_estimate=pl.CostEstimate(
             flops=batch * count * width * width * 8 * 1000,
@@ -1822,12 +1793,9 @@
     mine,
     theirs,
     far,
-    sent,
-    came,
-    back,
     result,
     table_sems,
-    state_sems,
+    *state_scratch,
 ):
     here = lax.axis_index("ctx")
     batch = table_ref.shape[1]
@@ -1835,9 +1803,7 @@
     half = count // 2
     kv_width = KVHEADS * HDIM
     exchange_barrier([partner_ctx(k) for k in range(1, count)])
-    states = StateExchange(
-        count, False, state_ref, totals_ref, result, sent, came, back, state_sems
-    )
+    states = StateExchange(count, False, state_ref, totals_ref, result, state_scratch)
     states.begin()
     first_pos = here * width
     acc[...] = jnp.zeros(acc.shape, F32)
@@ -1887,7 +1853,7 @@
     def step_of(i):
         return sum(((i // (1 << p)) % 2) * (1 << (high - p)) for p in range(high))
 
-    def pair(target, low):
+    def pair(target, low, begin=0, end=half):
         def one(i, carry):
             block = here ^ (step_of(i) + low)
 
@@ -1898,17 +1864,19 @@
 
             return carry
 
-        lax.fori_loop(0, half, one, 0)
+        lax.fori_loop(begin, end, one, 0)
 
     def table_copy(i):
         return remote(
             theirs.at[i], far.at[i], table_sems.at[0, i], table_sems.at[1, i], partner_ctx(1)
         )
 
-    pair(theirs, 1)
+    pair(theirs, 1, 0, half // 2)
+    states.middle()
+    pair(theirs, 1, half // 2)
     for i in range(half):
         table_copy(i).start()
-    states.middle()
+    states.carry()
     pair(mine, 0)
     for b in range(batch):
         for head in range(QHEADS):
@@ -1927,7 +1895,6 @@
     half = count // 2
     vmem = pl.BlockSpec(memory_space=pltpu.VMEM)
     dma = pltpu.SemaphoreType.DMA
-    share = state.shape[1] // count
     low = functools.partial(jax.ShapeDtypeStruct, dtype=BF16)
     near = (half, batch, width, kv_width)
     wide = pltpu.VMEM((batch, KVHEADS * HDIM, QHEADS * width), BF16)
@@ -1948,14 +1915,11 @@
             pltpu.VMEM(near, BF16),
             pltpu.VMEM(near, BF16),
             pltpu.VMEM(state.shape, BF16),
-            pltpu.VMEM((count, batch, share, STATE), BF16),
-            pltpu.VMEM((count, batch, share, STATE), BF16),
-            pltpu.VMEM(state.shape, BF16),
             dma((2, half)),
-            dma((4, count)),
-        ],
+        ]
+        + StateExchange.scratch(count, state),
         compiler_params=pltpu.CompilerParams(
-            collective_id=3, has_side_effects=True, vmem_limit_bytes=56 * MIB
+            collective_id=3, has_side_effects=True, vmem_limit_bytes=KERNEL_VMEM
         ),
         cost_estimate=pl.CostEstimate(
             flops=batch * count * width * width * 8 * 2000,
@@ -1964,6 +1928,265 @@
         ),
         name="mix_backward",
     )(starts, queries_t, table, attended_t, grad_t, logs, state, totals)
+
+
+def front_kernel(
+    count,
+    conv_tiles,
+    gate_tiles,
+    x_ref,
+    gain_ref,
+    start_ref,
+    own_ref,
+    weight_ref,
+    bias_ref,
+    normed_ref,
+    others_ref,
+    conv_ref,
+    edge_ref,
+    act_ref,
+    dt_ref,
+    q_ref,
+    gate_ref,
+    table_ref,
+    edge_x,
+    near,
+    table,
+    cross_sems,
+    core_sems,
+    side_sems,
+    last_sems,
+    table_sems,
+    edge_sems,
+):
+    here = lax.axis_index("ctx")
+    batch = table.shape[1]
+    rows = table.shape[2]
+    size = own_ref.shape[0]
+    chunks = own_ref.shape[1] // EARLY_TILE
+    half = count // 2
+    exchange_barrier(
+        [partner_wsh(1), partner_wsh(2)] + [partner_ctx(k) for k in range(1, count)]
+    )
+    right = (here + 1) % count
+
+    def edge_copy(b):
+        return remote(
+            x_ref.at[pl.ds((b + 1) * rows - 16, 16)],
+            edge_x.at[b],
+            edge_sems.at[0, b],
+            edge_sems.at[1, b],
+            (right, lax.axis_index("wsh")),
+        )
+
+    my_half = pl.ds(pl.multiple_of((here % 2) * (size // 2), 16), size // 2)
+    other_half = pl.ds(pl.multiple_of((1 - here % 2) * (size // 2), 16), size // 2)
+
+    def tile(place):
+        return pl.ds(pl.multiple_of(place * EARLY_TILE, EARLY_TILE), EARLY_TILE)
+
+    def columns(k):
+        return tile((k + gate_tiles) % chunks)
+
+    gate_from = chunks - gate_tiles
+
+    def cross_copy(k):
+        return remote(
+            own_ref.at[my_half, columns(k)],
+            near.at[0, my_half, columns(k)],
+            cross_sems.at[0, k],
+            cross_sems.at[1, k],
+            partner_wsh(2),
+        )
+
+    def side_copy(k):
+        return remote(
+            near.at[0, my_half, columns(k)],
+            near.at[0, my_half, columns(k)],
+            side_sems.at[0, k],
+            side_sems.at[1, k],
+            partner_ctx(1),
+        )
+
+    def side_in(k):
+        return remote(
+            near.at[0, other_half, columns(k)],
+            near.at[0, other_half, columns(k)],
+            side_sems.at[0, k],
+            side_sems.at[1, k],
+            partner_ctx(1),
+        )
+
+    def core_copy(k):
+        return remote(
+            own_ref.at[:, columns(k)],
+            near.at[1, :, columns(k)],
+            core_sems.at[0, k],
+            core_sems.at[1, k],
+            partner_wsh(1),
+        )
+
+    def last_copy(k):
+        return remote(
+            near.at[0, :, columns(k)],
+            near.at[2, :, columns(k)],
+            last_sems.at[0, k],
+            last_sems.at[1, k],
+            partner_wsh(1),
+        )
+
+    bits = ctx_bits(count)
+    high = len(bits) - 1
+
+    def step_of(i):
+        return sum(((i >> p) & 1) * (1 << (high - p)) for p in range(high))
+
+    def table_copy(i):
+        return remote(
+            table.at[0],
+            table.at[i],
+            table_sems.at[0, i],
+            table_sems.at[1, i],
+            partner_ctx(step_of(i)),
+        )
+
+    def send_first(k, carry):
+        cross_copy(k).start()
+        core_copy(k).start()
+        return carry
+
+    lax.fori_loop(0, chunks, send_first, 0)
+    for b in range(batch):
+        edge_copy(b).start()
+
+    def normalized(low):
+        wide = low.astype(F32)
+        return (wide * inv_rms(wide) * gain_ref[...]).astype(BF16)
+
+    normed_ref[...] = normalized(x_ref[...])
+    for b in range(batch):
+        edge_copy(b).wait()
+    edge_normed = normalized(
+        jnp.concatenate([edge_x[b] for b in range(batch)], axis=0)
+    )
+    edge_x[...] = edge_normed.reshape(edge_x.shape)
+
+    def product(pick, k):
+        total = None
+        for place, step in enumerate(NEAR):
+            block = own_ref[:, columns(k)] if place == 0 else near[place - 1, :, columns(k)]
+            part = mat(pick(near_at(step, size)), block)
+            total = part if total is None else total + part
+        return total
+
+    def compute(k):
+        core_copy(k).wait()
+        last_copy(k).wait()
+        value = product(lambda at: normed_ref[:, at], k)
+
+        @pl.when(k == 0)
+        def _():
+            table[0] = value.astype(BF16).reshape(table.shape[1:])
+            for i in range(1, half):
+                table_copy(i).start()
+
+        @pl.when((k > 0) & (k <= conv_tiles))
+        def _():
+            place = tile(k - 1)
+            conv_ref[:, place] = value
+            taps = weight_ref[:, place]
+            bias = bias_ref[:, place]
+            for b in range(batch):
+                edge = product(lambda at, b=b: edge_x[b, :, at], k)[16 - EDGE :]
+                edge_ref[b * EDGE : (b + 1) * EDGE, place] = edge
+                span = slice(b * rows, (b + 1) * rows)
+                total, _ = conv_sums(
+                    conv_inputs(edge, value[span]), taps, bias, start_ref[span]
+                )
+                act_ref[span, place] = total * sigmoid(total)
+
+        @pl.when(k == conv_tiles + 1)
+        def _():
+            dt_ref[...] = value
+
+        @pl.when((k > conv_tiles + 1) & (k < gate_from))
+        def _():
+            q_ref[tile(k - conv_tiles - 2), :] = value.T.astype(BF16)
+
+        @pl.when(k >= gate_from)
+        def _():
+            gate_ref[:, tile(k - gate_from)] = value
+
+    def one_step(t, carry):
+        @pl.when(t < chunks)
+        def _():
+            cross_copy(t).wait()
+            side_copy(t).start()
+
+        @pl.when((t >= 1) & (t <= chunks))
+        def _():
+            side_copy(t - 1).wait_send()
+            side_in(t - 1).wait_recv()
+            last_copy(t - 1).start()
+
+        pl.when(t >= 2)(functools.partial(compute, t - 2))
+        return carry
+
+    lax.fori_loop(0, chunks + 2, one_step, 0)
+    others_ref[...] = near[...]
+    for i in range(1, half):
+        table_copy(i).wait()
+    table_ref[...] = table[...]
+
+
+def front(count, batch, x, gain, rel_start, own, conv_weight, conv_bias, q_width):
+    tokens, depth = x.shape
+    size, columns = own.shape
+    rows = tokens // batch
+    channels = conv_weight.shape[1]
+    chunks = columns // EARLY_TILE
+    half = count // 2
+    vmem = pl.BlockSpec(memory_space=pltpu.VMEM)
+    dma = pltpu.SemaphoreType.DMA
+    low = functools.partial(jax.ShapeDtypeStruct, dtype=BF16)
+    wide = functools.partial(jax.ShapeDtypeStruct, dtype=F32)
+    table = (half, batch, rows, EARLY_TILE)
+    return pl.pallas_call(
+        functools.partial(
+            front_kernel, count, channels // EARLY_TILE, DSSM // EARLY_TILE
+        ),
+        in_specs=[vmem] * 6,
+        out_specs=[vmem] * 9,
+        out_shape=[
+            low((tokens, depth)),
+            low((3, size, columns)),
+            wide((tokens, channels)),
+            wide((batch * EDGE, channels)),
+            wide((tokens, channels)),
+            wide((tokens, EARLY_TILE)),
+            low((q_width, tokens)),
+            wide((tokens, DSSM)),
+            low(table),
+        ],
+        scratch_shapes=[
+            pltpu.VMEM((batch, 16, depth), BF16),
+            pltpu.VMEM((3, size, columns), BF16),
+            pltpu.VMEM(table, BF16),
+            dma((2, chunks)),
+            dma((2, chunks)),
+            dma((2, chunks)),
+            dma((2, chunks)),
+            dma((2, half)),
+            dma((2, batch)),
+        ],
+        compiler_params=pltpu.CompilerParams(
+            collective_id=4, has_side_effects=True, vmem_limit_bytes=KERNEL_VMEM
+        ),
+        cost_estimate=pl.CostEstimate(
+            flops=2 * tokens * depth * columns, bytes_accessed=20 * MIB, transcendentals=0
+        ),
+        name="front",
+    )(x, gain[None], rel_start, own, conv_weight, conv_bias[None])
 
 
 def local(
@@ -2001,41 +2224,40 @@
     x_low = inputs.reshape(tokens, features)
     grad_top = cotangent.reshape(tokens, features)
 
-    kv_near = gathered_near(kv_weight)
+    conv_tiles = channels // EARLY_TILE
+    gate_tiles = DSSM // EARLY_TILE
     early_shard = jnp.concatenate(
         [
+            in_weight[:, :DSSM],
+            kv_weight,
             in_weight[:, DSSM:],
             jnp.pad(dt_weight, ((0, 0), (0, EARLY_TILE - dt_weight.shape[1]))),
+            q_weight,
         ],
         axis=1,
     )
-    edge_x = passed_along(inputs[:, 0, rows - EDGE :], "ctx", 1).reshape(count * EDGE, features)
-
-    def normalized(low):
-        wide = low.astype(F32)
-        return (wide * inv_rms(wide) * norm1_gain).astype(BF16)
-
-    normed = normalized(x_low)
-    edge_normed = normalized(edge_x)
-    kv_rows = project(normed, kv_near, kv_width, BF16)
-    high_bits = bits_of("ctx")[1:]
-    keys = Gathering(kv_rows.reshape(count, rows, -1), high_bits[::-1])
-    early = gathered_near(early_shard, kv_near[1])
-    late_shard = jnp.concatenate([in_weight[:, :DSSM], q_weight], axis=1)
-    late = gathered_near(late_shard, early[1])
-    conv_rows, edge_rows, act, dt_rows = project_early(
+
+    normed, early_others, conv_rows, edge_rows, act, dt_rows, queries_t, gate_z, near_table = front(
+        ctx_count,
         count,
-        after(normed, kv_rows),
-        edge_normed,
+        x_low,
+        norm1_gain,
         rel_start,
+        early_shard,
         conv_weight,
         conv_bias,
-        early,
-    )
-    outs_shard = jnp.concatenate([out_weight, o_weight], axis=0)
-    outs = gathered_near(outs_shard, (late[1], dt_rows))
-    gu_full = gathered_near(gu_weight, (late[1], dt_rows))
-    down_full = gathered_near(down_weight, (late[1], dt_rows))
+        q_weight.shape[1],
+    )
+    high_bits = bits_of("ctx")[1:]
+    later_shards = after(
+        (
+            jnp.concatenate([out_weight, o_weight], axis=0),
+            gu_weight,
+            down_weight,
+        ),
+        dt_rows,
+    )
+    crossing = [swapped(shard, "wsh", 2) for shard in later_shards]
 
     def head_row(values):
         return jnp.pad(values, (0, 128 - MHEADS))[None]
@@ -2044,20 +2266,23 @@
     steps, decay, decay_t, to_end, total, fresh = ssd_state(
         count, act, dt_rows, bias_row, rate_row, rel_start
     )
-    late_rows = project(normed, late, 1024)
-    gate_z = late_rows[:, :DSSM]
-    queries_t = late_rows[:, DSSM:].astype(BF16).T
     starts_row = jnp.broadcast_to(starts[:, None, :], (count, 8, rows))
     attended_t, logs, key_table, state_in, totals = mix_forward(
-        ctx_count, starts_row, queries_t, keys.finish(), fresh, total
-    )
-
+        ctx_count, starts_row, queries_t, near_table, fresh, total
+    )
+
+    def near_blocks(which, held):
+        shard, across = later_shards[which], after(crossing[which], held)
+        return [shard, across, swapped(shard, "wsh", 1), swapped(across, "wsh", 1)]
+
+    outs = near_blocks(0, attended_t)
     skip_row = jnp.repeat(skip_gain, MDIM)[None]
     scanned = ssd_forward(count, act, steps, decay, decay_t, rel_start, state_in, skip_row)
     gate_sig = jax.nn.sigmoid(gate_z)
     gated = scanned * gate_z * gate_sig
     scale_m = inv_rms(gated)
     mixed = (gated * scale_m * mamba_gain).astype(BF16)
+    gu_full, down_full = near_blocks(1, mixed), near_blocks(2, mixed)
     middle, normed_two = out_project(x_low, mixed, attended_t, norm2_gain, outs)
 
     layer_out, grad_middle, branch, grad_norm2, hidden, grad_pair = mlp_both(
@@ -2098,8 +2323,22 @@
         totals,
     )
     key_grads = Scattering(dkv_near, high_bits)
-    grad_late = jnp.concatenate([grad_gate_z.astype(BF16), dq_t.T], axis=1)
-    grad_normed = unproject(jnp.zeros((tokens, features), F32), grad_late, late, 1024)
+    grad_gate_z = grad_gate_z.astype(BF16)
+    dq_rows = dq_t.T
+    grad_normed = unproject(
+        jnp.zeros((tokens, features), F32),
+        grad_gate_z,
+        [early_shard] + [early_others] * 3,
+        768,
+        near_specs(early_shard, 768, 0),
+    )
+    grad_normed = unproject(
+        grad_normed,
+        dq_rows,
+        [early_shard] + [early_others] * 3,
+        EARLY_TILE,
+        near_specs(early_shard, EARLY_TILE, gate_tiles + conv_tiles + 2),
+    )
 
     def total_of(kept, crossed):
         return (kept.astype(F32) + crossed.astype(F32)).astype(BF16)
@@ -2124,6 +2363,8 @@
         bias_row,
         rate_row,
     )
+    key_grads.advance(dx)
+    grad_kv_rows = key_grads.finish().reshape(tokens, -1)
     edge_back = passed_along(
         edge_grads(count, dx, db, dc, conv_rows, edge_rows, rel_start, conv_weight, conv_bias),
         "ctx",
@@ -2132,7 +2373,7 @@
     grad_early, conv_grads, input_grad, grad_norm1 = early_back(
         count,
         grad_normed,
-        key_grads.finish().reshape(tokens, -1),
+        grad_kv_rows,
         dx,
         db,
         dc,
@@ -2146,8 +2387,8 @@
         x_low,
         norm1_gain,
         grad_middle,
-        early,
-        kv_near,
+        early_shard,
+        early_others,
     )
     small_ssd = jnp.sum(small_ssd, axis=0)
     grad_dt_w = mat_left_t(normed, dt_grad[:, :MHEADS])
@@ -2171,23 +2412,24 @@
         ],
         axis=0,
     )
-    early_sum, late_sum, mix_sum, packed = reduce_grads(
+    early_sum, gate_sum, q_sum, mix_sum, packed = reduce_grads(
         ctx_count,
         kv_width + channels,
         normed,
         mixed,
         attended_t,
         grad_early,
-        grad_late,
+        grad_gate_z,
+        dq_rows,
         branch,
         packed,
     )
     in_sum, q_sum, kv_sum, out_sum, o_sum = finish(
         early_sum,
-        late_sum,
+        gate_sum,
         mix_sum,
+        q_sum,
         [w.shape for w in (in_weight, q_weight, kv_weight, out_weight, o_weight)],
-        channels,
     )
     totals_w = [in_sum, out_sum, q_sum, kv_sum, o_sum, gu_sum.astype(F32), down_sum.astype(F32)]
     small = []

time: 608 us -> 577 us (0.949)
  Pallas kernels: 394 us -> 456 us
  local copies, waits for them, and re-layouts: 68.6 us -> 26.2 us
  waiting for transfers between devices: 52 us -> 22.5 us
  starting transfers between devices: 30.6 us -> 17.8 us
    pallas_call x4 -> x2, Pallas kernels: 18.3 us -> 63.2 us  [the longest x1 58.7 us: front(): pl.pallas_call(functools.partial(front_kernel, count, channels // EARLY_T...]
    unnamed x230 -> x54, local copies, waits for them, and re-layouts: 48 us -> 8.12 us
    ppermute x26 -> x15, waiting for transfers between devices: 50.9 us -> 17.9 us  [swapped(): lax.ppermute(block, axis, [(i, i ^ bit) for i in range(lax.axis_size(axis...]
    pallas_call x1, Pallas kernels: 63.9 us -> 51.3 us  [mix_backward(): pl.pallas_call(functools.partial(mix_backward_kernel, count), in_specs=[v...]
    pallas_call x1, Pallas kernels: 134 us -> 145 us  [reduce_grads(): pl.pallas_call(functools.partial(grads_kernel, count, split, early_units,...]
    ppermute x26 -> x15, starting transfers between devices: 25 us -> 16.2 us  [swapped(): lax.ppermute(block, axis, [(i, i ^ bit) for i in range(lax.axis_size(axis...]
    pallas_call x4, Pallas kernels: 19.6 us -> 26.8 us  [block_grads(): pl.pallas_call(functools.partial(block_grads_kernel, steps), grid=(column...]
    concatenate x6 -> x1, other arithmetic: 9.05 us -> 2.18 us  [local(): jnp.concatenate([out_weight, o_weight], axis=0)]
  transfers between devices with their start and end apart: 29 -> 17, of which waited for: 10 -> 2; matrix products, arithmetic and copies ran while one was open for 8% -> 7% of each run, Pallas kernels for 61% -> 64%
where the time goes in v4:
time: 577 us; the launch traced here: 568 us
  Pallas kernels  456 us (79%)
  other arithmetic  29.9 us (5%)
  local copies, waits for them, and re-layouts  26.2 us (5%)
  waiting for transfers between devices  22.5 us (4%)
  starting transfers between devices  17.8 us (3%)
  between operations  14.9 us (3%)
    pallas_call x1, Pallas kernels, reduce_grads(): pl.pallas_call(functools.partial(grads_kernel, count, split, early_units,...  145 us
    pallas_call x1, Pallas kernels, front(): pl.pallas_call(functools.partial(front_kernel, count, channels // EARLY_T...  58.7 us
    pallas_call x1, Pallas kernels, mix_backward(): pl.pallas_call(functools.partial(mix_backward_kernel, count), in_specs=[v...  51.3 us
    pallas_call x1, Pallas kernels, mix_forward(): pl.pallas_call(functools.partial(mix_forward_kernel, count), in_specs=[vm...  47.1 us
    pallas_call x4, Pallas kernels, block_grads(): pl.pallas_call(functools.partial(block_grads_kernel, steps), grid=(column...  26.8 us
    pallas_call x1, Pallas kernels, mlp_both(): pl.pallas_call(mlp_kernel, grid_spec=pltpu.PrefetchScalarGridSpec(num_sca...  25.7 us
    pallas_call x1, Pallas kernels, ssd_backward(): pl.pallas_call(ssd_backward_kernel, grid=(count, NGROUP), in_specs=specs...  25 us
    pallas_call x1, Pallas kernels, early_back(): pl.pallas_call(functools.partial(early_back_kernel, count), grid=(tiles,)...  20.4 us
  transfers between devices with their start and end apart: 17, of which 2 were waited for; matrix products, arithmetic and copies ran while one was open for 7% of the time, Pallas kernels for 64%

profile of v4, /device:TPU:0, one launch (start us, length us, event | category | flops | bytes accessed | tf_op | source)
XLA Modules:
  0.0 568.3 jit_solution(11243211076615933300)
XLA Ops:
  14.2 2.2 pad_maximum_fusion.refs_0_
  16.4 58.7 %front.1 = (bf16[512,1024]{1,0:T(8,128)(2,1)}, bf16[3,256,4352]{2,1,0:T(8,128)(2,1)}, f32[512,1792]{1,0:T(8,128)}, f32[16,1792]{1,0:T(8,128)}, f32[512,1792]{1,0...) custom-call(bf16[512,1024]{1,0:T(8,128)(2,1)} %bitcast.70, ...), custom_call_target="tpu_custom_call" | custom-call | flops 4563402752 | bytes 20971520 | tf_op jit(solution)/shard_map/front/pallas_call | solution.py:2154
  79.7 7.0 %ssd_state.1 = (f32[512,128]{1,0:T(8,128)}, f32[512,128]{1,0:T(8,128)}, f32[2,128,256]{2,1,0:T(8,128)}, f32[512,128]{1,0:T(8,128)}, f32[2,8,128]{2,1,0:T(8,128)}, /*index=5*/f32[2,1536,128]{2,1,0:T(8,128)}) custom-call(f32[512,1792]{1,0:T(8,128)} %get-tuple-element.87.act_ref.x_ref.b_ref.c_ref, f32[512,256]{1,0:T(8,128)} %get-tuple-element.88.dt_ref, ...), custom_call_target="tpu_custom_call" | custom-call | flops 1000000000 | bytes 8388608 | tf_op jit(solution)/shard_map/ssd_state/pallas_call | solution.py:162
  87.3 47.1 %mix_forward.1 = (bf16[512,512]{1,0:T(8,128)(2,1)}, f32[2,8,256]{2,1,0:T(8,128)}, bf16[8,2,256,256]{3,2,1,0:T(8,128)(2,1)}, bf16[2,1536,128]{2,1,0:T(8,128)(2,1)}, f32[8,2,8,128]{3,2,1,0:T(8,128)}) custom-call(s32[2,8,256]{2,1,0:T(8,128)} %broadcast_in_dim.57.start_ref, bf16[512,512]{1,0:T(8,128)(2,1)} %get-tuple-element.92.q_ref, ...), custom_call_target="tpu_custom_call" | custom-call | flops 8388608000 | bytes 4194304 | tf_op jit(solution)/shard_map/mix_forward/pallas_call | solution.py:1739
  134.5 10.2 %ssd_forward.1.y_ref = f32[512,1536]{1,0:T(8,128)} custom-call(f32[512,1792]{1,0:T(8,128)} %get-tuple-element.87.act_ref.x_ref.b_ref.c_ref, f32[512,1792]{1,0:T(8,128)} %get-tuple-element.87.act_ref.x_ref.b_ref.c_ref, f32[512,1792]{1,0:T(8,128)} %get-tuple-element.87.act_ref.x_ref.b_ref.c_ref, f32[512,128]{1,0:T(8,128)} %get-tuple-element.89.step_ref, ...), custom_call_target="tpu_custom_call" | custom-call | flops 1258291200 | bytes 8388608 | tf_op jit(solution)/shard_map/ssd_forward/pallas_call | solution.py:396
  144.7 3.8 multiply_reduce_fusion.2
  150.4 17.9 %collective-permute-done.6.refs_9_ = bf16[512,1024]{1,0:T(8,128)(2,1)} collective-permute-done((bf16[512,1024]{1,0:T(8,128)(2,1)}, bf16[512,1024]{1,0:T(8,128)(2,1)}, u32[]{:S(2)}, u32[]{:S(2)}) %collective-permute-start.6) | collective-permute-done | bytes 1048608 | tf_op jit(solution)/shard_map/ppermute | solution.py:1089
  168.8 8.3 %out_project.1 = (f32[512,1024]{1,0:T(8,128)}, bf16[512,1024]{1,0:T(8,128)(2,1)}) custom-call(bf16[512,1024]{1,0:T(8,128)(2,1)} %bitcast.71, bf16[512,1536]{1,0:T(8,128)(2,1)} %multiply_convert_fusion.1.mixed_ref.mix_ref, bf16[512,512]{1,0:T(8,128)(2,1)} %get-tuple-element.98.heads_ref.attended_ref, f32[1,1024]{1,0:T(1,128)} %bitcast.80, ...), custom_call_target="tpu_custom_call" | custom-call | flops 2147483648 | bytes 12582912 | tf_op jit(solution)/shard_map/out_project/pallas_call | solution.py:589
  177.2 25.7 %mlp_both.1 = (bf16[512,1024]{1,0:T(8,128)(2,1)}, f32[512,1024]{1,0:T(8,128)}, bf16[512,1024]{1,0:T(8,128)(2,1)}, f32[1,1024]{1,0:T(1,128)}, bf16[512,2048]{1,0:T(8,128)(2,1)}, /*index=5*/bf16[2,512,2048]{2,1,0:T(8,128)(2,1)}) custom-call(s32[1]{0:T(128)} %bitcast.place_ref, bf16[512,1024]{1,0:T(8,128)(2,1)} %get-tuple-element.116.normed_ref.left_ref, ...), custom_call_target="tpu_custom_call" | custom-call | flops 12884901888 | bytes 31457280 | tf_op jit(solution)/shard_map/mlp_both/pallas_call | solution.py:709
  202.9 8.7 %block_grads.4 = bf16[512,4096]{1,0:T(8,128)(2,1)} custom-call(bf16[512,1024]{1,0:T(8,128)(2,1)} %get-tuple-element.116.normed_ref.left_ref, bf16[2,512,2048]{2,1,0:T(8,128)(2,1)} %get-tuple-element.109.right_ref), custom_call_target="tpu_custom_call" | custom-call | flops 2147483648 | bytes 6291456 | tf_op jit(solution)/shard_map/block_grads/pallas_call | solution.py:1035
  211.6 4.3 block_grads.5
  216.4 7.5 %out_unproject.1 = (f32[512,1536]{1,0:T(8,128)}, bf16[512,512]{1,0:T(8,128)(2,1)}) custom-call(bf16[512,1024]{1,0:T(8,128)(2,1)} %get-tuple-element.111.branch_ref, bf16[512,1024]{1,0:T(8,128)(2,1)} %pad_maximum_fusion.refs_0_, bf16[512,1024]{1,0:T(8,128)(2,1)} %collective-permute-done.refs_1_, bf16[512,1024]{1,0:T(8,128)(2,1)} %collective-permute-done.1.refs_2_, ...), custom_call_target="tpu_custom_call" | custom-call | flops 2147483648 | bytes 12582912 | tf_op jit(solution)/shard_map/out_unproject/pallas_call | solution.py:616
  223.9 2.8 multiply_reduce_fusion
  227.7 5.1 multiply_multiply_fusion
  232.8 5.2 state_grad.1.state_ref
  238.0 4.7 block_grads.7
  243.7 9.0 %block_grads.6 = (bf16[256,4096]{1,0:T(8,128)(2,1)}, bf16[256,4096]{1,0:T(8,128)(2,1)}) custom-call(bf16[512,1024]{1,0:T(8,128)(2,1)} %get-tuple-element.116.normed_ref.left_ref, bf16[2,512,2048]{2,1,0:T(8,128)(2,1)} %get-tuple-element.109.right_ref, bf16[512,4096]{1,0:T(8,128)(2,1)} %collective-permute-done.9.refs_0_), custom_call_target="tpu_custom_call" | custom-call | flops 2147483648 | bytes 6291456 | tf_op jit(solution)/shard_map/block_grads/pallas_call | solution.py:1035
  253.8 51.3 %mix_backward.1 = (bf16[512,512]{1,0:T(8,128)(2,1)}, bf16[4,2,256,256]{3,2,1,0:T(8,128)(2,1)}, bf16[2,1536,128]{2,1,0:T(8,128)(2,1)}) custom-call(s32[2,8,256]{2,1,0:T(8,128)} %broadcast_in_dim.57.start_ref, bf16[512,512]{1,0:T(8,128)(2,1)} %get-tuple-element.92.q_ref, bf16[8,2,256,256]{3,2,1,0:T(8,128)(2,1)} %get-tuple-element.114.table_ref, ...), custom_call_target="tpu_custom_call" | custom-call | flops 16777216000 | bytes 8388608 | tf_op jit(solution)/shard_map/mix_backward/pallas_call | solution.py:1902
  306.9 5.1 collective-permute-start.11
  313.6 6.2 %unproject.2.base_ref = f32[512,1024]{1,0:T(8,128)} custom-call(f32[512,1024]{1,0:T(8,128)} %broadcast_in_dim.60.base_ref, bf16[512,1536]{1,0:T(8,128)(2,1)} %get-tuple-element.217.grad_ref.gate_ref, bf16[256,4352]{1,0:T(8,128)(2,1)} %copy-done.1, bf16[3,256,4352]{2,1,0:T(8,128)(2,1)} %get-tuple-element.113.refs_1_.refs_2_.refs_3_, ...), custom_call_target="tpu_custom_call" | custom-call | flops 1610612736 | bytes 4718592 | tf_op jit(solution)/shard_map/unproject/pallas_call | solution.py:557
  319.7 2.6 add_convert_fusion.1
  322.3 2.0 copy.61
  324.4 4.6 unproject.3.base_ref
  330.5 4.2 collective-permute-start.12
  334.7 2.2 add_convert_fusion
  336.9 25.0 %ssd_backward.1 = (f32[512,1536]{1,0:T(8,128)}, f32[512,128]{1,0:T(8,128)}, f32[512,128]{1,0:T(8,128)}, bf16[512,256]{1,0:T(8,128)(2,1)}, f32[2,8,128]{2,1,0:T(8,128)}) custom-call(f32[512,1792]{1,0:T(8,128)} %get-tuple-element.87.act_ref.x_ref.b_ref.c_ref, f32[512,1792]{1,0:T(8,128)} %get-tuple-element.87.act_ref.x_ref.b_ref.c_ref, ...), custom_call_target="tpu_custom_call" | custom-call | flops 3145728000 | bytes 16777216 | tf_op jit(solution)/shard_map/ssd_backward/pallas_call | solution.py:436
  363.6 1.9 edge_grads.1
  367.9 4.5 collective-permute-done.15.came_ref
  373.1 20.4 %early_back.1 = (bf16[512,2304]{1,0:T(8,128)(2,1)}, f32[8,1792]{1,0:T(8,128)}, bf16[512,1024]{1,0:T(8,128)(2,1)}, f32[1,1024]{1,0:T(1,128)}) custom-call(f32[512,1024]{1,0:T(8,128)} %unproject.3.base_ref, bf16[512,256]{1,0:T(8,128)(2,1)} %bitcast.69, f32[512,1536]{1,0:T(8,128)} %get-tuple-element.131.dx_ref, f32[512,128]{1,0:T(8,128)} %get-tuple-element.133.db_ref, ...), custom_call_target="tpu_custom_call" | custom-call | flops 2415919104 | bytes 20971520 | tf_op jit(solution)/shard_map/early_back/pallas_call | solution.py:951
  396.6 145.3 %reduce_grads.1 = (bf16[256,2048]{1,0:T(8,128)(2,1)}, bf16[256,1536]{1,0:T(8,128)(2,1)}, bf16[256,512]{1,0:T(8,128)(2,1)}, bf16[512,1024]{1,0:T(8,128)(2,1)}, f32[320,128]{1,0:T(8,128)}) custom-call(bf16[512,1024]{1,0:T(8,128)(2,1)} %get-tuple-element.140.one_ref, bf16[512,1536]{1,0:T(8,128)(2,1)} %multiply_convert_fusion.1.mixed_ref.mix_ref, ...), custom_call_target="tpu_custom_call" | custom-call | flops 6499999744 | bytes 31457280 | tf_op jit(solution)/shard_map/reduce_grads/pallas_call | solution.py:1420
  548.1 4.5 finish.1
  555.3 4.2 convert_element_type.75
  (124 shorter events, 41.2 us)
Async XLA Ops:
  7.2 6.2 %copy-start.11 = (bf16[256,24]{0,1:T(8,128)(2,1)S(1)}, bf16[256,24]{0,1:T(8,128)(2,1)}, u32[]{:S(2)}) copy-start(bf16[256,24]{0,1:T(8,128)(2,1)} %param.24) | copy-start | bytes 36868
  7.2 6.3 %copy-start.13 = (f32[1792]{0:T(1024)S(1)}, f32[1792]{0:T(1024)}, u32[]{:S(2)}) copy-start(f32[1792]{0:T(1024)} %param.26) | copy-start | bytes 21508
  7.2 6.9 %copy-start.8 = (bf16[256,512]{1,0:T(8,128)(2,1)S(1)}, bf16[256,512]{1,0:T(8,128)(2,1)}, u32[]{:S(2)}) copy-start(bf16[256,512]{1,0:T(8,128)(2,1)} %param.32) | copy-start | bytes 786436
  7.2 7.0 %copy-start.7 = (bf16[384,1024]{1,0:T(8,128)(2,1)S(1)}, bf16[384,1024]{1,0:T(8,128)(2,1)}, u32[]{:S(2)}) copy-start(bf16[384,1024]{1,0:T(8,128)(2,1)} %param.31) | copy-start | bytes 2359300
  7.2 548.0 %all-reduce.11.cloned.1.call-start = ((), (), s32[]{:S(2)}) async-start(), calls=%async_computation | async-start | bytes 6291456 | tf_op jit(solution)/shard_map/psum | solution.py:2396
  16.4 62.1 %copy-start.15 = (f32[24]{0:T(128)S(1)}, f32[24]{0:T(128)}, u32[]{:S(2)}) copy-start(f32[24]{0:T(128)} %param.29) | copy-start | bytes 292
  16.4 62.8 %copy-start.16 = (f32[24]{0:T(128)S(1)}, f32[24]{0:T(128)}, u32[]{:S(2)}) copy-start(f32[24]{0:T(128)} %param.28) | copy-start | bytes 292
  16.4 62.8 %copy-start.17 = (f32[24]{0:T(128)S(1)}, f32[24]{0:T(128)}, u32[]{:S(2)}) copy-start(f32[24]{0:T(128)} %param.27) | copy-start | bytes 292
  75.1 74.8 %collective-permute-start = (bf16[512,1024]{1,0:T(8,128)(2,1)}, bf16[512,1024]{1,0:T(8,128)(2,1)}, u32[]{:S(2)}, u32[]{:S(2)}) collective-permute-start(bf16[512,1024]{1,0:T(8,128)(2,1)} %pad_maximum_fusion.refs_0_), channel_id=1, source_target_pairs={{0,2},{1,3},{2,0},{3,1},{4,6},{5,7},{6,4},{7,5},{8,10},{9,11},{10,... | collective-permute-start | bytes 3145736 | tf_op jit(solution)/shard_map/ppermute | solution.py:1089
  76.2 92.1 %collective-permute-start.1 = (bf16[512,1024]{1,0:T(8,128)(2,1)}, bf16[512,1024]{1,0:T(8,128)(2,1)}, u32[]{:S(2)}, u32[]{:S(2)}) collective-permute-start(bf16[512,1024]{1,0:T(8,128)(2,1)} %pad_maximum_fusion.refs_0_), channel_id=1, source_target_pairs={{0,1},{1,0},{2,3},{3,2},{4,5},{5,4},{6,7},{7,6},{8,9},{9,8},{10,11... | collective-permute-start | bytes 3145736 | tf_op jit(solution)/shard_map/ppermute | solution.py:1089
  76.3 73.7 %collective-permute-start.3 = (bf16[256,4096]{1,0:T(8,128)(2,1)}, bf16[256,4096]{1,0:T(8,128)(2,1)}, u32[]{:S(2)}, u32[]{:S(2)}) collective-permute-start(bf16[256,4096]{1,0:T(8,128)(2,1)} %refs_4_), channel_id=1, source_target_pairs={{0,2},{1,3},{2,0},{3,1},{4,6},{5,7},{6,4},{7,5},{8,10},{9,11},{10,... | collective-permute-start | bytes 6291464 | tf_op jit(solution)/shard_map/ppermute | solution.py:1089
  77.3 99.9 %collective-permute-start.4 = (bf16[256,4096]{1,0:T(8,128)(2,1)}, bf16[256,4096]{1,0:T(8,128)(2,1)}, u32[]{:S(2)}, u32[]{:S(2)}) collective-permute-start(bf16[256,4096]{1,0:T(8,128)(2,1)} %refs_4_), channel_id=1, source_target_pairs={{0,1},{1,0},{2,3},{3,2},{4,5},{5,4},{6,7},{7,6},{8,9},{9,8},{10,11... | collective-permute-start | bytes 6291464 | tf_op jit(solution)/shard_map/ppermute | solution.py:1089
  77.4 90.9 %collective-permute-start.6 = (bf16[512,1024]{1,0:T(8,128)(2,1)}, bf16[512,1024]{1,0:T(8,128)(2,1)}, u32[]{:S(2)}, u32[]{:S(2)}) collective-permute-start(bf16[512,1024]{1,0:T(8,128)(2,1)} %refs_8_), channel_id=1, source_target_pairs={{0,2},{1,3},{2,0},{3,1},{4,6},{5,7},{6,4},{7,5},{8,10},{9,11},{10,... | collective-permute-start | bytes 3145736 | tf_op jit(solution)/shard_map/ppermute | solution.py:1089
  144.7 3.8 copy-start.10
  149.9 27.2 %collective-permute-start.5 = (bf16[256,4096]{1,0:T(8,128)(2,1)}, bf16[256,4096]{1,0:T(8,128)(2,1)}, u32[]{:S(2)}, u32[]{:S(2)}) collective-permute-start(bf16[256,4096]{1,0:T(8,128)(2,1)} %collective-permute-done.3.refs_1_.refs_5_), channel_id=1, source_target_pairs={{0,1},{1,0},{2,3},{3,2},{4,5},{5,4},{6,7},{7,6},{8,9},{9,8},{10,11... | collective-permute-start | bytes 6291464 | tf_op jit(solution)/shard_map/ppermute | solution.py:1089
  149.9 18.9 %collective-permute-start.2 = (bf16[512,1024]{1,0:T(8,128)(2,1)}, bf16[512,1024]{1,0:T(8,128)(2,1)}, u32[]{:S(2)}, u32[]{:S(2)}) collective-permute-start(bf16[512,1024]{1,0:T(8,128)(2,1)} %collective-permute-done.refs_1_), channel_id=1, source_target_pairs={{0,1},{1,0},{2,3},{3,2},{4,5},{5,4},{6,7},{7,6},{8,9},{9,8},{10,11... | collective-permute-start | bytes 3145736 | tf_op jit(solution)/shard_map/ppermute | solution.py:1089
  168.3 8.8 %collective-permute-start.7 = (bf16[512,1024]{1,0:T(8,128)(2,1)}, bf16[512,1024]{1,0:T(8,128)(2,1)}, u32[]{:S(2)}, u32[]{:S(2)}) collective-permute-start(bf16[512,1024]{1,0:T(8,128)(2,1)} %refs_8_), channel_id=1, source_target_pairs={{0,1},{1,0},{2,3},{3,2},{4,5},{5,4},{6,7},{7,6},{8,9},{9,8},{10,11... | collective-permute-start | bytes 3145736 | tf_op jit(solution)/shard_map/ppermute | solution.py:1089
  168.3 8.8 %collective-permute-start.8 = (bf16[512,1024]{1,0:T(8,128)(2,1)}, bf16[512,1024]{1,0:T(8,128)(2,1)}, u32[]{:S(2)}, u32[]{:S(2)}) collective-permute-start(bf16[512,1024]{1,0:T(8,128)(2,1)} %collective-permute-done.6.refs_9_), channel_id=1, source_target_pairs={{0,1},{1,0},{2,3},{3,2},{4,5},{5,4},{6,7},{7,6},{8,9},{9,8},{10,11... | collective-permute-start | bytes 3145736 | tf_op jit(solution)/shard_map/ppermute | solution.py:1089
  211.6 32.1 %collective-permute-start.9 = (bf16[512,4096]{1,0:T(8,128)(2,1)}, bf16[512,4096]{1,0:T(8,128)(2,1)}, u32[]{:S(2)}, u32[]{:S(2)}) collective-permute-start(bf16[512,4096]{1,0:T(8,128)(2,1)} %block_grads.4), channel_id=1, source_target_pairs={{0,1},{1,0},{2,3},{3,2},{4,5},{5,4},{6,7},{7,6},{8,9},{9,8},{10,11... | collective-permute-start | bytes 12582920 | tf_op jit(solution)/shard_map/ppermute | solution.py:1089
  215.9 22.1 %collective-permute-start.10 = (bf16[1024,1024]{1,0:T(8,128)(2,1)}, bf16[1024,1024]{1,0:T(8,128)(2,1)}, u32[]{:S(2)}, u32[]{:S(2)}) collective-permute-start(bf16[1024,1024]{1,0:T(8,128)(2,1)} %block_grads.5), channel_id=1, source_target_pairs={{0,1},{1,0},{2,3},{3,2},{4,5},{5,4},{6,7},{7,6},{8,9},{9,8},{10,11... | collective-permute-start | bytes 6291464 | tf_op jit(solution)/shard_map/ppermute | solution.py:1089
  223.9 3.8 copy-start.2
  242.7 77.0 %collective-permute-start.14 = (bf16[512,1024]{1,0:T(8,128)(2,1)}, bf16[512,1024]{1,0:T(8,128)(2,1)}, u32[]{:S(2)}, u32[]{:S(2)}) collective-permute-start(bf16[512,1024]{1,0:T(8,128)(2,1)} %get-tuple-element.119), channel_id=1, source_target_pairs={{0,2},{1,3},{2,0},{3,1},{4,6},{5,7},{6,4},{7,5},{8,10},{9,11},{10,... | collective-permute-start | bytes 3145736 | tf_op jit(solution)/shard_map/ppermute | solution.py:1089
  252.8 81.9 %collective-permute-start.13 = (bf16[256,4096]{1,0:T(8,128)(2,1)}, bf16[256,4096]{1,0:T(8,128)(2,1)S(1)}, u32[]{:S(2)}, u32[]{:S(2)}) collective-permute-start(bf16[256,4096]{1,0:T(8,128)(2,1)} %get-tuple-element.117), channel_id=1, source_target_pairs={{0,2},{1,3},{2,0},{3,1},{4,6},{5,7},{6,4},{7,5},{8,10},{9,11},{10,... | collective-permute-start | bytes 6291464 | tf_op jit(solution)/shard_map/ppermute | solution.py:1089
  306.9 22.1 %collective-permute-start.11 = (bf16[2,2,256,256]{3,2,1,0:T(8,128)(2,1)}, bf16[2,2,256,256]{3,2,1,0:T(8,128)(2,1)}, u32[]{:S(2)}, u32[]{:S(2)}) collective-permute-start(bf16[2,2,256,256]{3,2,1,0:T(8,128)(2,1)} %slice.85), channel_id=1, source_target_pairs={{0,8},{4,12},{8,0},{12,4},{16,24},{20,28},{24,16},{28,20},{1,9},{5... | collective-permute-start | bytes 1572872 | tf_op jit(solution)/shard_map/ppermute | solution.py:1089
  313.6 6.2 %copy-start.5 = (bf16[512,1024]{1,0:T(8,128)(2,1)S(1)}, bf16[512,1024]{1,0:T(8,128)(2,1)}, u32[]{:S(2)}) copy-start(bf16[512,1024]{1,0:T(8,128)(2,1)} %get-tuple-element.128) | copy-start | bytes 3145732
  329.0 5.8 %copy-start.3 = (bf16[256,4096]{1,0:T(8,128)(2,1)S(1)}, bf16[256,4096]{1,0:T(8,128)(2,1)}, u32[]{:S(2)}) copy-start(bf16[256,4096]{1,0:T(8,128)(2,1)} %get-tuple-element.127) | copy-start | bytes 6291460
  330.5 36.6 %collective-permute-start.12 = (bf16[1,2,256,256]{3,2,1,0:T(8,128)(2,1)S(1)}, bf16[1,2,256,256]{3,2,1,0:T(8,128)(2,1)S(1)}, u32[]{:S(2)}, u32[]{:S(2)}) collective-permute-start(bf16[1,2,256,256]{3,2,1,0:T(8,128)(2,1)S(1)} %slice.109), channel_id=1, source_target_pairs={{0,16},{4,20},{8,24},{12,28},{16,0},{20,4},{24,8},{28,12},{1,17},{... | collective-permute-start | bytes 786440 | tf_op jit(solution)/shard_map/ppermute | solution.py:1089
  336.9 25.0 %copy-start.6 = (bf16[512,1024]{1,0:T(8,128)(2,1)S(1)}, bf16[512,1024]{1,0:T(8,128)(2,1)}, u32[]{:S(2)}) copy-start(bf16[512,1024]{1,0:T(8,128)(2,1)} %get-tuple-element.140.one_ref) | copy-start | bytes 3145732
  363.6 3.5 copy-start.12
  365.5 6.9 %collective-permute-start.15 = (f32[16,1792]{1,0:T(8,128)}, f32[16,1792]{1,0:T(8,128)S(1)}, u32[]{:S(2)}, u32[]{:S(2)}) collective-permute-start(f32[16,1792]{1,0:T(8,128)} %edge_grads.1), channel_id=1, source_target_pairs={{4,0},{8,4},{12,8},{16,12},{20,16},{24,20},{28,24},{5,1},{9,5},{13... | collective-permute-start | bytes 344072 | tf_op jit(solution)/shard_map/ppermute | solution.py:1085
  373.1 22.9 %copy-start.14 = (f32[1,1024]{1,0:T(1,128)S(1)}, f32[1,1024]{1,0:T(1,128)}, u32[]{:S(2)}) copy-start(f32[1,1024]{1,0:T(1,128)} %get-tuple-element.145) | copy-start | bytes 12292
  555.3 4.2 copy-start.4
  (4 other events, 6.3 us)
Sparse Core Ops, SparseCore 0:
  337.0 147.0 all-reduce.10

commit v5 on v4

--- a/solution.py
+++ b/solution.py
@@ -571,8 +571,10 @@
     )(base, grad, *weights)
 
 
-def out_proj_kernel(x_ref, mixed_ref, heads_ref, gain_ref, *refs):
-    *weights, middle_ref, normed_ref = refs
+def out_proj_kernel(
+    x_ref, mixed_ref, heads_ref, gain_ref, own_ref, others_ref, middle_ref, normed_ref
+):
+    weights = [own_ref] + [others_ref.at[place] for place in range(3)]
     wide = mixed_ref.shape[1] // 4
     narrow = heads_ref.shape[0] // 4
     middle_ref[...] = x_ref[...].astype(F32)
@@ -588,7 +590,7 @@
     vmem = pl.BlockSpec(memory_space=pltpu.VMEM)
     return pl.pallas_call(
         out_proj_kernel,
-        in_specs=[vmem] * 8,
+        in_specs=[vmem] * 6,
         out_specs=[vmem, vmem],
         out_shape=[jax.ShapeDtypeStruct(x.shape, F32), jax.ShapeDtypeStruct(x.shape, BF16)],
         compiler_params=pltpu.CompilerParams(vmem_limit_bytes=KERNEL_VMEM),
@@ -599,8 +601,8 @@
     )(x, mixed, heads_t, gain[None], *weights)
 
 
-def out_back_kernel(branch_ref, *refs):
-    *weights, mixed_ref, heads_ref = refs
+def out_back_kernel(branch_ref, own_ref, others_ref, mixed_ref, heads_ref):
+    weights = [own_ref] + [others_ref.at[place] for place in range(3)]
     wide = mixed_ref.shape[1] // 4
     narrow = heads_ref.shape[0] // 4
     for step, weight in zip(NEAR, weights):
@@ -615,7 +617,7 @@
     tokens = branch.shape[0]
     return pl.pallas_call(
         out_back_kernel,
-        in_specs=[vmem] * 5,
+        in_specs=[vmem] * 3,
         out_specs=[vmem, vmem],
         out_shape=[
             jax.ShapeDtypeStruct((tokens, mixed_width), F32),
@@ -1696,6 +1698,8 @@
 
     def pair(source, low, begin=0, end=half):
         def one(i, carry):
+            if low:
+                table_copy(i).wait()
             block = here ^ (step_of(i) + low)
 
             @pl.when(block <= here)
@@ -1707,16 +1711,14 @@
 
         lax.fori_loop(begin, end, one, 0)
 
-    pair(near_ref, 0, 0, half // 2)
+    pair(near_ref, 0)
     for k in range(1, count):
         total_copy(k, here).wait_send()
         total_copy(k, here ^ k).wait_recv()
     states.middle()
-    pair(near_ref, 0, half // 2)
+    pair(far, 1, 0, half // 2)
     states.carry()
-    for i in range(half):
-        table_copy(i).wait()
-    pair(far, 1)
+    pair(far, 1, half // 2)
     for b in range(batch):
         for head in range(QHEADS):
             out_ref[head * HDIM : (head + 1) * HDIM, b * width : (b + 1) * width] = (
@@ -1938,10 +1940,12 @@
     gain_ref,
     start_ref,
     own_ref,
+    tall_ref,
     weight_ref,
     bias_ref,
     normed_ref,
     others_ref,
+    tall_others,
     conv_ref,
     edge_ref,
     act_ref,
@@ -1951,11 +1955,13 @@
     table_ref,
     edge_x,
     near,
+    tall_near,
     table,
     cross_sems,
     core_sems,
     side_sems,
     last_sems,
+    tall_sems,
     table_sems,
     edge_sems,
 ):
@@ -2035,6 +2041,44 @@
             partner_wsh(1),
         )
 
+    tall_size = tall_ref.shape[0]
+    tall_chunks = tall_ref.shape[1] // EARLY_TILE
+    tall_mine = pl.ds(pl.multiple_of((here % 2) * (tall_size // 2), 16), tall_size // 2)
+    tall_theirs = pl.ds(pl.multiple_of((1 - here % 2) * (tall_size // 2), 16), tall_size // 2)
+
+    def tall_copy(source, target, kind, k, device):
+        return remote(
+            source, target, tall_sems.at[kind, 0, k], tall_sems.at[kind, 1, k], device
+        )
+
+    def tall_cross(k):
+        place = tall_near.at[0, tall_mine, tile(k)]
+        return tall_copy(tall_ref.at[tall_mine, tile(k)], place, 0, k, partner_wsh(2))
+
+    def tall_core(k):
+        place = tall_near.at[1, :, tile(k)]
+        return tall_copy(tall_ref.at[:, tile(k)], place, 1, k, partner_wsh(1))
+
+    def tall_side(k, rows_at):
+        place = tall_near.at[0, rows_at, tile(k)]
+        return tall_copy(place, place, 2, k, partner_ctx(1))
+
+    def tall_last(k):
+        place = tall_near.at[2, :, tile(k)]
+        return tall_copy(tall_near.at[0, :, tile(k)], place, 3, k, partner_wsh(1))
+
+    def tall_step(j):
+        @pl.when((j >= 0) & (j < tall_chunks))
+        def _():
+            tall_cross(j).wait()
+            tall_side(j, tall_mine).start()
+
+        @pl.when((j >= 2) & (j <= tall_chunks + 1))
+        def _():
+            tall_side(j - 2, tall_mine).wait_send()
+            tall_side(j - 2, tall_theirs).wait_recv()
+            tall_last(j - 2).start()
+
     bits = ctx_bits(count)
     high = len(bits) - 1
 
@@ -2055,7 +2099,14 @@
         core_copy(k).start()
         return carry
 
-    lax.fori_loop(0, chunks, send_first, 0)
+    def send_tall(k, carry):
+        tall_cross(k).start()
+        tall_core(k).start()
+        return carry
+
+    lax.fori_loop(0, gate_from, send_first, 0)
+    lax.fori_loop(0, tall_chunks, send_tall, 0)
+    lax.fori_loop(gate_from, chunks, send_first, 0)
     for b in range(batch):
         edge_copy(b).start()
 
@@ -2123,23 +2174,32 @@
             cross_copy(t).wait()
             side_copy(t).start()
 
-        @pl.when((t >= 1) & (t <= chunks))
+        @pl.when((t >= 2) & (t <= chunks + 1))
         def _():
-            side_copy(t - 1).wait_send()
-            side_in(t - 1).wait_recv()
-            last_copy(t - 1).start()
-
-        pl.when(t >= 2)(functools.partial(compute, t - 2))
+            side_copy(t - 2).wait_send()
+            side_in(t - 2).wait_recv()
+            last_copy(t - 2).start()
+
+        tall_step(t - gate_from)
+        pl.when(t >= 4)(functools.partial(compute, t - 4))
         return carry
 
-    lax.fori_loop(0, chunks + 2, one_step, 0)
+    lax.fori_loop(0, chunks + 4, one_step, 0)
     others_ref[...] = near[...]
+
+    def end_tall(k, carry):
+        tall_core(k).wait()
+        tall_last(k).wait()
+        return carry
+
+    lax.fori_loop(0, tall_chunks, end_tall, 0)
+    tall_others[...] = tall_near[...]
     for i in range(1, half):
         table_copy(i).wait()
     table_ref[...] = table[...]
 
 
-def front(count, batch, x, gain, rel_start, own, conv_weight, conv_bias, q_width):
+def front(count, batch, x, gain, rel_start, own, tall, conv_weight, conv_bias, q_width):
     tokens, depth = x.shape
     size, columns = own.shape
     rows = tokens // batch
@@ -2155,11 +2215,12 @@
         functools.partial(
             front_kernel, count, channels // EARLY_TILE, DSSM // EARLY_TILE
         ),
-        in_specs=[vmem] * 6,
-        out_specs=[vmem] * 9,
+        in_specs=[vmem] * 7,
+        out_specs=[vmem] * 10,
         out_shape=[
             low((tokens, depth)),
             low((3, size, columns)),
+            low((3,) + tall.shape),
             wide((tokens, channels)),
             wide((batch * EDGE, channels)),
             wide((tokens, channels)),
@@ -2171,11 +2232,13 @@
         scratch_shapes=[
             pltpu.VMEM((batch, 16, depth), BF16),
             pltpu.VMEM((3, size, columns), BF16),
+            pltpu.VMEM((3,) + tall.shape, BF16),
             pltpu.VMEM(table, BF16),
             dma((2, chunks)),
             dma((2, chunks)),
             dma((2, chunks)),
             dma((2, chunks)),
+            dma((4, 2, tall.shape[1] // EARLY_TILE)),
             dma((2, half)),
             dma((2, batch)),
         ],
@@ -2186,7 +2249,7 @@
             flops=2 * tokens * depth * columns, bytes_accessed=20 * MIB, transcendentals=0
         ),
         name="front",
-    )(x, gain[None], rel_start, own, conv_weight, conv_bias[None])
+    )(x, gain[None], rel_start, own, tall, conv_weight, conv_bias[None])
 
 
 def local(
@@ -2237,13 +2300,15 @@
         axis=1,
     )
 
-    normed, early_others, conv_rows, edge_rows, act, dt_rows, queries_t, gate_z, near_table = front(
+    outs_own = jnp.concatenate([out_weight, o_weight], axis=0)
+    normed, early_others, outs_others, conv_rows, edge_rows, act, dt_rows, queries_t, gate_z, near_table = front(
         ctx_count,
         count,
         x_low,
         norm1_gain,
         rel_start,
         early_shard,
+        outs_own,
         conv_weight,
         conv_bias,
         q_weight.shape[1],
@@ -2251,7 +2316,6 @@
     high_bits = bits_of("ctx")[1:]
     later_shards = after(
         (
-            jnp.concatenate([out_weight, o_weight], axis=0),
             gu_weight,
             down_weight,
         ),
@@ -2275,14 +2339,14 @@
         shard, across = later_shards[which], after(crossing[which], held)
         return [shard, across, swapped(shard, "wsh", 1), swapped(across, "wsh", 1)]
 
-    outs = near_blocks(0, attended_t)
+    outs = (outs_own, outs_others)
     skip_row = jnp.repeat(skip_gain, MDIM)[None]
     scanned = ssd_forward(count, act, steps, decay, decay_t, rel_start, state_in, skip_row)
     gate_sig = jax.nn.sigmoid(gate_z)
     gated = scanned * gate_z * gate_sig
     scale_m = inv_rms(gated)
     mixed = (gated * scale_m * mamba_gain).astype(BF16)
-    gu_full, down_full = near_blocks(1, mixed), near_blocks(2, mixed)
+    gu_full, down_full = near_blocks(0, mixed), near_blocks(1, mixed)
     middle, normed_two = out_project(x_low, mixed, attended_t, norm2_gain, outs)
 
     layer_out, grad_middle, branch, grad_norm2, hidden, grad_pair = mlp_both(
@@ -2300,17 +2364,17 @@
     down_sent = swapped(down_send, "wsh", 1)
     branch = after(branch, (gu_send, down_send))
     grad_mixed, grad_attended_t = out_unproject(branch, outs, DSSM, QHEADS * HDIM)
+    gu_left, down_left = after((normed_two, hidden), grad_attended_t)
+    gu_kept, gu_other = block_grads(gu_left, grad_pair, NEAR[:2], gu_sent)
+    down_kept, down_other = block_grads(down_left, grad_top[None], NEAR[:2], down_sent)
+    gu_crossed = swapped(gu_other, "wsh", 2)
+    down_crossed = swapped(down_other, "wsh", 2)
+
+    grad_mixed = after(grad_mixed, (gu_other, down_other))
     grad_gated, grad_mamba = rms_pull(gated, scale_m, mamba_gain, grad_mixed)
     grad_gate_z = grad_gated * scanned * gate_sig * (1.0 + gate_z * (1.0 - gate_sig))
     grad_scanned = grad_gated * gate_z * gate_sig
     grad_state = state_grad(count, grad_scanned, act, decay, rel_start)
-    gu_left, down_left = after((normed_two, hidden), grad_state)
-    gu_kept, gu_other = block_grads(gu_left, grad_pair, NEAR[:2], gu_sent)
-    down_kept, down_other = block_grads(down_left, grad_top[None], NEAR[:2], down_sent)
-    gu_crossed = swapped(gu_other, "wsh", 2)
-    down_crossed = swapped(down_other, "wsh", 2)
-
-    grad_attended_t = after(grad_attended_t, (gu_other, down_other))
     dq_t, dkv_near, later = mix_backward(
         ctx_count,
         starts_row,
@@ -2323,7 +2387,13 @@
         totals,
     )
     key_grads = Scattering(dkv_near, high_bits)
-    grad_gate_z = grad_gate_z.astype(BF16)
+
+    def total_of(kept, crossed):
+        return (kept.astype(F32) + crossed.astype(F32)).astype(BF16)
+
+    held = after((gu_crossed, down_crossed), dq_t)
+    parts = total_of(gu_kept, held[0]), total_of(down_kept, held[1])
+    grad_gate_z = after(grad_gate_z.astype(BF16), parts)
     dq_rows = dq_t.T
     grad_normed = unproject(
         jnp.zeros((tokens, features), F32),
@@ -2339,12 +2409,7 @@
         EARLY_TILE,
         near_specs(early_shard, EARLY_TILE, gate_tiles + conv_tiles + 2),
     )
-
-    def total_of(kept, crossed):
-        return (kept.astype(F32) + crossed.astype(F32)).astype(BF16)
-
-    parts = total_of(gu_kept, gu_crossed), total_of(down_kept, down_crossed)
-    later = after(later, (key_grads.advance(grad_normed), parts))
+    later = after(later, key_grads.advance(grad_normed))
     dx, db, dc, dt_grad, small_ssd = ssd_backward(
         count,
         act,

time: 577 us -> 566 us (0.981)
  waiting for transfers between devices: 22.5 us -> 4.58 us
  Pallas kernels: 456 us -> 464 us
    ppermute x15 -> x12, waiting for transfers between devices: 17.9 us -> 0.03 us  [swapped(): lax.ppermute(block, axis, [(i, i ^ bit) for i in range(lax.axis_size(axis...]
    pallas_call x1, Pallas kernels: 58.7 us -> 70.3 us  [front(): pl.pallas_call(functools.partial(front_kernel, count, channels // EARLY_T...]
    ppermute x15 -> x12, starting transfers between devices: 16.2 us -> 14.5 us  [swapped(): lax.ppermute(block, axis, [(i, i ^ bit) for i in range(lax.axis_size(axis...]
  transfers between devices with their start and end apart: 17 -> 14, of which waited for: 2 -> 1; matrix products, arithmetic and copies ran while one was open for 7% -> 7% of each run, Pallas kernels for 64% -> 64%
where the time goes in v5:
time: 566 us; the launch traced here: 557 us
  Pallas kernels  464 us (82%)
  local copies, waits for them, and re-layouts  28.4 us (5%)
  other arithmetic  28 us (5%)
  starting transfers between devices  16.1 us (3%)
  between operations  14.9 us (3%)
    pallas_call x1, Pallas kernels, reduce_grads(): pl.pallas_call(functools.partial(grads_kernel, count, split, early_units,...  141 us
    pallas_call x1, Pallas kernels, front(): pl.pallas_call(functools.partial(front_kernel, count, channels // EARLY_T...  70.3 us
    pallas_call x1, Pallas kernels, mix_backward(): pl.pallas_call(functools.partial(mix_backward_kernel, count), in_specs=[v...  51.1 us
    pallas_call x1, Pallas kernels, mix_forward(): pl.pallas_call(functools.partial(mix_forward_kernel, count), in_specs=[vm...  47.6 us
    pallas_call x4, Pallas kernels, block_grads(): pl.pallas_call(functools.partial(block_grads_kernel, steps), grid=(column...  26.6 us
    pallas_call x1, Pallas kernels, mlp_both(): pl.pallas_call(mlp_kernel, grid_spec=pltpu.PrefetchScalarGridSpec(num_sca...  25.7 us
    pallas_call x1, Pallas kernels, ssd_backward(): pl.pallas_call(ssd_backward_kernel, grid=(count, NGROUP), in_specs=specs...  25 us
    pallas_call x1, Pallas kernels, early_back(): pl.pallas_call(functools.partial(early_back_kernel, count), grid=(tiles,)...  20.4 us
  transfers between devices with their start and end apart: 14, of which 1 were waited for; matrix products, arithmetic and copies ran while one was open for 7% of the time, Pallas kernels for 64%

profile of v5, /device:TPU:0, one launch (start us, length us, event | category | flops | bytes accessed | tf_op | source)
XLA Modules:
  0.0 557.3 jit_solution(10195949494688627501)
XLA Ops:
  15.1 1.9 constant_dynamic-update-slice_fusion.2.tall_ref.own_ref
  17.0 70.3 %front.1 = (bf16[512,1024]{1,0:T(8,128)(2,1)}, bf16[3,256,4352]{2,1,0:T(8,128)(2,1)}, bf16[3,512,1024]{2,1,0:T(8,128)(2,1)}, f32[512,1792]{1,0:T(8,128)}, f32[16...) custom-call(bf16[512,1024]{1,0:T(8,128)(2,1)} %bitcast.70, ...), custom_call_target="tpu_custom_call" | custom-call | flops 4563402752 | bytes 20971520 | tf_op jit(solution)/shard_map/front/pallas_call | solution.py:2214
  90.7 7.0 %ssd_state.1 = (f32[512,128]{1,0:T(8,128)}, f32[512,128]{1,0:T(8,128)}, f32[2,128,256]{2,1,0:T(8,128)}, f32[512,128]{1,0:T(8,128)}, f32[2,8,128]{2,1,0:T(8,128)}, /*index=5*/f32[2,1536,128]{2,1,0:T(8,128)}) custom-call(f32[512,1792]{1,0:T(8,128)} %get-tuple-element.89.act_ref.x_ref.b_ref.c_ref, f32[512,256]{1,0:T(8,128)} %get-tuple-element.90.dt_ref, ...), custom_call_target="tpu_custom_call" | custom-call | flops 1000000000 | bytes 8388608 | tf_op jit(solution)/shard_map/ssd_state/pallas_call | solution.py:162
  98.3 47.6 %mix_forward.1 = (bf16[512,512]{1,0:T(8,128)(2,1)}, f32[2,8,256]{2,1,0:T(8,128)}, bf16[8,2,256,256]{3,2,1,0:T(8,128)(2,1)}, bf16[2,1536,128]{2,1,0:T(8,128)(2,1)}, f32[8,2,8,128]{3,2,1,0:T(8,128)}) custom-call(s32[2,8,256]{2,1,0:T(8,128)} %broadcast_in_dim.57.start_ref, bf16[512,512]{1,0:T(8,128)(2,1)} %get-tuple-element.94.q_ref, ...), custom_call_target="tpu_custom_call" | custom-call | flops 8388608000 | bytes 4194304 | tf_op jit(solution)/shard_map/mix_forward/pallas_call | solution.py:1741
  146.0 10.2 %ssd_forward.1.y_ref = f32[512,1536]{1,0:T(8,128)} custom-call(f32[512,1792]{1,0:T(8,128)} %get-tuple-element.89.act_ref.x_ref.b_ref.c_ref, f32[512,1792]{1,0:T(8,128)} %get-tuple-element.89.act_ref.x_ref.b_ref.c_ref, f32[512,1792]{1,0:T(8,128)} %get-tuple-element.89.act_ref.x_ref.b_ref.c_ref, f32[512,128]{1,0:T(8,128)} %get-tuple-element.91.step_ref, ...), custom_call_target="tpu_custom_call" | custom-call | flops 1258291200 | bytes 8388608 | tf_op jit(solution)/shard_map/ssd_forward/pallas_call | solution.py:396
  156.2 3.8 multiply_reduce_fusion.2
  161.9 8.4 %out_project.1 = (f32[512,1024]{1,0:T(8,128)}, bf16[512,1024]{1,0:T(8,128)(2,1)}) custom-call(bf16[512,1024]{1,0:T(8,128)(2,1)} %bitcast.71, bf16[512,1536]{1,0:T(8,128)(2,1)} %multiply_convert_fusion.1.mixed_ref.mix_ref, bf16[512,512]{1,0:T(8,128)(2,1)} %get-tuple-element.100.heads_ref.attended_ref, f32[1,1024]{1,0:T(1,128)} %bitcast.80, ...), custom_call_target="tpu_custom_call" | custom-call | flops 2147483648 | bytes 12582912 | tf_op jit(solution)/shard_map/out_project/pallas_call | solution.py:591
  170.3 25.7 %mlp_both.1 = (bf16[512,1024]{1,0:T(8,128)(2,1)}, f32[512,1024]{1,0:T(8,128)}, bf16[512,1024]{1,0:T(8,128)(2,1)}, f32[1,1024]{1,0:T(1,128)}, bf16[512,2048]{1,0:T(8,128)(2,1)}, /*index=5*/bf16[2,512,2048]{2,1,0:T(8,128)(2,1)}) custom-call(s32[1]{0:T(128)} %bitcast.place_ref, bf16[512,1024]{1,0:T(8,128)(2,1)} %get-tuple-element.115.normed_ref.left_ref, ...), custom_call_target="tpu_custom_call" | custom-call | flops 12884901888 | bytes 31457280 | tf_op jit(solution)/shard_map/mlp_both/pallas_call | solution.py:711
  196.1 8.8 %block_grads.4 = bf16[512,4096]{1,0:T(8,128)(2,1)} custom-call(bf16[512,1024]{1,0:T(8,128)(2,1)} %get-tuple-element.115.normed_ref.left_ref, bf16[2,512,2048]{2,1,0:T(8,128)(2,1)} %get-tuple-element.110.right_ref), custom_call_target="tpu_custom_call" | custom-call | flops 2147483648 | bytes 6291456 | tf_op jit(solution)/shard_map/block_grads/pallas_call | solution.py:1037
  205.3 4.3 block_grads.5
  209.6 7.5 %out_unproject.1 = (f32[512,1536]{1,0:T(8,128)}, bf16[512,512]{1,0:T(8,128)(2,1)}) custom-call(bf16[512,1024]{1,0:T(8,128)(2,1)} %get-tuple-element.112.branch_ref, bf16[512,1024]{1,0:T(8,128)(2,1)} %constant_dynamic-update-slice_fusion.2.tall_ref.own_ref, bf16[3,512,1024]{2,1,0:T(8,128)(2,1)} %get-tuple-element.101.others_ref), custom_call_target="tpu_custom_call" | custom-call | flops 2147483648 | bytes 12582912 | tf_op jit(solution)/shard_map/out_unproject/pallas_call | solution.py:618
  217.2 4.5 block_grads.7
  222.3 9.0 %block_grads.6 = (bf16[256,4096]{1,0:T(8,128)(2,1)}, bf16[256,4096]{1,0:T(8,128)(2,1)}) custom-call(bf16[512,1024]{1,0:T(8,128)(2,1)} %get-tuple-element.115.normed_ref.left_ref, bf16[2,512,2048]{2,1,0:T(8,128)(2,1)} %get-tuple-element.110.right_ref, bf16[512,4096]{1,0:T(8,128)(2,1)} %collective-permute-done.6.refs_0_), custom_call_target="tpu_custom_call" | custom-call | flops 2147483648 | bytes 6291456 | tf_op jit(solution)/shard_map/block_grads/pallas_call | solution.py:1037
  232.8 2.8 multiply_reduce_fusion
  236.6 5.1 multiply_multiply_fusion
  241.7 5.4 state_grad.1.state_ref
  247.1 51.1 %mix_backward.1 = (bf16[512,512]{1,0:T(8,128)(2,1)}, bf16[4,2,256,256]{3,2,1,0:T(8,128)(2,1)}, bf16[2,1536,128]{2,1,0:T(8,128)(2,1)}) custom-call(s32[2,8,256]{2,1,0:T(8,128)} %broadcast_in_dim.57.start_ref, bf16[512,512]{1,0:T(8,128)(2,1)} %get-tuple-element.94.q_ref, bf16[8,2,256,256]{3,2,1,0:T(8,128)(2,1)} %get-tuple-element.121.table_ref, ...), custom_call_target="tpu_custom_call" | custom-call | flops 16777216000 | bytes 8388608 | tf_op jit(solution)/shard_map/mix_backward/pallas_call | solution.py:1904
  298.2 2.2 copy.61
  301.5 5.1 collective-permute-start.10
  306.6 3.7 add_convert_fusion
  310.4 2.6 add_convert_fusion.1
  313.0 1.6 broadcast_in_dim.60.base_ref
  314.6 6.1 %unproject.2.base_ref = f32[512,1024]{1,0:T(8,128)} custom-call(f32[512,1024]{1,0:T(8,128)} %broadcast_in_dim.60.base_ref, bf16[512,1536]{1,0:T(8,128)(2,1)} %get-tuple-element.128.grad_ref.gate_ref, bf16[256,4352]{1,0:T(8,128)(2,1)} %copy-done.1, bf16[3,256,4352]{2,1,0:T(8,128)(2,1)} %get-tuple-element.129.refs_1_.refs_2_.refs_3_, ...), custom_call_target="tpu_custom_call" | custom-call | flops 1610612736 | bytes 4718592 | tf_op jit(solution)/shard_map/unproject/pallas_call | solution.py:557
  320.7 4.7 unproject.3.base_ref
  325.6 4.2 collective-permute-start.11
  329.9 25.0 %ssd_backward.1 = (f32[512,1536]{1,0:T(8,128)}, f32[512,128]{1,0:T(8,128)}, f32[512,128]{1,0:T(8,128)}, bf16[512,256]{1,0:T(8,128)(2,1)}, f32[2,8,128]{2,1,0:T(8,128)}) custom-call(f32[512,1792]{1,0:T(8,128)} %get-tuple-element.89.act_ref.x_ref.b_ref.c_ref, f32[512,1792]{1,0:T(8,128)} %get-tuple-element.89.act_ref.x_ref.b_ref.c_ref, ...), custom_call_target="tpu_custom_call" | custom-call | flops 3145728000 | bytes 16777216 | tf_op jit(solution)/shard_map/ssd_backward/pallas_call | solution.py:436
  356.6 1.9 edge_grads.1
  360.8 4.5 collective-permute-done.12.came_ref
  366.0 20.4 %early_back.1 = (bf16[512,2304]{1,0:T(8,128)(2,1)}, f32[8,1792]{1,0:T(8,128)}, bf16[512,1024]{1,0:T(8,128)(2,1)}, f32[1,1024]{1,0:T(1,128)}) custom-call(f32[512,1024]{1,0:T(8,128)} %unproject.3.base_ref, bf16[512,256]{1,0:T(8,128)(2,1)} %bitcast.69, f32[512,1536]{1,0:T(8,128)} %get-tuple-element.135.dx_ref, f32[512,128]{1,0:T(8,128)} %get-tuple-element.137.db_ref, ...), custom_call_target="tpu_custom_call" | custom-call | flops 2415919104 | bytes 20971520 | tf_op jit(solution)/shard_map/early_back/pallas_call | solution.py:953
  389.6 141.3 %reduce_grads.1 = (bf16[256,2048]{1,0:T(8,128)(2,1)}, bf16[256,1536]{1,0:T(8,128)(2,1)}, bf16[256,512]{1,0:T(8,128)(2,1)}, bf16[512,1024]{1,0:T(8,128)(2,1)}, f32[320,128]{1,0:T(8,128)}) custom-call(bf16[512,1024]{1,0:T(8,128)(2,1)} %get-tuple-element.144.one_ref, bf16[512,1536]{1,0:T(8,128)(2,1)} %multiply_convert_fusion.1.mixed_ref.mix_ref, ...), custom_call_target="tpu_custom_call" | custom-call | flops 6499999744 | bytes 31457280 | tf_op jit(solution)/shard_map/reduce_grads/pallas_call | solution.py:1422
  537.1 4.5 finish.1
  544.3 4.2 convert_element_type.75
  (121 shorter events, 36.7 us)
Async XLA Ops:
  7.2 6.2 %copy-start.12 = (bf16[256,24]{0,1:T(8,128)(2,1)S(1)}, bf16[256,24]{0,1:T(8,128)(2,1)}, u32[]{:S(2)}) copy-start(bf16[256,24]{0,1:T(8,128)(2,1)} %param.24) | copy-start | bytes 36868
  7.2 6.3 %copy-start.8 = (bf16[384,1024]{1,0:T(8,128)(2,1)S(1)}, bf16[384,1024]{1,0:T(8,128)(2,1)}, u32[]{:S(2)}) copy-start(bf16[384,1024]{1,0:T(8,128)(2,1)} %param.31) | copy-start | bytes 2359300
  7.2 7.2 %copy-start.14 = (f32[1792]{0:T(1024)S(1)}, f32[1792]{0:T(1024)}, u32[]{:S(2)}) copy-start(f32[1792]{0:T(1024)} %param.26) | copy-start | bytes 21508
  7.2 7.9 %copy-start.9 = (bf16[256,512]{1,0:T(8,128)(2,1)S(1)}, bf16[256,512]{1,0:T(8,128)(2,1)}, u32[]{:S(2)}) copy-start(bf16[256,512]{1,0:T(8,128)(2,1)} %param.32) | copy-start | bytes 786436
  7.2 537.0 %all-reduce.11.cloned.1.call-start = ((), (), s32[]{:S(2)}) async-start(), calls=%async_computation | async-start | bytes 6291456 | tf_op jit(solution)/shard_map/psum | solution.py:2461
  15.1 1.9 copy-start.1
  17.0 72.5 %copy-start.16 = (f32[24]{0:T(128)S(1)}, f32[24]{0:T(128)}, u32[]{:S(2)}) copy-start(f32[24]{0:T(128)} %param.29) | copy-start | bytes 292
  17.0 73.2 %copy-start.17 = (f32[24]{0:T(128)S(1)}, f32[24]{0:T(128)}, u32[]{:S(2)}) copy-start(f32[24]{0:T(128)} %param.28) | copy-start | bytes 292
  17.0 73.2 %copy-start.18 = (f32[24]{0:T(128)S(1)}, f32[24]{0:T(128)}, u32[]{:S(2)}) copy-start(f32[24]{0:T(128)} %param.27) | copy-start | bytes 292
  87.3 74.1 %collective-permute-start = (bf16[256,4096]{1,0:T(8,128)(2,1)}, bf16[256,4096]{1,0:T(8,128)(2,1)}, u32[]{:S(2)}, u32[]{:S(2)}) collective-permute-start(bf16[256,4096]{1,0:T(8,128)(2,1)} %refs_4_), channel_id=1, source_target_pairs={{0,2},{1,3},{2,0},{3,1},{4,6},{5,7},{6,4},{7,5},{8,10},{9,11},{10,... | collective-permute-start | bytes 6291464 | tf_op jit(solution)/shard_map/ppermute | solution.py:1091
  87.9 82.4 %collective-permute-start.1 = (bf16[256,4096]{1,0:T(8,128)(2,1)}, bf16[256,4096]{1,0:T(8,128)(2,1)}, u32[]{:S(2)}, u32[]{:S(2)}) collective-permute-start(bf16[256,4096]{1,0:T(8,128)(2,1)} %refs_4_), channel_id=1, source_target_pairs={{0,1},{1,0},{2,3},{3,2},{4,5},{5,4},{6,7},{7,6},{8,9},{9,8},{10,11... | collective-permute-start | bytes 6291464 | tf_op jit(solution)/shard_map/ppermute | solution.py:1091
  87.9 74.0 %collective-permute-start.3 = (bf16[512,1024]{1,0:T(8,128)(2,1)}, bf16[512,1024]{1,0:T(8,128)(2,1)}, u32[]{:S(2)}, u32[]{:S(2)}) collective-permute-start(bf16[512,1024]{1,0:T(8,128)(2,1)} %refs_8_), channel_id=1, source_target_pairs={{0,2},{1,3},{2,0},{3,1},{4,6},{5,7},{6,4},{7,5},{8,10},{9,11},{10,... | collective-permute-start | bytes 3145736 | tf_op jit(solution)/shard_map/ppermute | solution.py:1091
  156.2 3.8 copy-start.11
  161.4 8.9 %collective-permute-start.2 = (bf16[256,4096]{1,0:T(8,128)(2,1)}, bf16[256,4096]{1,0:T(8,128)(2,1)}, u32[]{:S(2)}, u32[]{:S(2)}) collective-permute-start(bf16[256,4096]{1,0:T(8,128)(2,1)} %collective-permute-done.refs_1_.refs_5_), channel_id=1, source_target_pairs={{0,1},{1,0},{2,3},{3,2},{4,5},{5,4},{6,7},{7,6},{8,9},{9,8},{10,11... | collective-permute-start | bytes 6291464 | tf_op jit(solution)/shard_map/ppermute | solution.py:1091
  161.4 8.9 %collective-permute-start.4 = (bf16[512,1024]{1,0:T(8,128)(2,1)}, bf16[512,1024]{1,0:T(8,128)(2,1)}, u32[]{:S(2)}, u32[]{:S(2)}) collective-permute-start(bf16[512,1024]{1,0:T(8,128)(2,1)} %refs_8_), channel_id=1, source_target_pairs={{0,1},{1,0},{2,3},{3,2},{4,5},{5,4},{6,7},{7,6},{8,9},{9,8},{10,11... | collective-permute-start | bytes 3145736 | tf_op jit(solution)/shard_map/ppermute | solution.py:1091
  161.9 8.4 %collective-permute-start.5 = (bf16[512,1024]{1,0:T(8,128)(2,1)}, bf16[512,1024]{1,0:T(8,128)(2,1)}, u32[]{:S(2)}, u32[]{:S(2)}) collective-permute-start(bf16[512,1024]{1,0:T(8,128)(2,1)} %collective-permute-done.3.refs_9_), channel_id=1, source_target_pairs={{0,1},{1,0},{2,3},{3,2},{4,5},{5,4},{6,7},{7,6},{8,9},{9,8},{10,11... | collective-permute-start | bytes 3145736 | tf_op jit(solution)/shard_map/ppermute | solution.py:1091
  204.8 17.5 %collective-permute-start.6 = (bf16[512,4096]{1,0:T(8,128)(2,1)}, bf16[512,4096]{1,0:T(8,128)(2,1)}, u32[]{:S(2)}, u32[]{:S(2)}) collective-permute-start(bf16[512,4096]{1,0:T(8,128)(2,1)} %block_grads.4), channel_id=1, source_target_pairs={{0,1},{1,0},{2,3},{3,2},{4,5},{5,4},{6,7},{7,6},{8,9},{9,8},{10,11... | collective-permute-start | bytes 12582920 | tf_op jit(solution)/shard_map/ppermute | solution.py:1091
  209.6 7.6 %collective-permute-start.7 = (bf16[1024,1024]{1,0:T(8,128)(2,1)}, bf16[1024,1024]{1,0:T(8,128)(2,1)}, u32[]{:S(2)}, u32[]{:S(2)}) collective-permute-start(bf16[1024,1024]{1,0:T(8,128)(2,1)} %block_grads.5), channel_id=1, source_target_pairs={{0,1},{1,0},{2,3},{3,2},{4,5},{5,4},{6,7},{7,6},{8,9},{9,8},{10,11... | collective-permute-start | bytes 6291464 | tf_op jit(solution)/shard_map/ppermute | solution.py:1091
  221.7 84.9 %collective-permute-start.9 = (bf16[512,1024]{1,0:T(8,128)(2,1)}, bf16[512,1024]{1,0:T(8,128)(2,1)}, u32[]{:S(2)}, u32[]{:S(2)}) collective-permute-start(bf16[512,1024]{1,0:T(8,128)(2,1)} %get-tuple-element.118), channel_id=1, source_target_pairs={{0,2},{1,3},{2,0},{3,1},{4,6},{5,7},{6,4},{7,5},{8,10},{9,11},{10,... | collective-permute-start | bytes 3145736 | tf_op jit(solution)/shard_map/ppermute | solution.py:1091
  231.4 75.3 %collective-permute-start.8 = (bf16[256,4096]{1,0:T(8,128)(2,1)}, bf16[256,4096]{1,0:T(8,128)(2,1)}, u32[]{:S(2)}, u32[]{:S(2)}) collective-permute-start(bf16[256,4096]{1,0:T(8,128)(2,1)} %get-tuple-element.116), channel_id=1, source_target_pairs={{0,2},{1,3},{2,0},{3,1},{4,6},{5,7},{6,4},{7,5},{8,10},{9,11},{10,... | collective-permute-start | bytes 6291464 | tf_op jit(solution)/shard_map/ppermute | solution.py:1091
  232.8 2.8 copy-start
  232.8 3.8 copy-start.2
  298.2 8.4 %copy-start.3 = (bf16[256,4096]{1,0:T(8,128)(2,1)S(1)}, bf16[256,4096]{1,0:T(8,128)(2,1)}, u32[]{:S(2)}) copy-start(bf16[256,4096]{1,0:T(8,128)(2,1)} %get-tuple-element.120) | copy-start | bytes 6291460
  301.5 24.0 %collective-permute-start.10 = (bf16[2,2,256,256]{3,2,1,0:T(8,128)(2,1)S(1)}, bf16[2,2,256,256]{3,2,1,0:T(8,128)(2,1)S(1)}, u32[]{:S(2)}, u32[]{:S(2)}) collective-permute-start(bf16[2,2,256,256]{3,2,1,0:T(8,128)(2,1)S(1)} %slice.85), channel_id=1, source_target_pairs={{0,8},{4,12},{8,0},{12,4},{16,24},{20,28},{24,16},{28,20},{1,9},{5... | collective-permute-start | bytes 1572872 | tf_op jit(solution)/shard_map/ppermute | solution.py:1091
  306.6 3.8 copy-start.5
  320.7 4.7 copy-start.6
  325.6 34.5 %collective-permute-start.11 = (bf16[1,2,256,256]{3,2,1,0:T(8,128)(2,1)S(1)}, bf16[1,2,256,256]{3,2,1,0:T(8,128)(2,1)S(1)}, u32[]{:S(2)}, u32[]{:S(2)}) collective-permute-start(bf16[1,2,256,256]{3,2,1,0:T(8,128)(2,1)S(1)} %slice.109), channel_id=1, source_target_pairs={{0,16},{4,20},{8,24},{12,28},{16,0},{20,4},{24,8},{28,12},{1,17},{... | collective-permute-start | bytes 786440 | tf_op jit(solution)/shard_map/ppermute | solution.py:1091
  329.9 25.0 %copy-start.7 = (bf16[512,1024]{1,0:T(8,128)(2,1)S(1)}, bf16[512,1024]{1,0:T(8,128)(2,1)}, u32[]{:S(2)}) copy-start(bf16[512,1024]{1,0:T(8,128)(2,1)} %get-tuple-element.144.one_ref) | copy-start | bytes 3145732
  356.6 3.4 copy-start.13
  358.5 6.9 %collective-permute-start.12 = (f32[16,1792]{1,0:T(8,128)}, f32[16,1792]{1,0:T(8,128)S(1)}, u32[]{:S(2)}, u32[]{:S(2)}) collective-permute-start(f32[16,1792]{1,0:T(8,128)} %edge_grads.1), channel_id=1, source_target_pairs={{4,0},{8,4},{12,8},{16,12},{20,16},{24,20},{28,24},{5,1},{9,5},{13... | collective-permute-start | bytes 344072 | tf_op jit(solution)/shard_map/ppermute | solution.py:1087
  366.0 22.9 %copy-start.15 = (f32[1,1024]{1,0:T(1,128)S(1)}, f32[1,1024]{1,0:T(1,128)}, u32[]{:S(2)}) copy-start(f32[1,1024]{1,0:T(1,128)} %get-tuple-element.149) | copy-start | bytes 12292
  544.3 4.2 copy-start.4
  (2 other events, 1.3 us)
Sparse Core Ops, SparseCore 0:
  313.1 160.8 all-reduce.10

commit v6 on v5

--- a/solution.py
+++ b/solution.py
@@ -1944,15 +1944,18 @@
     weight_ref,
     bias_ref,
     normed_ref,
-    others_ref,
-    tall_others,
-    conv_ref,
+    others_out,
+    tall_out,
+    conv_out,
     edge_ref,
-    act_ref,
+    act_out,
     dt_ref,
     q_ref,
+    gate_out,
+    table_ref,
+    conv_ref,
+    act_ref,
     gate_ref,
-    table_ref,
     edge_x,
     near,
     tall_near,
@@ -1964,6 +1967,7 @@
     tall_sems,
     table_sems,
     edge_sems,
+    out_sems,
 ):
     here = lax.axis_index("ctx")
     batch = table.shape[1]
@@ -2130,9 +2134,32 @@
             total = part if total is None else total + part
         return total
 
+    def others_copy(k):
+        return pltpu.make_async_copy(
+            near.at[:, :, columns(k)], others_out.at[:, :, columns(k)], out_sems.at[0, k]
+        )
+
+    def conv_copy(k):
+        return pltpu.make_async_copy(
+            conv_ref.at[:, tile(k - 1)], conv_out.at[:, tile(k - 1)], out_sems.at[1, k]
+        )
+
+    def act_copy(k):
+        return pltpu.make_async_copy(
+            act_ref.at[:, tile(k - 1)], act_out.at[:, tile(k - 1)], out_sems.at[2, k]
+        )
+
+    def gate_copy(k):
+        return pltpu.make_async_copy(
+            gate_ref.at[:, tile(k - gate_from)],
+            gate_out.at[:, tile(k - gate_from)],
+            out_sems.at[1, k],
+        )
+
     def compute(k):
         core_copy(k).wait()
         last_copy(k).wait()
+        others_copy(k).start()
         value = product(lambda at: normed_ref[:, at], k)
 
         @pl.when(k == 0)
@@ -2147,14 +2174,17 @@
             conv_ref[:, place] = value
             taps = weight_ref[:, place]
             bias = bias_ref[:, place]
+            edges = product(lambda at: edge_x[:, :, at].reshape(batch * 16, size), k)
             for b in range(batch):
-                edge = product(lambda at, b=b: edge_x[b, :, at], k)[16 - EDGE :]
+                edge = edges[(b + 1) * 16 - EDGE : (b + 1) * 16]
                 edge_ref[b * EDGE : (b + 1) * EDGE, place] = edge
                 span = slice(b * rows, (b + 1) * rows)
                 total, _ = conv_sums(
                     conv_inputs(edge, value[span]), taps, bias, start_ref[span]
                 )
                 act_ref[span, place] = total * sigmoid(total)
+            conv_copy(k).start()
+            act_copy(k).start()
 
         @pl.when(k == conv_tiles + 1)
         def _():
@@ -2167,6 +2197,7 @@
         @pl.when(k >= gate_from)
         def _():
             gate_ref[:, tile(k - gate_from)] = value
+            gate_copy(k).start()
 
     def one_step(t, carry):
         @pl.when(t < chunks)
@@ -2185,15 +2216,31 @@
         return carry
 
     lax.fori_loop(0, chunks + 4, one_step, 0)
-    others_ref[...] = near[...]
-
     def end_tall(k, carry):
         tall_core(k).wait()
         tall_last(k).wait()
         return carry
 
     lax.fori_loop(0, tall_chunks, end_tall, 0)
-    tall_others[...] = tall_near[...]
+    whole_tall = pltpu.make_async_copy(tall_near, tall_out, out_sems.at[2, 0])
+    whole_tall.start()
+
+    def end_outs(k, carry):
+        others_copy(k).wait()
+
+        @pl.when((k > 0) & (k <= conv_tiles))
+        def _():
+            conv_copy(k).wait()
+            act_copy(k).wait()
+
+        @pl.when(k >= gate_from)
+        def _():
+            gate_copy(k).wait()
+
+        return carry
+
+    lax.fori_loop(0, chunks, end_outs, 0)
+    whole_tall.wait()
     for i in range(1, half):
         table_copy(i).wait()
     table_ref[...] = table[...]
@@ -2207,6 +2254,7 @@
     chunks = columns // EARLY_TILE
     half = count // 2
     vmem = pl.BlockSpec(memory_space=pltpu.VMEM)
+    hbm = pl.BlockSpec(memory_space=pl.ANY)
     dma = pltpu.SemaphoreType.DMA
     low = functools.partial(jax.ShapeDtypeStruct, dtype=BF16)
     wide = functools.partial(jax.ShapeDtypeStruct, dtype=F32)
@@ -2216,7 +2264,7 @@
             front_kernel, count, channels // EARLY_TILE, DSSM // EARLY_TILE
         ),
         in_specs=[vmem] * 7,
-        out_specs=[vmem] * 10,
+        out_specs=[vmem, hbm, hbm, hbm, vmem, hbm, vmem, vmem, hbm, vmem],
         out_shape=[
             low((tokens, depth)),
             low((3, size, columns)),
@@ -2230,6 +2278,9 @@
             low(table),
         ],
         scratch_shapes=[
+            pltpu.VMEM((tokens, channels), F32),
+            pltpu.VMEM((tokens, channels), F32),
+            pltpu.VMEM((tokens, DSSM), F32),
             pltpu.VMEM((batch, 16, depth), BF16),
             pltpu.VMEM((3, size, columns), BF16),
             pltpu.VMEM((3,) + tall.shape, BF16),
@@ -2241,6 +2292,7 @@
             dma((4, 2, tall.shape[1] // EARLY_TILE)),
             dma((2, half)),
             dma((2, batch)),
+            dma((3, chunks)),
         ],
         compiler_params=pltpu.CompilerParams(
             collective_id=4, has_side_effects=True, vmem_limit_bytes=KERNEL_VMEM

time: 566 us -> 562 us (level)
  transfers between devices with their start and end apart: 14 -> 14, of which waited for: 1 -> 1; matrix products, arithmetic and copies ran while one was open for 7% -> 7% of each run, Pallas kernels for 64% -> 65%
where the time goes in v6:
time: 562 us; the launch traced here: 552 us
  Pallas kernels  459 us (82%)
  local copies, waits for them, and re-layouts  28.3 us (5%)
  other arithmetic  28 us (5%)
  starting transfers between devices  16.1 us (3%)
  between operations  14.9 us (3%)
    pallas_call x1, Pallas kernels, reduce_grads(): pl.pallas_call(functools.partial(grads_kernel, count, split, early_units,...  141 us
    pallas_call x1, Pallas kernels, front(): pl.pallas_call(functools.partial(front_kernel, count, channels // EARLY_T...  65.9 us
    pallas_call x1, Pallas kernels, mix_backward(): pl.pallas_call(functools.partial(mix_backward_kernel, count), in_specs=[v...  51.1 us
    pallas_call x1, Pallas kernels, mix_forward(): pl.pallas_call(functools.partial(mix_forward_kernel, count), in_specs=[vm...  47.6 us
    pallas_call x4, Pallas kernels, block_grads(): pl.pallas_call(functools.partial(block_grads_kernel, steps), grid=(column...  26.6 us
    pallas_call x1, Pallas kernels, mlp_both(): pl.pallas_call(mlp_kernel, grid_spec=pltpu.PrefetchScalarGridSpec(num_sca...  25.7 us
    pallas_call x1, Pallas kernels, ssd_backward(): pl.pallas_call(ssd_backward_kernel, grid=(count, NGROUP), in_specs=specs...  25 us
    pallas_call x1, Pallas kernels, early_back(): pl.pallas_call(functools.partial(early_back_kernel, count), grid=(tiles,)...  20.4 us
  transfers between devices with their start and end apart: 14, of which 1 were waited for; matrix products, arithmetic and copies ran while one was open for 7% of the time, Pallas kernels for 65%

profile of v6, /device:TPU:0, one launch (start us, length us, event | category | flops | bytes accessed | tf_op | source)
XLA Modules:
  0.0 552.0 jit_solution(9804642706654039049)
XLA Ops:
  15.1 1.9 constant_dynamic-update-slice_fusion.2.tall_ref.own_ref
  17.0 65.9 %front.1 = (bf16[512,1024]{1,0:T(8,128)(2,1)}, bf16[3,256,4352]{2,1,0:T(8,128)(2,1)}, bf16[3,512,1024]{2,1,0:T(8,128)(2,1)}, f32[512,1792]{1,0:T(8,128)}, f32[16...) custom-call(bf16[512,1024]{1,0:T(8,128)(2,1)} %bitcast.70, ...), custom_call_target="tpu_custom_call" | custom-call | flops 4563402752 | bytes 20971520 | tf_op jit(solution)/shard_map/front/pallas_call | solution.py:2262
  86.2 7.0 %ssd_state.1 = (f32[512,128]{1,0:T(8,128)}, f32[512,128]{1,0:T(8,128)}, f32[2,128,256]{2,1,0:T(8,128)}, f32[512,128]{1,0:T(8,128)}, f32[2,8,128]{2,1,0:T(8,128)}, /*index=5*/f32[2,1536,128]{2,1,0:T(8,128)}) custom-call(f32[512,1792]{1,0:T(8,128)} %get-tuple-element.89.act_ref.x_ref.b_ref.c_ref, f32[512,256]{1,0:T(8,128)} %get-tuple-element.90.dt_ref, ...), custom_call_target="tpu_custom_call" | custom-call | flops 1000000000 | bytes 8388608 | tf_op jit(solution)/shard_map/ssd_state/pallas_call | solution.py:162
  93.9 47.6 %mix_forward.1 = (bf16[512,512]{1,0:T(8,128)(2,1)}, f32[2,8,256]{2,1,0:T(8,128)}, bf16[8,2,256,256]{3,2,1,0:T(8,128)(2,1)}, bf16[2,1536,128]{2,1,0:T(8,128)(2,1)}, f32[8,2,8,128]{3,2,1,0:T(8,128)}) custom-call(s32[2,8,256]{2,1,0:T(8,128)} %broadcast_in_dim.57.start_ref, bf16[512,512]{1,0:T(8,128)(2,1)} %get-tuple-element.94.q_ref, ...), custom_call_target="tpu_custom_call" | custom-call | flops 8388608000 | bytes 4194304 | tf_op jit(solution)/shard_map/mix_forward/pallas_call | solution.py:1741
  141.5 10.2 %ssd_forward.1.y_ref = f32[512,1536]{1,0:T(8,128)} custom-call(f32[512,1792]{1,0:T(8,128)} %get-tuple-element.89.act_ref.x_ref.b_ref.c_ref, f32[512,1792]{1,0:T(8,128)} %get-tuple-element.89.act_ref.x_ref.b_ref.c_ref, f32[512,1792]{1,0:T(8,128)} %get-tuple-element.89.act_ref.x_ref.b_ref.c_ref, f32[512,128]{1,0:T(8,128)} %get-tuple-element.91.step_ref, ...), custom_call_target="tpu_custom_call" | custom-call | flops 1258291200 | bytes 8388608 | tf_op jit(solution)/shard_map/ssd_forward/pallas_call | solution.py:396
  151.7 3.8 multiply_reduce_fusion.2
  157.5 8.4 %out_project.1 = (f32[512,1024]{1,0:T(8,128)}, bf16[512,1024]{1,0:T(8,128)(2,1)}) custom-call(bf16[512,1024]{1,0:T(8,128)(2,1)} %bitcast.71, bf16[512,1536]{1,0:T(8,128)(2,1)} %multiply_convert_fusion.1.mixed_ref.mix_ref, bf16[512,512]{1,0:T(8,128)(2,1)} %get-tuple-element.100.heads_ref.attended_ref, f32[1,1024]{1,0:T(1,128)} %bitcast.80, ...), custom_call_target="tpu_custom_call" | custom-call | flops 2147483648 | bytes 12582912 | tf_op jit(solution)/shard_map/out_project/pallas_call | solution.py:591
  165.9 25.7 %mlp_both.1 = (bf16[512,1024]{1,0:T(8,128)(2,1)}, f32[512,1024]{1,0:T(8,128)}, bf16[512,1024]{1,0:T(8,128)(2,1)}, f32[1,1024]{1,0:T(1,128)}, bf16[512,2048]{1,0:T(8,128)(2,1)}, /*index=5*/bf16[2,512,2048]{2,1,0:T(8,128)(2,1)}) custom-call(s32[1]{0:T(128)} %bitcast.place_ref, bf16[512,1024]{1,0:T(8,128)(2,1)} %get-tuple-element.115.normed_ref.left_ref, ...), custom_call_target="tpu_custom_call" | custom-call | flops 12884901888 | bytes 31457280 | tf_op jit(solution)/shard_map/mlp_both/pallas_call | solution.py:711
  191.6 8.8 %block_grads.4 = bf16[512,4096]{1,0:T(8,128)(2,1)} custom-call(bf16[512,1024]{1,0:T(8,128)(2,1)} %get-tuple-element.115.normed_ref.left_ref, bf16[2,512,2048]{2,1,0:T(8,128)(2,1)} %get-tuple-element.110.right_ref), custom_call_target="tpu_custom_call" | custom-call | flops 2147483648 | bytes 6291456 | tf_op jit(solution)/shard_map/block_grads/pallas_call | solution.py:1037
  200.9 4.3 block_grads.5
  205.2 7.5 %out_unproject.1 = (f32[512,1536]{1,0:T(8,128)}, bf16[512,512]{1,0:T(8,128)(2,1)}) custom-call(bf16[512,1024]{1,0:T(8,128)(2,1)} %get-tuple-element.112.branch_ref, bf16[512,1024]{1,0:T(8,128)(2,1)} %constant_dynamic-update-slice_fusion.2.tall_ref.own_ref, bf16[3,512,1024]{2,1,0:T(8,128)(2,1)} %get-tuple-element.101.others_ref), custom_call_target="tpu_custom_call" | custom-call | flops 2147483648 | bytes 12582912 | tf_op jit(solution)/shard_map/out_unproject/pallas_call | solution.py:618
  212.7 4.5 block_grads.7
  217.9 9.0 %block_grads.6 = (bf16[256,4096]{1,0:T(8,128)(2,1)}, bf16[256,4096]{1,0:T(8,128)(2,1)}) custom-call(bf16[512,1024]{1,0:T(8,128)(2,1)} %get-tuple-element.115.normed_ref.left_ref, bf16[2,512,2048]{2,1,0:T(8,128)(2,1)} %get-tuple-element.110.right_ref, bf16[512,4096]{1,0:T(8,128)(2,1)} %collective-permute-done.6.refs_0_), custom_call_target="tpu_custom_call" | custom-call | flops 2147483648 | bytes 6291456 | tf_op jit(solution)/shard_map/block_grads/pallas_call | solution.py:1037
  228.3 2.8 multiply_reduce_fusion
  232.1 5.1 multiply_multiply_fusion
  237.2 5.4 state_grad.1.state_ref
  242.6 51.1 %mix_backward.1 = (bf16[512,512]{1,0:T(8,128)(2,1)}, bf16[4,2,256,256]{3,2,1,0:T(8,128)(2,1)}, bf16[2,1536,128]{2,1,0:T(8,128)(2,1)}) custom-call(s32[2,8,256]{2,1,0:T(8,128)} %broadcast_in_dim.57.start_ref, bf16[512,512]{1,0:T(8,128)(2,1)} %get-tuple-element.94.q_ref, bf16[8,2,256,256]{3,2,1,0:T(8,128)(2,1)} %get-tuple-element.121.table_ref, ...), custom_call_target="tpu_custom_call" | custom-call | flops 16777216000 | bytes 8388608 | tf_op jit(solution)/shard_map/mix_backward/pallas_call | solution.py:1904
  293.7 2.2 copy.61
  297.0 5.1 collective-permute-start.10
  302.2 3.7 add_convert_fusion
  305.9 2.6 add_convert_fusion.1
  308.6 1.6 broadcast_in_dim.60.base_ref
  310.1 6.1 %unproject.2.base_ref = f32[512,1024]{1,0:T(8,128)} custom-call(f32[512,1024]{1,0:T(8,128)} %broadcast_in_dim.60.base_ref, bf16[512,1536]{1,0:T(8,128)(2,1)} %get-tuple-element.128.grad_ref.gate_ref, bf16[256,4352]{1,0:T(8,128)(2,1)} %copy-done.1, bf16[3,256,4352]{2,1,0:T(8,128)(2,1)} %get-tuple-element.129.refs_1_.refs_2_.refs_3_, ...), custom_call_target="tpu_custom_call" | custom-call | flops 1610612736 | bytes 4718592 | tf_op jit(solution)/shard_map/unproject/pallas_call | solution.py:557
  316.3 4.7 unproject.3.base_ref
  321.1 4.2 collective-permute-start.11
  325.4 25.0 %ssd_backward.1 = (f32[512,1536]{1,0:T(8,128)}, f32[512,128]{1,0:T(8,128)}, f32[512,128]{1,0:T(8,128)}, bf16[512,256]{1,0:T(8,128)(2,1)}, f32[2,8,128]{2,1,0:T(8,128)}) custom-call(f32[512,1792]{1,0:T(8,128)} %get-tuple-element.89.act_ref.x_ref.b_ref.c_ref, f32[512,1792]{1,0:T(8,128)} %get-tuple-element.89.act_ref.x_ref.b_ref.c_ref, ...), custom_call_target="tpu_custom_call" | custom-call | flops 3145728000 | bytes 16777216 | tf_op jit(solution)/shard_map/ssd_backward/pallas_call | solution.py:436
  352.1 1.9 edge_grads.1
  356.4 4.5 collective-permute-done.12.came_ref
  361.5 20.4 %early_back.1 = (bf16[512,2304]{1,0:T(8,128)(2,1)}, f32[8,1792]{1,0:T(8,128)}, bf16[512,1024]{1,0:T(8,128)(2,1)}, f32[1,1024]{1,0:T(1,128)}) custom-call(f32[512,1024]{1,0:T(8,128)} %unproject.3.base_ref, bf16[512,256]{1,0:T(8,128)(2,1)} %bitcast.69, f32[512,1536]{1,0:T(8,128)} %get-tuple-element.135.dx_ref, f32[512,128]{1,0:T(8,128)} %get-tuple-element.137.db_ref, ...), custom_call_target="tpu_custom_call" | custom-call | flops 2415919104 | bytes 20971520 | tf_op jit(solution)/shard_map/early_back/pallas_call | solution.py:953
  385.1 140.5 %reduce_grads.1 = (bf16[256,2048]{1,0:T(8,128)(2,1)}, bf16[256,1536]{1,0:T(8,128)(2,1)}, bf16[256,512]{1,0:T(8,128)(2,1)}, bf16[512,1024]{1,0:T(8,128)(2,1)}, f32[320,128]{1,0:T(8,128)}) custom-call(bf16[512,1024]{1,0:T(8,128)(2,1)} %get-tuple-element.144.one_ref, bf16[512,1536]{1,0:T(8,128)(2,1)} %multiply_convert_fusion.1.mixed_ref.mix_ref, ...), custom_call_target="tpu_custom_call" | custom-call | flops 6499999744 | bytes 31457280 | tf_op jit(solution)/shard_map/reduce_grads/pallas_call | solution.py:1422
  531.8 4.5 finish.1
  539.0 4.2 convert_element_type.75
  (121 shorter events, 36.7 us)
Async XLA Ops:
  7.2 6.2 %copy-start.12 = (bf16[256,24]{0,1:T(8,128)(2,1)S(1)}, bf16[256,24]{0,1:T(8,128)(2,1)}, u32[]{:S(2)}) copy-start(bf16[256,24]{0,1:T(8,128)(2,1)} %param.24) | copy-start | bytes 36868
  7.2 6.3 %copy-start.8 = (bf16[384,1024]{1,0:T(8,128)(2,1)S(1)}, bf16[384,1024]{1,0:T(8,128)(2,1)}, u32[]{:S(2)}) copy-start(bf16[384,1024]{1,0:T(8,128)(2,1)} %param.31) | copy-start | bytes 2359300
  7.2 7.2 %copy-start.14 = (f32[1792]{0:T(1024)S(1)}, f32[1792]{0:T(1024)}, u32[]{:S(2)}) copy-start(f32[1792]{0:T(1024)} %param.26) | copy-start | bytes 21508
  7.2 7.9 %copy-start.9 = (bf16[256,512]{1,0:T(8,128)(2,1)S(1)}, bf16[256,512]{1,0:T(8,128)(2,1)}, u32[]{:S(2)}) copy-start(bf16[256,512]{1,0:T(8,128)(2,1)} %param.32) | copy-start | bytes 786436
  7.2 531.7 %all-reduce.11.cloned.1.call-start = ((), (), s32[]{:S(2)}) async-start(), calls=%async_computation | async-start | bytes 6291456 | tf_op jit(solution)/shard_map/psum | solution.py:2513
  15.1 1.9 copy-start.1
  17.0 68.0 %copy-start.16 = (f32[24]{0:T(128)S(1)}, f32[24]{0:T(128)}, u32[]{:S(2)}) copy-start(f32[24]{0:T(128)} %param.29) | copy-start | bytes 292
  17.0 68.7 %copy-start.17 = (f32[24]{0:T(128)S(1)}, f32[24]{0:T(128)}, u32[]{:S(2)}) copy-start(f32[24]{0:T(128)} %param.28) | copy-start | bytes 292
  17.0 68.7 %copy-start.18 = (f32[24]{0:T(128)S(1)}, f32[24]{0:T(128)}, u32[]{:S(2)}) copy-start(f32[24]{0:T(128)} %param.27) | copy-start | bytes 292
  82.9 74.1 %collective-permute-start = (bf16[256,4096]{1,0:T(8,128)(2,1)}, bf16[256,4096]{1,0:T(8,128)(2,1)}, u32[]{:S(2)}, u32[]{:S(2)}) collective-permute-start(bf16[256,4096]{1,0:T(8,128)(2,1)} %refs_4_), channel_id=1, source_target_pairs={{0,2},{1,3},{2,0},{3,1},{4,6},{5,7},{6,4},{7,5},{8,10},{9,11},{10,... | collective-permute-start | bytes 6291464 | tf_op jit(solution)/shard_map/ppermute | solution.py:1091
  83.4 82.4 %collective-permute-start.1 = (bf16[256,4096]{1,0:T(8,128)(2,1)}, bf16[256,4096]{1,0:T(8,128)(2,1)}, u32[]{:S(2)}, u32[]{:S(2)}) collective-permute-start(bf16[256,4096]{1,0:T(8,128)(2,1)} %refs_4_), channel_id=1, source_target_pairs={{0,1},{1,0},{2,3},{3,2},{4,5},{5,4},{6,7},{7,6},{8,9},{9,8},{10,11... | collective-permute-start | bytes 6291464 | tf_op jit(solution)/shard_map/ppermute | solution.py:1091
  83.4 74.0 %collective-permute-start.3 = (bf16[512,1024]{1,0:T(8,128)(2,1)}, bf16[512,1024]{1,0:T(8,128)(2,1)}, u32[]{:S(2)}, u32[]{:S(2)}) collective-permute-start(bf16[512,1024]{1,0:T(8,128)(2,1)} %refs_8_), channel_id=1, source_target_pairs={{0,2},{1,3},{2,0},{3,1},{4,6},{5,7},{6,4},{7,5},{8,10},{9,11},{10,... | collective-permute-start | bytes 3145736 | tf_op jit(solution)/shard_map/ppermute | solution.py:1091
  151.7 3.8 copy-start.11
  157.0 8.9 %collective-permute-start.2 = (bf16[256,4096]{1,0:T(8,128)(2,1)}, bf16[256,4096]{1,0:T(8,128)(2,1)}, u32[]{:S(2)}, u32[]{:S(2)}) collective-permute-start(bf16[256,4096]{1,0:T(8,128)(2,1)} %collective-permute-done.refs_1_.refs_5_), channel_id=1, source_target_pairs={{0,1},{1,0},{2,3},{3,2},{4,5},{5,4},{6,7},{7,6},{8,9},{9,8},{10,11... | collective-permute-start | bytes 6291464 | tf_op jit(solution)/shard_map/ppermute | solution.py:1091
  157.0 8.9 %collective-permute-start.4 = (bf16[512,1024]{1,0:T(8,128)(2,1)}, bf16[512,1024]{1,0:T(8,128)(2,1)}, u32[]{:S(2)}, u32[]{:S(2)}) collective-permute-start(bf16[512,1024]{1,0:T(8,128)(2,1)} %refs_8_), channel_id=1, source_target_pairs={{0,1},{1,0},{2,3},{3,2},{4,5},{5,4},{6,7},{7,6},{8,9},{9,8},{10,11... | collective-permute-start | bytes 3145736 | tf_op jit(solution)/shard_map/ppermute | solution.py:1091
  157.5 8.4 %collective-permute-start.5 = (bf16[512,1024]{1,0:T(8,128)(2,1)}, bf16[512,1024]{1,0:T(8,128)(2,1)}, u32[]{:S(2)}, u32[]{:S(2)}) collective-permute-start(bf16[512,1024]{1,0:T(8,128)(2,1)} %collective-permute-done.3.refs_9_), channel_id=1, source_target_pairs={{0,1},{1,0},{2,3},{3,2},{4,5},{5,4},{6,7},{7,6},{8,9},{9,8},{10,11... | collective-permute-start | bytes 3145736 | tf_op jit(solution)/shard_map/ppermute | solution.py:1091
  200.4 17.5 %collective-permute-start.6 = (bf16[512,4096]{1,0:T(8,128)(2,1)}, bf16[512,4096]{1,0:T(8,128)(2,1)}, u32[]{:S(2)}, u32[]{:S(2)}) collective-permute-start(bf16[512,4096]{1,0:T(8,128)(2,1)} %block_grads.4), channel_id=1, source_target_pairs={{0,1},{1,0},{2,3},{3,2},{4,5},{5,4},{6,7},{7,6},{8,9},{9,8},{10,11... | collective-permute-start | bytes 12582920 | tf_op jit(solution)/shard_map/ppermute | solution.py:1091
  205.1 7.6 %collective-permute-start.7 = (bf16[1024,1024]{1,0:T(8,128)(2,1)}, bf16[1024,1024]{1,0:T(8,128)(2,1)}, u32[]{:S(2)}, u32[]{:S(2)}) collective-permute-start(bf16[1024,1024]{1,0:T(8,128)(2,1)} %block_grads.5), channel_id=1, source_target_pairs={{0,1},{1,0},{2,3},{3,2},{4,5},{5,4},{6,7},{7,6},{8,9},{9,8},{10,11... | collective-permute-start | bytes 6291464 | tf_op jit(solution)/shard_map/ppermute | solution.py:1091
  217.3 84.9 %collective-permute-start.9 = (bf16[512,1024]{1,0:T(8,128)(2,1)}, bf16[512,1024]{1,0:T(8,128)(2,1)}, u32[]{:S(2)}, u32[]{:S(2)}) collective-permute-start(bf16[512,1024]{1,0:T(8,128)(2,1)} %get-tuple-element.118), channel_id=1, source_target_pairs={{0,2},{1,3},{2,0},{3,1},{4,6},{5,7},{6,4},{7,5},{8,10},{9,11},{10,... | collective-permute-start | bytes 3145736 | tf_op jit(solution)/shard_map/ppermute | solution.py:1091
  226.9 75.3 %collective-permute-start.8 = (bf16[256,4096]{1,0:T(8,128)(2,1)}, bf16[256,4096]{1,0:T(8,128)(2,1)}, u32[]{:S(2)}, u32[]{:S(2)}) collective-permute-start(bf16[256,4096]{1,0:T(8,128)(2,1)} %get-tuple-element.116), channel_id=1, source_target_pairs={{0,2},{1,3},{2,0},{3,1},{4,6},{5,7},{6,4},{7,5},{8,10},{9,11},{10,... | collective-permute-start | bytes 6291464 | tf_op jit(solution)/shard_map/ppermute | solution.py:1091
  228.3 2.8 copy-start
  228.3 3.8 copy-start.2
  293.7 8.4 %copy-start.3 = (bf16[256,4096]{1,0:T(8,128)(2,1)S(1)}, bf16[256,4096]{1,0:T(8,128)(2,1)}, u32[]{:S(2)}) copy-start(bf16[256,4096]{1,0:T(8,128)(2,1)} %get-tuple-element.120) | copy-start | bytes 6291460
  297.0 24.0 %collective-permute-start.10 = (bf16[2,2,256,256]{3,2,1,0:T(8,128)(2,1)S(1)}, bf16[2,2,256,256]{3,2,1,0:T(8,128)(2,1)S(1)}, u32[]{:S(2)}, u32[]{:S(2)}) collective-permute-start(bf16[2,2,256,256]{3,2,1,0:T(8,128)(2,1)S(1)} %slice.85), channel_id=1, source_target_pairs={{0,8},{4,12},{8,0},{12,4},{16,24},{20,28},{24,16},{28,20},{1,9},{5... | collective-permute-start | bytes 1572872 | tf_op jit(solution)/shard_map/ppermute | solution.py:1091
  302.2 3.8 copy-start.5
  316.3 4.7 copy-start.6
  321.1 34.4 %collective-permute-start.11 = (bf16[1,2,256,256]{3,2,1,0:T(8,128)(2,1)S(1)}, bf16[1,2,256,256]{3,2,1,0:T(8,128)(2,1)S(1)}, u32[]{:S(2)}, u32[]{:S(2)}) collective-permute-start(bf16[1,2,256,256]{3,2,1,0:T(8,128)(2,1)S(1)} %slice.109), channel_id=1, source_target_pairs={{0,16},{4,20},{8,24},{12,28},{16,0},{20,4},{24,8},{28,12},{1,17},{... | collective-permute-start | bytes 786440 | tf_op jit(solution)/shard_map/ppermute | solution.py:1091
  325.4 25.0 %copy-start.7 = (bf16[512,1024]{1,0:T(8,128)(2,1)S(1)}, bf16[512,1024]{1,0:T(8,128)(2,1)}, u32[]{:S(2)}) copy-start(bf16[512,1024]{1,0:T(8,128)(2,1)} %get-tuple-element.144.one_ref) | copy-start | bytes 3145732
  352.1 3.4 copy-start.13
  354.0 6.9 %collective-permute-start.12 = (f32[16,1792]{1,0:T(8,128)}, f32[16,1792]{1,0:T(8,128)S(1)}, u32[]{:S(2)}, u32[]{:S(2)}) collective-permute-start(f32[16,1792]{1,0:T(8,128)} %edge_grads.1), channel_id=1, source_target_pairs={{4,0},{8,4},{12,8},{16,12},{20,16},{24,20},{28,24},{5,1},{9,5},{13... | collective-permute-start | bytes 344072 | tf_op jit(solution)/shard_map/ppermute | solution.py:1087
  361.5 22.9 %copy-start.15 = (f32[1,1024]{1,0:T(1,128)S(1)}, f32[1,1024]{1,0:T(1,128)}, u32[]{:S(2)}) copy-start(f32[1,1024]{1,0:T(1,128)} %get-tuple-element.149) | copy-start | bytes 12292
  539.0 4.2 copy-start.4
  (2 other events, 1.3 us)
Sparse Core Ops, SparseCore 0:
  308.7 160.8 all-reduce.10

commit v7 on v6

--- a/solution.py
+++ b/solution.py
@@ -538,13 +538,14 @@
     ]
 
 
-def unproject_kernel(base_ref, grad_ref, *refs):
-    *weights, out_ref = refs
+def unproject_kernel(has_base, *refs):
+    base_ref = refs[0] if has_base else None
+    grad_ref, *weights, out_ref = refs[1:] if has_base else refs
     size = weights[0].shape[0]
 
     @pl.when(pl.program_id(0) == 0)
     def _():
-        out_ref[...] = base_ref[...]
+        out_ref[...] = base_ref[...] if has_base else jnp.zeros(out_ref.shape, F32)
 
     for step, weight in zip(NEAR, weights):
         out_ref[:, near_at(step, size)] += mat_right_t(grad_ref[...], weight[...])
@@ -555,9 +556,10 @@
     size = weights[0].shape[0]
     whole = pl.BlockSpec((tokens, 4 * size), lambda i: (0, 0))
     return pl.pallas_call(
-        unproject_kernel,
+        functools.partial(unproject_kernel, base is not None),
         grid=(columns // tile,),
-        in_specs=[whole, pl.BlockSpec((tokens, tile), lambda i: (0, i))]
+        in_specs=([] if base is None else [whole])
+        + [pl.BlockSpec((tokens, tile), lambda i: (0, i))]
         + (specs or [pl.BlockSpec((size, tile), lambda i: (0, i))] * 4),
         out_specs=whole,
         out_shape=jax.ShapeDtypeStruct((tokens, 4 * size), F32),
@@ -568,7 +570,7 @@
             transcendentals=0,
         ),
         name="unproject",
-    )(base, grad, *weights)
+    )(*([] if base is None else [base]), grad, *weights)
 
 
 def out_proj_kernel(
@@ -1055,30 +1057,63 @@
 
 
 def finish_kernel(
-    early_ref, gate_ref, mix_ref, q_low_ref, in_ref, q_ref, kv_ref, out_ref, o_ref
+    early_ref,
+    gate_ref,
+    out_low,
+    o_low,
+    q_low,
+    gu_low,
+    down_low,
+    in_ref,
+    q_ref,
+    kv_ref,
+    out_ref,
+    o_ref,
+    gu_ref,
+    down_ref,
 ):
     kv_width = kv_ref.shape[1]
     gate = gate_ref.shape[1]
     in_ref[:, :gate] = gate_ref[...].astype(F32)
     in_ref[:, gate:] = early_ref[:, kv_width:].astype(F32)
-    q_ref[...] = q_low_ref[...].astype(F32)
     kv_ref[...] = early_ref[:, :kv_width].astype(F32)
-    split = out_ref.shape[0]
-    out_ref[...] = mix_ref[:split].astype(F32)
-    o_ref[...] = mix_ref[split:].astype(F32)
-
-
-def finish(early, gate, mix, q, shapes):
-    vmem = pl.BlockSpec(memory_space=pltpu.VMEM)
+    for low, target in (
+        (q_low, q_ref),
+        (out_low, out_ref),
+        (o_low, o_ref),
+        (gu_low, gu_ref),
+        (down_low, down_ref),
+    ):
+        target[...] = low[...].astype(F32)
+
+
+FINISH_STEPS = 4
+
+
+def finish(early, gate, mix, q, gu, down, shapes):
+    def rows_of(shape, skip=0):
+        size = shape[0] // FINISH_STEPS
+        return pl.BlockSpec((size, shape[1]), lambda i: (skip // size + i, 0))
+
+    out_shape, o_shape = shapes[3], shapes[4]
     return pl.pallas_call(
         finish_kernel,
-        in_specs=[vmem] * 4,
-        out_specs=[vmem] * 5,
+        grid=(FINISH_STEPS,),
+        in_specs=[
+            rows_of(early.shape),
+            rows_of(gate.shape),
+            rows_of(out_shape),
+            rows_of(o_shape, out_shape[0]),
+            rows_of(q.shape),
+            rows_of(gu.shape),
+            rows_of(down.shape),
+        ],
+        out_specs=[rows_of(shape) for shape in shapes],
         out_shape=[jax.ShapeDtypeStruct(shape, F32) for shape in shapes],
         compiler_params=pltpu.CompilerParams(vmem_limit_bytes=KERNEL_VMEM),
-        cost_estimate=pl.CostEstimate(flops=MIB, bytes_accessed=10 * MIB, transcendentals=0),
+        cost_estimate=pl.CostEstimate(flops=MIB, bytes_accessed=20 * MIB, transcendentals=0),
         name="finish",
-    )(early, gate, mix, q)
+    )(early, gate, mix, mix, q, gu, down)
 
 
 def passed_along(block, axis, distance):
@@ -2448,7 +2483,7 @@
     grad_gate_z = after(grad_gate_z.astype(BF16), parts)
     dq_rows = dq_t.T
     grad_normed = unproject(
-        jnp.zeros((tokens, features), F32),
+        None,
         grad_gate_z,
         [early_shard] + [early_others] * 3,
         768,
@@ -2541,14 +2576,27 @@
         branch,
         packed,
     )
-    in_sum, q_sum, kv_sum, out_sum, o_sum = finish(
+    in_sum, q_sum, kv_sum, out_sum, o_sum, gu_sum, down_sum = finish(
         early_sum,
         gate_sum,
         mix_sum,
         q_sum,
-        [w.shape for w in (in_weight, q_weight, kv_weight, out_weight, o_weight)],
-    )
-    totals_w = [in_sum, out_sum, q_sum, kv_sum, o_sum, gu_sum.astype(F32), down_sum.astype(F32)]
+        gu_sum,
+        down_sum,
+        [
+            w.shape
+            for w in (
+                in_weight,
+                q_weight,
+                kv_weight,
+                out_weight,
+                o_weight,
+                gu_weight,
+                down_weight,
+            )
+        ],
+    )
+    totals_w = [in_sum, out_sum, q_sum, kv_sum, o_sum, gu_sum, down_sum]
     small = []
     place = 0
     for piece in pieces:

time: 562 us -> 559 us (level)
  other arithmetic: 28 us -> 22.3 us
    convert_element_type x2 -> x0, other arithmetic: 5.75 us -> none  [the longest x1 4.19 us: local(): gu_sum.astype(F32)]
where the time goes in v7:
time: 559 us; the launch traced here: 549 us
  Pallas kernels  464 us (83%)
  local copies, waits for them, and re-layouts  26.8 us (5%)
  other arithmetic  22.3 us (4%)
  starting transfers between devices  15.6 us (3%)
  between operations  14.9 us (3%)
    pallas_call x1, Pallas kernels, reduce_grads(): pl.pallas_call(functools.partial(grads_kernel, count, split, early_units,...  142 us
    pallas_call x1, Pallas kernels, front(): pl.pallas_call(functools.partial(front_kernel, count, channels // EARLY_T...  65.9 us
    pallas_call x1, Pallas kernels, mix_backward(): pl.pallas_call(functools.partial(mix_backward_kernel, count), in_specs=[v...  51.2 us
    pallas_call x1, Pallas kernels, mix_forward(): pl.pallas_call(functools.partial(mix_forward_kernel, count), in_specs=[vm...  47.6 us
    pallas_call x4, Pallas kernels, block_grads(): pl.pallas_call(functools.partial(block_grads_kernel, steps), grid=(column...  26.7 us
    pallas_call x1, Pallas kernels, mlp_both(): pl.pallas_call(mlp_kernel, grid_spec=pltpu.PrefetchScalarGridSpec(num_sca...  25.7 us
    pallas_call x1, Pallas kernels, ssd_backward(): pl.pallas_call(ssd_backward_kernel, grid=(count, NGROUP), in_specs=specs...  25 us
    pallas_call x1, Pallas kernels, early_back(): pl.pallas_call(functools.partial(early_back_kernel, count), grid=(tiles,)...  20.7 us
  transfers between devices with their start and end apart: 14, of which 1 were waited for; matrix products, arithmetic and copies ran while one was open for 7% of the time, Pallas kernels for 65%

profile of v7, /device:TPU:0, one launch (start us, length us, event | category | flops | bytes accessed | tf_op | source)
XLA Modules:
  0.0 549.2 jit_solution(8641855304842016822)
XLA Ops:
  15.1 1.9 constant_dynamic-update-slice_fusion.2.tall_ref.own_ref
  17.0 65.9 %front.1 = (bf16[512,1024]{1,0:T(8,128)(2,1)}, bf16[3,256,4352]{2,1,0:T(8,128)(2,1)}, bf16[3,512,1024]{2,1,0:T(8,128)(2,1)}, f32[512,1792]{1,0:T(8,128)}, f32[16...) custom-call(bf16[512,1024]{1,0:T(8,128)(2,1)} %bitcast.70, ...), custom_call_target="tpu_custom_call" | custom-call | flops 4563402752 | bytes 20971520 | tf_op jit(solution)/shard_map/front/pallas_call | solution.py:2297
  83.4 1.5 collective-permute-start.3
  86.3 7.0 %ssd_state.1 = (f32[512,128]{1,0:T(8,128)}, f32[512,128]{1,0:T(8,128)}, f32[2,128,256]{2,1,0:T(8,128)}, f32[512,128]{1,0:T(8,128)}, f32[2,8,128]{2,1,0:T(8,128)}, /*index=5*/f32[2,1536,128]{2,1,0:T(8,128)}) custom-call(f32[512,1792]{1,0:T(8,128)} %get-tuple-element.91.act_ref.x_ref.b_ref.c_ref, f32[512,256]{1,0:T(8,128)} %get-tuple-element.92.dt_ref, ...), custom_call_target="tpu_custom_call" | custom-call | flops 1000000000 | bytes 8388608 | tf_op jit(solution)/shard_map/ssd_state/pallas_call | solution.py:162
  93.9 47.6 %mix_forward.1 = (bf16[512,512]{1,0:T(8,128)(2,1)}, f32[2,8,256]{2,1,0:T(8,128)}, bf16[8,2,256,256]{3,2,1,0:T(8,128)(2,1)}, bf16[2,1536,128]{2,1,0:T(8,128)(2,1)}, f32[8,2,8,128]{3,2,1,0:T(8,128)}) custom-call(s32[2,8,256]{2,1,0:T(8,128)} %broadcast_in_dim.54.start_ref, bf16[512,512]{1,0:T(8,128)(2,1)} %get-tuple-element.96.q_ref, ...), custom_call_target="tpu_custom_call" | custom-call | flops 8388608000 | bytes 4194304 | tf_op jit(solution)/shard_map/mix_forward/pallas_call | solution.py:1776
  141.5 10.2 %ssd_forward.1.y_ref = f32[512,1536]{1,0:T(8,128)} custom-call(f32[512,1792]{1,0:T(8,128)} %get-tuple-element.91.act_ref.x_ref.b_ref.c_ref, f32[512,1792]{1,0:T(8,128)} %get-tuple-element.91.act_ref.x_ref.b_ref.c_ref, f32[512,1792]{1,0:T(8,128)} %get-tuple-element.91.act_ref.x_ref.b_ref.c_ref, f32[512,128]{1,0:T(8,128)} %get-tuple-element.93.step_ref, ...), custom_call_target="tpu_custom_call" | custom-call | flops 1258291200 | bytes 8388608 | tf_op jit(solution)/shard_map/ssd_forward/pallas_call | solution.py:396
  151.7 3.8 multiply_reduce_fusion.2
  155.5 1.5 multiply_convert_fusion.1.mixed_ref.mix_ref
  157.5 8.4 %out_project.1 = (f32[512,1024]{1,0:T(8,128)}, bf16[512,1024]{1,0:T(8,128)(2,1)}) custom-call(bf16[512,1024]{1,0:T(8,128)(2,1)} %bitcast.71, bf16[512,1536]{1,0:T(8,128)(2,1)} %multiply_convert_fusion.1.mixed_ref.mix_ref, bf16[512,512]{1,0:T(8,128)(2,1)} %get-tuple-element.102.heads_ref.attended_ref, f32[1,1024]{1,0:T(1,128)} %bitcast.80, ...), custom_call_target="tpu_custom_call" | custom-call | flops 2147483648 | bytes 12582912 | tf_op jit(solution)/shard_map/out_project/pallas_call | solution.py:593
  165.9 25.7 %mlp_both.1 = (bf16[512,1024]{1,0:T(8,128)(2,1)}, f32[512,1024]{1,0:T(8,128)}, bf16[512,1024]{1,0:T(8,128)(2,1)}, f32[1,1024]{1,0:T(1,128)}, bf16[512,2048]{1,0:T(8,128)(2,1)}, /*index=5*/bf16[2,512,2048]{2,1,0:T(8,128)(2,1)}) custom-call(s32[1]{0:T(128)} %bitcast.place_ref, bf16[512,1024]{1,0:T(8,128)(2,1)} %get-tuple-element.117.normed_ref.left_ref, ...), custom_call_target="tpu_custom_call" | custom-call | flops 12884901888 | bytes 31457280 | tf_op jit(solution)/shard_map/mlp_both/pallas_call | solution.py:713
  191.6 8.8 %block_grads.4 = bf16[512,4096]{1,0:T(8,128)(2,1)} custom-call(bf16[512,1024]{1,0:T(8,128)(2,1)} %get-tuple-element.117.normed_ref.left_ref, bf16[2,512,2048]{2,1,0:T(8,128)(2,1)} %get-tuple-element.112.right_ref), custom_call_target="tpu_custom_call" | custom-call | flops 2147483648 | bytes 6291456 | tf_op jit(solution)/shard_map/block_grads/pallas_call | solution.py:1039
  200.9 4.3 block_grads.5
  205.2 7.5 %out_unproject.1 = (f32[512,1536]{1,0:T(8,128)}, bf16[512,512]{1,0:T(8,128)(2,1)}) custom-call(bf16[512,1024]{1,0:T(8,128)(2,1)} %get-tuple-element.114.branch_ref, bf16[512,1024]{1,0:T(8,128)(2,1)} %constant_dynamic-update-slice_fusion.2.tall_ref.own_ref, bf16[3,512,1024]{2,1,0:T(8,128)(2,1)} %get-tuple-element.103.others_ref), custom_call_target="tpu_custom_call" | custom-call | flops 2147483648 | bytes 12582912 | tf_op jit(solution)/shard_map/out_unproject/pallas_call | solution.py:620
  212.7 4.5 block_grads.7
  217.9 9.1 %block_grads.6 = (bf16[256,4096]{1,0:T(8,128)(2,1)}, bf16[256,4096]{1,0:T(8,128)(2,1)}) custom-call(bf16[512,1024]{1,0:T(8,128)(2,1)} %get-tuple-element.117.normed_ref.left_ref, bf16[2,512,2048]{2,1,0:T(8,128)(2,1)} %get-tuple-element.112.right_ref, bf16[512,4096]{1,0:T(8,128)(2,1)} %collective-permute-done.6.refs_0_), custom_call_target="tpu_custom_call" | custom-call | flops 2147483648 | bytes 6291456 | tf_op jit(solution)/shard_map/block_grads/pallas_call | solution.py:1039
  228.4 2.8 multiply_reduce_fusion
  232.2 5.1 multiply_multiply_fusion
  237.3 5.3 state_grad.1.state_ref
  242.7 51.2 %mix_backward.1 = (bf16[512,512]{1,0:T(8,128)(2,1)}, bf16[4,2,256,256]{3,2,1,0:T(8,128)(2,1)}, bf16[2,1536,128]{2,1,0:T(8,128)(2,1)}) custom-call(s32[2,8,256]{2,1,0:T(8,128)} %broadcast_in_dim.54.start_ref, bf16[512,512]{1,0:T(8,128)(2,1)} %get-tuple-element.96.q_ref, bf16[8,2,256,256]{3,2,1,0:T(8,128)(2,1)} %get-tuple-element.123.table_ref, ...), custom_call_target="tpu_custom_call" | custom-call | flops 16777216000 | bytes 8388608 | tf_op jit(solution)/shard_map/mix_backward/pallas_call | solution.py:1939
  293.9 2.2 copy.61
  297.2 5.1 collective-permute-start.10
  302.3 3.8 add_convert_fusion
  306.1 2.6 add_convert_fusion.1
  308.7 5.4 unproject.2.refs_0_
  314.1 5.0 unproject.3.base_ref
  319.2 4.0 collective-permute-start.11
  323.2 25.0 %ssd_backward.1 = (f32[512,1536]{1,0:T(8,128)}, f32[512,128]{1,0:T(8,128)}, f32[512,128]{1,0:T(8,128)}, bf16[512,256]{1,0:T(8,128)(2,1)}, f32[2,8,128]{2,1,0:T(8,128)}) custom-call(f32[512,1792]{1,0:T(8,128)} %get-tuple-element.91.act_ref.x_ref.b_ref.c_ref, f32[512,1792]{1,0:T(8,128)} %get-tuple-element.91.act_ref.x_ref.b_ref.c_ref, ...), custom_call_target="tpu_custom_call" | custom-call | flops 3145728000 | bytes 16777216 | tf_op jit(solution)/shard_map/ssd_backward/pallas_call | solution.py:436
  349.9 1.9 edge_grads.1
  353.9 4.8 collective-permute-done.12.came_ref
  359.3 20.7 %early_back.1 = (bf16[512,2304]{1,0:T(8,128)(2,1)}, f32[8,1792]{1,0:T(8,128)}, bf16[512,1024]{1,0:T(8,128)(2,1)}, f32[1,1024]{1,0:T(1,128)}) custom-call(f32[512,1024]{1,0:T(8,128)} %unproject.3.base_ref, bf16[512,256]{1,0:T(8,128)(2,1)} %bitcast.69, f32[512,1536]{1,0:T(8,128)} %get-tuple-element.137.dx_ref, f32[512,128]{1,0:T(8,128)} %get-tuple-element.139.db_ref, ...), custom_call_target="tpu_custom_call" | custom-call | flops 2415919104 | bytes 20971520 | tf_op jit(solution)/shard_map/early_back/pallas_call | solution.py:955
  383.2 142.3 %reduce_grads.1 = (bf16[256,2048]{1,0:T(8,128)(2,1)}, bf16[256,1536]{1,0:T(8,128)(2,1)}, bf16[256,512]{1,0:T(8,128)(2,1)}, bf16[512,1024]{1,0:T(8,128)(2,1)}, f32[320,128]{1,0:T(8,128)}) custom-call(bf16[512,1024]{1,0:T(8,128)(2,1)} %get-tuple-element.146.one_ref, bf16[512,1536]{1,0:T(8,128)(2,1)} %multiply_convert_fusion.1.mixed_ref.mix_ref, ...), custom_call_target="tpu_custom_call" | custom-call | flops 6499999744 | bytes 31457280 | tf_op jit(solution)/shard_map/reduce_grads/pallas_call | solution.py:1457
  534.3 7.6 %finish.1 = (f32[256,3328]{1,0:T(8,128)}, f32[256,512]{1,0:T(8,128)}, f32[256,256]{1,0:T(8,128)}, f32[384,1024]{1,0:T(8,128)}, f32[128,1024]{1,0:T(8,128)}, /*index=5*/f32[256,4096]{1,0:T(8,128)}, f32[512,1024]{1,0:T(8,128)}) custom-call(bf16[256,2048]{1,0:T(8,128)(2,1)} %get-tuple-element.153.early_ref, bf16[256,1536]{1,0:T(8,128)(2,1)} %get-tuple-element.154.gate_ref, ...), custom_call_target="tpu_custom_call" | custom-call | flops 1048576 | bytes 20971520 | tf_op jit(solution)/shard_map/finish/pallas_call | solution.py:1099
  (116 shorter events, 31.8 us)
Async XLA Ops:
  7.2 6.2 %copy-start.11 = (bf16[256,24]{0,1:T(8,128)(2,1)S(1)}, bf16[256,24]{0,1:T(8,128)(2,1)}, u32[]{:S(2)}) copy-start(bf16[256,24]{0,1:T(8,128)(2,1)} %param.24) | copy-start | bytes 36868
  7.2 6.3 %copy-start.7 = (bf16[384,1024]{1,0:T(8,128)(2,1)S(1)}, bf16[384,1024]{1,0:T(8,128)(2,1)}, u32[]{:S(2)}) copy-start(bf16[384,1024]{1,0:T(8,128)(2,1)} %param.31) | copy-start | bytes 2359300
  7.2 7.2 %copy-start.13 = (f32[1792]{0:T(1024)S(1)}, f32[1792]{0:T(1024)}, u32[]{:S(2)}) copy-start(f32[1792]{0:T(1024)} %param.26) | copy-start | bytes 21508
  7.2 7.9 %copy-start.8 = (bf16[256,512]{1,0:T(8,128)(2,1)S(1)}, bf16[256,512]{1,0:T(8,128)(2,1)}, u32[]{:S(2)}) copy-start(bf16[256,512]{1,0:T(8,128)(2,1)} %param.32) | copy-start | bytes 786436
  7.2 527.1 %all-reduce.11.cloned.1.call-start = ((), (), s32[]{:S(2)}) async-start(), calls=%async_computation | async-start | bytes 6291456 | tf_op jit(solution)/shard_map/psum | solution.py:2548
  15.1 1.9 copy-start.1
  17.0 68.0 %copy-start.15 = (f32[24]{0:T(128)S(1)}, f32[24]{0:T(128)}, u32[]{:S(2)}) copy-start(f32[24]{0:T(128)} %param.29) | copy-start | bytes 292
  17.0 68.8 %copy-start.16 = (f32[24]{0:T(128)S(1)}, f32[24]{0:T(128)}, u32[]{:S(2)}) copy-start(f32[24]{0:T(128)} %param.28) | copy-start | bytes 292
  17.0 68.8 %copy-start.17 = (f32[24]{0:T(128)S(1)}, f32[24]{0:T(128)}, u32[]{:S(2)}) copy-start(f32[24]{0:T(128)} %param.27) | copy-start | bytes 292
  82.9 74.1 %collective-permute-start = (bf16[256,4096]{1,0:T(8,128)(2,1)}, bf16[256,4096]{1,0:T(8,128)(2,1)}, u32[]{:S(2)}, u32[]{:S(2)}) collective-permute-start(bf16[256,4096]{1,0:T(8,128)(2,1)} %refs_4_), channel_id=1, source_target_pairs={{0,2},{1,3},{2,0},{3,1},{4,6},{5,7},{6,4},{7,5},{8,10},{9,11},{10,... | collective-permute-start | bytes 6291464 | tf_op jit(solution)/shard_map/ppermute | solution.py:1126
  83.4 82.4 %collective-permute-start.1 = (bf16[256,4096]{1,0:T(8,128)(2,1)}, bf16[256,4096]{1,0:T(8,128)(2,1)}, u32[]{:S(2)}, u32[]{:S(2)}) collective-permute-start(bf16[256,4096]{1,0:T(8,128)(2,1)} %refs_4_), channel_id=1, source_target_pairs={{0,1},{1,0},{2,3},{3,2},{4,5},{5,4},{6,7},{7,6},{8,9},{9,8},{10,11... | collective-permute-start | bytes 6291464 | tf_op jit(solution)/shard_map/ppermute | solution.py:1126
  83.4 74.1 %collective-permute-start.3 = (bf16[512,1024]{1,0:T(8,128)(2,1)}, bf16[512,1024]{1,0:T(8,128)(2,1)}, u32[]{:S(2)}, u32[]{:S(2)}) collective-permute-start(bf16[512,1024]{1,0:T(8,128)(2,1)} %refs_8_), channel_id=1, source_target_pairs={{0,2},{1,3},{2,0},{3,1},{4,6},{5,7},{6,4},{7,5},{8,10},{9,11},{10,... | collective-permute-start | bytes 3145736 | tf_op jit(solution)/shard_map/ppermute | solution.py:1126
  151.7 3.8 copy-start.10
  157.0 8.9 %collective-permute-start.2 = (bf16[256,4096]{1,0:T(8,128)(2,1)}, bf16[256,4096]{1,0:T(8,128)(2,1)}, u32[]{:S(2)}, u32[]{:S(2)}) collective-permute-start(bf16[256,4096]{1,0:T(8,128)(2,1)} %collective-permute-done.refs_1_.refs_5_), channel_id=1, source_target_pairs={{0,1},{1,0},{2,3},{3,2},{4,5},{5,4},{6,7},{7,6},{8,9},{9,8},{10,11... | collective-permute-start | bytes 6291464 | tf_op jit(solution)/shard_map/ppermute | solution.py:1126
  157.0 8.9 %collective-permute-start.4 = (bf16[512,1024]{1,0:T(8,128)(2,1)}, bf16[512,1024]{1,0:T(8,128)(2,1)}, u32[]{:S(2)}, u32[]{:S(2)}) collective-permute-start(bf16[512,1024]{1,0:T(8,128)(2,1)} %refs_8_), channel_id=1, source_target_pairs={{0,1},{1,0},{2,3},{3,2},{4,5},{5,4},{6,7},{7,6},{8,9},{9,8},{10,11... | collective-permute-start | bytes 3145736 | tf_op jit(solution)/shard_map/ppermute | solution.py:1126
  157.5 8.4 %collective-permute-start.5 = (bf16[512,1024]{1,0:T(8,128)(2,1)}, bf16[512,1024]{1,0:T(8,128)(2,1)}, u32[]{:S(2)}, u32[]{:S(2)}) collective-permute-start(bf16[512,1024]{1,0:T(8,128)(2,1)} %collective-permute-done.3.refs_9_), channel_id=1, source_target_pairs={{0,1},{1,0},{2,3},{3,2},{4,5},{5,4},{6,7},{7,6},{8,9},{9,8},{10,11... | collective-permute-start | bytes 3145736 | tf_op jit(solution)/shard_map/ppermute | solution.py:1126
  200.4 17.5 %collective-permute-start.6 = (bf16[512,4096]{1,0:T(8,128)(2,1)}, bf16[512,4096]{1,0:T(8,128)(2,1)}, u32[]{:S(2)}, u32[]{:S(2)}) collective-permute-start(bf16[512,4096]{1,0:T(8,128)(2,1)} %block_grads.4), channel_id=1, source_target_pairs={{0,1},{1,0},{2,3},{3,2},{4,5},{5,4},{6,7},{7,6},{8,9},{9,8},{10,11... | collective-permute-start | bytes 12582920 | tf_op jit(solution)/shard_map/ppermute | solution.py:1126
  205.2 7.6 %collective-permute-start.7 = (bf16[1024,1024]{1,0:T(8,128)(2,1)}, bf16[1024,1024]{1,0:T(8,128)(2,1)}, u32[]{:S(2)}, u32[]{:S(2)}) collective-permute-start(bf16[1024,1024]{1,0:T(8,128)(2,1)} %block_grads.5), channel_id=1, source_target_pairs={{0,1},{1,0},{2,3},{3,2},{4,5},{5,4},{6,7},{7,6},{8,9},{9,8},{10,11... | collective-permute-start | bytes 6291464 | tf_op jit(solution)/shard_map/ppermute | solution.py:1126
  217.3 85.0 %collective-permute-start.9 = (bf16[512,1024]{1,0:T(8,128)(2,1)}, bf16[512,1024]{1,0:T(8,128)(2,1)}, u32[]{:S(2)}, u32[]{:S(2)}) collective-permute-start(bf16[512,1024]{1,0:T(8,128)(2,1)} %get-tuple-element.120), channel_id=1, source_target_pairs={{0,2},{1,3},{2,0},{3,1},{4,6},{5,7},{6,4},{7,5},{8,10},{9,11},{10,... | collective-permute-start | bytes 3145736 | tf_op jit(solution)/shard_map/ppermute | solution.py:1126
  227.0 75.3 %collective-permute-start.8 = (bf16[256,4096]{1,0:T(8,128)(2,1)}, bf16[256,4096]{1,0:T(8,128)(2,1)}, u32[]{:S(2)}, u32[]{:S(2)}) collective-permute-start(bf16[256,4096]{1,0:T(8,128)(2,1)} %get-tuple-element.118), channel_id=1, source_target_pairs={{0,2},{1,3},{2,0},{3,1},{4,6},{5,7},{6,4},{7,5},{8,10},{9,11},{10,... | collective-permute-start | bytes 6291464 | tf_op jit(solution)/shard_map/ppermute | solution.py:1126
  228.4 2.8 copy-start
  228.4 3.8 copy-start.2
  293.9 8.4 %copy-start.3 = (bf16[256,4096]{1,0:T(8,128)(2,1)S(1)}, bf16[256,4096]{1,0:T(8,128)(2,1)}, u32[]{:S(2)}) copy-start(bf16[256,4096]{1,0:T(8,128)(2,1)} %get-tuple-element.122) | copy-start | bytes 6291460
  297.2 21.9 %collective-permute-start.10 = (bf16[2,2,256,256]{3,2,1,0:T(8,128)(2,1)S(1)}, bf16[2,2,256,256]{3,2,1,0:T(8,128)(2,1)S(1)}, u32[]{:S(2)}, u32[]{:S(2)}) collective-permute-start(bf16[2,2,256,256]{3,2,1,0:T(8,128)(2,1)S(1)} %slice.85), channel_id=1, source_target_pairs={{0,8},{4,12},{8,0},{12,4},{16,24},{20,28},{24,16},{28,20},{1,9},{5... | collective-permute-start | bytes 1572872 | tf_op jit(solution)/shard_map/ppermute | solution.py:1126
  302.3 3.8 copy-start.4
  314.1 5.0 copy-start.5
  319.2 33.9 %collective-permute-start.11 = (bf16[1,2,256,256]{3,2,1,0:T(8,128)(2,1)S(1)}, bf16[1,2,256,256]{3,2,1,0:T(8,128)(2,1)S(1)}, u32[]{:S(2)}, u32[]{:S(2)}) collective-permute-start(bf16[1,2,256,256]{3,2,1,0:T(8,128)(2,1)S(1)} %slice.109), channel_id=1, source_target_pairs={{0,16},{4,20},{8,24},{12,28},{16,0},{20,4},{24,8},{28,12},{1,17},{... | collective-permute-start | bytes 786440 | tf_op jit(solution)/shard_map/ppermute | solution.py:1126
  323.2 25.0 %copy-start.6 = (bf16[512,1024]{1,0:T(8,128)(2,1)S(1)}, bf16[512,1024]{1,0:T(8,128)(2,1)}, u32[]{:S(2)}) copy-start(bf16[512,1024]{1,0:T(8,128)(2,1)} %get-tuple-element.146.one_ref) | copy-start | bytes 3145732
  349.9 3.2 copy-start.12
  351.8 6.9 %collective-permute-start.12 = (f32[16,1792]{1,0:T(8,128)}, f32[16,1792]{1,0:T(8,128)S(1)}, u32[]{:S(2)}, u32[]{:S(2)}) collective-permute-start(f32[16,1792]{1,0:T(8,128)} %edge_grads.1), channel_id=1, source_target_pairs={{4,0},{8,4},{12,8},{16,12},{20,16},{24,20},{28,24},{5,1},{9,5},{13... | collective-permute-start | bytes 344072 | tf_op jit(solution)/shard_map/ppermute | solution.py:1122
  359.3 23.1 %copy-start.14 = (f32[1,1024]{1,0:T(1,128)S(1)}, f32[1,1024]{1,0:T(1,128)}, u32[]{:S(2)}) copy-start(f32[1,1024]{1,0:T(1,128)} %get-tuple-element.151) | copy-start | bytes 12292
  382.5 0.7 copy-start.18
  (1 other events, 0.6 us)
Sparse Core Ops, SparseCore 0:
  308.8 160.6 all-reduce.10
